TPU v7x, 32 devices: a whole 2x2x4 slice. The times are simulated.
32 devices in a mesh: dp: 4 (over z), fsdp: 8 (over y, x, core).
Axes of the slice: x: 2, y: 2, z: 4, core: 2. Of those that a mesh axis runs over, the one named last changes fastest.
Arguments:
- inputs: bfloat16 [2048, 8192], P('dp', 'fsdp'), may hold values from -6 to 6
- cotangent: bfloat16 [2, 2048, 1024], P(None, 'dp', 'fsdp'), may hold values from -0.29882812 to 0.29882812
- feedback: float32 [2, 4, 8192, 1024], P(None, 'dp', 'fsdp'), may hold values from -6 to 6
- q_init: float32 [2, 1024, 128], replicated, may hold values from -0.1875 to 0.1875
- factor_ranks: int32 [2], replicated, may hold values from 8 to 128, as said below
Outputs:
- factor_p: float32 [2, 8192, 128], P(None, 'fsdp')
- factor_q: float32 [2, 1024, 128], replicated
- new_error: float32 [2, 4, 8192, 1024], P(None, 'dp', 'fsdp')
Inputs may be any that keep to these rules, and one draw needn't show every extreme that they name: `factor_ranks`: some projection has rank 128.
All inputs are finite; a program needn't handle non-finite values.
Results may differ from a plain program's by a relative error of at most 0.0003.
Values may be sent and summed in bfloat16 or wider, within the bound.
No kernel may reach another device: no remote copies, remote signals or barrier semaphores. Data moves between devices by JAX's collectives and lax.ppermute only.
A program may use at most 64 MiB of HBM per device.

v0:
```python
import jax
import jax.numpy as jnp
from jax import lax
from jax.sharding import PartitionSpec as P

PRECISE = lax.Precision.HIGHEST


def triangle_solve(lower_factor, right_side):
    return jax.scipy.linalg.solve_triangular(lower_factor, right_side, lower=True)


def local(inputs, cotangent, feedback, q_init, factor_ranks):
    rank_width = q_init.shape[2]
    local_grad = jnp.einsum(
        "td,mtk->mdk",
        inputs,
        lax.all_gather(cotangent, "fsdp", axis=2, tiled=True),
        preferred_element_type=jnp.float32,
    )
    full_grad = feedback[:, 0] + local_grad
    rank_mask = (jnp.arange(rank_width)[None, :] < factor_ranks[:, None]).astype(jnp.float32)
    masked_q = q_init * rank_mask[:, None, :]
    left_local = jnp.einsum("mdk,mkr->mdr", full_grad, masked_q, precision=PRECISE)
    left_sum = lax.psum(left_local, "dp")
    gram_local = jnp.einsum("mdr,mds->mrs", left_sum, left_sum, precision=PRECISE)
    gram_matrix = lax.psum(gram_local, "fsdp") + jax.vmap(jnp.diag)(1.0 - rank_mask)
    chol_lower = jnp.linalg.cholesky(gram_matrix)
    solved = jax.vmap(triangle_solve)(chol_lower, jnp.swapaxes(left_sum, 1, 2))
    factor_p = jnp.swapaxes(solved, 1, 2)
    right_local = jnp.einsum("mdk,mdr->mkr", full_grad, factor_p, precision=PRECISE)
    right_rows = lax.psum_scatter(right_local, "fsdp", scatter_dimension=1, tiled=True)
    right_rows = lax.psum(right_rows, "dp")
    factor_q = lax.all_gather(right_rows, "fsdp", axis=1, tiled=True)
    low_rank = jnp.einsum("mdr,mkr->mdk", factor_p, factor_q, precision=PRECISE)
    new_error = (full_grad - low_rank)[:, None]
    return (factor_p, factor_q, new_error)


def solution(mesh):
    placed = (P("dp", "fsdp"), P(None, "dp", "fsdp"), P(None, "dp", "fsdp", None), P(), P())
    return jax.shard_map(
        local,
        mesh=mesh,
        in_specs=placed,
        out_specs=(P(None, "fsdp", None), P(), P(None, "dp", "fsdp", None)),
        check_vma=False,
    )
```

profile of v0, /device:TPU:0, one launch (start us, length us, event | category | flops | bytes accessed | tf_op | source)
XLA Modules:
  0.0 357.2 jit_solution(16133712871157152800)
XLA Ops:
  7.2 0.0 copy-start
  7.2 0.0 all-gather.3.cloned.1.call-start
  7.2 1.9 copy.19
  9.1 0.0 all-gather.3.cloned.1.call-update
  9.1 0.0 copy-start.4
  9.1 0.0 all-reduce.4.cloned.1.call-start
  9.2 8.7 %copy.18 = f32[2,1,1024,1024]{2,3,0,1:T(8,128)} copy(f32[2,1,1024,1024]{3,2,1,0:T(8,128)} %param.7) | data formatting | bytes 16777216 | tf_op args[2]
  17.9 0.0 copy-done.4
  17.9 0.1 compare_convert_fusion
  17.9 0.0 copy-start.3
  17.9 23.2 %all-gather.3.cloned.1.call-done = bf16[2,512,1024]{1,2,0:T(8,128)(2,1)} async-done(((bf16[2,512,128]{1,2,0:T(8,128)(2,1)}), bf16[2,512,1024]{1,2,0:T(8,128)(2,1)}) %all-gather.3.cloned.1.call-update) | async-done | bytes 2097168 | tf_op jit(solution)/shard_map/all_gather | solution.py:18
  41.1 0.0 copy-done
  41.1 6.5 %bitcast_add_fusion = f32[2,1024,1024]{1,2,0:T(8,128)S(1)} fusion(f32[2,1,1024,1024]{2,3,0,1:T(8,128)} %copy.18, bf16[2,512,1024]{1,2,0:T(8,128)(2,1)} %all-gather.3.cloned.1.call-done, bf16[512,1024]{1,0:T(8,128)(2,1)S(1)} %copy-done), kind=kOutput, calls=%fused_computation | convolution fusion | flops 2149580800 | bytes 19922944 | tf_op jit(solution)/shard_map/td,mtk->mdk/dot_general | solution.py:15
  47.6 0.0 copy-start.1
  47.6 3.4 copy-done.1
  51.0 0.0 copy-done.3
  51.0 14.7 %fusion.1 = f32[2,1024,128]{2,1,0:T(8,128)} fusion(f32[2,1024,1024]{1,2,0:T(8,128)S(1)} %bitcast_add_fusion, f32[2,1024,128]{2,1,0:T(8,128)S(1)} %copy-done.3, f32[2,128]{1,0:T(2,128)S(1)} %compare_convert_fusion), kind=kOutput, calls=%fused_computation.3 | convolution fusion | flops 3221487616 | bytes 10486784 | tf_op jit(solution)/shard_map/mdk,mkr->mdr/dot_general | solution.py:24
  65.7 0.0 all-reduce.4.cloned.1.call-update
  65.7 0.0 all-reduce.6.cloned.1.call-start
  65.8 0.1 broadcast_subtract_fusion
  65.8 51.8 %all-reduce.4.cloned.1.call-done = f32[2,1024,128]{2,1,0:T(8,128)} async-done(((f32[2,1024,128]{2,1,0:T(8,128)}), f32[2,1024,128]{2,1,0:T(8,128)}) %all-reduce.4.cloned.1.call-update) | async-done | bytes 1048592 | tf_op jit(solution)/shard_map/psum | solution.py:25
  117.7 4.0 %fusion.7 = f32[2,128,128]{2,1,0:T(8,128)} fusion(f32[2,1024,128]{2,1,0:T(8,128)} %all-reduce.4.cloned.1.call-done), kind=kOutput, calls=%fused_computation.18 | convolution fusion | flops 402653184 | bytes 1179648 | tf_op jit(solution)/shard_map/mdr,mds->mrs/dot_general | solution.py:26
  121.7 0.0 all-reduce.6.cloned.1.call-update
  121.7 0.0 reduce-scatter.2.cloned.1.call-start
  121.8 52.4 %all-reduce.6.cloned.1.call-done = f32[2,128,128]{2,1,0:T(8,128)} async-done(((f32[2,128,128]{2,1,0:T(8,128)}), f32[2,128,128]{2,1,0:T(8,128)}) %all-reduce.6.cloned.1.call-update) | async-done | bytes 131088 | tf_op jit(solution)/shard_map/psum | solution.py:27
  174.2 1.0 select_add_fusion
  175.2 0.1 copy.22
  175.3 1.0 fusion.6
  176.3 23.5 %custom-call.8 = f32[2,128,128]{2,1,0:T(8,128)S(1)} custom-call(f32[2,128,128]{2,1,0:T(8,128)S(1)} %fusion.6), custom_call_target="Cholesky" | custom-call | tf_op jit(solution)/shard_map/jit(cholesky)/cholesky | solution.py:28
  199.8 0.1 compare_reduce_fusion
  199.9 0.1 select_bitcast_fusion
  200.0 19.7 %custom-call.9 = f32[2,1,128,128]{2,3,1,0:T(8,128)S(1)} custom-call(f32[2,1,128,128]{3,2,1,0:T(8,128)S(1)} %select_bitcast_fusion), custom_call_target="InvertDiagBlocksLowerTriangular" | custom-call | tf_op jit(solution)/shard_map/vmap(jit(_solve_triangular))/triangular_solve | solution.py:10
  219.7 2.3 fusion.4
  222.0 9.8 %fusion.8 = f32[2,1024,128]{2,1,0:T(8,128)} fusion(f32[2,1024,1024]{1,2,0:T(8,128)} %copy-done.1, f32[2,128,1024]{2,1,0:T(8,128)S(1)} %fusion.4), kind=kOutput, calls=%fused_computation.19 | convolution fusion | flops 3221225472 | bytes 10485760 | tf_op jit(solution)/shard_map/mdk,mdr->mkr/dot_general | solution.py:31
  231.8 0.0 reduce-scatter.2.cloned.1.call-update
  231.9 0.0 all-reduce.8.cloned.1.call-start
  231.9 35.5 %reduce-scatter.2.cloned.1.call-done = f32[2,128,128]{2,1,0:T(8,128)} async-done(((f32[2,1024,128]{2,1,0:T(8,128)}), f32[2,128,128]{2,1,0:T(8,128)}) %reduce-scatter.2.cloned.1.call-update) | async-done | bytes 131088 | tf_op jit(solution)/shard_map/reduce_scatter | solution.py:32
  267.4 0.0 all-reduce.8.cloned.1.call-update
  267.5 0.0 all-gather.5.cloned.1.call-start
  267.5 36.5 %all-reduce.8.cloned.1.call-done = f32[2,128,128]{2,1,0:T(8,128)} async-done(((f32[2,128,128]{2,1,0:T(8,128)}), f32[2,128,128]{2,1,0:T(8,128)}) %all-reduce.8.cloned.1.call-update) | async-done | bytes 131088 | tf_op jit(solution)/shard_map/psum | solution.py:33
  304.0 0.0 all-gather.5.cloned.1.call-update
  304.1 1.3 copy.26
  305.4 23.8 %all-gather.5.cloned.1.call-done = f32[2,1024,128]{2,1,0:T(8,128)} async-done(((f32[2,128,128]{2,1,0:T(8,128)}), f32[2,1024,128]{2,1,0:T(8,128)}) %all-gather.5.cloned.1.call-update) | async-done | bytes 1048592 | tf_op jit(solution)/shard_map/all_gather | solution.py:34
  329.1 11.5 %subtract_bitcast_fusion = f32[2,1,1024,1024]{2,3,0,1:T(8,128)} fusion(f32[2,1024,1024]{1,2,0:T(8,128)} %copy-done.1, f32[2,128,1024]{2,1,0:T(8,128)S(1)} %fusion.4, f32[2,1024,128]{2,1,0:T(8,128)} %all-gather.5.cloned.1.call-done), kind=kOutput, calls=%fused_computation.1 | convolution fusion | flops 3223322624 | bytes 18874368 | tf_op jit(solution)/shard_map/mdr,mkr->mdk/dot_general | solution.py:35
  340.6 0.0 copy-start.2
  340.6 8.8 %copy.27 = f32[2,1,1024,1024]{3,2,1,0:T(8,128)} copy(f32[2,1,1024,1024]{2,3,0,1:T(8,128)} %subtract_bitcast_fusion) | data formatting | bytes 16777216
  349.4 0.0 copy-done.2
  349.4 1.0 copy.37
  (3 shorter events, 0.1 us)
Async XLA Ops:
  7.2 34.0 %copy-start = (bf16[512,1024]{1,0:T(8,128)(2,1)S(1)}, bf16[512,1024]{1,0:T(8,128)(2,1)}, u32[]{:S(2)}) copy-start(bf16[512,1024]{1,0:T(8,128)(2,1)} %param.5) | copy-start | bytes 3145732
  7.2 33.9 %all-gather.3.cloned.1.call-start = ((), (), s32[]{:S(2)}) async-start(), calls=%async_computation.1 | async-start | bytes 2359296 | tf_op jit(solution)/shard_map/all_gather | solution.py:18
  9.1 8.7 %copy-start.4 = (s32[2]{0:T(128)S(1)}, s32[2]{0:T(128)}, u32[]{:S(2)}) copy-start(s32[2]{0:T(128)} %param.9) | copy-start | bytes 28
  9.1 108.5 %all-reduce.4.cloned.1.call-start = ((), (), s32[]{:S(2)}) async-start(), calls=%async_computation.2 | async-start | bytes 2097152 | tf_op jit(solution)/shard_map/psum | solution.py:25
  17.9 33.1 %copy-start.3 = (f32[2,1024,128]{2,1,0:T(8,128)S(1)}, f32[2,1024,128]{2,1,0:T(8,128)}, u32[]{:S(2)}) copy-start(f32[2,1024,128]{2,1,0:T(8,128)} %param.8) | copy-start | bytes 3145732
  47.6 3.4 copy-start.1
  65.7 108.5 %all-reduce.6.cloned.1.call-start = ((), (), s32[]{:S(2)}) async-start(), calls=%async_computation.3 | async-start | bytes 262144 | tf_op jit(solution)/shard_map/psum | solution.py:27
  121.7 145.7 %reduce-scatter.2.cloned.1.call-start = ((), (), s32[]{:S(2)}) async-start(), calls=%async_computation.4 | async-start | bytes 1179648 | tf_op jit(solution)/shard_map/reduce_scatter | solution.py:32
  231.9 72.2 %all-reduce.8.cloned.1.call-start = ((), (), s32[]{:S(2)}) async-start(), calls=%async_computation.5 | async-start | bytes 262144 | tf_op jit(solution)/shard_map/psum | solution.py:33
  267.5 61.7 %all-gather.5.cloned.1.call-start = ((), (), s32[]{:S(2)}) async-start(), calls=%async_computation.6 | async-start | bytes 1179648 | tf_op jit(solution)/shard_map/all_gather | solution.py:34
  340.6 8.8 %copy-start.2 = (f32[2,1024,128]{2,1,0:T(8,128)S(1)}, f32[2,1024,128]{2,1,0:T(8,128)}, u32[]{:S(2)}) copy-start(f32[2,1024,128]{2,1,0:T(8,128)} %all-gather.5.cloned.1.call-done) | copy-start | bytes 3145732
Sparse Core Ops, SparseCore 0:
  10.5 30.5 all-gather.2
  65.8 51.8 all-reduce.3
  121.8 52.3 all-reduce.5
  232.0 35.3 reduce-scatter.1
  269.6 34.4 all-reduce.7
  306.0 23.1 all-gather.4
where the time goes:
time: 358 us; the launch traced here: 357 us
  waiting for transfers between devices  223 us (62%)
  matrix products  48.8 us (14%)
  other arithmetic  45.6 us (13%)
  local copies, waits for them, and re-layouts  25.1 us (7%)
  between operations  14.2 us (4%)
    psum x1, waiting for transfers between devices, local(): lax.psum(gram_local, 'fsdp') + jax.vmap(jnp.diag)(1.0 - rank_mask)  52.4 us
    psum x1, waiting for transfers between devices, local(): left_sum = lax.psum(left_local, 'dp')  51.8 us
    psum x1, waiting for transfers between devices, local(): right_rows = lax.psum(right_rows, 'dp')  36.5 us
    reduce_scatter x1, waiting for transfers between devices, local(): lax.psum_scatter(right_local, 'fsdp', scatter_dimension=1, tiled=True)  35.5 us
    unnamed x15, local copies, waits for them, and re-layouts  25 us
    all_gather x1, waiting for transfers between devices, local(): factor_q = lax.all_gather(right_rows, 'fsdp', axis=1, tiled=True)  23.8 us
    another operation x4, other arithmetic, local(): chol_lower = jnp.linalg.cholesky(gram_matrix)  23.6 us
    all_gather x1, waiting for transfers between devices, local(): lax.all_gather(cotangent, 'fsdp', axis=2, tiled=True)  23.2 us
  transfers between devices with their start and end apart: 6, of which 6 were waited for; matrix products, arithmetic and copies ran while one was open for 3% of the time, Pallas kernels for 0%

commit v1 on v0

v1 whole, which is shorter than its diff:
```python
import functools

import jax
import jax.numpy as jnp
from jax import lax
from jax.experimental import pallas as pl
from jax.experimental.pallas import tpu as pltpu
from jax.sharding import PartitionSpec as P

F32 = jnp.float32
BF16 = jnp.bfloat16
VMEM = pl.BlockSpec(memory_space=pltpu.VMEM)
SMEM = pl.BlockSpec(memory_space=pltpu.SMEM)
MIB = 1024 * 1024


def halves(x):
    high = x.astype(BF16)
    return high, (x - high.astype(F32)).astype(BF16)


def mm(a, b):
    return jnp.dot(a, b, preferred_element_type=F32)


def mm_nt(a, b):
    return lax.dot_general(a, b, (((1,), (1,)), ((), ())), preferred_element_type=F32)


def params(size, steps=1):
    return pltpu.CompilerParams(
        vmem_limit_bytes=size * MIB, dimension_semantics=("arbitrary",) * steps
    )


def tile_of(rows):
    return min(rows, 256)


def feedback_q_kernel(ranks_ref, fb_ref, q_ref, out_ref, q2_ref):
    m = pl.program_id(0)

    @pl.when(pl.program_id(1) == 0)
    def _():
        width = q_ref.shape[2]
        column = lax.broadcasted_iota(jnp.int32, q_ref.shape[1:], 1)
        q_high, q_low = halves(jnp.where(column < ranks_ref[m], q_ref[0], 0.0))
        q2_ref[:, :width] = q_high
        q2_ref[:, width:] = q_low

    width = q_ref.shape[2]
    high, low = halves(fb_ref[0, 0])
    both = mm(high, q2_ref[...])
    out_ref[0] = both[:, :width] + both[:, width:] + mm(low, q2_ref[:, :width])


def feedback_q(feedback, q_init, ranks):
    count, _, rows, columns = feedback.shape
    width = q_init.shape[2]
    tile = tile_of(rows)
    return pl.pallas_call(
        feedback_q_kernel,
        grid_spec=pltpu.PrefetchScalarGridSpec(
            num_scalar_prefetch=1,
            grid=(count, rows // tile),
            in_specs=[
                pl.BlockSpec((1, 1, tile, columns), lambda m, i, r: (m, 0, i, 0)),
                pl.BlockSpec((1, columns, width), lambda m, i, r: (m, 0, 0)),
            ],
            out_specs=pl.BlockSpec((1, tile, width), lambda m, i, r: (m, i, 0)),
            scratch_shapes=[pltpu.VMEM((columns, 2 * width), BF16)],
        ),
        out_shape=jax.ShapeDtypeStruct((count, rows, width), F32),
        compiler_params=params(24, 2),
        name="feedback_q",
    )(ranks, feedback, q_init)


def fill_cotangent(order_ref, cot_ref, whole_ref):
    blocks, width = cot_ref.shape[0], cot_ref.shape[3]
    for a in range(blocks):
        whole_ref[:, a * width : (a + 1) * width] = cot_ref[order_ref[a], 0]


def left_kernel(ranks_ref, order_ref, cot_ref, q_ref, in_ref, fbq_ref, out_ref, whole_ref):
    m = pl.program_id(0)
    width = q_ref.shape[2]
    fill_cotangent(order_ref, cot_ref, whole_ref)
    column = lax.broadcasted_iota(jnp.int32, q_ref.shape[1:], 1)
    q_high, q_low = halves(jnp.where(column < ranks_ref[m], q_ref[0], 0.0))
    both = mm(whole_ref[...], jnp.concatenate([q_high, q_low], axis=1))
    c_high, c_low = halves(both[:, :width] + both[:, width:])
    both = mm(in_ref[...], jnp.concatenate([c_high, c_low], axis=1))
    out_ref[0] = fbq_ref[0] + (both[:, :width] + both[:, width:])


def left(cot, order, q_init, inputs_t, fbq, ranks):
    count, rows, width = fbq.shape
    blocks, _, tokens, block = cot.shape
    columns = q_init.shape[1]
    return pl.pallas_call(
        left_kernel,
        grid_spec=pltpu.PrefetchScalarGridSpec(
            num_scalar_prefetch=2,
            grid=(count,),
            in_specs=[
                pl.BlockSpec((blocks, 1, tokens, block), lambda m, r, o: (0, m, 0, 0)),
                pl.BlockSpec((1, columns, width), lambda m, r, o: (m, 0, 0)),
                pl.BlockSpec((rows, tokens), lambda m, r, o: (0, 0)),
                pl.BlockSpec((1, rows, width), lambda m, r, o: (m, 0, 0)),
            ],
            out_specs=pl.BlockSpec((1, rows, width), lambda m, r, o: (m, 0, 0)),
            scratch_shapes=[pltpu.VMEM((tokens, columns), BF16)],
        ),
        out_shape=jax.ShapeDtypeStruct((count, rows, width), F32),
        compiler_params=params(24),
        name="left",
    )(ranks, order, cot, q_init, inputs_t, fbq)


def full_kernel(order_ref, cot_ref, in_ref, fb_ref, out_ref, whole_ref):
    @pl.when(pl.program_id(1) == 0)
    def _():
        fill_cotangent(order_ref, cot_ref, whole_ref)

    out_ref[0, 0] = fb_ref[0, 0] + mm(in_ref[...], whole_ref[...])


def full(cot, order, inputs_t, feedback):
    count, _, rows, columns = feedback.shape
    blocks, _, tokens, block = cot.shape
    tile = tile_of(rows)
    return pl.pallas_call(
        full_kernel,
        grid_spec=pltpu.PrefetchScalarGridSpec(
            num_scalar_prefetch=1,
            grid=(count, rows // tile),
            in_specs=[
                pl.BlockSpec((blocks, 1, tokens, block), lambda m, i, o: (0, m, 0, 0)),
                pl.BlockSpec((tile, tokens), lambda m, i, o: (i, 0)),
                pl.BlockSpec((1, 1, tile, columns), lambda m, i, o: (m, 0, i, 0)),
            ],
            out_specs=pl.BlockSpec((1, 1, tile, columns), lambda m, i, o: (m, 0, i, 0)),
            scratch_shapes=[pltpu.VMEM((tokens, columns), BF16)],
        ),
        out_shape=jax.ShapeDtypeStruct(feedback.shape, F32),
        compiler_params=params(24, 2),
        name="full",
    )(order, cot, inputs_t, feedback)


def right_kernel(full_ref, p_ref, out_ref):
    width = p_ref.shape[2]
    p_high, p_low = halves(p_ref[0].T)
    g_high, g_low = halves(full_ref[0, 0])
    both = mm(jnp.concatenate([p_high, p_low], axis=0), g_high)
    part = both[:width] + both[width:] + mm(p_high, g_low)

    @pl.when(pl.program_id(1) == 0)
    def _():
        out_ref[0] = part

    @pl.when(pl.program_id(1) > 0)
    def _():
        out_ref[0] += part


def right(full_grad, p):
    count, _, rows, columns = full_grad.shape
    width = p.shape[2]
    tile = tile_of(rows)
    return pl.pallas_call(
        right_kernel,
        grid=(count, rows // tile),
        in_specs=[
            pl.BlockSpec((1, 1, tile, columns), lambda m, i: (m, 0, i, 0)),
            pl.BlockSpec((1, tile, width), lambda m, i: (m, i, 0)),
        ],
        out_specs=pl.BlockSpec((1, width, columns), lambda m, i: (m, 0, 0)),
        out_shape=jax.ShapeDtypeStruct((count, width, columns), F32),
        compiler_params=params(24, 2),
        name="right",
    )(full_grad, p)


def gram_kernel(p_ref, out_ref):
    width = p_ref.shape[2]
    high, low = halves(p_ref[0])
    high_t, low_t = halves(p_ref[0].T)
    both = mm(high_t, jnp.concatenate([high, low], axis=1))
    out_ref[0] = both[:, :width] + both[:, width:] + mm(low_t, high)


def gram(p):
    count, rows, width = p.shape
    return pl.pallas_call(
        gram_kernel,
        grid=(count,),
        in_specs=[pl.BlockSpec((1, rows, width), lambda m: (m, 0, 0))],
        out_specs=pl.BlockSpec((1, width, width), lambda m: (m, 0, 0)),
        out_shape=jax.ShapeDtypeStruct((count, width, width), F32),
        compiler_params=params(24),
        name="gram",
    )(p)


def factor_kernel(ranks_ref, g_ref, p_ref, inv_ref, out_ref):
    count, n, _ = g_ref.shape
    lane = lax.broadcasted_iota(jnp.int32, (8, n), 1)
    sub = lax.broadcasted_iota(jnp.int32, (8, n), 0)
    work = []
    for m in range(count):
        free = jnp.where(lane < ranks_ref[m], 0.0, 1.0)
        blocks = []
        for b in range(n // 8):
            g = g_ref[m, 8 * b : 8 * b + 8, :]
            blocks.append(jnp.where(lane == sub + 8 * b, g + free, g))
        work.append(blocks)
    for k in range(n):
        top, s = divmod(k, 8)
        for blocks in work:
            row = jnp.broadcast_to(blocks[top][s : s + 1, :], (8, n))
            scale = lax.rsqrt(jnp.broadcast_to(row[:, k : k + 1], (8, n)))
            row = jnp.where(lane == k, scale, row * scale)
            for b in range(top, n // 8):
                x = blocks[b]
                times = jnp.broadcast_to(x[:, k : k + 1], (8, n)) * scale
                y = jnp.where(lane == k, 0.0, x) - times * row
                if b == top:
                    y = jnp.where(sub > s, y, jnp.where(sub == s, row, x))
                blocks[b] = y
    for m in range(count):
        for b in range(n // 8):
            inv_ref[m, 8 * b : 8 * b + 8, :] = jnp.where(lane <= sub + 8 * b, work[m][b], 0.0)
        i_high, i_low = halves(inv_ref[m])
        p_high, p_low = halves(p_ref[m])
        both = mm_nt(p_high, jnp.concatenate([i_high, i_low], axis=0))
        out_ref[m] = both[:, :n] + both[:, n:] + mm_nt(p_low, i_high)


def factor(gram_sum, p, ranks):
    return pl.pallas_call(
        factor_kernel,
        in_specs=[SMEM, VMEM, VMEM],
        out_specs=[VMEM, VMEM],
        out_shape=[
            jax.ShapeDtypeStruct(gram_sum.shape, F32),
            jax.ShapeDtypeStruct(p.shape, F32),
        ],
        compiler_params=pltpu.CompilerParams(vmem_limit_bytes=24 * MIB),
        name="factor",
    )(ranks, gram_sum, p)


def error_kernel(full_ref, fp_ref, inv_ref, rt_ref, err_ref, fq_ref, q3_ref):
    width = inv_ref.shape[1]

    @pl.when(pl.program_id(1) == 0)
    def _():
        i_high, i_low = halves(inv_ref[0])
        r_high, r_low = halves(rt_ref[0])
        both = mm(jnp.concatenate([i_high, i_low], axis=0), r_high)
        fq_t = both[:width] + both[width:] + mm(i_high, r_low)
        fq_ref[0] = fq_t.T
        q_high, q_low = halves(fq_t)
        q3_ref[:width] = q_high
        q3_ref[width : 2 * width] = q_high
        q3_ref[2 * width :] = q_low

    p_high, p_low = halves(fp_ref[0])
    low_rank = mm(jnp.concatenate([p_high, p_low, p_high], axis=1), q3_ref[...])
    err_ref[0, 0] = full_ref[0, 0] - low_rank


def error(full_grad, factor_p, inverse, rt):
    count, _, rows, columns = full_grad.shape
    width = rt.shape[1]
    tile = tile_of(rows)
    return pl.pallas_call(
        error_kernel,
        grid=(count, rows // tile),
        in_specs=[
            pl.BlockSpec((1, 1, tile, columns), lambda m, i: (m, 0, i, 0)),
            pl.BlockSpec((1, tile, width), lambda m, i: (m, i, 0)),
            pl.BlockSpec((1, width, width), lambda m, i: (m, 0, 0)),
            pl.BlockSpec((1, width, columns), lambda m, i: (m, 0, 0)),
        ],
        out_specs=[
            pl.BlockSpec((1, 1, tile, columns), lambda m, i: (m, 0, i, 0)),
            pl.BlockSpec((1, columns, width), lambda m, i: (m, 0, 0)),
        ],
        out_shape=[
            jax.ShapeDtypeStruct(full_grad.shape, F32),
            jax.ShapeDtypeStruct((count, columns, width), F32),
        ],
        scratch_shapes=[pltpu.VMEM((3 * width, columns), BF16)],
        compiler_params=params(24, 2),
        name="error",
    )(full_grad, factor_p, inverse, rt)


def power_of_two(n):
    return n & (n - 1) == 0


def across(x, axis, bit):
    size = lax.axis_size(axis)
    return lax.ppermute(x, axis, [(i, i ^ bit) for i in range(size)])


def bits_of(axis):
    size = lax.axis_size(axis)
    return [1 << b for b in range(size.bit_length() - 1)]


def gather_blocks(x, axis, split_axis):
    bits = bits_of(axis)
    held = {0: x}
    slow = bits[1:][::-1]
    while slow:
        if len(slow) >= 2:
            one, two = slow[:2]
            slow = slow[2:]
            keys = list(held)
            by_one = {r: across(held[r], axis, one) for r in keys}
            by_two = {r: across(held[r], axis, two) for r in keys}
            for r in keys:
                held[r ^ one] = by_one[r]
                held[r ^ two] = by_two[r]
                first, _ = jnp.split(by_two[r], 2, axis=split_axis)
                _, second = jnp.split(by_one[r], 2, axis=split_axis)
                held[r ^ one ^ two] = jnp.concatenate(
                    [across(first, axis, one), across(second, axis, two)], axis=split_axis
                )
        else:
            one = slow.pop()
            held.update({r ^ one: across(held[r], axis, one) for r in list(held)})
    held.update({r ^ 1: across(held[r], axis, 1) for r in list(held)})
    return [held[r] for r in range(len(held))]


def gather_cotangent(cotangent):
    size = lax.axis_size("fsdp")
    width = cotangent.shape[2]
    if power_of_two(size) and size > 1 and width % 128 == 0:
        blocks = gather_blocks(cotangent, "fsdp", 1)
        order = jnp.arange(size, dtype=jnp.int32) ^ lax.axis_index("fsdp")
        return jnp.stack(blocks), order
    whole = lax.all_gather(cotangent, "fsdp", axis=2, tiled=True)
    return whole[None], jnp.zeros((1,), jnp.int32)


def sum_dp(x):
    size = lax.axis_size("dp")
    if not (power_of_two(size) and size > 1):
        return lax.psum(x, "dp")
    bits = bits_of("dp")
    low = lax.axis_index("dp") & 1
    half = x.shape[1] // 2
    mine = lax.dynamic_slice_in_dim(x, low * half, half, 1)
    other = lax.dynamic_slice_in_dim(x, (1 - low) * half, half, 1)
    mine = mine + across(other, "dp", 1)
    for bit in bits[1:]:
        mine = mine + across(mine, "dp", bit)
    theirs = across(mine, "dp", 1)
    first = jnp.where(low == 0, mine, theirs)
    second = jnp.where(low == 0, theirs, mine)
    return jnp.concatenate([first, second], axis=1)


def sum_fsdp(x):
    size = lax.axis_size("fsdp")
    if not (power_of_two(size) and size > 1):
        return lax.psum(x, "fsdp")
    for bit in bits_of("fsdp"):
        x = x + across(x, "fsdp", bit)
    return x


def sum_all(x):
    size = lax.axis_size("fsdp")
    if not (power_of_two(size) and size > 1):
        rows = lax.psum_scatter(x, "fsdp", scatter_dimension=1, tiled=True)
        rows = lax.psum(rows, "dp")
        return lax.all_gather(rows, "fsdp", axis=1, tiled=True)
    me = lax.axis_index("fsdp")
    bits = bits_of("fsdp")
    for bit in bits:
        half = x.shape[1] // 2
        side = (me & bit) // bit
        mine = lax.dynamic_slice_in_dim(x, side * half, half, 1)
        other = lax.dynamic_slice_in_dim(x, (1 - side) * half, half, 1)
        x = mine + across(other, "fsdp", bit)
    if power_of_two(lax.axis_size("dp")):
        for bit in bits_of("dp"):
            x = x + across(x, "dp", bit)
    else:
        x = lax.psum(x, "dp")
    for bit in bits[::-1]:
        side = (me & bit) // bit
        theirs = across(x, "fsdp", bit)
        first = jnp.where(side == 0, x, theirs)
        second = jnp.where(side == 0, theirs, x)
        x = jnp.concatenate([first, second], axis=1)
    return x


def local(inputs, cotangent, feedback, q_init, factor_ranks):
    cot, order = gather_cotangent(cotangent)
    inputs_t = inputs.T
    fbq = feedback_q(feedback, q_init, factor_ranks)
    p = sum_dp(left(cot, order, q_init, inputs_t, fbq, factor_ranks))
    full_grad = full(cot, order, inputs_t, feedback)
    gram_sum = sum_fsdp(gram(p))
    rt = sum_all(right(full_grad, p))
    inverse, factor_p = factor(gram_sum, p, factor_ranks)
    new_error, factor_q = error(full_grad, factor_p, inverse, rt)
    return (factor_p, factor_q, new_error)


def solution(mesh):
    placed = (P("dp", "fsdp"), P(None, "dp", "fsdp"), P(None, "dp", "fsdp", None), P(), P())
    return jax.shard_map(
        local,
        mesh=mesh,
        in_specs=placed,
        out_specs=(P(None, "fsdp", None), P(), P(None, "dp", "fsdp", None)),
        check_vma=False,
    )
```

time: 358 us -> 177 us (0.49)
  waiting for transfers between devices: 223 us -> 83.2 us
  matrix products: 48.8 us -> 0 us
  Pallas kernels: 0 us -> 43.9 us
  other arithmetic: 45.6 us -> 3.94 us
  starting transfers between devices: 0.24 us -> 23.3 us
  between operations: 14.2 us -> 1.04 us
  local copies, waits for them, and re-layouts: 25.1 us -> 21.1 us
    psum x3 -> x0, waiting for transfers between devices: 141 us -> none  [the longest x1 52.4 us: local(): lax.psum(gram_local, 'fsdp') + jax.vmap(jnp.diag)(1.0 - rank_mask)]
    ppermute x0 -> x22, waiting for transfers between devices: none -> 83.2 us  [across(): return lax.ppermute(x, axis, [(i, i ^ bit) for i in range(size)])]
    all_gather x2 -> x0, waiting for transfers between devices: 46.9 us -> none  [the longest x1 23.8 us: local(): factor_q = lax.all_gather(right_rows, 'fsdp', axis=1, tiled=True)]
    dot_general x5 -> x0, matrix products: 46.5 us -> none  [the longest x1 14.7 us: local(): jnp.einsum('mdk,mkr->mdr', full_grad, masked_q, precision=PRECISE)]
    pallas_call x0 -> x7, Pallas kernels: none -> 43.9 us  [the longest x1 19.4 us: factor(): pl.pallas_call(factor_kernel, in_specs=[SMEM, VMEM, VMEM], out_specs=[VME...]
    another operation x7 -> x0, other arithmetic: 43.4 us -> none  [the longest x4 23.6 us: local(): chol_lower = jnp.linalg.cholesky(gram_matrix)]
    reduce_scatter x1 -> x0, waiting for transfers between devices: 35.5 us -> none  [local(): lax.psum_scatter(right_local, 'fsdp', scatter_dimension=1, tiled=True)]
    ppermute x0 -> x22, starting transfers between devices: none -> 23.3 us  [across(): return lax.ppermute(x, axis, [(i, i ^ bit) for i in range(size)])]
  transfers between devices with their start and end apart: 6 -> 22, of which waited for: 6 -> 15; matrix products, arithmetic and copies ran while one was open for 3% -> 3% of each run, Pallas kernels for 0% -> 17%
where the time goes in v1:
time: 177 us
  waiting for transfers between devices  83.2 us (47%)
  Pallas kernels  43.9 us (25%)
  starting transfers between devices  23.3 us (13%)
  local copies, waits for them, and re-layouts  21.1 us (12%)
  other arithmetic  3.94 us (2%)
    ppermute x22, waiting for transfers between devices, across(): return lax.ppermute(x, axis, [(i, i ^ bit) for i in range(size)])  83.2 us
    ppermute x22, starting transfers between devices, across(): return lax.ppermute(x, axis, [(i, i ^ bit) for i in range(size)])  23.3 us
    pallas_call x1, Pallas kernels, factor(): pl.pallas_call(factor_kernel, in_specs=[SMEM, VMEM, VMEM], out_specs=[VME...  19.4 us
    unnamed x29, local copies, waits for them, and re-layouts  19.2 us
    pallas_call x1, Pallas kernels, error(): pl.pallas_call(error_kernel, grid=(count, rows // tile), in_specs=[pl.Blo...  7.15 us
    pallas_call x1, Pallas kernels, full(): pl.pallas_call(full_kernel, grid_spec=pltpu.PrefetchScalarGridSpec(num_sc...  5 us
    pallas_call x1, Pallas kernels, feedback_q(): pl.pallas_call(feedback_q_kernel, grid_spec=pltpu.PrefetchScalarGridSpec(...  4.35 us
    pallas_call x1, Pallas kernels, right(): pl.pallas_call(right_kernel, grid=(count, rows // tile), in_specs=[pl.Blo...  3.83 us
  transfers between devices with their start and end apart: 22, of which 15 were waited for; matrix products, arithmetic and copies ran while one was open for 3% of the time, Pallas kernels for 17%

profile of v1, /device:TPU:0, one launch (start us, length us, event | category | flops | bytes accessed | tf_op | source)
XLA Modules:
  0.0 176.5 jit_solution(6418701089074027791)
XLA Ops:
  0.6 0.0 copy-start.5
  0.7 0.5 collective-permute-start
  1.2 2.6 %collective-permute-start.3 = (bf16[2,512,128]{2,1,0:T(8,128)(2,1)}, bf16[2,512,128]{2,1,0:T(8,128)(2,1)S(1)}, u32[]{:S(2)}, u32[]{:S(2)}) collective-permute-start(bf16[2,512,128]{2,1,0:T(8,128)(2,1)} %param.6), channel_id=1, source_target_pairs={{0,4},{1,5},{2,6},{3,7},{4,0},{5,1},{6,2},{7,3},{8,12},{9,13},{10,... | collective-permute-start | bytes 786440 | tf_op jit(solution)/shard_map/ppermute | solution.py:308
  3.8 1.5 collective-permute-start.1
  5.3 1.5 copy.8
  6.8 0.0 copy-start.2
  6.8 3.4 %copy-done.2 = f32[2,1,1024,1024]{3,2,1,0:T(8,128)S(1)} copy-done((f32[2,1,1024,1024]{3,2,1,0:T(8,128)S(1)}, f32[2,1,1024,1024]{3,2,1,0:T(8,128)}, u32[]{:S(2)}) %copy-start.2) | copy-done | bytes 8388632
  10.2 4.4 %feedback_q.1.fbq_ref = f32[2,1024,128]{2,1,0:T(8,128)S(1)} custom-call(s32[2]{0:T(128)S(1)} %copy-done.8, f32[2,1,1024,1024]{3,2,1,0:T(8,128)S(1)} %copy-done.2, f32[2,1024,128]{2,1,0:T(8,128)S(1)} %copy-done.5), custom_call_target="tpu_custom_call" | custom-call | tf_op jit(solution)/shard_map/feedback_q/pallas_call | solution.py:61
  14.6 0.6 collective-permute-start.6
  15.2 0.9 split.8
  16.1 0.0 copy-start.6
  16.1 0.2 collective-permute-start.5
  16.3 0.5 collective-permute-start.2
  16.8 1.0 bitcast_dynamic-update-slice_fusion.6
  17.8 1.0 bitcast_dynamic-update-slice_fusion.5
  18.8 2.4 %collective-permute-done.5 = bf16[2,256,128]{2,1,0:T(8,128)(2,1)S(1)} collective-permute-done((bf16[2,256,128]{2,1,0:T(8,128)(2,1)S(1)}, bf16[2,256,128]{2,1,0:T(8,128)(2,1)S(1)}, u32[]{:S(2)}, u32[]{:S(2)}) %collective-permute-start.5) | collective-permute-done | bytes 131104 | tf_op jit(solution)/shard_map/ppermute | solution.py:308
  21.3 0.1 collective-permute-start.7
  21.5 1.3 collective-permute-done.7
  22.9 3.3 %left.1 = f32[2,1024,128]{2,1,0:T(8,128)S(1)} custom-call(s32[2]{0:T(128)S(1)} %copy-done.8, s32[8]{0:T(128)S(1)} %iota_xor_fusion.order_ref, bf16[8,2,512,128]{3,2,1,0:T(8,128)(2,1)S(1)} %bitcast_dynamic-update-slice_fusion.cot_ref, f32[2,1024,128]{2,1,0:T(8,128)S(1)} %copy-done.6, bf16[1024,512]{1,0:T(8,128)(2,1)S(1)} %bitcast.17, ...), custom_call_target="tpu_custom_call" | custom-call | tf_op jit(solution)/shard_map/left/pallas_call | solution.py:101
  26.3 1.0 copy-done.4
  27.2 0.8 constant_dynamic-slice_fusion.3
  28.0 1.6 collective-permute-start.8
  29.6 12.7 %collective-permute-done.8 = f32[2,512,128]{2,1,0:T(8,128)} collective-permute-done((f32[2,512,128]{2,1,0:T(8,128)}, f32[2,512,128]{2,1,0:T(8,128)}, u32[]{:S(2)}, u32[]{:S(2)}) %collective-permute-start.8) | collective-permute-done | bytes 524320 | tf_op jit(solution)/shard_map/ppermute | solution.py:308
  42.3 1.3 dynamic-slice_add_fusion.1
  43.6 2.7 %collective-permute-start.9 = (f32[2,512,128]{2,1,0:T(8,128)S(1)}, f32[2,512,128]{2,1,0:T(8,128)S(1)}, u32[]{:S(2)}, u32[]{:S(2)}) collective-permute-start(f32[2,512,128]{2,1,0:T(8,128)S(1)} %dynamic-slice_add_fusion.1), channel_id=1, source_target_pairs={{0,16},{8,24},{16,0},{24,8},{1,17},{9,25},{17,1},{25,9},{2,18},{10... | collective-permute-start | bytes 1572872 | tf_op jit(solution)/shard_map/ppermute | solution.py:308
  46.2 22.7 %collective-permute-done.9 = f32[2,512,128]{2,1,0:T(8,128)S(1)} collective-permute-done((f32[2,512,128]{2,1,0:T(8,128)S(1)}, f32[2,512,128]{2,1,0:T(8,128)S(1)}, u32[]{:S(2)}, u32[]{:S(2)}) %collective-permute-start.9) | collective-permute-done | bytes 524320 | tf_op jit(solution)/shard_map/ppermute | solution.py:308
  68.9 0.8 add.60
  69.8 0.7 collective-permute-start.10
  70.4 3.4 %copy-done.3 = f32[2,1,1024,1024]{3,2,1,0:T(8,128)S(1)} copy-done((f32[2,1,1024,1024]{3,2,1,0:T(8,128)S(1)}, f32[2,1,1024,1024]{3,2,1,0:T(8,128)}, u32[]{:S(2)}) %copy-start.3) | copy-done | bytes 8388632
  73.8 5.0 %full.1.full_ref = f32[2,1,1024,1024]{3,2,1,0:T(8,128)S(1)} custom-call(s32[8]{0:T(128)S(1)} %iota_xor_fusion.order_ref, bf16[8,2,512,128]{3,2,1,0:T(8,128)(2,1)S(1)} %bitcast_dynamic-update-slice_fusion.cot_ref, bf16[1024,512]{1,0:T(8,128)(2,1)S(1)} %bitcast.18, f32[2,1,1024,1024]{3,2,1,0:T(8,128)S(1)} %copy-done.3), custom_call_target="tpu_custom_call" | custom-call | tf_op jit(solution)/shard_map/full/pallas_call | solution.py:133
  78.8 4.0 %collective-permute-done.10 = f32[2,512,128]{2,1,0:T(8,128)} collective-permute-done((f32[2,512,128]{2,1,0:T(8,128)}, f32[2,512,128]{2,1,0:T(8,128)}, u32[]{:S(2)}, u32[]{:S(2)}) %collective-permute-start.10) | collective-permute-done | bytes 524320 | tf_op jit(solution)/shard_map/ppermute | solution.py:308
  82.9 1.3 broadcast_select_fusion.3
  84.1 0.1 pad_maximum_fusion.p_ref
  84.2 3.8 %right.1 = f32[2,128,1024]{2,1,0:T(8,128)S(1)} custom-call(f32[2,1,1024,1024]{3,2,1,0:T(8,128)S(1)} %full.1.full_ref, f32[2,1024,128]{2,1,0:T(8,128)S(1)} %pad_maximum_fusion.p_ref), custom_call_target="tpu_custom_call" | custom-call | tf_op jit(solution)/shard_map/right/pallas_call | solution.py:172
  88.1 3.4 %copy-done = f32[2,1,1024,1024]{3,2,1,0:T(8,128)} copy-done((f32[2,1,1024,1024]{3,2,1,0:T(8,128)}, f32[2,1,1024,1024]{3,2,1,0:T(8,128)S(1)}, u32[]{:S(2)}) %copy-start) | copy-done | bytes 8388632
  91.5 0.1 collective-permute-start.14
  91.6 1.9 %collective-permute-done.14 = f32[2,64,1024]{2,1,0:T(8,128)S(1)} collective-permute-done((f32[2,64,1024]{2,1,0:T(8,128)S(1)}, f32[2,64,1024]{2,1,0:T(8,128)S(1)}, u32[]{:S(2)}, u32[]{:S(2)}) %collective-permute-start.14) | collective-permute-done | bytes 524320 | tf_op jit(solution)/shard_map/ppermute | solution.py:308
  93.5 0.1 dynamic-slice_add_fusion
  93.6 1.5 collective-permute-start.15
  95.1 6.9 %collective-permute-done.15 = f32[2,32,1024]{2,1,0:T(8,128)S(1)} collective-permute-done((f32[2,32,1024]{2,1,0:T(8,128)S(1)}, f32[2,32,1024]{2,1,0:T(8,128)S(1)}, u32[]{:S(2)}, u32[]{:S(2)}) %collective-permute-start.15) | collective-permute-done | bytes 262176 | tf_op jit(solution)/shard_map/ppermute | solution.py:308
  102.1 0.6 collective-permute-start.16
  102.6 4.5 %collective-permute-done.16 = f32[2,16,1024]{2,1,0:T(8,128)S(1)} collective-permute-done((f32[2,16,1024]{2,1,0:T(8,128)S(1)}, f32[2,16,1024]{2,1,0:T(8,128)S(1)}, u32[]{:S(2)}, u32[]{:S(2)}) %collective-permute-start.16) | collective-permute-done | bytes 131104 | tf_op jit(solution)/shard_map/ppermute | solution.py:308
  107.1 1.8 %collective-permute-start.17 = (f32[2,16,1024]{2,1,0:T(8,128)S(1)}, f32[2,16,1024]{2,1,0:T(8,128)S(1)}, u32[]{:S(2)}, u32[]{:S(2)}) collective-permute-start(f32[2,16,1024]{2,1,0:T(8,128)S(1)} %dynamic-slice_add_fusion.3), channel_id=1, source_target_pairs={{0,8},{8,0},{16,24},{24,16},{1,9},{9,1},{17,25},{25,17},{2,10},{10... | collective-permute-start | bytes 393224 | tf_op jit(solution)/shard_map/ppermute | solution.py:308
  108.9 3.2 %collective-permute-done.17 = f32[2,16,1024]{2,1,0:T(8,128)S(1)} collective-permute-done((f32[2,16,1024]{2,1,0:T(8,128)S(1)}, f32[2,16,1024]{2,1,0:T(8,128)S(1)}, u32[]{:S(2)}, u32[]{:S(2)}) %collective-permute-start.17) | collective-permute-done | bytes 131104 | tf_op jit(solution)/shard_map/ppermute | solution.py:308
  112.2 3.8 %collective-permute-start.18 = (f32[2,16,1024]{2,1,0:T(8,128)S(1)}, f32[2,16,1024]{2,1,0:T(8,128)S(1)}, u32[]{:S(2)}, u32[]{:S(2)}) collective-permute-start(f32[2,16,1024]{2,1,0:T(8,128)S(1)} %add.73), channel_id=1, source_target_pairs={{0,16},{8,24},{16,0},{24,8},{1,17},{9,25},{17,1},{25,9},{2,18},{10... | collective-permute-start | bytes 393224 | tf_op jit(solution)/shard_map/ppermute | solution.py:308
  116.0 4.4 %collective-permute-done.18 = f32[2,16,1024]{2,1,0:T(8,128)S(1)} collective-permute-done((f32[2,16,1024]{2,1,0:T(8,128)S(1)}, f32[2,16,1024]{2,1,0:T(8,128)S(1)}, u32[]{:S(2)}, u32[]{:S(2)}) %collective-permute-start.18) | collective-permute-done | bytes 131104 | tf_op jit(solution)/shard_map/ppermute | solution.py:308
  120.3 0.5 collective-permute-start.19
  120.8 4.5 %collective-permute-done.19 = f32[2,16,1024]{2,1,0:T(8,128)S(1)} collective-permute-done((f32[2,16,1024]{2,1,0:T(8,128)S(1)}, f32[2,16,1024]{2,1,0:T(8,128)S(1)}, u32[]{:S(2)}, u32[]{:S(2)}) %collective-permute-start.19) | collective-permute-done | bytes 131104 | tf_op jit(solution)/shard_map/ppermute | solution.py:308
  125.4 1.5 collective-permute-start.20
  126.9 5.0 %collective-permute-done.20 = f32[2,32,1024]{2,1,0:T(8,128)S(1)} collective-permute-done((f32[2,32,1024]{2,1,0:T(8,128)S(1)}, f32[2,32,1024]{2,1,0:T(8,128)S(1)}, u32[]{:S(2)}, u32[]{:S(2)}) %collective-permute-start.20) | collective-permute-done | bytes 262176 | tf_op jit(solution)/shard_map/ppermute | solution.py:308
  131.9 0.1 collective-permute-start.21
  132.0 0.9 gram.1
  132.9 0.5 collective-permute-start.11
  133.5 1.0 collective-permute-done.11
  134.5 1.5 collective-permute-start.12
  136.0 4.3 %collective-permute-done.12 = f32[2,128,128]{2,1,0:T(8,128)S(1)} collective-permute-done((f32[2,128,128]{2,1,0:T(8,128)S(1)}, f32[2,128,128]{2,1,0:T(8,128)S(1)}, u32[]{:S(2)}, u32[]{:S(2)}) %collective-permute-start.12) | collective-permute-done | bytes 131104 | tf_op jit(solution)/shard_map/ppermute | solution.py:308
  140.4 0.5 collective-permute-start.13
  140.9 4.5 %collective-permute-done.13 = f32[2,128,128]{2,1,0:T(8,128)S(1)} collective-permute-done((f32[2,128,128]{2,1,0:T(8,128)S(1)}, f32[2,128,128]{2,1,0:T(8,128)S(1)}, u32[]{:S(2)}, u32[]{:S(2)}) %collective-permute-start.13) | collective-permute-done | bytes 131104 | tf_op jit(solution)/shard_map/ppermute | solution.py:308
  145.4 19.4 %factor.1 = (f32[2,128,128]{2,1,0:T(8,128)S(1)}, f32[2,1024,128]{2,1,0:T(8,128)}) custom-call(s32[2]{0:T(128)S(1)} %copy-done.8, f32[2,128,128]{2,1,0:T(8,128)S(1)} %add.63.g_ref, f32[2,1024,128]{2,1,0:T(8,128)S(1)} %pad_maximum_fusion.p_ref), custom_call_target="tpu_custom_call" | custom-call | tf_op jit(solution)/shard_map/factor/pallas_call | solution.py:242
  164.8 0.1 broadcast_select_fusion.1
  164.9 0.1 pad_maximum_fusion.1.rt_ref
  165.0 1.0 copy-done.7
  166.0 3.4 %copy-done.1 = f32[2,1,1024,1024]{3,2,1,0:T(8,128)S(1)} copy-done((f32[2,1,1024,1024]{3,2,1,0:T(8,128)S(1)}, f32[2,1,1024,1024]{3,2,1,0:T(8,128)}, u32[]{:S(2)}) %copy-start.1) | copy-done | bytes 8388632
  169.4 7.2 %error.1 = (f32[2,1,1024,1024]{3,2,1,0:T(8,128)}, f32[2,1024,128]{2,1,0:T(8,128)}) custom-call(f32[2,1,1024,1024]{3,2,1,0:T(8,128)S(1)} %copy-done.1, f32[2,1024,128]{2,1,0:T(8,128)S(1)} %copy-done.7, f32[2,128,128]{2,1,0:T(8,128)S(1)} %get-tuple-element.8.inv_ref, f32[2,128,1024]{2,1,0:T(8,128)S(1)} %pad_maximum_fusion.1.rt_ref), custom_call_target="tpu_custom_call" | custom-call | tf_op jit(solution)/shard_map/error/pallas_call | solution.py:279
  (43 shorter events, 0.6 us)
Async XLA Ops:
  0.6 6.1 %copy-start.8 = (s32[2]{0:T(128)S(1)}, s32[2]{0:T(128)}, u32[]{:S(2)}) copy-start(s32[2]{0:T(128)} %ranks_ref.5) | copy-start | bytes 28
  0.6 6.1 %copy-start.5 = (f32[2,1024,128]{2,1,0:T(8,128)S(1)}, f32[2,1024,128]{2,1,0:T(8,128)}, u32[]{:S(2)}) copy-start(f32[2,1024,128]{2,1,0:T(8,128)} %q_ref.3) | copy-start | bytes 3145732
  0.7 16.1 %collective-permute-start = (bf16[2,512,128]{2,1,0:T(8,128)(2,1)}, bf16[2,512,128]{2,1,0:T(8,128)(2,1)}, u32[]{:S(2)}, u32[]{:S(2)}) collective-permute-start(bf16[2,512,128]{2,1,0:T(8,128)(2,1)} %param.6), channel_id=1, source_target_pairs={{0,1},{1,0},{2,3},{3,2},{4,5},{5,4},{6,7},{7,6},{8,9},{9,8},{10,11... | collective-permute-start | bytes 786440 | tf_op jit(solution)/shard_map/ppermute | solution.py:308
  1.2 13.4 %collective-permute-start.3 = (bf16[2,512,128]{2,1,0:T(8,128)(2,1)}, bf16[2,512,128]{2,1,0:T(8,128)(2,1)S(1)}, u32[]{:S(2)}, u32[]{:S(2)}) collective-permute-start(bf16[2,512,128]{2,1,0:T(8,128)(2,1)} %param.6), channel_id=1, source_target_pairs={{0,4},{1,5},{2,6},{3,7},{4,0},{5,1},{6,2},{7,3},{8,12},{9,13},{10,... | collective-permute-start | bytes 786440 | tf_op jit(solution)/shard_map/ppermute | solution.py:308
  3.8 11.4 %collective-permute-start.1 = (bf16[2,512,128]{2,1,0:T(8,128)(2,1)}, bf16[2,512,128]{2,1,0:T(8,128)(2,1)}, u32[]{:S(2)}, u32[]{:S(2)}) collective-permute-start(bf16[2,512,128]{2,1,0:T(8,128)(2,1)} %param.6), channel_id=1, source_target_pairs={{0,2},{1,3},{2,0},{3,1},{4,6},{5,7},{6,4},{7,5},{8,10},{9,11},{10,... | collective-permute-start | bytes 786440 | tf_op jit(solution)/shard_map/ppermute | solution.py:308
  6.8 3.4 %copy-start.2 = (f32[2,1,1024,1024]{3,2,1,0:T(8,128)S(1)}, f32[2,1,1024,1024]{3,2,1,0:T(8,128)}, u32[]{:S(2)}) copy-start(f32[2,1,1024,1024]{3,2,1,0:T(8,128)} %fb_ref.3) | copy-start | bytes 25165828
  10.2 4.4 %copy-start.9 = (bf16[2,512,128]{2,1,0:T(8,128)(2,1)S(1)}, bf16[2,512,128]{2,1,0:T(8,128)(2,1)}, u32[]{:S(2)}) copy-start(bf16[2,512,128]{2,1,0:T(8,128)(2,1)} %param.6) | copy-start | bytes 786436
  14.6 6.6 %collective-permute-start.6 = (bf16[2,256,128]{2,1,0:T(8,128)(2,1)S(1)}, bf16[2,256,128]{2,1,0:T(8,128)(2,1)S(1)}, u32[]{:S(2)}, u32[]{:S(2)}) collective-permute-start(bf16[2,256,128]{2,1,0:T(8,128)(2,1)S(1)} %split.9), channel_id=1, source_target_pairs={{0,2},{1,3},{2,0},{3,1},{4,6},{5,7},{6,4},{7,5},{8,10},{9,11},{10,... | collective-permute-start | bytes 393224 | tf_op jit(solution)/shard_map/ppermute | solution.py:308
  16.1 6.8 %copy-start.6 = (f32[2,1024,128]{2,1,0:T(8,128)S(1)}, f32[2,1024,128]{2,1,0:T(8,128)}, u32[]{:S(2)}) copy-start(f32[2,1024,128]{2,1,0:T(8,128)} %q_ref.3) | copy-start | bytes 3145732
  16.1 5.1 %collective-permute-start.5 = (bf16[2,256,128]{2,1,0:T(8,128)(2,1)S(1)}, bf16[2,256,128]{2,1,0:T(8,128)(2,1)S(1)}, u32[]{:S(2)}, u32[]{:S(2)}) collective-permute-start(bf16[2,256,128]{2,1,0:T(8,128)(2,1)S(1)} %split.8), channel_id=1, source_target_pairs={{0,4},{1,5},{2,6},{3,7},{4,0},{5,1},{6,2},{7,3},{8,12},{9,13},{10,... | collective-permute-start | bytes 393224 | tf_op jit(solution)/shard_map/ppermute | solution.py:308
  16.3 5.1 %collective-permute-start.4 = (bf16[2,512,128]{2,1,0:T(8,128)(2,1)S(1)}, bf16[2,512,128]{2,1,0:T(8,128)(2,1)S(1)}, u32[]{:S(2)}, u32[]{:S(2)}) collective-permute-start(bf16[2,512,128]{2,1,0:T(8,128)(2,1)S(1)} %collective-permute-done.3), channel_id=1, source_target_pairs={{0,1},{1,0},{2,3},{3,2},{4,5},{5,4},{6,7},{7,6},{8,9},{9,8},{10,11... | collective-permute-start | bytes 786440 | tf_op jit(solution)/shard_map/ppermute | solution.py:308
  16.3 5.0 %collective-permute-start.2 = (bf16[2,512,128]{2,1,0:T(8,128)(2,1)}, bf16[2,512,128]{2,1,0:T(8,128)(2,1)S(1)}, u32[]{:S(2)}, u32[]{:S(2)}) collective-permute-start(bf16[2,512,128]{2,1,0:T(8,128)(2,1)} %collective-permute-done.1), channel_id=1, source_target_pairs={{0,1},{1,0},{2,3},{3,2},{4,5},{5,4},{6,7},{7,6},{8,9},{9,8},{10,11... | collective-permute-start | bytes 786440 | tf_op jit(solution)/shard_map/ppermute | solution.py:308
  21.3 1.6 collective-permute-start.7
  26.2 1.0 copy-start.4
  28.0 14.3 %collective-permute-start.8 = (f32[2,512,128]{2,1,0:T(8,128)}, f32[2,512,128]{2,1,0:T(8,128)}, u32[]{:S(2)}, u32[]{:S(2)}) collective-permute-start(f32[2,512,128]{2,1,0:T(8,128)} %constant_dynamic-slice_fusion.3), channel_id=1, source_target_pairs={{0,8},{8,0},{16,24},{24,16},{1,9},{9,1},{17,25},{25,17},{2,10},{10... | collective-permute-start | bytes 1572872 | tf_op jit(solution)/shard_map/ppermute | solution.py:308
  43.6 25.3 %collective-permute-start.9 = (f32[2,512,128]{2,1,0:T(8,128)S(1)}, f32[2,512,128]{2,1,0:T(8,128)S(1)}, u32[]{:S(2)}, u32[]{:S(2)}) collective-permute-start(f32[2,512,128]{2,1,0:T(8,128)S(1)} %dynamic-slice_add_fusion.1), channel_id=1, source_target_pairs={{0,16},{8,24},{16,0},{24,8},{1,17},{9,25},{17,1},{25,9},{2,18},{10... | collective-permute-start | bytes 1572872 | tf_op jit(solution)/shard_map/ppermute | solution.py:308
  69.8 13.1 %collective-permute-start.10 = (f32[2,512,128]{2,1,0:T(8,128)}, f32[2,512,128]{2,1,0:T(8,128)}, u32[]{:S(2)}, u32[]{:S(2)}) collective-permute-start(f32[2,512,128]{2,1,0:T(8,128)} %add.60), channel_id=1, source_target_pairs={{0,8},{8,0},{16,24},{24,16},{1,9},{9,1},{17,25},{25,17},{2,10},{10... | collective-permute-start | bytes 1572872 | tf_op jit(solution)/shard_map/ppermute | solution.py:308
  70.4 3.4 %copy-start.3 = (f32[2,1,1024,1024]{3,2,1,0:T(8,128)S(1)}, f32[2,1,1024,1024]{3,2,1,0:T(8,128)}, u32[]{:S(2)}) copy-start(f32[2,1,1024,1024]{3,2,1,0:T(8,128)} %fb_ref.3) | copy-start | bytes 25165828
  88.1 3.4 %copy-start = (f32[2,1,1024,1024]{3,2,1,0:T(8,128)}, f32[2,1,1024,1024]{3,2,1,0:T(8,128)S(1)}, u32[]{:S(2)}) copy-start(f32[2,1,1024,1024]{3,2,1,0:T(8,128)S(1)} %full.1.full_ref) | copy-start | bytes 25165828
  91.5 2.0 %collective-permute-start.14 = (f32[2,64,1024]{2,1,0:T(8,128)S(1)}, f32[2,64,1024]{2,1,0:T(8,128)S(1)}, u32[]{:S(2)}, u32[]{:S(2)}) collective-permute-start(f32[2,64,1024]{2,1,0:T(8,128)S(1)} %constant_dynamic-slice_fusion.2), channel_id=1, source_target_pairs={{0,1},{1,0},{2,3},{3,2},{4,5},{5,4},{6,7},{7,6},{8,9},{9,8},{10,11... | collective-permute-start | bytes 1572872 | tf_op jit(solution)/shard_map/ppermute | solution.py:308
  93.6 8.4 %collective-permute-start.15 = (f32[2,32,1024]{2,1,0:T(8,128)S(1)}, f32[2,32,1024]{2,1,0:T(8,128)S(1)}, u32[]{:S(2)}, u32[]{:S(2)}) collective-permute-start(f32[2,32,1024]{2,1,0:T(8,128)S(1)} %constant_dynamic-slice_fusion.1), channel_id=1, source_target_pairs={{0,2},{1,3},{2,0},{3,1},{4,6},{5,7},{6,4},{7,5},{8,10},{9,11},{10,... | collective-permute-start | bytes 786440 | tf_op jit(solution)/shard_map/ppermute | solution.py:308
  102.1 5.0 %collective-permute-start.16 = (f32[2,16,1024]{2,1,0:T(8,128)S(1)}, f32[2,16,1024]{2,1,0:T(8,128)S(1)}, u32[]{:S(2)}, u32[]{:S(2)}) collective-permute-start(f32[2,16,1024]{2,1,0:T(8,128)S(1)} %constant_dynamic-slice_fusion), channel_id=1, source_target_pairs={{0,4},{1,5},{2,6},{3,7},{4,0},{5,1},{6,2},{7,3},{8,12},{9,13},{10,... | collective-permute-start | bytes 393224 | tf_op jit(solution)/shard_map/ppermute | solution.py:308
  107.1 5.0 %collective-permute-start.17 = (f32[2,16,1024]{2,1,0:T(8,128)S(1)}, f32[2,16,1024]{2,1,0:T(8,128)S(1)}, u32[]{:S(2)}, u32[]{:S(2)}) collective-permute-start(f32[2,16,1024]{2,1,0:T(8,128)S(1)} %dynamic-slice_add_fusion.3), channel_id=1, source_target_pairs={{0,8},{8,0},{16,24},{24,16},{1,9},{9,1},{17,25},{25,17},{2,10},{10... | collective-permute-start | bytes 393224 | tf_op jit(solution)/shard_map/ppermute | solution.py:308
  112.2 8.1 %collective-permute-start.18 = (f32[2,16,1024]{2,1,0:T(8,128)S(1)}, f32[2,16,1024]{2,1,0:T(8,128)S(1)}, u32[]{:S(2)}, u32[]{:S(2)}) collective-permute-start(f32[2,16,1024]{2,1,0:T(8,128)S(1)} %add.73), channel_id=1, source_target_pairs={{0,16},{8,24},{16,0},{24,8},{1,17},{9,25},{17,1},{25,9},{2,18},{10... | collective-permute-start | bytes 393224 | tf_op jit(solution)/shard_map/ppermute | solution.py:308
  120.3 5.0 %collective-permute-start.19 = (f32[2,16,1024]{2,1,0:T(8,128)S(1)}, f32[2,16,1024]{2,1,0:T(8,128)S(1)}, u32[]{:S(2)}, u32[]{:S(2)}) collective-permute-start(f32[2,16,1024]{2,1,0:T(8,128)S(1)} %add.74), channel_id=1, source_target_pairs={{0,4},{1,5},{2,6},{3,7},{4,0},{5,1},{6,2},{7,3},{8,12},{9,13},{10,... | collective-permute-start | bytes 393224 | tf_op jit(solution)/shard_map/ppermute | solution.py:308
  125.4 6.4 %collective-permute-start.20 = (f32[2,32,1024]{2,1,0:T(8,128)S(1)}, f32[2,32,1024]{2,1,0:T(8,128)S(1)}, u32[]{:S(2)}, u32[]{:S(2)}) collective-permute-start(f32[2,32,1024]{2,1,0:T(8,128)S(1)} %pad_maximum_fusion.3), channel_id=1, source_target_pairs={{0,2},{1,3},{2,0},{3,1},{4,6},{5,7},{6,4},{7,5},{8,10},{9,11},{10,... | collective-permute-start | bytes 786440 | tf_op jit(solution)/shard_map/ppermute | solution.py:308
  131.9 32.8 %collective-permute-start.21 = (f32[2,64,1024]{2,1,0:T(8,128)S(1)}, f32[2,64,1024]{2,1,0:T(8,128)S(1)}, u32[]{:S(2)}, u32[]{:S(2)}) collective-permute-start(f32[2,64,1024]{2,1,0:T(8,128)S(1)} %pad_maximum_fusion.2), channel_id=1, source_target_pairs={{0,1},{1,0},{2,3},{3,2},{4,5},{5,4},{6,7},{7,6},{8,9},{9,8},{10,11... | collective-permute-start | bytes 1572872 | tf_op jit(solution)/shard_map/ppermute | solution.py:308
  132.9 1.5 collective-permute-start.11
  134.5 5.8 %collective-permute-start.12 = (f32[2,128,128]{2,1,0:T(8,128)S(1)}, f32[2,128,128]{2,1,0:T(8,128)S(1)}, u32[]{:S(2)}, u32[]{:S(2)}) collective-permute-start(f32[2,128,128]{2,1,0:T(8,128)S(1)} %add.61), channel_id=1, source_target_pairs={{0,2},{1,3},{2,0},{3,1},{4,6},{5,7},{6,4},{7,5},{8,10},{9,11},{10,... | collective-permute-start | bytes 393224 | tf_op jit(solution)/shard_map/ppermute | solution.py:308
  140.4 5.0 %collective-permute-start.13 = (f32[2,128,128]{2,1,0:T(8,128)S(1)}, f32[2,128,128]{2,1,0:T(8,128)S(1)}, u32[]{:S(2)}, u32[]{:S(2)}) collective-permute-start(f32[2,128,128]{2,1,0:T(8,128)S(1)} %add.62), channel_id=1, source_target_pairs={{0,4},{1,5},{2,6},{3,7},{4,0},{5,1},{6,2},{7,3},{8,12},{9,13},{10,... | collective-permute-start | bytes 393224 | tf_op jit(solution)/shard_map/ppermute | solution.py:308
  164.8 1.2 copy-start.7
  166.0 3.4 %copy-start.1 = (f32[2,1,1024,1024]{3,2,1,0:T(8,128)S(1)}, f32[2,1,1024,1024]{3,2,1,0:T(8,128)}, u32[]{:S(2)}) copy-start(f32[2,1,1024,1024]{3,2,1,0:T(8,128)} %copy-done) | copy-start | bytes 25165828

commit v2 on v1

--- a/solution.py
+++ b/solution.py
@@ -71,7 +71,7 @@
             scratch_shapes=[pltpu.VMEM((columns, 2 * width), BF16)],
         ),
         out_shape=jax.ShapeDtypeStruct((count, rows, width), F32),
-        compiler_params=params(24, 2),
+        compiler_params=params(56, 2),
         name="feedback_q",
     )(ranks, feedback, q_init)
 
@@ -113,9 +113,120 @@
             scratch_shapes=[pltpu.VMEM((tokens, columns), BF16)],
         ),
         out_shape=jax.ShapeDtypeStruct((count, rows, width), F32),
-        compiler_params=params(24),
+        compiler_params=params(32),
         name="left",
     )(ranks, order, cot, q_init, inputs_t, fbq)
+
+
+GROUPS = 16
+
+
+def encode(x, out_ref):
+    rows, width = x.shape
+    grouped = x.reshape(GROUPS, rows // GROUPS, width)
+    top = jnp.max(jnp.abs(grouped), axis=1)
+    level = jnp.ceil(jnp.log(jnp.maximum(top, 1e-30)) * 32.0) + 1.0
+    up = jnp.exp(level * (-1.0 / 32.0)) * 32767.0
+    code = jnp.round(grouped * up[:, None, :]).reshape(rows, width)
+    out_ref[:rows] = code.astype(jnp.int32).astype(jnp.int16)
+    out_ref[rows:] = level.astype(jnp.int32).astype(jnp.int16)
+
+
+def decode(ref):
+    rows = ref.shape[0] - GROUPS
+    width = ref.shape[1]
+    level = ref[rows:].astype(jnp.int32).astype(F32)
+    down = jnp.exp(level * (1.0 / 32.0)) * (1.0 / 32767.0)
+    code = ref[:rows].astype(jnp.int32).astype(F32).reshape(GROUPS, rows // GROUPS, width)
+    return (code * down[:, None, :]).reshape(rows, width)
+
+
+def left_code_kernel(
+    m, ranks_ref, order_ref, low_ref, cot_ref, q_ref, in_ref, fbq_ref, mine_ref, code_ref, whole_ref, p_ref
+):
+    width = q_ref.shape[2]
+    fill_cotangent(order_ref, cot_ref, whole_ref)
+    column = lax.broadcasted_iota(jnp.int32, q_ref.shape[1:], 1)
+    q_high, q_low = halves(jnp.where(column < ranks_ref[m], q_ref[0], 0.0))
+    both = mm(whole_ref[...], jnp.concatenate([q_high, q_low], axis=1))
+    c_high, c_low = halves(both[:, :width] + both[:, width:])
+    both = mm(in_ref[...], jnp.concatenate([c_high, c_low], axis=1))
+    p_ref[...] = (fbq_ref[0] + (both[:, :width] + both[:, width:])).reshape(p_ref.shape)
+    mine_ref[...] = p_ref[low_ref[0]]
+    encode(p_ref[1 - low_ref[0]], code_ref)
+
+
+def left_code(m, cot, order, low, q_init, inputs_t, fbq, ranks):
+    count, rows, width = fbq.shape
+    blocks, _, tokens, block = cot.shape
+    columns = q_init.shape[1]
+    half = rows // 2
+    return pl.pallas_call(
+        functools.partial(left_code_kernel, m),
+        grid_spec=pltpu.PrefetchScalarGridSpec(
+            num_scalar_prefetch=3,
+            grid=(1,),
+            in_specs=[
+                pl.BlockSpec((blocks, 1, tokens, block), lambda i, *_: (0, m, 0, 0)),
+                pl.BlockSpec((1, columns, width), lambda i, *_: (m, 0, 0)),
+                pl.BlockSpec((rows, tokens), lambda i, *_: (0, 0)),
+                pl.BlockSpec((1, rows, width), lambda i, *_: (m, 0, 0)),
+            ],
+            out_specs=[
+                pl.BlockSpec((half, width), lambda i, *_: (0, 0)),
+                pl.BlockSpec((half + GROUPS, width), lambda i, *_: (0, 0)),
+            ],
+            scratch_shapes=[
+                pltpu.VMEM((tokens, columns), BF16),
+                pltpu.VMEM((2, half, width), F32),
+            ],
+        ),
+        out_shape=[
+            jax.ShapeDtypeStruct((half, width), F32),
+            jax.ShapeDtypeStruct((half + GROUPS, width), jnp.int16),
+        ],
+        compiler_params=params(32),
+        name=f"left_code_{m}",
+    )(ranks, order, low, cot, q_init, inputs_t, fbq)
+
+
+def add_kernel(mine_ref, theirs_ref, out_ref):
+    mine = mine_ref[...] if mine_ref.dtype == F32 else decode(mine_ref)
+    encode(mine + decode(theirs_ref), out_ref)
+
+
+def add_code(mine, theirs):
+    return pl.pallas_call(
+        add_kernel,
+        in_specs=[VMEM, VMEM],
+        out_specs=VMEM,
+        out_shape=jax.ShapeDtypeStruct(theirs.shape, jnp.int16),
+        compiler_params=pltpu.CompilerParams(vmem_limit_bytes=32 * MIB),
+        name="add_code",
+    )(mine, theirs)
+
+
+def whole_left_kernel(low_ref, mine_ref, theirs_ref, p_ref, gram_ref):
+    half, width = mine_ref.shape[0] - GROUPS, mine_ref.shape[1]
+    low = low_ref[0]
+    p_ref[pl.ds(pl.multiple_of(low * half, half), half)] = decode(mine_ref)
+    p_ref[pl.ds(pl.multiple_of((1 - low) * half, half), half)] = decode(theirs_ref)
+    gram_ref[...] = gram_of(p_ref[...])
+
+
+def whole_left(low, mine, theirs):
+    half, width = mine.shape[0] - GROUPS, mine.shape[1]
+    return pl.pallas_call(
+        whole_left_kernel,
+        in_specs=[SMEM, VMEM, VMEM],
+        out_specs=[VMEM, VMEM],
+        out_shape=[
+            jax.ShapeDtypeStruct((2 * half, width), F32),
+            jax.ShapeDtypeStruct((width, width), F32),
+        ],
+        compiler_params=pltpu.CompilerParams(vmem_limit_bytes=32 * MIB),
+        name="whole_left",
+    )(low, mine, theirs)
 
 
 def full_kernel(order_ref, cot_ref, in_ref, fb_ref, out_ref, whole_ref):
@@ -144,51 +255,55 @@
             scratch_shapes=[pltpu.VMEM((tokens, columns), BF16)],
         ),
         out_shape=jax.ShapeDtypeStruct(feedback.shape, F32),
-        compiler_params=params(24, 2),
+        compiler_params=params(56, 2),
         name="full",
     )(order, cot, inputs_t, feedback)
 
 
 def right_kernel(full_ref, p_ref, out_ref):
-    width = p_ref.shape[2]
-    p_high, p_low = halves(p_ref[0].T)
+    width = p_ref.shape[1]
+    p_high, p_low = halves(p_ref[...].T)
     g_high, g_low = halves(full_ref[0, 0])
     both = mm(jnp.concatenate([p_high, p_low], axis=0), g_high)
     part = both[:width] + both[width:] + mm(p_high, g_low)
 
-    @pl.when(pl.program_id(1) == 0)
+    @pl.when(pl.program_id(0) == 0)
     def _():
-        out_ref[0] = part
-
-    @pl.when(pl.program_id(1) > 0)
+        out_ref[...] = part
+
+    @pl.when(pl.program_id(0) > 0)
     def _():
-        out_ref[0] += part
-
-
-def right(full_grad, p):
-    count, _, rows, columns = full_grad.shape
-    width = p.shape[2]
+        out_ref[...] += part
+
+
+def right(m, full_grad, p):
+    _, _, rows, columns = full_grad.shape
+    width = p.shape[1]
     tile = tile_of(rows)
     return pl.pallas_call(
         right_kernel,
-        grid=(count, rows // tile),
+        grid=(rows // tile,),
         in_specs=[
-            pl.BlockSpec((1, 1, tile, columns), lambda m, i: (m, 0, i, 0)),
-            pl.BlockSpec((1, tile, width), lambda m, i: (m, i, 0)),
-        ],
-        out_specs=pl.BlockSpec((1, width, columns), lambda m, i: (m, 0, 0)),
-        out_shape=jax.ShapeDtypeStruct((count, width, columns), F32),
-        compiler_params=params(24, 2),
-        name="right",
+            pl.BlockSpec((1, 1, tile, columns), lambda i: (m, 0, i, 0)),
+            pl.BlockSpec((tile, width), lambda i: (i, 0)),
+        ],
+        out_specs=pl.BlockSpec((width, columns), lambda i: (0, 0)),
+        out_shape=jax.ShapeDtypeStruct((width, columns), F32),
+        compiler_params=params(56),
+        name=f"right_{m}",
     )(full_grad, p)
 
 
+def gram_of(p):
+    width = p.shape[1]
+    high, low = halves(p)
+    high_t, low_t = halves(p.T)
+    both = mm(high_t, jnp.concatenate([high, low], axis=1))
+    return both[:, :width] + both[:, width:] + mm(low_t, high)
+
+
 def gram_kernel(p_ref, out_ref):
-    width = p_ref.shape[2]
-    high, low = halves(p_ref[0])
-    high_t, low_t = halves(p_ref[0].T)
-    both = mm(high_t, jnp.concatenate([high, low], axis=1))
-    out_ref[0] = both[:, :width] + both[:, width:] + mm(low_t, high)
+    out_ref[0] = gram_of(p_ref[0])
 
 
 def gram(p):
@@ -199,7 +314,7 @@
         in_specs=[pl.BlockSpec((1, rows, width), lambda m: (m, 0, 0))],
         out_specs=pl.BlockSpec((1, width, width), lambda m: (m, 0, 0)),
         out_shape=jax.ShapeDtypeStruct((count, width, width), F32),
-        compiler_params=params(24),
+        compiler_params=params(32),
         name="gram",
     )(p)
 
@@ -294,7 +409,7 @@
             jax.ShapeDtypeStruct((count, columns, width), F32),
         ],
         scratch_shapes=[pltpu.VMEM((3 * width, columns), BF16)],
-        compiler_params=params(24, 2),
+        compiler_params=params(56, 2),
         name="error",
     )(full_grad, factor_p, inverse, rt)
 
@@ -350,70 +465,114 @@
     return whole[None], jnp.zeros((1,), jnp.int32)
 
 
-def sum_dp(x):
-    size = lax.axis_size("dp")
+def cut(x, side, bit, axis):
+    half = x.shape[axis] // 2
+    mine = lax.dynamic_slice_in_dim(x, side * half, half, axis)
+    other = lax.dynamic_slice_in_dim(x, (1 - side) * half, half, axis)
+    return mine, other
+
+
+def side_of(bit):
+    return (lax.axis_index("fsdp") & bit) // bit
+
+
+def halve(x, bit):
+    mine, other = cut(x, side_of(bit), bit, 1)
+    return mine + across(other, "fsdp", bit)
+
+
+def unhalve(x, bit):
+    theirs = across(x, "fsdp", bit)
+    side = side_of(bit)
+    first = jnp.where(side == 0, x, theirs)
+    second = jnp.where(side == 0, theirs, x)
+    return jnp.concatenate([first, second], axis=1)
+
+
+def scatter_sum(x, bits):
+    if not bits:
+        return x
+    if len(bits) == 1 or x.shape[1] < 8:
+        return scatter_sum(halve(x, bits[0]), bits[1:])
+    one, two = bits[:2]
+    a, b = jnp.split(x, 2, axis=1)
+    a, b = halve(a, one), halve(b, two)
+    a, b = halve(a, two), halve(b, one)
+    return scatter_sum(jnp.concatenate([a, b], axis=1), bits[2:])
+
+
+def gather_sum(x, bits, rows):
+    if not bits:
+        return x
+    if len(bits) == 1 or rows < 8:
+        return unhalve(gather_sum(x, bits[1:], rows // 2), bits[0])
+    one, two = bits[:2]
+    a, b = jnp.split(gather_sum(x, bits[2:], rows // 4), 2, axis=1)
+    a, b = unhalve(a, two), unhalve(b, one)
+    a, b = unhalve(a, one), unhalve(b, two)
+    return jnp.concatenate([a, b], axis=1)
+
+
+def tie(*values):
+    return lax.optimization_barrier(values)
+
+
+def sums(gram_part, rt_parts, p, ranks):
+    size = lax.axis_size("fsdp")
+    replicas = lax.axis_size("dp")
     if not (power_of_two(size) and size > 1):
-        return lax.psum(x, "dp")
-    bits = bits_of("dp")
-    low = lax.axis_index("dp") & 1
-    half = x.shape[1] // 2
-    mine = lax.dynamic_slice_in_dim(x, low * half, half, 1)
-    other = lax.dynamic_slice_in_dim(x, (1 - low) * half, half, 1)
-    mine = mine + across(other, "dp", 1)
-    for bit in bits[1:]:
-        mine = mine + across(mine, "dp", bit)
-    theirs = across(mine, "dp", 1)
-    first = jnp.where(low == 0, mine, theirs)
-    second = jnp.where(low == 0, theirs, mine)
-    return jnp.concatenate([first, second], axis=1)
-
-
-def sum_fsdp(x):
-    size = lax.axis_size("fsdp")
-    if not (power_of_two(size) and size > 1):
-        return lax.psum(x, "fsdp")
-    for bit in bits_of("fsdp"):
-        x = x + across(x, "fsdp", bit)
-    return x
-
-
-def sum_all(x):
-    size = lax.axis_size("fsdp")
-    if not (power_of_two(size) and size > 1):
-        rows = lax.psum_scatter(x, "fsdp", scatter_dimension=1, tiled=True)
+        gram_sum = lax.psum(gram_part, "fsdp")
+        inverse, factor_p = factor(gram_sum, p, ranks)
+        rows = lax.psum_scatter(jnp.stack(rt_parts), "fsdp", scatter_dimension=1, tiled=True)
         rows = lax.psum(rows, "dp")
-        return lax.all_gather(rows, "fsdp", axis=1, tiled=True)
-    me = lax.axis_index("fsdp")
+        return inverse, factor_p, lax.all_gather(rows, "fsdp", axis=1, tiled=True)
     bits = bits_of("fsdp")
+    rt = jnp.concatenate([halve(part[None], 1) for part in rt_parts], axis=0)
+    rows = rt.shape[1]
+    gram_sum = gram_part
     for bit in bits:
-        half = x.shape[1] // 2
-        side = (me & bit) // bit
-        mine = lax.dynamic_slice_in_dim(x, side * half, half, 1)
-        other = lax.dynamic_slice_in_dim(x, (1 - side) * half, half, 1)
-        x = mine + across(other, "fsdp", bit)
-    if power_of_two(lax.axis_size("dp")):
-        for bit in bits_of("dp"):
-            x = x + across(x, "dp", bit)
+        gram_sum = gram_sum + across(gram_sum, "fsdp", bit)
+    rt = scatter_sum(rt, bits[1:])
+    if power_of_two(replicas):
+        steps = bits_of("dp")
+        for bit in steps[:-1]:
+            rt = rt + across(rt, "dp", bit)
+        gram_sum, rt = tie(gram_sum, rt)
+        theirs = across(rt, "dp", steps[-1]) if steps else 0.0
+        inverse, factor_p = factor(gram_sum, p, ranks)
+        theirs, inverse, factor_p = tie(theirs, inverse, factor_p)
+        rt = rt + theirs
     else:
-        x = lax.psum(x, "dp")
-    for bit in bits[::-1]:
-        side = (me & bit) // bit
-        theirs = across(x, "fsdp", bit)
-        first = jnp.where(side == 0, x, theirs)
-        second = jnp.where(side == 0, theirs, x)
-        x = jnp.concatenate([first, second], axis=1)
-    return x
+        rt = lax.psum(rt, "dp")
+        inverse, factor_p = factor(gram_sum, p, ranks)
+    return inverse, factor_p, unhalve(gather_sum(rt, bits[1:], rows), 1)
+
+
+def left_sums(cot, order, q_init, inputs_t, fbq, ranks):
+    replicas = lax.axis_size("dp")
+    count = fbq.shape[0]
+    if not (power_of_two(replicas) and replicas > 1):
+        p = lax.psum(left(cot, order, q_init, inputs_t, fbq, ranks), "dp")
+        return [p[m] for m in range(count)], gram(p)
+    low = (lax.axis_index("dp") & 1).reshape(1)
+    whole = []
+    for m in range(count):
+        mine, other = left_code(m, cot, order, low, q_init, inputs_t, fbq, ranks)
+        mine = add_code(mine, across(other, "dp", 1))
+        for bit in bits_of("dp")[1:]:
+            mine = add_code(mine, across(mine, "dp", bit))
+        whole.append(whole_left(low, mine, across(mine, "dp", 1)))
+    return [p for p, _ in whole], jnp.stack([part for _, part in whole])
 
 
 def local(inputs, cotangent, feedback, q_init, factor_ranks):
     cot, order = gather_cotangent(cotangent)
     inputs_t = inputs.T
     fbq = feedback_q(feedback, q_init, factor_ranks)
-    p = sum_dp(left(cot, order, q_init, inputs_t, fbq, factor_ranks))
+    p, gram_part = left_sums(cot, order, q_init, inputs_t, fbq, factor_ranks)
     full_grad = full(cot, order, inputs_t, feedback)
-    gram_sum = sum_fsdp(gram(p))
-    rt = sum_all(right(full_grad, p))
-    inverse, factor_p = factor(gram_sum, p, factor_ranks)
+    rt_parts = [right(m, full_grad, p[m]) for m in range(len(p))]
+    inverse, factor_p, rt = sums(gram_part, rt_parts, jnp.stack(p), factor_ranks)
     new_error, factor_q = error(full_grad, factor_p, inverse, rt)
     return (factor_p, factor_q, new_error)
 

time: 177 us -> 150 us (0.85)
  waiting for transfers between devices: 83.2 us -> 41 us
  Pallas kernels: 43.9 us -> 68.9 us
  local copies, waits for them, and re-layouts: 21.1 us -> 8.92 us
  starting transfers between devices: 23.3 us -> 26.5 us
    ppermute x22 -> x30, waiting for transfers between devices: 83.2 us -> 41 us  [across(): return lax.ppermute(x, axis, [(i, i ^ bit) for i in range(size)])]
    unnamed x29 -> x35, local copies, waits for them, and re-layouts: 19.2 us -> 5.95 us
    pallas_call x1, Pallas kernels: 5 us -> 12.7 us  [full(): pl.pallas_call(full_kernel, grid_spec=pltpu.PrefetchScalarGridSpec(num_sc...]
    pallas_call x3 -> x10, Pallas kernels: 8.09 us -> 15 us  [the longest x2 9.56 us: right(): pl.pallas_call(right_kernel, grid=(rows // tile,), in_specs=[pl.BlockSpec...]
    pallas_call x1, Pallas kernels: 4.35 us -> 9.53 us  [feedback_q(): pl.pallas_call(feedback_q_kernel, grid_spec=pltpu.PrefetchScalarGridSpec(...]
    pallas_call x1, Pallas kernels: 7.15 us -> 12.2 us  [error(): pl.pallas_call(error_kernel, grid=(count, rows // tile), in_specs=[pl.Blo...]
    ppermute x22 -> x30, starting transfers between devices: 23.3 us -> 26.5 us  [across(): return lax.ppermute(x, axis, [(i, i ^ bit) for i in range(size)])]
  transfers between devices with their start and end apart: 22 -> 30, of which waited for: 15 -> 18; matrix products, arithmetic and copies ran while one was open for 3% -> 5% of each run, Pallas kernels for 17% -> 36%
where the time goes in v2:
time: 150 us; the launch traced here: 149 us
  Pallas kernels  68.9 us (46%)
  waiting for transfers between devices  41 us (27%)
  starting transfers between devices  26.5 us (18%)
  local copies, waits for them, and re-layouts  8.92 us (6%)
  other arithmetic  2.55 us (2%)
    ppermute x30, waiting for transfers between devices, across(): return lax.ppermute(x, axis, [(i, i ^ bit) for i in range(size)])  41 us
    ppermute x30, starting transfers between devices, across(): return lax.ppermute(x, axis, [(i, i ^ bit) for i in range(size)])  26.5 us
    pallas_call x1, Pallas kernels, factor(): pl.pallas_call(factor_kernel, in_specs=[SMEM, VMEM, VMEM], out_specs=[VME...  19.4 us
    pallas_call x1, Pallas kernels, full(): pl.pallas_call(full_kernel, grid_spec=pltpu.PrefetchScalarGridSpec(num_sc...  12.7 us
    pallas_call x1, Pallas kernels, error(): pl.pallas_call(error_kernel, grid=(count, rows // tile), in_specs=[pl.Blo...  12.2 us
    pallas_call x2, Pallas kernels, right(): pl.pallas_call(right_kernel, grid=(rows // tile,), in_specs=[pl.BlockSpec...  9.56 us
    pallas_call x1, Pallas kernels, feedback_q(): pl.pallas_call(feedback_q_kernel, grid_spec=pltpu.PrefetchScalarGridSpec(...  9.53 us
    unnamed x35, local copies, waits for them, and re-layouts  5.95 us
  transfers between devices with their start and end apart: 30, of which 18 were waited for; matrix products, arithmetic and copies ran while one was open for 5% of the time, Pallas kernels for 36%

profile of v2, /device:TPU:0, one launch (start us, length us, event | category | flops | bytes accessed | tf_op | source)
XLA Modules:
  0.0 149.1 jit_solution(8046312785560069464)
XLA Ops:
  0.6 0.5 collective-permute-start
  1.1 2.6 %collective-permute-start.3 = (bf16[2,512,128]{2,1,0:T(8,128)(2,1)}, bf16[2,512,128]{2,1,0:T(8,128)(2,1)S(1)}, u32[]{:S(2)}, u32[]{:S(2)}) collective-permute-start(bf16[2,512,128]{2,1,0:T(8,128)(2,1)} %param.6), channel_id=1, source_target_pairs={{0,4},{1,5},{2,6},{3,7},{4,0},{5,1},{6,2},{7,3},{8,12},{9,13},{10,... | collective-permute-start | bytes 786440 | tf_op jit(solution)/shard_map/ppermute | solution.py:423
  3.7 1.5 %collective-permute-start.1 = (bf16[2,512,128]{2,1,0:T(8,128)(2,1)}, bf16[2,512,128]{2,1,0:T(8,128)(2,1)}, u32[]{:S(2)}, u32[]{:S(2)}) collective-permute-start(bf16[2,512,128]{2,1,0:T(8,128)(2,1)} %param.6), channel_id=1, source_target_pairs={{0,2},{1,3},{2,0},{3,1},{4,6},{5,7},{6,4},{7,5},{8,10},{9,11},{10,... | collective-permute-start | bytes 786440 | tf_op jit(solution)/shard_map/ppermute | solution.py:423
  5.2 1.5 %copy.8 = bf16[512,1024]{0,1:T(8,128)(2,1)S(1)} copy(bf16[512,1024]{1,0:T(8,128)(2,1)} %param.5) | data formatting | bytes 2097152 | tf_op args[0]
  6.8 9.5 %feedback_q.1.fbq_ref = f32[2,1024,128]{2,1,0:T(8,128)} custom-call(s32[2]{0:T(128)} %ranks_ref.7, f32[2,1,1024,1024]{3,2,1,0:T(8,128)} %fb_ref.3, f32[2,1024,128]{2,1,0:T(8,128)} %q_ref.5), custom_call_target="tpu_custom_call" | custom-call | tf_op jit(solution)/shard_map/feedback_q/pallas_call | solution.py:61
  16.4 0.6 collective-permute-start.6
  17.0 0.9 split.24
  18.1 0.5 collective-permute-start.2
  18.6 1.0 bitcast_dynamic-update-slice_fusion.6
  19.6 1.0 bitcast_dynamic-update-slice_fusion.5
  20.5 2.4 %collective-permute-done.5 = bf16[2,256,128]{2,1,0:T(8,128)(2,1)S(1)} collective-permute-done((bf16[2,256,128]{2,1,0:T(8,128)(2,1)S(1)}, bf16[2,256,128]{2,1,0:T(8,128)(2,1)S(1)}, u32[]{:S(2)}, u32[]{:S(2)}) %collective-permute-start.5) | collective-permute-done | bytes 131104 | tf_op jit(solution)/shard_map/ppermute | solution.py:423
  23.3 1.3 collective-permute-done.7
  24.7 2.0 %left_code_0.1 = (f32[512,128]{1,0:T(8,128)S(1)}, s16[528,128]{1,0:T(8,128)(2,1)S(1)}) custom-call(s32[2]{0:T(128)S(1)} %copy-done.9, s32[8]{0:T(128)S(1)} %iota_xor_fusion.order_ref, s32[1]{0:T(128)} %bitcast.low_ref, bf16[8,2,512,128]{3,2,1,0:T(8,128)(2,1)S(1)} %bitcast_dynamic-update-slice_fusion.cot_ref, f32[2,1024,128]{2,1,0:T(8,128)S(1)} %copy-done.2, ...), custom_call_target="tpu_custom_call" | custom-call | tf_op jit(solution)/shard_map/left_code_0/pallas_call | solution.py:164
  26.7 1.6 %collective-permute-start.8 = (s16[528,128]{1,0:T(8,128)(2,1)S(1)}, s16[528,128]{1,0:T(8,128)(2,1)S(1)}, u32[]{:S(2)}, u32[]{:S(2)}) collective-permute-start(s16[528,128]{1,0:T(8,128)(2,1)S(1)} %get-tuple-element.21), channel_id=1, source_target_pairs={{0,8},{8,0},{16,24},{24,16},{1,9},{9,1},{17,25},{25,17},{2,10},{10... | collective-permute-start | bytes 405512 | tf_op jit(solution)/shard_map/ppermute | solution.py:423
  28.4 2.0 %left_code_1.1 = (f32[512,128]{1,0:T(8,128)S(1)}, s16[528,128]{1,0:T(8,128)(2,1)S(1)}) custom-call(s32[2]{0:T(128)S(1)} %copy-done.9, s32[8]{0:T(128)S(1)} %iota_xor_fusion.order_ref, s32[1]{0:T(128)} %bitcast.low_ref, bf16[8,2,512,128]{3,2,1,0:T(8,128)(2,1)S(1)} %bitcast_dynamic-update-slice_fusion.cot_ref, f32[2,1024,128]{2,1,0:T(8,128)S(1)} %copy-done.2, ...), custom_call_target="tpu_custom_call" | custom-call | tf_op jit(solution)/shard_map/left_code_1/pallas_call | solution.py:164
  30.4 0.5 collective-permute-start.11
  30.9 1.5 %collective-permute-done.8.theirs_ref = s16[528,128]{1,0:T(8,128)(2,1)S(1)} collective-permute-done((s16[528,128]{1,0:T(8,128)(2,1)S(1)}, s16[528,128]{1,0:T(8,128)(2,1)S(1)}, u32[]{:S(2)}, u32[]{:S(2)}) %collective-permute-start.8) | collective-permute-done | bytes 135200 | tf_op jit(solution)/shard_map/ppermute | solution.py:423
  32.6 2.6 %collective-permute-start.9 = (s16[528,128]{1,0:T(8,128)(2,1)S(1)}, s16[528,128]{1,0:T(8,128)(2,1)S(1)}, u32[]{:S(2)}, u32[]{:S(2)}) collective-permute-start(s16[528,128]{1,0:T(8,128)(2,1)S(1)} %add_code.4.mine_ref), channel_id=1, source_target_pairs={{0,16},{8,24},{16,0},{24,8},{1,17},{9,25},{17,1},{25,9},{2,18},{10... | collective-permute-start | bytes 405512 | tf_op jit(solution)/shard_map/ppermute | solution.py:423
  35.2 2.1 %collective-permute-done.11.theirs_ref = s16[528,128]{1,0:T(8,128)(2,1)S(1)} collective-permute-done((s16[528,128]{1,0:T(8,128)(2,1)S(1)}, s16[528,128]{1,0:T(8,128)(2,1)S(1)}, u32[]{:S(2)}, u32[]{:S(2)}) %collective-permute-start.11) | collective-permute-done | bytes 135200 | tf_op jit(solution)/shard_map/ppermute | solution.py:423
  37.5 2.2 %collective-permute-start.12 = (s16[528,128]{1,0:T(8,128)(2,1)S(1)}, s16[528,128]{1,0:T(8,128)(2,1)S(1)}, u32[]{:S(2)}, u32[]{:S(2)}) collective-permute-start(s16[528,128]{1,0:T(8,128)(2,1)S(1)} %add_code.6.mine_ref), channel_id=1, source_target_pairs={{0,16},{8,24},{16,0},{24,8},{1,17},{9,25},{17,1},{25,9},{2,18},{10... | collective-permute-start | bytes 405512 | tf_op jit(solution)/shard_map/ppermute | solution.py:423
  39.7 5.2 %collective-permute-done.9.theirs_ref = s16[528,128]{1,0:T(8,128)(2,1)S(1)} collective-permute-done((s16[528,128]{1,0:T(8,128)(2,1)S(1)}, s16[528,128]{1,0:T(8,128)(2,1)S(1)}, u32[]{:S(2)}, u32[]{:S(2)}) %collective-permute-start.9) | collective-permute-done | bytes 135200 | tf_op jit(solution)/shard_map/ppermute | solution.py:423
  44.9 0.2 add_code.5.mine_ref
  45.2 1.9 %collective-permute-done.12.theirs_ref = s16[528,128]{1,0:T(8,128)(2,1)S(1)} collective-permute-done((s16[528,128]{1,0:T(8,128)(2,1)S(1)}, s16[528,128]{1,0:T(8,128)(2,1)S(1)}, u32[]{:S(2)}, u32[]{:S(2)}) %collective-permute-start.12) | collective-permute-done | bytes 135200 | tf_op jit(solution)/shard_map/ppermute | solution.py:423
  47.3 0.6 collective-permute-start.13
  47.9 3.2 %collective-permute-done.10.theirs_ref = s16[528,128]{1,0:T(8,128)(2,1)S(1)} collective-permute-done((s16[528,128]{1,0:T(8,128)(2,1)S(1)}, s16[528,128]{1,0:T(8,128)(2,1)S(1)}, u32[]{:S(2)}, u32[]{:S(2)}) %collective-permute-start.10) | collective-permute-done | bytes 135200 | tf_op jit(solution)/shard_map/ppermute | solution.py:423
  51.1 0.4 whole_left.2
  51.5 0.8 copy-done.4
  52.4 0.7 collective-permute-done.13.theirs_ref
  53.0 0.4 whole_left.3
  53.5 0.8 copy-done.6
  54.4 12.7 %full.1.full_ref = f32[2,1,1024,1024]{3,2,1,0:T(8,128)} custom-call(s32[8]{0:T(128)} %copy-done.10, bf16[8,2,512,128]{3,2,1,0:T(8,128)(2,1)} %copy-done, bf16[1024,512]{1,0:T(8,128)(2,1)} %bitcast.32, f32[2,1,1024,1024]{3,2,1,0:T(8,128)} %fb_ref.3), custom_call_target="tpu_custom_call" | custom-call | tf_op jit(solution)/shard_map/full/pallas_call | solution.py:244
  67.2 4.7 %right_1.1 = f32[128,1024]{1,0:T(8,128)} custom-call(f32[2,1,1024,1024]{3,2,1,0:T(8,128)} %full.1.full_ref, f32[1024,128]{1,0:T(8,128)} %copy-done.6), custom_call_target="tpu_custom_call" | custom-call | tf_op jit(solution)/shard_map/right_1/pallas_call | solution.py:283
  71.9 1.6 %collective-permute-start.15 = (f32[2,128,128]{2,1,0:T(8,128)S(1)}, f32[2,128,128]{2,1,0:T(8,128)S(1)}, u32[]{:S(2)}, u32[]{:S(2)}) collective-permute-start(f32[2,128,128]{2,1,0:T(8,128)S(1)} %fusion.5), channel_id=1, source_target_pairs={{0,2},{1,3},{2,0},{3,1},{4,6},{5,7},{6,4},{7,5},{8,10},{9,11},{10,... | collective-permute-start | bytes 393224 | tf_op jit(solution)/shard_map/ppermute | solution.py:423
  73.5 1.0 dynamic-slice_bitcast_fusion
  74.5 4.8 %right_0.1 = f32[128,1024]{1,0:T(8,128)} custom-call(f32[2,1,1024,1024]{3,2,1,0:T(8,128)} %full.1.full_ref, f32[1024,128]{1,0:T(8,128)} %copy-done.4), custom_call_target="tpu_custom_call" | custom-call | tf_op jit(solution)/shard_map/right_0/pallas_call | solution.py:283
  79.3 0.2 collective-permute-start.18
  79.5 1.0 dynamic-slice_bitcast_fusion.1
  80.5 0.4 collective-permute-start.17
  80.9 0.5 collective-permute-start.16
  81.5 0.6 collective-permute-done.17
  82.1 1.0 bitcast_add_fusion.1
  83.1 1.0 collective-permute-start.21
  84.2 0.6 collective-permute-start.19
  84.8 4.6 %collective-permute-done.21 = f32[2,16,1024]{2,1,0:T(8,128)S(1)} collective-permute-done((f32[2,16,1024]{2,1,0:T(8,128)S(1)}, f32[2,16,1024]{2,1,0:T(8,128)S(1)}, u32[]{:S(2)}, u32[]{:S(2)}) %collective-permute-start.21) | collective-permute-done | bytes 131104 | tf_op jit(solution)/shard_map/ppermute | solution.py:423
  89.4 0.6 collective-permute-start.22
  90.0 0.8 collective-permute-start.20
  90.9 2.9 %collective-permute-done.22 = f32[2,8,1024]{2,1,0:T(8,128)S(1)} collective-permute-done((f32[2,8,1024]{2,1,0:T(8,128)S(1)}, f32[2,8,1024]{2,1,0:T(8,128)S(1)}, u32[]{:S(2)}, u32[]{:S(2)}) %collective-permute-start.22) | collective-permute-done | bytes 65568 | tf_op jit(solution)/shard_map/ppermute | solution.py:423
  93.7 0.6 collective-permute-done.20
  94.4 0.3 collective-permute-start.23
  94.7 4.7 %collective-permute-done.23 = f32[2,16,1024]{2,1,0:T(8,128)S(1)} collective-permute-done((f32[2,16,1024]{2,1,0:T(8,128)S(1)}, f32[2,16,1024]{2,1,0:T(8,128)S(1)}, u32[]{:S(2)}, u32[]{:S(2)}) %collective-permute-start.23) | collective-permute-done | bytes 131104 | tf_op jit(solution)/shard_map/ppermute | solution.py:423
  99.4 1.9 %collective-permute-start.24 = (f32[2,16,1024]{2,1,0:T(8,128)S(1)}, f32[2,16,1024]{2,1,0:T(8,128)S(1)}, u32[]{:S(2)}, u32[]{:S(2)}) collective-permute-start(f32[2,16,1024]{2,1,0:T(8,128)S(1)} %fusion.4), channel_id=1, source_target_pairs={{0,16},{8,24},{16,0},{24,8},{1,17},{9,25},{17,1},{25,9},{2,18},{10... | collective-permute-start | bytes 393224 | tf_op jit(solution)/shard_map/ppermute | solution.py:423
  101.4 19.4 %factor.1 = (f32[2,128,128]{2,1,0:T(8,128)S(1)}, f32[2,1024,128]{2,1,0:T(8,128)}) custom-call(s32[2]{0:T(128)S(1)} %copy-done.9, f32[2,128,128]{2,1,0:T(8,128)S(1)} %add.70.g_ref, f32[2,1024,128]{2,1,0:T(8,128)S(1)} %pad_maximum_fusion.p_ref), custom_call_target="tpu_custom_call" | custom-call | tf_op jit(solution)/shard_map/factor/pallas_call | solution.py:357
  120.8 0.6 copy-done.8
  121.5 1.1 collective-permute-start.25
  122.6 1.0 collective-permute-start.27
  123.6 2.9 %collective-permute-done.25 = f32[2,8,1024]{2,1,0:T(8,128)S(1)} collective-permute-done((f32[2,8,1024]{2,1,0:T(8,128)S(1)}, f32[2,8,1024]{2,1,0:T(8,128)S(1)}, u32[]{:S(2)}, u32[]{:S(2)}) %collective-permute-start.25) | collective-permute-done | bytes 65568 | tf_op jit(solution)/shard_map/ppermute | solution.py:423
  126.4 1.1 collective-permute-done.27
  127.6 1.0 collective-permute-start.28
  128.6 1.6 %collective-permute-start.26 = (f32[2,16,1024]{2,1,0:T(8,128)S(1)}, f32[2,16,1024]{2,1,0:T(8,128)S(1)}, u32[]{:S(2)}, u32[]{:S(2)}) collective-permute-start(f32[2,16,1024]{2,1,0:T(8,128)S(1)} %pad_maximum_fusion.5), channel_id=1, source_target_pairs={{0,2},{1,3},{2,0},{3,1},{4,6},{5,7},{6,4},{7,5},{8,10},{9,11},{10,... | collective-permute-start | bytes 393224 | tf_op jit(solution)/shard_map/ppermute | solution.py:423
  130.2 2.4 %collective-permute-done.28 = f32[2,16,1024]{2,1,0:T(8,128)S(1)} collective-permute-done((f32[2,16,1024]{2,1,0:T(8,128)S(1)}, f32[2,16,1024]{2,1,0:T(8,128)S(1)}, u32[]{:S(2)}, u32[]{:S(2)}) %collective-permute-start.28) | collective-permute-done | bytes 131104 | tf_op jit(solution)/shard_map/ppermute | solution.py:423
  132.6 1.0 collective-permute-done.26
  133.8 1.9 %collective-permute-done.29 = f32[2,64,1024]{2,1,0:T(8,128)S(1)} collective-permute-done((f32[2,64,1024]{2,1,0:T(8,128)S(1)}, f32[2,64,1024]{2,1,0:T(8,128)S(1)}, u32[]{:S(2)}, u32[]{:S(2)}) %collective-permute-start.29) | collective-permute-done | bytes 524320 | tf_op jit(solution)/shard_map/ppermute | solution.py:423
  135.8 1.0 pad_maximum_fusion.1.rt_ref
  136.9 12.2 %error.1 = (f32[2,1,1024,1024]{3,2,1,0:T(8,128)}, f32[2,1024,128]{2,1,0:T(8,128)}) custom-call(f32[2,1,1024,1024]{3,2,1,0:T(8,128)} %full.1.full_ref, f32[2,1024,128]{2,1,0:T(8,128)} %get-tuple-element.17.fp_ref, f32[2,128,128]{2,1,0:T(8,128)} %copy-done.8, f32[2,128,1024]{2,1,0:T(8,128)} %pad_maximum_fusion.1.rt_ref), custom_call_target="tpu_custom_call" | custom-call | tf_op jit(solution)/shard_map/error/pallas_call | solution.py:394
  (80 shorter events, 1.9 us)
Async XLA Ops:
  0.6 17.9 %collective-permute-start = (bf16[2,512,128]{2,1,0:T(8,128)(2,1)}, bf16[2,512,128]{2,1,0:T(8,128)(2,1)}, u32[]{:S(2)}, u32[]{:S(2)}) collective-permute-start(bf16[2,512,128]{2,1,0:T(8,128)(2,1)} %param.6), channel_id=1, source_target_pairs={{0,1},{1,0},{2,3},{3,2},{4,5},{5,4},{6,7},{7,6},{8,9},{9,8},{10,11... | collective-permute-start | bytes 786440 | tf_op jit(solution)/shard_map/ppermute | solution.py:423
  1.1 15.2 %collective-permute-start.3 = (bf16[2,512,128]{2,1,0:T(8,128)(2,1)}, bf16[2,512,128]{2,1,0:T(8,128)(2,1)S(1)}, u32[]{:S(2)}, u32[]{:S(2)}) collective-permute-start(bf16[2,512,128]{2,1,0:T(8,128)(2,1)} %param.6), channel_id=1, source_target_pairs={{0,4},{1,5},{2,6},{3,7},{4,0},{5,1},{6,2},{7,3},{8,12},{9,13},{10,... | collective-permute-start | bytes 786440 | tf_op jit(solution)/shard_map/ppermute | solution.py:423
  3.7 13.2 %collective-permute-start.1 = (bf16[2,512,128]{2,1,0:T(8,128)(2,1)}, bf16[2,512,128]{2,1,0:T(8,128)(2,1)}, u32[]{:S(2)}, u32[]{:S(2)}) collective-permute-start(bf16[2,512,128]{2,1,0:T(8,128)(2,1)} %param.6), channel_id=1, source_target_pairs={{0,2},{1,3},{2,0},{3,1},{4,6},{5,7},{6,4},{7,5},{8,10},{9,11},{10,... | collective-permute-start | bytes 786440 | tf_op jit(solution)/shard_map/ppermute | solution.py:423
  5.2 23.1 %copy-start.10 = (s32[8]{0:T(128)}, s32[8]{0:T(128)S(1)}, u32[]{:S(2)}) copy-start(s32[8]{0:T(128)S(1)} %iota_xor_fusion.order_ref) | copy-start | bytes 100
  6.7 21.6 %copy-start.1 = (bf16[512,1024]{0,1:T(8,128)(2,1)}, bf16[512,1024]{0,1:T(8,128)(2,1)S(1)}, u32[]{:S(2)}) copy-start(bf16[512,1024]{0,1:T(8,128)(2,1)S(1)} %copy.8) | copy-start | bytes 3145732
  6.8 9.5 %copy-start.12 = (bf16[2,512,128]{2,1,0:T(8,128)(2,1)S(1)}, bf16[2,512,128]{2,1,0:T(8,128)(2,1)}, u32[]{:S(2)}) copy-start(bf16[2,512,128]{2,1,0:T(8,128)(2,1)} %param.6) | copy-start | bytes 786436
  16.4 6.6 %collective-permute-start.6 = (bf16[2,256,128]{2,1,0:T(8,128)(2,1)S(1)}, bf16[2,256,128]{2,1,0:T(8,128)(2,1)S(1)}, u32[]{:S(2)}, u32[]{:S(2)}) collective-permute-start(bf16[2,256,128]{2,1,0:T(8,128)(2,1)S(1)} %split.25), channel_id=1, source_target_pairs={{0,2},{1,3},{2,0},{3,1},{4,6},{5,7},{6,4},{7,5},{8,10},{9,11},{10,... | collective-permute-start | bytes 393224 | tf_op jit(solution)/shard_map/ppermute | solution.py:423
  17.9 6.8 %copy-start.2 = (f32[2,1024,128]{2,1,0:T(8,128)S(1)}, f32[2,1024,128]{2,1,0:T(8,128)}, u32[]{:S(2)}) copy-start(f32[2,1024,128]{2,1,0:T(8,128)} %q_ref.5) | copy-start | bytes 3145732
  17.9 6.8 %copy-start.3 = (f32[2,1024,128]{2,1,0:T(8,128)S(1)}, f32[2,1024,128]{2,1,0:T(8,128)}, u32[]{:S(2)}) copy-start(f32[2,1024,128]{2,1,0:T(8,128)} %feedback_q.1.fbq_ref) | copy-start | bytes 3145732
  17.9 6.8 %copy-start.9 = (s32[2]{0:T(128)S(1)}, s32[2]{0:T(128)}, u32[]{:S(2)}) copy-start(s32[2]{0:T(128)} %ranks_ref.7) | copy-start | bytes 28
  17.9 5.1 %collective-permute-start.5 = (bf16[2,256,128]{2,1,0:T(8,128)(2,1)S(1)}, bf16[2,256,128]{2,1,0:T(8,128)(2,1)S(1)}, u32[]{:S(2)}, u32[]{:S(2)}) collective-permute-start(bf16[2,256,128]{2,1,0:T(8,128)(2,1)S(1)} %split.24), channel_id=1, source_target_pairs={{0,4},{1,5},{2,6},{3,7},{4,0},{5,1},{6,2},{7,3},{8,12},{9,13},{10,... | collective-permute-start | bytes 393224 | tf_op jit(solution)/shard_map/ppermute | solution.py:423
  18.1 5.2 %collective-permute-start.4 = (bf16[2,512,128]{2,1,0:T(8,128)(2,1)S(1)}, bf16[2,512,128]{2,1,0:T(8,128)(2,1)S(1)}, u32[]{:S(2)}, u32[]{:S(2)}) collective-permute-start(bf16[2,512,128]{2,1,0:T(8,128)(2,1)S(1)} %collective-permute-done.3), channel_id=1, source_target_pairs={{0,1},{1,0},{2,3},{3,2},{4,5},{5,4},{6,7},{7,6},{8,9},{9,8},{10,11... | collective-permute-start | bytes 786440 | tf_op jit(solution)/shard_map/ppermute | solution.py:423
  18.1 5.0 %collective-permute-start.2 = (bf16[2,512,128]{2,1,0:T(8,128)(2,1)}, bf16[2,512,128]{2,1,0:T(8,128)(2,1)S(1)}, u32[]{:S(2)}, u32[]{:S(2)}) collective-permute-start(bf16[2,512,128]{2,1,0:T(8,128)(2,1)} %collective-permute-done.1), channel_id=1, source_target_pairs={{0,1},{1,0},{2,3},{3,2},{4,5},{5,4},{6,7},{7,6},{8,9},{9,8},{10,11... | collective-permute-start | bytes 786440 | tf_op jit(solution)/shard_map/ppermute | solution.py:423
  23.0 1.6 %collective-permute-start.7 = (bf16[2,512,128]{2,1,0:T(8,128)(2,1)S(1)}, bf16[2,512,128]{2,1,0:T(8,128)(2,1)S(1)}, u32[]{:S(2)}, u32[]{:S(2)}) collective-permute-start(bf16[2,512,128]{2,1,0:T(8,128)(2,1)S(1)} %constant_dynamic-update-slice_fusion), channel_id=1, source_target_pairs={{0,1},{1,0},{2,3},{3,2},{4,5},{5,4},{6,7},{7,6},{8,9},{9,8},{10,11... | collective-permute-start | bytes 786440 | tf_op jit(solution)/shard_map/ppermute | solution.py:423
  24.7 3.7 %copy-start = (bf16[8,2,512,128]{3,2,1,0:T(8,128)(2,1)}, bf16[8,2,512,128]{3,2,1,0:T(8,128)(2,1)S(1)}, u32[]{:S(2)}) copy-start(bf16[8,2,512,128]{3,2,1,0:T(8,128)(2,1)S(1)} %bitcast_dynamic-update-slice_fusion.cot_ref) | copy-start | bytes 6291460
  26.7 5.7 %collective-permute-start.8 = (s16[528,128]{1,0:T(8,128)(2,1)S(1)}, s16[528,128]{1,0:T(8,128)(2,1)S(1)}, u32[]{:S(2)}, u32[]{:S(2)}) collective-permute-start(s16[528,128]{1,0:T(8,128)(2,1)S(1)} %get-tuple-element.21), channel_id=1, source_target_pairs={{0,8},{8,0},{16,24},{24,16},{1,9},{9,1},{17,25},{25,17},{2,10},{10... | collective-permute-start | bytes 405512 | tf_op jit(solution)/shard_map/ppermute | solution.py:423
  30.4 7.0 %collective-permute-start.11 = (s16[528,128]{1,0:T(8,128)(2,1)S(1)}, s16[528,128]{1,0:T(8,128)(2,1)S(1)}, u32[]{:S(2)}, u32[]{:S(2)}) collective-permute-start(s16[528,128]{1,0:T(8,128)(2,1)S(1)} %get-tuple-element.24), channel_id=1, source_target_pairs={{0,8},{8,0},{16,24},{24,16},{1,9},{9,1},{17,25},{25,17},{2,10},{10... | collective-permute-start | bytes 405512 | tf_op jit(solution)/shard_map/ppermute | solution.py:423
  32.6 12.3 %collective-permute-start.9 = (s16[528,128]{1,0:T(8,128)(2,1)S(1)}, s16[528,128]{1,0:T(8,128)(2,1)S(1)}, u32[]{:S(2)}, u32[]{:S(2)}) collective-permute-start(s16[528,128]{1,0:T(8,128)(2,1)S(1)} %add_code.4.mine_ref), channel_id=1, source_target_pairs={{0,16},{8,24},{16,0},{24,8},{1,17},{9,25},{17,1},{25,9},{2,18},{10... | collective-permute-start | bytes 405512 | tf_op jit(solution)/shard_map/ppermute | solution.py:423
  37.5 9.7 %collective-permute-start.12 = (s16[528,128]{1,0:T(8,128)(2,1)S(1)}, s16[528,128]{1,0:T(8,128)(2,1)S(1)}, u32[]{:S(2)}, u32[]{:S(2)}) collective-permute-start(s16[528,128]{1,0:T(8,128)(2,1)S(1)} %add_code.6.mine_ref), channel_id=1, source_target_pairs={{0,16},{8,24},{16,0},{24,8},{1,17},{9,25},{17,1},{25,9},{2,18},{10... | collective-permute-start | bytes 405512 | tf_op jit(solution)/shard_map/ppermute | solution.py:423
  45.1 6.0 %collective-permute-start.10 = (s16[528,128]{1,0:T(8,128)(2,1)S(1)}, s16[528,128]{1,0:T(8,128)(2,1)S(1)}, u32[]{:S(2)}, u32[]{:S(2)}) collective-permute-start(s16[528,128]{1,0:T(8,128)(2,1)S(1)} %add_code.5.mine_ref), channel_id=1, source_target_pairs={{0,8},{8,0},{16,24},{24,16},{1,9},{9,1},{17,25},{25,17},{2,10},{10... | collective-permute-start | bytes 405512 | tf_op jit(solution)/shard_map/ppermute | solution.py:423
  47.3 5.7 %collective-permute-start.13 = (s16[528,128]{1,0:T(8,128)(2,1)S(1)}, s16[528,128]{1,0:T(8,128)(2,1)S(1)}, u32[]{:S(2)}, u32[]{:S(2)}) collective-permute-start(s16[528,128]{1,0:T(8,128)(2,1)S(1)} %add_code.7.mine_ref), channel_id=1, source_target_pairs={{0,8},{8,0},{16,24},{24,16},{1,9},{9,1},{17,25},{25,17},{2,10},{10... | collective-permute-start | bytes 405512 | tf_op jit(solution)/shard_map/ppermute | solution.py:423
  51.5 0.8 copy-start.4
  53.5 0.8 copy-start.6
  54.3 17.6 %collective-permute-start.14 = (f32[2,128,128]{2,1,0:T(8,128)S(1)}, f32[2,128,128]{2,1,0:T(8,128)S(1)}, u32[]{:S(2)}, u32[]{:S(2)}) collective-permute-start(f32[2,128,128]{2,1,0:T(8,128)S(1)} %pad_maximum_fusion.3), channel_id=1, source_target_pairs={{0,1},{1,0},{2,3},{3,2},{4,5},{5,4},{6,7},{7,6},{8,9},{9,8},{10,11... | collective-permute-start | bytes 393224 | tf_op jit(solution)/shard_map/ppermute | solution.py:423
  71.9 8.9 %collective-permute-start.15 = (f32[2,128,128]{2,1,0:T(8,128)S(1)}, f32[2,128,128]{2,1,0:T(8,128)S(1)}, u32[]{:S(2)}, u32[]{:S(2)}) collective-permute-start(f32[2,128,128]{2,1,0:T(8,128)S(1)} %fusion.5), channel_id=1, source_target_pairs={{0,2},{1,3},{2,0},{3,1},{4,6},{5,7},{6,4},{7,5},{8,10},{9,11},{10,... | collective-permute-start | bytes 393224 | tf_op jit(solution)/shard_map/ppermute | solution.py:423
  74.5 6.9 %copy-start.11 = (f32[128,1024]{1,0:T(8,128)S(1)}, f32[128,1024]{1,0:T(8,128)}, u32[]{:S(2)}) copy-start(f32[128,1024]{1,0:T(8,128)} %right_1.1) | copy-start | bytes 1572868
  79.3 2.1 %collective-permute-start.18 = (f32[1,64,1024]{2,1,0:T(8,128)S(1)}, f32[1,64,1024]{2,1,0:T(8,128)S(1)}, u32[]{:S(2)}, u32[]{:S(2)}) collective-permute-start(f32[1,64,1024]{2,1,0:T(8,128)S(1)} %dynamic-slice_bitcast_fusion), channel_id=1, source_target_pairs={{0,1},{1,0},{2,3},{3,2},{4,5},{5,4},{6,7},{7,6},{8,9},{9,8},{10,11... | collective-permute-start | bytes 786440 | tf_op jit(solution)/shard_map/ppermute | solution.py:423
  80.5 1.6 %collective-permute-start.17 = (f32[1,64,1024]{2,1,0:T(8,128)S(1)}, f32[1,64,1024]{2,1,0:T(8,128)S(1)}, u32[]{:S(2)}, u32[]{:S(2)}) collective-permute-start(f32[1,64,1024]{2,1,0:T(8,128)S(1)} %dynamic-slice_bitcast_fusion.1), channel_id=1, source_target_pairs={{0,1},{1,0},{2,3},{3,2},{4,5},{5,4},{6,7},{7,6},{8,9},{9,8},{10,11... | collective-permute-start | bytes 786440 | tf_op jit(solution)/shard_map/ppermute | solution.py:423
  80.9 13.8 %collective-permute-start.16 = (f32[2,128,128]{2,1,0:T(8,128)S(1)}, f32[2,128,128]{2,1,0:T(8,128)S(1)}, u32[]{:S(2)}, u32[]{:S(2)}) collective-permute-start(f32[2,128,128]{2,1,0:T(8,128)S(1)} %fusion.7), channel_id=1, source_target_pairs={{0,4},{1,5},{2,6},{3,7},{4,0},{5,1},{6,2},{7,3},{8,12},{9,13},{10,... | collective-permute-start | bytes 393224 | tf_op jit(solution)/shard_map/ppermute | solution.py:423
  83.1 18.3 %copy-start.5 = (f32[1024,128]{1,0:T(8,128)S(1)}, f32[1024,128]{1,0:T(8,128)}, u32[]{:S(2)}) copy-start(f32[1024,128]{1,0:T(8,128)} %copy-done.4) | copy-start | bytes 1572868
  83.1 18.3 %copy-start.7 = (f32[1024,128]{1,0:T(8,128)S(1)}, f32[1024,128]{1,0:T(8,128)}, u32[]{:S(2)}) copy-start(f32[1024,128]{1,0:T(8,128)} %copy-done.6) | copy-start | bytes 1572868
  83.1 6.2 %collective-permute-start.21 = (f32[2,16,1024]{2,1,0:T(8,128)S(1)}, f32[2,16,1024]{2,1,0:T(8,128)S(1)}, u32[]{:S(2)}, u32[]{:S(2)}) collective-permute-start(f32[2,16,1024]{2,1,0:T(8,128)S(1)} %fusion.1), channel_id=1, source_target_pairs={{0,4},{1,5},{2,6},{3,7},{4,0},{5,1},{6,2},{7,3},{8,12},{9,13},{10,... | collective-permute-start | bytes 393224 | tf_op jit(solution)/shard_map/ppermute | solution.py:423
  84.2 5.8 %collective-permute-start.19 = (f32[2,16,1024]{2,1,0:T(8,128)S(1)}, f32[2,16,1024]{2,1,0:T(8,128)S(1)}, u32[]{:S(2)}, u32[]{:S(2)}) collective-permute-start(f32[2,16,1024]{2,1,0:T(8,128)S(1)} %constant_dynamic-slice_fusion.2), channel_id=1, source_target_pairs={{0,2},{1,3},{2,0},{3,1},{4,6},{5,7},{6,4},{7,5},{8,10},{9,11},{10,... | collective-permute-start | bytes 393224 | tf_op jit(solution)/shard_map/ppermute | solution.py:423
  89.4 4.3 %collective-permute-start.22 = (f32[2,8,1024]{2,1,0:T(8,128)S(1)}, f32[2,8,1024]{2,1,0:T(8,128)S(1)}, u32[]{:S(2)}, u32[]{:S(2)}) collective-permute-start(f32[2,8,1024]{2,1,0:T(8,128)S(1)} %constant_dynamic-slice_fusion), channel_id=1, source_target_pairs={{0,2},{1,3},{2,0},{3,1},{4,6},{5,7},{6,4},{7,5},{8,10},{9,11},{10,... | collective-permute-start | bytes 196616 | tf_op jit(solution)/shard_map/ppermute | solution.py:423
  90.0 4.3 %collective-permute-start.20 = (f32[2,8,1024]{2,1,0:T(8,128)S(1)}, f32[2,8,1024]{2,1,0:T(8,128)S(1)}, u32[]{:S(2)}, u32[]{:S(2)}) collective-permute-start(f32[2,8,1024]{2,1,0:T(8,128)S(1)} %constant_dynamic-slice_fusion.1), channel_id=1, source_target_pairs={{0,4},{1,5},{2,6},{3,7},{4,0},{5,1},{6,2},{7,3},{8,12},{9,13},{10,... | collective-permute-start | bytes 196616 | tf_op jit(solution)/shard_map/ppermute | solution.py:423
  94.4 5.0 %collective-permute-start.23 = (f32[2,16,1024]{2,1,0:T(8,128)S(1)}, f32[2,16,1024]{2,1,0:T(8,128)S(1)}, u32[]{:S(2)}, u32[]{:S(2)}) collective-permute-start(f32[2,16,1024]{2,1,0:T(8,128)S(1)} %pad_maximum_fusion.4), channel_id=1, source_target_pairs={{0,8},{8,0},{16,24},{24,16},{1,9},{9,1},{17,25},{25,17},{2,10},{10... | collective-permute-start | bytes 393224 | tf_op jit(solution)/shard_map/ppermute | solution.py:423
  99.4 22.0 %collective-permute-start.24 = (f32[2,16,1024]{2,1,0:T(8,128)S(1)}, f32[2,16,1024]{2,1,0:T(8,128)S(1)}, u32[]{:S(2)}, u32[]{:S(2)}) collective-permute-start(f32[2,16,1024]{2,1,0:T(8,128)S(1)} %fusion.4), channel_id=1, source_target_pairs={{0,16},{8,24},{16,0},{24,8},{1,17},{9,25},{17,1},{25,9},{2,18},{10... | collective-permute-start | bytes 393224 | tf_op jit(solution)/shard_map/ppermute | solution.py:423
  120.8 0.7 copy-start.8
  121.5 5.0 %collective-permute-start.25 = (f32[2,8,1024]{2,1,0:T(8,128)S(1)}, f32[2,8,1024]{2,1,0:T(8,128)S(1)}, u32[]{:S(2)}, u32[]{:S(2)}) collective-permute-start(f32[2,8,1024]{2,1,0:T(8,128)S(1)} %get-tuple-element.49), channel_id=1, source_target_pairs={{0,4},{1,5},{2,6},{3,7},{4,0},{5,1},{6,2},{7,3},{8,12},{9,13},{10,... | collective-permute-start | bytes 196616 | tf_op jit(solution)/shard_map/ppermute | solution.py:423
  122.6 5.0 %collective-permute-start.27 = (f32[2,8,1024]{2,1,0:T(8,128)S(1)}, f32[2,8,1024]{2,1,0:T(8,128)S(1)}, u32[]{:S(2)}, u32[]{:S(2)}) collective-permute-start(f32[2,8,1024]{2,1,0:T(8,128)S(1)} %get-tuple-element.50), channel_id=1, source_target_pairs={{0,2},{1,3},{2,0},{3,1},{4,6},{5,7},{6,4},{7,5},{8,10},{9,11},{10,... | collective-permute-start | bytes 196616 | tf_op jit(solution)/shard_map/ppermute | solution.py:423
  127.6 5.0 %collective-permute-start.28 = (f32[2,16,1024]{2,1,0:T(8,128)S(1)}, f32[2,16,1024]{2,1,0:T(8,128)S(1)}, u32[]{:S(2)}, u32[]{:S(2)}) collective-permute-start(f32[2,16,1024]{2,1,0:T(8,128)S(1)} %pad_maximum_fusion.6), channel_id=1, source_target_pairs={{0,4},{1,5},{2,6},{3,7},{4,0},{5,1},{6,2},{7,3},{8,12},{9,13},{10,... | collective-permute-start | bytes 393224 | tf_op jit(solution)/shard_map/ppermute | solution.py:423
  128.6 5.0 %collective-permute-start.26 = (f32[2,16,1024]{2,1,0:T(8,128)S(1)}, f32[2,16,1024]{2,1,0:T(8,128)S(1)}, u32[]{:S(2)}, u32[]{:S(2)}) collective-permute-start(f32[2,16,1024]{2,1,0:T(8,128)S(1)} %pad_maximum_fusion.5), channel_id=1, source_target_pairs={{0,2},{1,3},{2,0},{3,1},{4,6},{5,7},{6,4},{7,5},{8,10},{9,11},{10,... | collective-permute-start | bytes 393224 | tf_op jit(solution)/shard_map/ppermute | solution.py:423
  133.7 2.0 %collective-permute-start.29 = (f32[2,64,1024]{2,1,0:T(8,128)S(1)}, f32[2,64,1024]{2,1,0:T(8,128)S(1)}, u32[]{:S(2)}, u32[]{:S(2)}) collective-permute-start(f32[2,64,1024]{2,1,0:T(8,128)S(1)} %pad_maximum_fusion.2), channel_id=1, source_target_pairs={{0,1},{1,0},{2,3},{3,2},{4,5},{5,4},{6,7},{7,6},{8,9},{9,8},{10,11... | collective-permute-start | bytes 1572872 | tf_op jit(solution)/shard_map/ppermute | solution.py:423

commit v3 on v0

v3 whole, which is shorter than its diff:
```python
import functools

import jax
import jax.numpy as jnp
from jax import lax
from jax.experimental import pallas as pl
from jax.experimental.pallas import tpu as pltpu
from jax.sharding import PartitionSpec as P

F32 = jnp.float32
BF16 = jnp.bfloat16
VMEM = pl.BlockSpec(memory_space=pltpu.VMEM)
SMEM = pl.BlockSpec(memory_space=pltpu.SMEM)
MIB = 1024 * 1024


def halves(x):
    high = x.astype(BF16)
    return high, (x - high.astype(F32)).astype(BF16)


def mm(a, b):
    return jnp.dot(a, b, preferred_element_type=F32)


def mm_nt(a, b):
    return lax.dot_general(a, b, (((1,), (1,)), ((), ())), preferred_element_type=F32)


def params(size, steps=1):
    return pltpu.CompilerParams(
        vmem_limit_bytes=size * MIB, dimension_semantics=("arbitrary",) * steps
    )


def tile_of(rows):
    return min(rows, 256)


def in_vmem(shape, dtype):
    return pltpu.VMEM(shape, dtype)


def stay(x):
    return pltpu.with_memory_space_constraint(x, pltpu.VMEM)


def masked_halves(q, rank):
    column = lax.broadcasted_iota(jnp.int32, q.shape, 1)
    return halves(jnp.where(column < rank, q, 0.0))


def feedback_q_kernel(ranks_ref, fb_ref, q_ref, in_ref, held_ref, out_ref, in_t_ref, q2_ref, sems):
    count, rows, _ = held_ref.shape
    width = q_ref.shape[2]
    tile = tile_of(rows)
    copies = []
    for m in range(count):
        for i in range(rows // tile):
            part = pl.ds(i * tile, tile)
            copies.append(
                pltpu.make_async_copy(fb_ref.at[m, 0, part], held_ref.at[m, part], sems.at[len(copies)])
            )
            copies[-1].start()
    in_t_ref[...] = in_ref[...].T
    for m in range(count):
        q_high, q_low = masked_halves(q_ref[m], ranks_ref[m])
        q2_ref[m, :, :width] = q_high
        q2_ref[m, :, width:] = q_low
    for m in range(count):
        for i in range(rows // tile):
            part = pl.ds(i * tile, tile)
            copies[m * (rows // tile) + i].wait()
            high, low = halves(held_ref[m, part])
            both = mm(high, q2_ref[m])
            out_ref[m, part] = both[:, :width] + both[:, width:] + mm(low, q2_ref[m, :, :width])


def feedback_q(feedback, q_init, inputs, ranks):
    count, _, rows, columns = feedback.shape
    width = q_init.shape[2]
    return pl.pallas_call(
        feedback_q_kernel,
        in_specs=[SMEM, pl.BlockSpec(memory_space=pltpu.HBM), VMEM, VMEM],
        out_specs=[VMEM, VMEM, VMEM],
        out_shape=[
            in_vmem((count, rows, columns), F32),
            jax.ShapeDtypeStruct((count, rows, width), F32),
            jax.ShapeDtypeStruct(inputs.shape[::-1], inputs.dtype),
        ],
        scratch_shapes=[
            pltpu.VMEM((count, columns, 2 * width), BF16),
            pltpu.SemaphoreType.DMA((count * (rows // tile_of(rows)),)),
        ],
        compiler_params=pltpu.CompilerParams(vmem_limit_bytes=16 * MIB),
        name="feedback_q",
    )(ranks, pltpu.with_memory_space_constraint(feedback, pltpu.HBM), q_init, inputs)


def fill_cotangent(blocks, whole_ref):
    if len(blocks) == 1:
        whole_ref[...] = blocks[0][0]
        return
    me = lax.axis_index("fsdp")
    for r, block in enumerate(blocks):
        width = block.shape[2]
        start = pl.multiple_of((me ^ r) * width, width)
        whole_ref[:, pl.ds(start, width)] = block[0]


def gradient_q(whole, q, rank, inputs_t):
    width = q.shape[1]
    q_high, q_low = masked_halves(q, rank)
    both = mm(whole, jnp.concatenate([q_high, q_low], axis=1))
    c_high, c_low = halves(both[:, :width] + both[:, width:])
    both = mm(inputs_t, jnp.concatenate([c_high, c_low], axis=1))
    return both[:, :width] + both[:, width:]


def at_block(shape, m):
    return pl.BlockSpec((1, *shape[1:]), lambda *_: (m,) + (0,) * (len(shape) - 1))


def block_of(pieces, m):
    for piece in pieces:
        if m < piece.shape[0]:
            return piece, m
        m -= piece.shape[0]
    raise ValueError(m)


def left_kernel(m, ranks_ref, q_ref, in_ref, fbq_ref, *refs):
    *blocks, out_ref, whole_ref = refs
    fill_cotangent(blocks, whole_ref)
    out_ref[...] = fbq_ref[0] + gradient_q(whole_ref[...], q_ref[0], ranks_ref[m], in_ref[...])


def left(m, blocks, q_init, inputs_t, fbq, ranks):
    _, rows, width = fbq.shape
    arrays, indices = zip(*(block_of(pieces, m) for pieces in blocks))
    shape = (arrays[0].shape[1], q_init.shape[1])
    return pl.pallas_call(
        functools.partial(left_kernel, m),
        grid=(1,),
        in_specs=[SMEM, at_block(q_init.shape, m), VMEM, at_block(fbq.shape, m)]
        + [at_block(a.shape, i) for a, i in zip(arrays, indices)],
        out_specs=[
            pl.BlockSpec((rows, width), lambda i: (0, 0)),
            pl.BlockSpec(shape, lambda i: (0, 0)),
        ],
        out_shape=[
            jax.ShapeDtypeStruct((rows, width), F32),
            jax.ShapeDtypeStruct(shape, BF16),
        ],
        compiler_params=params(16),
        name=f"left_{m}",
    )(ranks, q_init, inputs_t, fbq, *arrays)


GROUPS = 16
LANES = 128


def encode(x, out_ref):
    rows, width = x.shape
    grouped = x.reshape(GROUPS, rows // GROUPS, width)
    top = jnp.max(jnp.abs(grouped), axis=1)
    level = jnp.ceil(jnp.log(jnp.maximum(top, 1e-30)) * 32.0) + 1.0
    up = jnp.exp(level * (-1.0 / 32.0)) * 32767.0
    code = jnp.round(grouped * up[:, None, :]).reshape(rows, width)
    out_ref[:rows] = code.astype(jnp.int32).astype(jnp.int16)
    out_ref[rows:] = level.astype(jnp.int32).astype(jnp.int16)


def decode(ref):
    rows = ref.shape[0] - GROUPS
    width = ref.shape[1]
    level = ref[rows:].astype(jnp.int32).astype(F32)
    down = jnp.exp(level * (1.0 / 32.0)) * (1.0 / 32767.0)
    code = ref[:rows].astype(jnp.int32).astype(F32).reshape(GROUPS, rows // GROUPS, width)
    return (code * down[:, None, :]).reshape(rows, width)


def left_code_kernel(m, ranks_ref, q_ref, in_ref, fbq_ref, *refs):
    *blocks, mine_ref, code_ref, whole_ref, p_ref = refs
    fill_cotangent(blocks, whole_ref)
    p = fbq_ref[0] + gradient_q(whole_ref[...], q_ref[0], ranks_ref[m], in_ref[...])
    p_ref[...] = p.reshape(p_ref.shape)
    low = lax.axis_index("dp") & 1
    mine_ref[...] = p_ref[low]
    encode(p_ref[1 - low], code_ref)


def left_code(m, blocks, q_init, inputs_t, fbq, ranks):
    _, rows, width = fbq.shape
    arrays, indices = zip(*(block_of(pieces, m) for pieces in blocks))
    shape = (arrays[0].shape[1], q_init.shape[1])
    half = rows // 2
    return pl.pallas_call(
        functools.partial(left_code_kernel, m),
        grid=(1,),
        in_specs=[SMEM, at_block(q_init.shape, m), VMEM, at_block(fbq.shape, m)]
        + [at_block(a.shape, i) for a, i in zip(arrays, indices)],
        out_specs=[
            pl.BlockSpec((half, width), lambda i: (0, 0)),
            pl.BlockSpec((half + GROUPS, width), lambda i: (0, 0)),
            pl.BlockSpec(shape, lambda i: (0, 0)),
        ],
        out_shape=[
            jax.ShapeDtypeStruct((half, width), F32),
            jax.ShapeDtypeStruct((half + GROUPS, width), jnp.int16),
            jax.ShapeDtypeStruct(shape, BF16),
        ],
        scratch_shapes=[pltpu.VMEM((2, half, width), F32)],
        compiler_params=params(16),
        name=f"left_code_{m}",
    )(ranks, q_init, inputs_t, fbq, *arrays)


def add_kernel(mine_ref, theirs_ref, out_ref):
    mine = mine_ref[...] if mine_ref.dtype == F32 else decode(mine_ref)
    encode(mine + decode(theirs_ref), out_ref)


def add_code(mine, theirs):
    return pl.pallas_call(
        add_kernel,
        in_specs=[VMEM, VMEM],
        out_specs=VMEM,
        out_shape=jax.ShapeDtypeStruct(theirs.shape, jnp.int16),
        compiler_params=pltpu.CompilerParams(vmem_limit_bytes=16 * MIB),
        name="add_code",
    )(mine, theirs)


def whole_left_kernel(mine_ref, theirs_ref, p_ref, gram_ref):
    half, width = mine_ref.shape[0] - GROUPS, mine_ref.shape[1]
    low = lax.axis_index("dp") & 1
    p_ref[pl.ds(pl.multiple_of(low * half, half), half)] = decode(mine_ref)
    p_ref[pl.ds(pl.multiple_of((1 - low) * half, half), half)] = decode(theirs_ref)
    gram_ref[...] = gram_of(p_ref[...])


def whole_left(mine, theirs):
    half, width = mine.shape[0] - GROUPS, mine.shape[1]
    return pl.pallas_call(
        whole_left_kernel,
        in_specs=[VMEM, VMEM],
        out_specs=[VMEM, VMEM],
        out_shape=[
            jax.ShapeDtypeStruct((2 * half, width), F32),
            jax.ShapeDtypeStruct((width, width), F32),
        ],
        compiler_params=pltpu.CompilerParams(vmem_limit_bytes=16 * MIB),
        name="whole_left",
    )(mine, theirs)


def full_kernel(m, held_ref, in_ref, whole_ref, out_ref):
    rows = out_ref.shape[0]
    tile = tile_of(rows)
    for i in range(rows // tile):
        part = pl.ds(i * tile, tile)
        out_ref[part] = held_ref[m, part] + mm(in_ref[part], whole_ref[...])


def full(m, held, inputs_t, whole):
    _, rows, columns = held.shape
    return pl.pallas_call(
        functools.partial(full_kernel, m),
        in_specs=[VMEM, VMEM, VMEM],
        out_specs=VMEM,
        out_shape=in_vmem((rows, columns), F32),
        compiler_params=pltpu.CompilerParams(vmem_limit_bytes=16 * MIB),
        name=f"full_{m}",
    )(stay(held), inputs_t, whole)


def right_kernel(full_ref, p_ref, mine_ref, other_ref, both_ref):
    rows, width = p_ref.shape
    tile = tile_of(rows)
    total = None
    for i in range(rows // tile):
        part = pl.ds(i * tile, tile)
        p_high, p_low = halves(p_ref[part].T)
        g_high, g_low = halves(full_ref[part])
        both = mm(jnp.concatenate([p_high, p_low], axis=0), g_high)
        term = both[:width] + both[width:] + mm(p_high, g_low)
        total = term if total is None else total + term
    lanes = both_ref.shape[2]
    tiles = total.shape[1] // lanes
    stacked = [total[:, t * lanes : (t + 1) * lanes] for t in range(tiles)]
    both_ref[...] = jnp.concatenate(stacked, axis=0).reshape(both_ref.shape)
    side = lax.axis_index("fsdp") & 1
    mine_ref[...] = both_ref[side]
    other_ref[...] = both_ref[1 - side]


def right(m, full_grad, p):
    width = p.shape[1]
    half = full_grad.shape[1] * width // LANES // 2
    return pl.pallas_call(
        right_kernel,
        in_specs=[VMEM, VMEM],
        out_specs=[VMEM, VMEM],
        out_shape=[jax.ShapeDtypeStruct((half, LANES), F32)] * 2,
        scratch_shapes=[pltpu.VMEM((2, half, LANES), F32)],
        compiler_params=pltpu.CompilerParams(vmem_limit_bytes=16 * MIB),
        name=f"right_{m}",
    )(stay(full_grad), p)


def tree(values):
    while len(values) > 1:
        values = [sum(values[i : i + 2][1:], values[i]) for i in range(0, len(values), 2)]
    return values[0]


def merge_kernel(count, plain, coded, parts, bit, *refs):
    terms, refs = refs[: plain * count], refs[plain * count :]
    codes, refs = refs[:coded], refs[coded:]
    decoded = [decode(code) for code in codes]
    rows = (decoded[0] if decoded else terms[0]).shape[0] // (count if decoded else 1)
    sums = []
    for m in range(count):
        values = [terms[t * count + m][...] for t in range(plain)]
        values += [value[m * rows : (m + 1) * rows] for value in decoded]
        sums.append(tree(values))
    if parts == 1:
        encode(jnp.concatenate(sums, axis=0), refs[0])
        return
    *outs, cut_ref = refs
    own = (lax.axis_index("fsdp") >> (bit.bit_length() - 1)) & (parts - 1)
    for m in range(count):
        cut_ref[m] = sums[m].reshape(cut_ref.shape[1:])
        outs[m][...] = cut_ref[m, own]
    for r in range(1, parts):
        encode(jnp.concatenate([cut_ref[m, own ^ r] for m in range(count)], axis=0), outs[count + r - 1])


def merge(terms, codes, name, parts=1, bit=1):
    count = len(terms[0]) if terms else 1
    if terms:
        rows = terms[0][0].shape[0]
        lanes = terms[0][0].shape[1]
    else:
        rows = codes[0].shape[0] - GROUPS
        lanes = codes[0].shape[1]
    share = rows // parts
    code = jax.ShapeDtypeStruct((count * share + GROUPS, lanes), jnp.int16)
    plain = [jax.ShapeDtypeStruct((share, lanes), F32)] * count if parts > 1 else []
    outs = plain + [code] * max(parts - 1, 1)
    flat = [x for term in terms for x in term]
    results = pl.pallas_call(
        functools.partial(merge_kernel, count, len(terms), len(codes), parts, bit),
        in_specs=[VMEM] * (len(flat) + len(codes)),
        out_specs=[VMEM] * len(outs),
        out_shape=outs,
        scratch_shapes=[pltpu.VMEM((count, parts, share, lanes), F32)] if parts > 1 else [],
        compiler_params=pltpu.CompilerParams(vmem_limit_bytes=16 * MIB),
        name=name,
    )(*flat, *codes)
    return (results[:count], results[count:]) if parts > 1 else results[0]


def gram_of(p):
    width = p.shape[1]
    high, low = halves(p)
    high_t, low_t = halves(p.T)
    both = mm(high_t, jnp.concatenate([high, low], axis=1))
    return both[:, :width] + both[:, width:] + mm(low_t, high)


def gram_kernel(p_ref, out_ref):
    out_ref[0] = gram_of(p_ref[0])


def gram(p):
    count, rows, width = p.shape
    return pl.pallas_call(
        gram_kernel,
        grid=(count,),
        in_specs=[pl.BlockSpec((1, rows, width), lambda m: (m, 0, 0))],
        out_specs=pl.BlockSpec((1, width, width), lambda m: (m, 0, 0)),
        out_shape=jax.ShapeDtypeStruct((count, width, width), F32),
        compiler_params=params(16),
        name="gram",
    )(p)


def cholesky_inverse(work, n):
    lane = lax.broadcasted_iota(jnp.int32, (8, n), 1)
    sub = lax.broadcasted_iota(jnp.int32, (8, n), 0)

    def wide(x):
        return jnp.broadcast_to(x, (8, n))

    for b in range(n // 8):
        at = 8 * b
        panels = []
        for blocks in work:
            head = blocks[b]
            columns = [wide(head[:, at + j : at + j + 1]) for j in range(8)]
            scales, lows, tops = [], [], []
            for s in range(8):
                scale = lax.rsqrt(wide(columns[s][s : s + 1, :]))
                low = columns[s] * scale
                for j in range(s + 1, 8):
                    columns[j] = columns[j] - low * wide(low[j : j + 1, :])
                row = jnp.where(lane == at + s, scale, wide(head[s : s + 1, :]) * scale)
                below = jnp.where(lane == at + s, 0.0, head) - low * row
                head = jnp.where(sub > s, below, jnp.where(sub == s, row, head))
                scales.append(scale)
                lows.append(low)
                tops.append(jnp.where((lane > at + s) & (lane < at + 8), 0.0, row))
            blocks[b] = head
            panels.append((scales, lows, tops))
        for c in range(b + 1, n // 8):
            for blocks, (scales, lows, tops) in zip(work, panels):
                x = blocks[c]
                columns = [wide(x[:, at + j : at + j + 1]) for j in range(8)]
                y = jnp.where((lane >= at) & (lane < at + 8), 0.0, x)
                for s in range(8):
                    low = columns[s] * scales[s]
                    for j in range(s + 1, 8):
                        columns[j] = columns[j] - low * wide(lows[s][j : j + 1, :])
                    y = y - low * tops[s]
                blocks[c] = y


def factor_kernel(terms, ranks_ref, *refs):
    gram_refs, refs = refs[:terms], refs[terms:]
    inv_ref, out_ref = refs[-2:]
    p_refs = refs[:-2]
    count, n, _ = inv_ref.shape
    lane = lax.broadcasted_iota(jnp.int32, (8, n), 1)
    sub = lax.broadcasted_iota(jnp.int32, (8, n), 0)
    work = []
    for m in range(count):
        free = jnp.where(lane < ranks_ref[m], 0.0, 1.0)
        blocks = []
        for b in range(n // 8):
            g = tree([ref[m, 8 * b : 8 * b + 8, :] for ref in gram_refs])
            blocks.append(jnp.where(lane == sub + 8 * b, g + free, g))
        work.append(blocks)
    cholesky_inverse(work, n)
    for m in range(count):
        for b in range(n // 8):
            inv_ref[m, 8 * b : 8 * b + 8, :] = jnp.where(lane <= sub + 8 * b, work[m][b], 0.0)
        i_high, i_low = halves(inv_ref[m])
        p_high, p_low = halves(p_refs[m][...])
        both = mm_nt(p_high, jnp.concatenate([i_high, i_low], axis=0))
        out_ref[m] = both[:, :n] + both[:, n:] + mm_nt(p_low, i_high)


def factor(grams, p, ranks):
    count = len(p)
    return pl.pallas_call(
        functools.partial(factor_kernel, len(grams)),
        in_specs=[SMEM] + [VMEM] * (len(grams) + count),
        out_specs=[VMEM, VMEM],
        out_shape=[
            jax.ShapeDtypeStruct(grams[0].shape, F32),
            jax.ShapeDtypeStruct((count, *p[0].shape), F32),
        ],
        compiler_params=pltpu.CompilerParams(vmem_limit_bytes=16 * MIB),
        name="factor",
    )(ranks, *grams, *p)


def error_kernel(count, pieces, groups, fp_ref, inv_ref, *refs):
    codes, refs = refs[:pieces], refs[pieces:]
    full_refs, (err_ref, fq_ref, right_ref, q_ref, buf_ref, sems) = refs[:count], refs[count:]
    rows, width = fp_ref.shape[1:]
    tile = tile_of(rows)
    share = right_ref.shape[1] // pieces
    me = lax.axis_index("fsdp") if pieces > 1 else 0
    for r, code in enumerate(codes):
        value = decode(code)
        place = (me ^ r) & 1 if pieces > 1 else 0
        for bit, members in groups:
            place = place * members + (((me ^ r) >> (bit.bit_length() - 1)) & (members - 1))
        at = pl.ds(pl.multiple_of(place * share, share), share)
        for m in range(count):
            right_ref[m, at] = value[m * share : (m + 1) * share]
    copies = []
    for m in range(count):
        i_high, i_low = halves(inv_ref[m])
        tiles = [right_ref[m, t : t + width] for t in range(0, right_ref.shape[1], width)]
        r_high, r_low = halves(jnp.concatenate(tiles, axis=1))
        both = mm(jnp.concatenate([i_high, i_low], axis=0), r_high)
        fq_t = both[:width] + both[width:] + mm(i_high, r_low)
        q_high, q_low = halves(fq_t)
        q3 = jnp.concatenate([q_high, q_high, q_low], axis=0)
        for i in range(rows // tile):
            part = pl.ds(i * tile, tile)
            p_high, p_low = halves(fp_ref[m, part])
            low_rank = mm(jnp.concatenate([p_high, p_low, p_high], axis=1), q3)
            buf_ref[m, part] = full_refs[m][part] - low_rank
            copies.append(
                pltpu.make_async_copy(buf_ref.at[m, part], err_ref.at[m, 0, part], sems.at[len(copies)])
            )
            copies[-1].start()
        q_ref[m] = fq_t.T
        copies.append(pltpu.make_async_copy(q_ref.at[m], fq_ref.at[m], sems.at[len(copies)]))
        copies[-1].start()
    for copy in copies:
        copy.wait()


def error(full_grad, factor_p, inverse, codes):
    count, rows, width = factor_p.shape
    columns = full_grad[0].shape[1]
    out = pl.BlockSpec(memory_space=pltpu.HBM)
    groups = groups_of("fsdp") if len(codes) > 1 else []
    return pl.pallas_call(
        functools.partial(error_kernel, count, len(codes), groups),
        in_specs=[VMEM] * (2 + len(codes) + count),
        out_specs=[out, out],
        out_shape=[
            jax.ShapeDtypeStruct((count, 1, rows, columns), F32),
            jax.ShapeDtypeStruct((count, columns, width), F32),
        ],
        scratch_shapes=[
            pltpu.VMEM((count, columns * width // LANES, LANES), F32),
            pltpu.VMEM((count, columns, width), F32),
            pltpu.VMEM((count, rows, columns), F32),
            pltpu.SemaphoreType.DMA((count * (rows // tile_of(rows) + 1),)),
        ],
        compiler_params=pltpu.CompilerParams(vmem_limit_bytes=24 * MIB),
        name="error",
    )(factor_p, inverse, *codes, *[stay(x) for x in full_grad])


def power_of_two(n):
    return n & (n - 1) == 0


def across(x, axis, bit):
    size = lax.axis_size(axis)
    return lax.ppermute(x, axis, [(i, i ^ bit) for i in range(size)])


def bits_of(axis):
    size = lax.axis_size(axis)
    return [1 << b for b in range(size.bit_length() - 1)]


def groups_of(axis):
    bits = bits_of(axis)[1:]
    return [(bits[i], 1 << len(bits[i : i + 2])) for i in range(0, len(bits), 2)]


def gather_blocks(x, axis, beside=()):
    held = {0: x}
    for bit, members in groups_of(axis)[::-1]:
        for r in list(held):
            for k in range(1, members):
                held[r ^ (k * bit)] = across(held[r], axis, k * bit)
    order = list(held)
    values = tie(*[held[r] for r in order], *beside)
    held, beside = dict(zip(order, values)), values[len(order) :]
    held.update({r ^ 1: across(held[r], axis, 1) for r in order})
    return [held[r] for r in range(len(held))], beside


def gather_cotangent(cotangent, beside):
    size = lax.axis_size("fsdp")
    count, _, width = cotangent.shape
    if power_of_two(size) and size > 1 and width % 128 == 0 and count > 1:
        lists = []
        for m in range(count):
            blocks, beside = gather_blocks(cotangent[m : m + 1], "fsdp", beside)
            lists.append(blocks)
        blocks = [list(pieces) for pieces in zip(*lists)]
        return blocks, beside
    whole = lax.all_gather(cotangent, "fsdp", axis=2, tiled=True)
    return [[whole]], beside


def tie(*values):
    return lax.optimization_barrier(values)


def sums(gram_part, full_grad, p, ranks):
    size = lax.axis_size("fsdp")
    replicas = lax.axis_size("dp")
    count = len(p)
    if not (power_of_two(size) and size > 1):
        inverse, factor_p = factor([lax.psum(gram_part, "fsdp")], p, ranks)
        pairs = [right(m, full_grad[m], p[m]) for m in range(count)]
        ordered = [jnp.stack(pair) for pair in pairs]
        odd = (lax.axis_index("fsdp") & 1) == 1
        whole = jnp.stack([jnp.where(odd, x[::-1], x).reshape(-1, x.shape[2]) for x in ordered])
        return inverse, factor_p, [merge([list(lax.psum(whole, ("fsdp", "dp")))], [], "code")]
    groups = groups_of("fsdp")

    gram_part = gram_part + across(gram_part, "fsdp", 1)
    for bit, members in groups[:-1]:
        gram_part = tree([gram_part] + [across(gram_part, "fsdp", k * bit) for k in range(1, members)])
    grams = [gram_part]
    for bit, members in groups[-1:]:
        grams += [across(gram_part, "fsdp", k * bit) for k in range(1, members)]

    pairs = [right(m, full_grad[m], p[m]) for m in range(count)]
    terms = [[mine for mine, _ in pairs], [across(other, "fsdp", 1) for _, other in pairs]]
    codes = []
    for bit, members in groups:
        keep, others = merge(terms, codes, f"part_{bit}", members, bit)
        codes = [across(others[k - 1], "fsdp", k * bit) for k in range(1, members)]
        terms = [keep]
    code = merge(terms, codes, "code")
    if power_of_two(replicas) and replicas > 1:
        *grams, code = tie(*grams, code)
        theirs = [across(code, "dp", k) for k in range(1, replicas)]
        inverse, factor_p = factor(grams, p, ranks)
        *theirs, inverse, factor_p = tie(*theirs, inverse, factor_p)
        code = merge([], [code] + theirs, "code_sum")
    else:
        inverse, factor_p = factor(grams, p, ranks)
        code = merge([[lax.psum(plain(code), "dp")]], [], "code_sum")
    return inverse, factor_p, gather_blocks(code, "fsdp")[0]


def plain_kernel(code_ref, out_ref):
    out_ref[...] = decode(code_ref)


def plain(code):
    return pl.pallas_call(
        plain_kernel,
        in_specs=[VMEM],
        out_specs=VMEM,
        out_shape=jax.ShapeDtypeStruct((code.shape[0] - GROUPS, code.shape[1]), F32),
        name="plain",
    )(code)


def left_sums(blocks, q_init, inputs_t, held, fbq, ranks):
    replicas = lax.axis_size("dp")
    count = fbq.shape[0]
    if not (power_of_two(replicas) and replicas > 1):
        parts = [left(m, blocks, q_init, inputs_t, fbq, ranks) for m in range(count)]
        p = lax.psum(jnp.stack([part for part, _ in parts]), "dp")
        full_grad = [full(m, held, inputs_t, parts[m][1]) for m in range(count)]
        return [p[m] for m in range(count)], full_grad, gram(p)
    whole, full_grad = [], []
    for m in range(count):
        mine, other, cot = left_code(m, blocks, q_init, inputs_t, fbq, ranks)
        mine = add_code(mine, across(other, "dp", 1))
        for step, bit in enumerate(bits_of("dp")[1:]):
            if step == 0:
                mine, cot = tie(mine, cot)
                theirs, grad = tie(across(mine, "dp", bit), full(m, held, inputs_t, cot))
                full_grad.append(grad)
            else:
                theirs = across(mine, "dp", bit)
            mine = add_code(mine, theirs)
        if len(full_grad) == m:
            full_grad.append(full(m, held, inputs_t, cot))
        whole.append(whole_left(mine, across(mine, "dp", 1)))
    return [p for p, _ in whole], full_grad, jnp.stack([part for _, part in whole])


def local(inputs, cotangent, feedback, q_init, factor_ranks):
    beside = feedback_q(feedback, q_init, inputs, factor_ranks)
    blocks, (held, fbq, inputs_t) = gather_cotangent(cotangent, beside)
    p, full_grad, gram_part = left_sums(blocks, q_init, inputs_t, held, fbq, factor_ranks)
    inverse, factor_p, codes = sums(gram_part, full_grad, p, factor_ranks)
    new_error, factor_q = error(full_grad, factor_p, inverse, codes)
    return (factor_p, factor_q, new_error)


def solution(mesh):
    placed = (P("dp", "fsdp"), P(None, "dp", "fsdp"), P(None, "dp", "fsdp", None), P(), P())
    return jax.shard_map(
        local,
        mesh=mesh,
        in_specs=placed,
        out_specs=(P(None, "fsdp", None), P(), P(None, "dp", "fsdp", None)),
        check_vma=False,
    )
```

time: 358 us -> 95.8 us (0.27)
  waiting for transfers between devices: 223 us -> 22.8 us
  matrix products: 48.8 us -> 0 us
  other arithmetic: 45.6 us -> 0.03 us
  starting transfers between devices: 0.24 us -> 36.9 us
  Pallas kernels: 0 us -> 29.5 us
  local copies, waits for them, and re-layouts: 25.1 us -> 5.32 us
  between operations: 14.2 us -> 1.04 us
    psum x3 -> x0, waiting for transfers between devices: 141 us -> none  [the longest x1 52.4 us: local(): lax.psum(gram_local, 'fsdp') + jax.vmap(jnp.diag)(1.0 - rank_mask)]
    all_gather x2 -> x0, waiting for transfers between devices: 46.9 us -> none  [the longest x1 23.8 us: local(): factor_q = lax.all_gather(right_rows, 'fsdp', axis=1, tiled=True)]
    dot_general x5 -> x0, matrix products: 46.5 us -> none  [the longest x1 14.7 us: local(): jnp.einsum('mdk,mkr->mdr', full_grad, masked_q, precision=PRECISE)]
    another operation x7 -> x1, other arithmetic: 43.4 us -> 0.01 us  [left_sums(): jnp.stack([part for _, part in whole])]
    ppermute x0 -> x39, starting transfers between devices: none -> 36.9 us  [across(): return lax.ppermute(x, axis, [(i, i ^ bit) for i in range(size)])]
    reduce_scatter x1 -> x0, waiting for transfers between devices: 35.5 us -> none  [local(): lax.psum_scatter(right_local, 'fsdp', scatter_dimension=1, tiled=True)]
    pallas_call x0 -> x18, Pallas kernels: none -> 29.5 us  [the longest x1 7.88 us: factor(): pl.pallas_call(functools.partial(factor_kernel, len(grams)), in_specs=[SM...]
    ppermute x0 -> x39, waiting for transfers between devices: none -> 22.8 us  [across(): return lax.ppermute(x, axis, [(i, i ^ bit) for i in range(size)])]
  transfers between devices with their start and end apart: 6 -> 39, of which waited for: 6 -> 16; matrix products, arithmetic and copies ran while one was open for 3% -> 0% of each run, Pallas kernels for 0% -> 26%
where the time goes in v3:
time: 95.8 us; the launch traced here: 95.6 us
  starting transfers between devices  36.9 us (39%)
  Pallas kernels  29.5 us (31%)
  waiting for transfers between devices  22.8 us (24%)
  local copies, waits for them, and re-layouts  5.32 us (6%)
  between operations  1.04 us (1%)
    ppermute x39, starting transfers between devices, across(): return lax.ppermute(x, axis, [(i, i ^ bit) for i in range(size)])  36.9 us
    ppermute x39, waiting for transfers between devices, across(): return lax.ppermute(x, axis, [(i, i ^ bit) for i in range(size)])  22.8 us
    pallas_call x1, Pallas kernels, factor(): pl.pallas_call(functools.partial(factor_kernel, len(grams)), in_specs=[SM...  7.88 us
    pallas_call x1, Pallas kernels, feedback_q(): pl.pallas_call(feedback_q_kernel, in_specs=[SMEM, pl.BlockSpec(memory_spa...  5.31 us
    pallas_call x1, Pallas kernels, error(): pl.pallas_call(functools.partial(error_kernel, count, len(codes), groups)...  4.54 us
    pallas_call x2, Pallas kernels, left_code(): pl.pallas_call(functools.partial(left_code_kernel, m), grid=(1,), in_spec...  4.54 us
    unnamed x10, local copies, waits for them, and re-layouts  4.33 us
    pallas_call x2, Pallas kernels, full(): pl.pallas_call(functools.partial(full_kernel, m), in_specs=[VMEM, VMEM, V...  2.69 us
  transfers between devices with their start and end apart: 39, of which 16 were waited for; matrix products, arithmetic and copies ran while one was open for 0% of the time, Pallas kernels for 26%

profile of v3, /device:TPU:0, one launch (start us, length us, event | category | flops | bytes accessed | tf_op | source)
XLA Modules:
  0.0 95.6 jit_solution(6519914040880242592)
XLA Ops:
  0.6 1.0 %fusion.1 = (bf16[1,512,128]{2,1,0:T(8,128)(2,1)S(1)}, bf16[1,512,128]{2,1,0:T(8,128)(2,1)S(1)}) fusion(bf16[2,512,128]{2,1,0:T(8,128)(2,1)} %param.6), kind=kLoop, calls=%fused_computation.2 | loop fusion | bytes 524288 | tf_op jit(solution)/shard_map/slice | solution.py:573
  1.6 4.0 %collective-permute-start.5 = (bf16[1,512,128]{2,1,0:T(8,128)(2,1)S(1)}, bf16[1,512,128]{2,1,0:T(8,128)(2,1)S(1)}, u32[]{:S(2)}, u32[]{:S(2)}) collective-permute-start(bf16[1,512,128]{2,1,0:T(8,128)(2,1)S(1)} %get-tuple-element.73.refs_0_), channel_id=1, source_target_pairs={{0,6},{1,7},{2,4},{3,5},{4,2},{5,3},{6,0},{7,1},{8,14},{9,15},{10,... | collective-permute-start | bytes 393224 | tf_op jit(solution)/shard_map/ppermute | solution.py:541
  5.6 0.5 collective-permute-start.4
  6.2 2.8 %collective-permute-start.2 = (bf16[1,512,128]{2,1,0:T(8,128)(2,1)S(1)}, bf16[1,512,128]{2,1,0:T(8,128)(2,1)S(1)}, u32[]{:S(2)}, u32[]{:S(2)}) collective-permute-start(bf16[1,512,128]{2,1,0:T(8,128)(2,1)S(1)} %get-tuple-element.85.refs_0_), channel_id=1, source_target_pairs={{0,6},{1,7},{2,4},{3,5},{4,2},{5,3},{6,0},{7,1},{8,14},{9,15},{10,... | collective-permute-start | bytes 393224 | tf_op jit(solution)/shard_map/ppermute | solution.py:541
  9.1 0.5 collective-permute-start.1
  9.6 2.3 %collective-permute-start = (bf16[1,512,128]{2,1,0:T(8,128)(2,1)S(1)}, bf16[1,512,128]{2,1,0:T(8,128)(2,1)S(1)}, u32[]{:S(2)}, u32[]{:S(2)}) collective-permute-start(bf16[1,512,128]{2,1,0:T(8,128)(2,1)S(1)} %get-tuple-element.85.refs_0_), channel_id=1, source_target_pairs={{0,2},{1,3},{2,0},{3,1},{4,6},{5,7},{6,4},{7,5},{8,10},{9,11},{10,... | collective-permute-start | bytes 393224 | tf_op jit(solution)/shard_map/ppermute | solution.py:541
  11.9 1.2 %copy-done = f32[2,1024,128]{2,1,0:T(8,128)S(1)} copy-done((f32[2,1024,128]{2,1,0:T(8,128)S(1)}, f32[2,1024,128]{2,1,0:T(8,128)}, u32[]{:S(2)}) %copy-start) | copy-done | bytes 1048600
  13.1 1.2 %copy-done.2 = bf16[512,1024]{1,0:T(8,128)(2,1)S(1)} copy-done((bf16[512,1024]{1,0:T(8,128)(2,1)S(1)}, bf16[512,1024]{1,0:T(8,128)(2,1)}, u32[]{:S(2)}) %copy-start.2) | copy-done | bytes 1048600
  14.4 0.7 copy-done.3
  15.0 5.3 %feedback_q.1 = (f32[2,1024,1024]{2,1,0:T(8,128)S(1)}, f32[2,1024,128]{2,1,0:T(8,128)S(1)}, bf16[1024,512]{1,0:T(8,128)(2,1)S(1)}) custom-call(s32[2]{0:T(128)S(1)} %copy-done.3, f32[2,1,1024,1024]{3,2,1,0:T(8,128)} %fb_ref.1, f32[2,1024,128]{2,1,0:T(8,128)S(1)} %copy-done, bf16[512,1024]{1,0:T(8,128)(2,1)S(1)} %copy-done.2), custom_call_target="tpu_custom_call" | custom-call | tf_op jit(solution)/shard_map/feedback_q/pallas_call | solution.py:82
  20.5 0.5 collective-permute-start.14
  21.0 0.4 collective-permute-start.16
  21.5 0.2 collective-permute-done.13.refs_1_
  21.8 0.2 collective-permute-start.7
  22.0 0.3 collective-permute-start.8
  22.3 0.2 collective-permute-start.9
  22.5 2.3 %left_code_1.1 = (f32[512,128]{1,0:T(8,128)S(1)}, s16[528,128]{1,0:T(8,128)(2,1)S(1)}, bf16[512,1024]{1,0:T(8,128)(2,1)S(1)}) custom-call(s32[2]{0:T(128)S(1)} %copy-done.3, f32[2,1024,128]{2,1,0:T(8,128)S(1)} %copy-done, bf16[1024,512]{1,0:T(8,128)(2,1)S(1)} %get-tuple-element.71.in_ref, f32[2,1024,128]{2,1,0:T(8,128)S(1)} %get-tuple-element.72.fbq_ref, ...), custom_call_target="tpu_custom_call" | custom-call | tf_op jit(solution)/shard_map/left_code_1/pallas_call | solution.py:199
  24.8 1.6 %collective-permute-start.17 = (s16[528,128]{1,0:T(8,128)(2,1)S(1)}, s16[528,128]{1,0:T(8,128)(2,1)S(1)}, u32[]{:S(2)}, u32[]{:S(2)}) collective-permute-start(s16[528,128]{1,0:T(8,128)(2,1)S(1)} %get-tuple-element.90), channel_id=1, source_target_pairs={{0,8},{8,0},{16,24},{24,16},{1,9},{9,1},{17,25},{25,17},{2,10},{10... | collective-permute-start | bytes 405512 | tf_op jit(solution)/shard_map/ppermute | solution.py:541
  26.4 2.3 %left_code_0.1 = (f32[512,128]{1,0:T(8,128)S(1)}, s16[528,128]{1,0:T(8,128)(2,1)S(1)}, bf16[512,1024]{1,0:T(8,128)(2,1)S(1)}) custom-call(s32[2]{0:T(128)S(1)} %copy-done.3, f32[2,1024,128]{2,1,0:T(8,128)S(1)} %copy-done, bf16[1024,512]{1,0:T(8,128)(2,1)S(1)} %get-tuple-element.71.in_ref, f32[2,1024,128]{2,1,0:T(8,128)S(1)} %get-tuple-element.72.fbq_ref, ...), custom_call_target="tpu_custom_call" | custom-call | tf_op jit(solution)/shard_map/left_code_0/pallas_call | solution.py:199
  28.7 0.5 collective-permute-start.10
  29.2 1.4 %collective-permute-done.17.theirs_ref = s16[528,128]{1,0:T(8,128)(2,1)S(1)} collective-permute-done((s16[528,128]{1,0:T(8,128)(2,1)S(1)}, s16[528,128]{1,0:T(8,128)(2,1)S(1)}, u32[]{:S(2)}, u32[]{:S(2)}) %collective-permute-start.17) | collective-permute-done | bytes 135200 | tf_op jit(solution)/shard_map/ppermute | solution.py:541
  30.8 2.7 %collective-permute-start.18 = (s16[528,128]{1,0:T(8,128)(2,1)S(1)}, s16[528,128]{1,0:T(8,128)(2,1)S(1)}, u32[]{:S(2)}, u32[]{:S(2)}) collective-permute-start(s16[528,128]{1,0:T(8,128)(2,1)S(1)} %add_code.6.mine_ref), channel_id=1, source_target_pairs={{0,16},{8,24},{16,0},{24,8},{1,17},{9,25},{17,1},{25,9},{2,18},{10... | collective-permute-start | bytes 405512 | tf_op jit(solution)/shard_map/ppermute | solution.py:541
  33.4 2.8 %collective-permute-done.10.theirs_ref = s16[528,128]{1,0:T(8,128)(2,1)S(1)} collective-permute-done((s16[528,128]{1,0:T(8,128)(2,1)S(1)}, s16[528,128]{1,0:T(8,128)(2,1)S(1)}, u32[]{:S(2)}, u32[]{:S(2)}) %collective-permute-start.10) | collective-permute-done | bytes 135200 | tf_op jit(solution)/shard_map/ppermute | solution.py:541
  36.4 1.6 %collective-permute-start.11 = (s16[528,128]{1,0:T(8,128)(2,1)S(1)}, s16[528,128]{1,0:T(8,128)(2,1)S(1)}, u32[]{:S(2)}, u32[]{:S(2)}) collective-permute-start(s16[528,128]{1,0:T(8,128)(2,1)S(1)} %add_code.4.mine_ref), channel_id=1, source_target_pairs={{0,16},{8,24},{16,0},{24,8},{1,17},{9,25},{17,1},{25,9},{2,18},{10... | collective-permute-start | bytes 405512 | tf_op jit(solution)/shard_map/ppermute | solution.py:541
  38.0 1.3 %full_1.1.full_ref.refs_9_ = f32[1024,1024]{1,0:T(8,128)S(1)} custom-call(f32[2,1024,1024]{2,1,0:T(8,128)S(1)} %get-tuple-element.81.held_ref, bf16[1024,512]{1,0:T(8,128)(2,1)S(1)} %get-tuple-element.71.in_ref, bf16[512,1024]{1,0:T(8,128)(2,1)S(1)} %get-tuple-element.93.whole_ref), custom_call_target="tpu_custom_call" | custom-call | tf_op jit(solution)/shard_map/full_1/pallas_call | solution.py:269
  39.4 3.6 %collective-permute-done.18.theirs_ref = s16[528,128]{1,0:T(8,128)(2,1)S(1)} collective-permute-done((s16[528,128]{1,0:T(8,128)(2,1)S(1)}, s16[528,128]{1,0:T(8,128)(2,1)S(1)}, u32[]{:S(2)}, u32[]{:S(2)}) %collective-permute-start.18) | collective-permute-done | bytes 135200 | tf_op jit(solution)/shard_map/ppermute | solution.py:541
  43.0 0.2 add_code.7.mine_ref
  43.2 0.4 collective-permute-start.19
  43.6 1.3 %full_0.1.full_ref.refs_8_ = f32[1024,1024]{1,0:T(8,128)S(1)} custom-call(f32[2,1024,1024]{2,1,0:T(8,128)S(1)} %get-tuple-element.81.held_ref, bf16[1024,512]{1,0:T(8,128)(2,1)S(1)} %get-tuple-element.71.in_ref, bf16[512,1024]{1,0:T(8,128)(2,1)S(1)} %get-tuple-element.82.whole_ref), custom_call_target="tpu_custom_call" | custom-call | tf_op jit(solution)/shard_map/full_0/pallas_call | solution.py:269
  44.9 0.7 collective-permute-done.11.theirs_ref
  45.6 0.2 add_code.5.mine_ref
  45.8 1.1 %collective-permute-start.12 = (s16[528,128]{1,0:T(8,128)(2,1)S(1)}, s16[528,128]{1,0:T(8,128)(2,1)S(1)}, u32[]{:S(2)}, u32[]{:S(2)}) collective-permute-start(s16[528,128]{1,0:T(8,128)(2,1)S(1)} %add_code.5.mine_ref), channel_id=1, source_target_pairs={{0,8},{8,0},{16,24},{24,16},{1,9},{9,1},{17,25},{25,17},{2,10},{10... | collective-permute-start | bytes 405512 | tf_op jit(solution)/shard_map/ppermute | solution.py:541
  46.9 1.8 %collective-permute-done.19.theirs_ref = s16[528,128]{1,0:T(8,128)(2,1)S(1)} collective-permute-done((s16[528,128]{1,0:T(8,128)(2,1)S(1)}, s16[528,128]{1,0:T(8,128)(2,1)S(1)}, u32[]{:S(2)}, u32[]{:S(2)}) %collective-permute-start.19) | collective-permute-done | bytes 135200 | tf_op jit(solution)/shard_map/ppermute | solution.py:541
  48.7 0.5 whole_left.3
  49.2 1.1 %right_1.1 = (f32[512,128]{1,0:T(8,128)S(1)}, f32[512,128]{1,0:T(8,128)S(1)}) custom-call(f32[1024,1024]{1,0:T(8,128)S(1)} %full_1.1.full_ref.refs_9_, f32[1024,128]{1,0:T(8,128)S(1)} %get-tuple-element.100.p_ref.refs_5_), custom_call_target="tpu_custom_call" | custom-call | tf_op jit(solution)/shard_map/right_1/pallas_call | solution.py:302
  50.4 0.9 collective-permute-done.12.theirs_ref
  51.3 0.6 whole_left.2
  51.9 1.1 %right_0.1 = (f32[512,128]{1,0:T(8,128)S(1)}, f32[512,128]{1,0:T(8,128)S(1)}) custom-call(f32[1024,1024]{1,0:T(8,128)S(1)} %full_0.1.full_ref.refs_8_, f32[1024,128]{1,0:T(8,128)S(1)} %get-tuple-element.97.p_ref.refs_4_), custom_call_target="tpu_custom_call" | custom-call | tf_op jit(solution)/shard_map/right_0/pallas_call | solution.py:302
  53.2 0.6 collective-permute-start.20
  53.7 0.9 collective-permute-done.24.refs_2_
  54.7 0.3 part_2.1
  55.0 3.0 %collective-permute-start.23 = (f32[2,128,128]{2,1,0:T(8,128)S(1)}, f32[2,128,128]{2,1,0:T(8,128)S(1)}, u32[]{:S(2)}, u32[]{:S(2)}) collective-permute-start(f32[2,128,128]{2,1,0:T(8,128)S(1)} %fusion.refs_0_), channel_id=1, source_target_pairs={{0,6},{1,7},{2,4},{3,5},{4,2},{5,3},{6,0},{7,1},{8,14},{9,15},{10,... | collective-permute-start | bytes 393224 | tf_op jit(solution)/shard_map/ppermute | solution.py:541
  58.1 0.5 collective-permute-start.22
  58.7 1.9 %collective-permute-start.27 = (s16[272,128]{1,0:T(8,128)(2,1)S(1)}, s16[272,128]{1,0:T(8,128)(2,1)S(1)}, u32[]{:S(2)}, u32[]{:S(2)}) collective-permute-start(s16[272,128]{1,0:T(8,128)(2,1)S(1)} %get-tuple-element.107), channel_id=1, source_target_pairs={{0,4},{1,5},{2,6},{3,7},{4,0},{5,1},{6,2},{7,3},{8,12},{9,13},{10,... | collective-permute-start | bytes 208904 | tf_op jit(solution)/shard_map/ppermute | solution.py:541
  60.6 1.4 %collective-permute-start.28 = (s16[272,128]{1,0:T(8,128)(2,1)S(1)}, s16[272,128]{1,0:T(8,128)(2,1)S(1)}, u32[]{:S(2)}, u32[]{:S(2)}) collective-permute-start(s16[272,128]{1,0:T(8,128)(2,1)S(1)} %get-tuple-element.108), channel_id=1, source_target_pairs={{0,6},{1,7},{2,4},{3,5},{4,2},{5,3},{6,0},{7,1},{8,14},{9,15},{10,... | collective-permute-start | bytes 208904 | tf_op jit(solution)/shard_map/ppermute | solution.py:541
  62.1 6.4 %collective-permute-done.27.refs_3_ = s16[272,128]{1,0:T(8,128)(2,1)S(1)} collective-permute-done((s16[272,128]{1,0:T(8,128)(2,1)S(1)}, s16[272,128]{1,0:T(8,128)(2,1)S(1)}, u32[]{:S(2)}, u32[]{:S(2)}) %collective-permute-start.27) | collective-permute-done | bytes 69664 | tf_op jit(solution)/shard_map/ppermute | solution.py:541
  68.6 3.5 %collective-permute-start.31 = (s16[272,128]{1,0:T(8,128)(2,1)S(1)}, s16[272,128]{1,0:T(8,128)(2,1)S(1)}, u32[]{:S(2)}, u32[]{:S(2)}) collective-permute-start(s16[272,128]{1,0:T(8,128)(2,1)S(1)} %code.1.refs_0_), channel_id=1, source_target_pairs={{0,24},{8,16},{16,8},{24,0},{1,25},{9,17},{17,9},{25,1},{2,26},{10... | collective-permute-start | bytes 208904 | tf_op jit(solution)/shard_map/ppermute | solution.py:541
  72.1 0.9 collective-permute-start.29
  73.0 7.9 %factor.1 = (f32[2,128,128]{2,1,0:T(8,128)S(1)}, f32[2,1024,128]{2,1,0:T(8,128)}) custom-call(s32[2]{0:T(128)S(1)} %copy-done.4, f32[2,128,128]{2,1,0:T(8,128)S(1)} %fusion.refs_0_, f32[2,128,128]{2,1,0:T(8,128)S(1)} %collective-permute-done.21.refs_1_, f32[2,128,128]{2,1,0:T(8,128)S(1)} %collective-permute-done.22.refs_2_, ...), custom_call_target="tpu_custom_call" | custom-call | tf_op jit(solution)/shard_map/factor/pallas_call | solution.py:458
  80.9 0.2 code_sum.1.refs_0_
  81.1 0.9 collective-permute-start.34
  82.0 1.4 %collective-permute-start.33 = (s16[272,128]{1,0:T(8,128)(2,1)S(1)}, s16[272,128]{1,0:T(8,128)(2,1)S(1)}, u32[]{:S(2)}, u32[]{:S(2)}) collective-permute-start(s16[272,128]{1,0:T(8,128)(2,1)S(1)} %code_sum.1.refs_0_), channel_id=1, source_target_pairs={{0,4},{1,5},{2,6},{3,7},{4,0},{5,1},{6,2},{7,3},{8,12},{9,13},{10,... | collective-permute-start | bytes 208904 | tf_op jit(solution)/shard_map/ppermute | solution.py:541
  83.4 1.3 %collective-permute-start.32 = (s16[272,128]{1,0:T(8,128)(2,1)S(1)}, s16[272,128]{1,0:T(8,128)(2,1)S(1)}, u32[]{:S(2)}, u32[]{:S(2)}) collective-permute-start(s16[272,128]{1,0:T(8,128)(2,1)S(1)} %code_sum.1.refs_0_), channel_id=1, source_target_pairs={{0,2},{1,3},{2,0},{3,1},{4,6},{5,7},{6,4},{7,5},{8,10},{9,11},{10,... | collective-permute-start | bytes 208904 | tf_op jit(solution)/shard_map/ppermute | solution.py:541
  84.7 1.8 %collective-permute-done.34.refs_6_ = s16[272,128]{1,0:T(8,128)(2,1)S(1)} collective-permute-done((s16[272,128]{1,0:T(8,128)(2,1)S(1)}, s16[272,128]{1,0:T(8,128)(2,1)S(1)}, u32[]{:S(2)}, u32[]{:S(2)}) %collective-permute-start.34) | collective-permute-done | bytes 69664 | tf_op jit(solution)/shard_map/ppermute | solution.py:541
  86.5 0.5 collective-permute-done.33.refs_4_
  87.0 0.7 collective-permute-done.32.refs_2_
  87.7 0.5 collective-permute-start.36
  88.2 0.5 collective-permute-start.38
  88.7 0.2 collective-permute-done.35.refs_1_
  89.0 0.2 collective-permute-done.36.refs_3_
  89.1 0.4 collective-permute-done.37.refs_5_
  89.5 0.2 collective-permute-done.38.refs_7_
  89.6 1.2 %copy-done.1 = f32[2,1024,128]{2,1,0:T(8,128)S(1)} copy-done((f32[2,1024,128]{2,1,0:T(8,128)S(1)}, f32[2,1024,128]{2,1,0:T(8,128)}, u32[]{:S(2)}) %copy-start.1) | copy-done | bytes 1048600
  90.9 4.5 %error.1 = (f32[2,1,1024,1024]{3,2,1,0:T(8,128)}, f32[2,1024,128]{2,1,0:T(8,128)}) custom-call(f32[2,1024,128]{2,1,0:T(8,128)S(1)} %copy-done.1, f32[2,128,128]{2,1,0:T(8,128)S(1)} %get-tuple-element.117.inv_ref, s16[272,128]{1,0:T(8,128)(2,1)S(1)} %code_sum.1.refs_0_, s16[272,128]{1,0:T(8,128)(2,1)S(1)} %collective-permute-done.35.refs_1_, ...), custom_call_target="tpu_custom_call" | custom-call | tf_op jit(solution)/shard_map/error/pallas_call | solution.py:516
  (45 shorter events, 1.3 us)
Async XLA Ops:
  1.6 8.0 %collective-permute-start.5 = (bf16[1,512,128]{2,1,0:T(8,128)(2,1)S(1)}, bf16[1,512,128]{2,1,0:T(8,128)(2,1)S(1)}, u32[]{:S(2)}, u32[]{:S(2)}) collective-permute-start(bf16[1,512,128]{2,1,0:T(8,128)(2,1)S(1)} %get-tuple-element.73.refs_0_), channel_id=1, source_target_pairs={{0,6},{1,7},{2,4},{3,5},{4,2},{5,3},{6,0},{7,1},{8,14},{9,15},{10,... | collective-permute-start | bytes 393224 | tf_op jit(solution)/shard_map/ppermute | solution.py:541
  5.6 14.7 %collective-permute-start.4 = (bf16[1,512,128]{2,1,0:T(8,128)(2,1)S(1)}, bf16[1,512,128]{2,1,0:T(8,128)(2,1)S(1)}, u32[]{:S(2)}, u32[]{:S(2)}) collective-permute-start(bf16[1,512,128]{2,1,0:T(8,128)(2,1)S(1)} %get-tuple-element.73.refs_0_), channel_id=1, source_target_pairs={{0,4},{1,5},{2,6},{3,7},{4,0},{5,1},{6,2},{7,3},{8,12},{9,13},{10,... | collective-permute-start | bytes 393224 | tf_op jit(solution)/shard_map/ppermute | solution.py:541
  6.1 14.3 %collective-permute-start.3 = (bf16[1,512,128]{2,1,0:T(8,128)(2,1)S(1)}, bf16[1,512,128]{2,1,0:T(8,128)(2,1)S(1)}, u32[]{:S(2)}, u32[]{:S(2)}) collective-permute-start(bf16[1,512,128]{2,1,0:T(8,128)(2,1)S(1)} %get-tuple-element.73.refs_0_), channel_id=1, source_target_pairs={{0,2},{1,3},{2,0},{3,1},{4,6},{5,7},{6,4},{7,5},{8,10},{9,11},{10,... | collective-permute-start | bytes 393224 | tf_op jit(solution)/shard_map/ppermute | solution.py:541
  6.2 14.1 %collective-permute-start.2 = (bf16[1,512,128]{2,1,0:T(8,128)(2,1)S(1)}, bf16[1,512,128]{2,1,0:T(8,128)(2,1)S(1)}, u32[]{:S(2)}, u32[]{:S(2)}) collective-permute-start(bf16[1,512,128]{2,1,0:T(8,128)(2,1)S(1)} %get-tuple-element.85.refs_0_), channel_id=1, source_target_pairs={{0,6},{1,7},{2,4},{3,5},{4,2},{5,3},{6,0},{7,1},{8,14},{9,15},{10,... | collective-permute-start | bytes 393224 | tf_op jit(solution)/shard_map/ppermute | solution.py:541
  9.1 11.3 %collective-permute-start.1 = (bf16[1,512,128]{2,1,0:T(8,128)(2,1)S(1)}, bf16[1,512,128]{2,1,0:T(8,128)(2,1)S(1)}, u32[]{:S(2)}, u32[]{:S(2)}) collective-permute-start(bf16[1,512,128]{2,1,0:T(8,128)(2,1)S(1)} %get-tuple-element.85.refs_0_), channel_id=1, source_target_pairs={{0,4},{1,5},{2,6},{3,7},{4,0},{5,1},{6,2},{7,3},{8,12},{9,13},{10,... | collective-permute-start | bytes 393224 | tf_op jit(solution)/shard_map/ppermute | solution.py:541
  9.6 10.8 %collective-permute-start = (bf16[1,512,128]{2,1,0:T(8,128)(2,1)S(1)}, bf16[1,512,128]{2,1,0:T(8,128)(2,1)S(1)}, u32[]{:S(2)}, u32[]{:S(2)}) collective-permute-start(bf16[1,512,128]{2,1,0:T(8,128)(2,1)S(1)} %get-tuple-element.85.refs_0_), channel_id=1, source_target_pairs={{0,2},{1,3},{2,0},{3,1},{4,6},{5,7},{6,4},{7,5},{8,10},{9,11},{10,... | collective-permute-start | bytes 393224 | tf_op jit(solution)/shard_map/ppermute | solution.py:541
  11.9 1.2 %copy-start = (f32[2,1024,128]{2,1,0:T(8,128)S(1)}, f32[2,1024,128]{2,1,0:T(8,128)}, u32[]{:S(2)}) copy-start(f32[2,1024,128]{2,1,0:T(8,128)} %q_ref.5) | copy-start | bytes 3145732
  13.1 1.2 %copy-start.2 = (bf16[512,1024]{1,0:T(8,128)(2,1)S(1)}, bf16[512,1024]{1,0:T(8,128)(2,1)}, u32[]{:S(2)}) copy-start(bf16[512,1024]{1,0:T(8,128)(2,1)} %in_ref.1) | copy-start | bytes 3145732
  14.4 0.7 copy-start.3
  20.4 1.4 %collective-permute-start.13 = (bf16[1,512,128]{2,1,0:T(8,128)(2,1)S(1)}, bf16[1,512,128]{2,1,0:T(8,128)(2,1)S(1)}, u32[]{:S(2)}, u32[]{:S(2)}) collective-permute-start(bf16[1,512,128]{2,1,0:T(8,128)(2,1)S(1)} %get-tuple-element.85.refs_0_), channel_id=1, source_target_pairs={{0,1},{1,0},{2,3},{3,2},{4,5},{5,4},{6,7},{7,6},{8,9},{9,8},{10,11... | collective-permute-start | bytes 393224 | tf_op jit(solution)/shard_map/ppermute | solution.py:541
  20.5 1.5 %collective-permute-start.14 = (bf16[1,512,128]{2,1,0:T(8,128)(2,1)S(1)}, bf16[1,512,128]{2,1,0:T(8,128)(2,1)S(1)}, u32[]{:S(2)}, u32[]{:S(2)}) collective-permute-start(bf16[1,512,128]{2,1,0:T(8,128)(2,1)S(1)} %collective-permute-done.refs_2_), channel_id=1, source_target_pairs={{0,1},{1,0},{2,3},{3,2},{4,5},{5,4},{6,7},{7,6},{8,9},{9,8},{10,11... | collective-permute-start | bytes 393224 | tf_op jit(solution)/shard_map/ppermute | solution.py:541
  21.0 1.4 %collective-permute-start.15 = (bf16[1,512,128]{2,1,0:T(8,128)(2,1)S(1)}, bf16[1,512,128]{2,1,0:T(8,128)(2,1)S(1)}, u32[]{:S(2)}, u32[]{:S(2)}) collective-permute-start(bf16[1,512,128]{2,1,0:T(8,128)(2,1)S(1)} %collective-permute-done.1.refs_4_), channel_id=1, source_target_pairs={{0,1},{1,0},{2,3},{3,2},{4,5},{5,4},{6,7},{7,6},{8,9},{9,8},{10,11... | collective-permute-start | bytes 393224 | tf_op jit(solution)/shard_map/ppermute | solution.py:541
  21.0 1.5 %collective-permute-start.16 = (bf16[1,512,128]{2,1,0:T(8,128)(2,1)S(1)}, bf16[1,512,128]{2,1,0:T(8,128)(2,1)S(1)}, u32[]{:S(2)}, u32[]{:S(2)}) collective-permute-start(bf16[1,512,128]{2,1,0:T(8,128)(2,1)S(1)} %collective-permute-done.2.refs_6_), channel_id=1, source_target_pairs={{0,1},{1,0},{2,3},{3,2},{4,5},{5,4},{6,7},{7,6},{8,9},{9,8},{10,11... | collective-permute-start | bytes 393224 | tf_op jit(solution)/shard_map/ppermute | solution.py:541
  21.5 5.0 %collective-permute-start.6 = (bf16[1,512,128]{2,1,0:T(8,128)(2,1)S(1)}, bf16[1,512,128]{2,1,0:T(8,128)(2,1)S(1)}, u32[]{:S(2)}, u32[]{:S(2)}) collective-permute-start(bf16[1,512,128]{2,1,0:T(8,128)(2,1)S(1)} %get-tuple-element.73.refs_0_), channel_id=1, source_target_pairs={{0,1},{1,0},{2,3},{3,2},{4,5},{5,4},{6,7},{7,6},{8,9},{9,8},{10,11... | collective-permute-start | bytes 393224 | tf_op jit(solution)/shard_map/ppermute | solution.py:541
  21.8 4.6 %collective-permute-start.7 = (bf16[1,512,128]{2,1,0:T(8,128)(2,1)S(1)}, bf16[1,512,128]{2,1,0:T(8,128)(2,1)S(1)}, u32[]{:S(2)}, u32[]{:S(2)}) collective-permute-start(bf16[1,512,128]{2,1,0:T(8,128)(2,1)S(1)} %collective-permute-done.3.refs_2_), channel_id=1, source_target_pairs={{0,1},{1,0},{2,3},{3,2},{4,5},{5,4},{6,7},{7,6},{8,9},{9,8},{10,11... | collective-permute-start | bytes 393224 | tf_op jit(solution)/shard_map/ppermute | solution.py:541
  22.0 4.5 %collective-permute-start.8 = (bf16[1,512,128]{2,1,0:T(8,128)(2,1)S(1)}, bf16[1,512,128]{2,1,0:T(8,128)(2,1)S(1)}, u32[]{:S(2)}, u32[]{:S(2)}) collective-permute-start(bf16[1,512,128]{2,1,0:T(8,128)(2,1)S(1)} %collective-permute-done.4.refs_4_), channel_id=1, source_target_pairs={{0,1},{1,0},{2,3},{3,2},{4,5},{5,4},{6,7},{7,6},{8,9},{9,8},{10,11... | collective-permute-start | bytes 393224 | tf_op jit(solution)/shard_map/ppermute | solution.py:541
  22.3 4.1 %collective-permute-start.9 = (bf16[1,512,128]{2,1,0:T(8,128)(2,1)S(1)}, bf16[1,512,128]{2,1,0:T(8,128)(2,1)S(1)}, u32[]{:S(2)}, u32[]{:S(2)}) collective-permute-start(bf16[1,512,128]{2,1,0:T(8,128)(2,1)S(1)} %collective-permute-done.5.refs_6_), channel_id=1, source_target_pairs={{0,1},{1,0},{2,3},{3,2},{4,5},{5,4},{6,7},{7,6},{8,9},{9,8},{10,11... | collective-permute-start | bytes 393224 | tf_op jit(solution)/shard_map/ppermute | solution.py:541
  24.8 5.9 %collective-permute-start.17 = (s16[528,128]{1,0:T(8,128)(2,1)S(1)}, s16[528,128]{1,0:T(8,128)(2,1)S(1)}, u32[]{:S(2)}, u32[]{:S(2)}) collective-permute-start(s16[528,128]{1,0:T(8,128)(2,1)S(1)} %get-tuple-element.90), channel_id=1, source_target_pairs={{0,8},{8,0},{16,24},{24,16},{1,9},{9,1},{17,25},{25,17},{2,10},{10... | collective-permute-start | bytes 405512 | tf_op jit(solution)/shard_map/ppermute | solution.py:541
  28.7 7.5 %collective-permute-start.10 = (s16[528,128]{1,0:T(8,128)(2,1)S(1)}, s16[528,128]{1,0:T(8,128)(2,1)S(1)}, u32[]{:S(2)}, u32[]{:S(2)}) collective-permute-start(s16[528,128]{1,0:T(8,128)(2,1)S(1)} %get-tuple-element.78), channel_id=1, source_target_pairs={{0,8},{8,0},{16,24},{24,16},{1,9},{9,1},{17,25},{25,17},{2,10},{10... | collective-permute-start | bytes 405512 | tf_op jit(solution)/shard_map/ppermute | solution.py:541
  30.8 12.2 %collective-permute-start.18 = (s16[528,128]{1,0:T(8,128)(2,1)S(1)}, s16[528,128]{1,0:T(8,128)(2,1)S(1)}, u32[]{:S(2)}, u32[]{:S(2)}) collective-permute-start(s16[528,128]{1,0:T(8,128)(2,1)S(1)} %add_code.6.mine_ref), channel_id=1, source_target_pairs={{0,16},{8,24},{16,0},{24,8},{1,17},{9,25},{17,1},{25,9},{2,18},{10... | collective-permute-start | bytes 405512 | tf_op jit(solution)/shard_map/ppermute | solution.py:541
  36.4 9.2 %collective-permute-start.11 = (s16[528,128]{1,0:T(8,128)(2,1)S(1)}, s16[528,128]{1,0:T(8,128)(2,1)S(1)}, u32[]{:S(2)}, u32[]{:S(2)}) collective-permute-start(s16[528,128]{1,0:T(8,128)(2,1)S(1)} %add_code.4.mine_ref), channel_id=1, source_target_pairs={{0,16},{8,24},{16,0},{24,8},{1,17},{9,25},{17,1},{25,9},{2,18},{10... | collective-permute-start | bytes 405512 | tf_op jit(solution)/shard_map/ppermute | solution.py:541
  43.2 5.5 %collective-permute-start.19 = (s16[528,128]{1,0:T(8,128)(2,1)S(1)}, s16[528,128]{1,0:T(8,128)(2,1)S(1)}, u32[]{:S(2)}, u32[]{:S(2)}) collective-permute-start(s16[528,128]{1,0:T(8,128)(2,1)S(1)} %add_code.7.mine_ref), channel_id=1, source_target_pairs={{0,8},{8,0},{16,24},{24,16},{1,9},{9,1},{17,25},{25,17},{2,10},{10... | collective-permute-start | bytes 405512 | tf_op jit(solution)/shard_map/ppermute | solution.py:541
  44.9 28.1 %copy-start.4 = (s32[2]{0:T(128)S(1)}, s32[2]{0:T(128)}, u32[]{:S(2)}) copy-start(s32[2]{0:T(128)} %ranks_ref.7) | copy-start | bytes 28
  45.8 5.5 %collective-permute-start.12 = (s16[528,128]{1,0:T(8,128)(2,1)S(1)}, s16[528,128]{1,0:T(8,128)(2,1)S(1)}, u32[]{:S(2)}, u32[]{:S(2)}) collective-permute-start(s16[528,128]{1,0:T(8,128)(2,1)S(1)} %add_code.5.mine_ref), channel_id=1, source_target_pairs={{0,8},{8,0},{16,24},{24,16},{1,9},{9,1},{17,25},{25,17},{2,10},{10... | collective-permute-start | bytes 405512 | tf_op jit(solution)/shard_map/ppermute | solution.py:541
  50.3 3.4 %collective-permute-start.25 = (f32[512,128]{1,0:T(8,128)S(1)}, f32[512,128]{1,0:T(8,128)S(1)}, u32[]{:S(2)}, u32[]{:S(2)}) collective-permute-start(f32[512,128]{1,0:T(8,128)S(1)} %get-tuple-element.103), channel_id=1, source_target_pairs={{0,1},{1,0},{2,3},{3,2},{4,5},{5,4},{6,7},{7,6},{8,9},{9,8},{10,11... | collective-permute-start | bytes 786440 | tf_op jit(solution)/shard_map/ppermute | solution.py:541
  53.1 1.6 %collective-permute-start.24 = (f32[512,128]{1,0:T(8,128)S(1)}, f32[512,128]{1,0:T(8,128)S(1)}, u32[]{:S(2)}, u32[]{:S(2)}) collective-permute-start(f32[512,128]{1,0:T(8,128)S(1)} %get-tuple-element.102), channel_id=1, source_target_pairs={{0,1},{1,0},{2,3},{3,2},{4,5},{5,4},{6,7},{7,6},{8,9},{9,8},{10,11... | collective-permute-start | bytes 786440 | tf_op jit(solution)/shard_map/ppermute | solution.py:541
  53.2 1.8 %collective-permute-start.20 = (f32[2,128,128]{2,1,0:T(8,128)S(1)}, f32[2,128,128]{2,1,0:T(8,128)S(1)}, u32[]{:S(2)}, u32[]{:S(2)}) collective-permute-start(f32[2,128,128]{2,1,0:T(8,128)S(1)} %pad_maximum_fusion), channel_id=1, source_target_pairs={{0,1},{1,0},{2,3},{3,2},{4,5},{5,4},{6,7},{7,6},{8,9},{9,8},{10,11... | collective-permute-start | bytes 393224 | tf_op jit(solution)/shard_map/ppermute | solution.py:541
  54.9 5.7 %collective-permute-start.26 = (s16[272,128]{1,0:T(8,128)(2,1)S(1)}, s16[272,128]{1,0:T(8,128)(2,1)S(1)}, u32[]{:S(2)}, u32[]{:S(2)}) collective-permute-start(s16[272,128]{1,0:T(8,128)(2,1)S(1)} %get-tuple-element.106), channel_id=1, source_target_pairs={{0,2},{1,3},{2,0},{3,1},{4,6},{5,7},{6,4},{7,5},{8,10},{9,11},{10,... | collective-permute-start | bytes 208904 | tf_op jit(solution)/shard_map/ppermute | solution.py:541
  55.0 13.5 %collective-permute-start.23 = (f32[2,128,128]{2,1,0:T(8,128)S(1)}, f32[2,128,128]{2,1,0:T(8,128)S(1)}, u32[]{:S(2)}, u32[]{:S(2)}) collective-permute-start(f32[2,128,128]{2,1,0:T(8,128)S(1)} %fusion.refs_0_), channel_id=1, source_target_pairs={{0,6},{1,7},{2,4},{3,5},{4,2},{5,3},{6,0},{7,1},{8,14},{9,15},{10,... | collective-permute-start | bytes 393224 | tf_op jit(solution)/shard_map/ppermute | solution.py:541
  58.1 10.5 %collective-permute-start.22 = (f32[2,128,128]{2,1,0:T(8,128)S(1)}, f32[2,128,128]{2,1,0:T(8,128)S(1)}, u32[]{:S(2)}, u32[]{:S(2)}) collective-permute-start(f32[2,128,128]{2,1,0:T(8,128)S(1)} %fusion.refs_0_), channel_id=1, source_target_pairs={{0,4},{1,5},{2,6},{3,7},{4,0},{5,1},{6,2},{7,3},{8,12},{9,13},{10,... | collective-permute-start | bytes 393224 | tf_op jit(solution)/shard_map/ppermute | solution.py:541
  58.6 10.0 %collective-permute-start.21 = (f32[2,128,128]{2,1,0:T(8,128)S(1)}, f32[2,128,128]{2,1,0:T(8,128)S(1)}, u32[]{:S(2)}, u32[]{:S(2)}) collective-permute-start(f32[2,128,128]{2,1,0:T(8,128)S(1)} %fusion.refs_0_), channel_id=1, source_target_pairs={{0,2},{1,3},{2,0},{3,1},{4,6},{5,7},{6,4},{7,5},{8,10},{9,11},{10,... | collective-permute-start | bytes 393224 | tf_op jit(solution)/shard_map/ppermute | solution.py:541
  58.7 9.7 %collective-permute-start.27 = (s16[272,128]{1,0:T(8,128)(2,1)S(1)}, s16[272,128]{1,0:T(8,128)(2,1)S(1)}, u32[]{:S(2)}, u32[]{:S(2)}) collective-permute-start(s16[272,128]{1,0:T(8,128)(2,1)S(1)} %get-tuple-element.107), channel_id=1, source_target_pairs={{0,4},{1,5},{2,6},{3,7},{4,0},{5,1},{6,2},{7,3},{8,12},{9,13},{10,... | collective-permute-start | bytes 208904 | tf_op jit(solution)/shard_map/ppermute | solution.py:541
  60.6 7.8 %collective-permute-start.28 = (s16[272,128]{1,0:T(8,128)(2,1)S(1)}, s16[272,128]{1,0:T(8,128)(2,1)S(1)}, u32[]{:S(2)}, u32[]{:S(2)}) collective-permute-start(s16[272,128]{1,0:T(8,128)(2,1)S(1)} %get-tuple-element.108), channel_id=1, source_target_pairs={{0,6},{1,7},{2,4},{3,5},{4,2},{5,3},{6,0},{7,1},{8,14},{9,15},{10,... | collective-permute-start | bytes 208904 | tf_op jit(solution)/shard_map/ppermute | solution.py:541
  68.6 12.3 %collective-permute-start.31 = (s16[272,128]{1,0:T(8,128)(2,1)S(1)}, s16[272,128]{1,0:T(8,128)(2,1)S(1)}, u32[]{:S(2)}, u32[]{:S(2)}) collective-permute-start(s16[272,128]{1,0:T(8,128)(2,1)S(1)} %code.1.refs_0_), channel_id=1, source_target_pairs={{0,24},{8,16},{16,8},{24,0},{1,25},{9,17},{17,9},{25,1},{2,26},{10... | collective-permute-start | bytes 208904 | tf_op jit(solution)/shard_map/ppermute | solution.py:541
  72.1 8.8 %collective-permute-start.30 = (s16[272,128]{1,0:T(8,128)(2,1)S(1)}, s16[272,128]{1,0:T(8,128)(2,1)S(1)}, u32[]{:S(2)}, u32[]{:S(2)}) collective-permute-start(s16[272,128]{1,0:T(8,128)(2,1)S(1)} %code.1.refs_0_), channel_id=1, source_target_pairs={{0,16},{8,24},{16,0},{24,8},{1,17},{9,25},{17,1},{25,9},{2,18},{10... | collective-permute-start | bytes 208904 | tf_op jit(solution)/shard_map/ppermute | solution.py:541
  72.1 8.8 %collective-permute-start.29 = (s16[272,128]{1,0:T(8,128)(2,1)S(1)}, s16[272,128]{1,0:T(8,128)(2,1)S(1)}, u32[]{:S(2)}, u32[]{:S(2)}) collective-permute-start(s16[272,128]{1,0:T(8,128)(2,1)S(1)} %code.1.refs_0_), channel_id=1, source_target_pairs={{0,8},{8,0},{16,24},{24,16},{1,9},{9,1},{17,25},{25,17},{2,10},{10... | collective-permute-start | bytes 208904 | tf_op jit(solution)/shard_map/ppermute | solution.py:541
  81.1 5.4 %collective-permute-start.34 = (s16[272,128]{1,0:T(8,128)(2,1)S(1)}, s16[272,128]{1,0:T(8,128)(2,1)S(1)}, u32[]{:S(2)}, u32[]{:S(2)}) collective-permute-start(s16[272,128]{1,0:T(8,128)(2,1)S(1)} %code_sum.1.refs_0_), channel_id=1, source_target_pairs={{0,6},{1,7},{2,4},{3,5},{4,2},{5,3},{6,0},{7,1},{8,14},{9,15},{10,... | collective-permute-start | bytes 208904 | tf_op jit(solution)/shard_map/ppermute | solution.py:541
  82.0 5.1 %collective-permute-start.33 = (s16[272,128]{1,0:T(8,128)(2,1)S(1)}, s16[272,128]{1,0:T(8,128)(2,1)S(1)}, u32[]{:S(2)}, u32[]{:S(2)}) collective-permute-start(s16[272,128]{1,0:T(8,128)(2,1)S(1)} %code_sum.1.refs_0_), channel_id=1, source_target_pairs={{0,4},{1,5},{2,6},{3,7},{4,0},{5,1},{6,2},{7,3},{8,12},{9,13},{10,... | collective-permute-start | bytes 208904 | tf_op jit(solution)/shard_map/ppermute | solution.py:541
  83.4 4.3 %collective-permute-start.32 = (s16[272,128]{1,0:T(8,128)(2,1)S(1)}, s16[272,128]{1,0:T(8,128)(2,1)S(1)}, u32[]{:S(2)}, u32[]{:S(2)}) collective-permute-start(s16[272,128]{1,0:T(8,128)(2,1)S(1)} %code_sum.1.refs_0_), channel_id=1, source_target_pairs={{0,2},{1,3},{2,0},{3,1},{4,6},{5,7},{6,4},{7,5},{8,10},{9,11},{10,... | collective-permute-start | bytes 208904 | tf_op jit(solution)/shard_map/ppermute | solution.py:541
  87.7 1.3 %collective-permute-start.35 = (s16[272,128]{1,0:T(8,128)(2,1)S(1)}, s16[272,128]{1,0:T(8,128)(2,1)S(1)}, u32[]{:S(2)}, u32[]{:S(2)}) collective-permute-start(s16[272,128]{1,0:T(8,128)(2,1)S(1)} %code_sum.1.refs_0_), channel_id=1, source_target_pairs={{0,1},{1,0},{2,3},{3,2},{4,5},{5,4},{6,7},{7,6},{8,9},{9,8},{10,11... | collective-permute-start | bytes 208904 | tf_op jit(solution)/shard_map/ppermute | solution.py:541
  87.7 1.4 %collective-permute-start.36 = (s16[272,128]{1,0:T(8,128)(2,1)S(1)}, s16[272,128]{1,0:T(8,128)(2,1)S(1)}, u32[]{:S(2)}, u32[]{:S(2)}) collective-permute-start(s16[272,128]{1,0:T(8,128)(2,1)S(1)} %collective-permute-done.32.refs_2_), channel_id=1, source_target_pairs={{0,1},{1,0},{2,3},{3,2},{4,5},{5,4},{6,7},{7,6},{8,9},{9,8},{10,11... | collective-permute-start | bytes 208904 | tf_op jit(solution)/shard_map/ppermute | solution.py:541
  88.2 1.3 %collective-permute-start.37 = (s16[272,128]{1,0:T(8,128)(2,1)S(1)}, s16[272,128]{1,0:T(8,128)(2,1)S(1)}, u32[]{:S(2)}, u32[]{:S(2)}) collective-permute-start(s16[272,128]{1,0:T(8,128)(2,1)S(1)} %collective-permute-done.33.refs_4_), channel_id=1, source_target_pairs={{0,1},{1,0},{2,3},{3,2},{4,5},{5,4},{6,7},{7,6},{8,9},{9,8},{10,11... | collective-permute-start | bytes 208904 | tf_op jit(solution)/shard_map/ppermute | solution.py:541
  88.2 1.4 %collective-permute-start.38 = (s16[272,128]{1,0:T(8,128)(2,1)S(1)}, s16[272,128]{1,0:T(8,128)(2,1)S(1)}, u32[]{:S(2)}, u32[]{:S(2)}) collective-permute-start(s16[272,128]{1,0:T(8,128)(2,1)S(1)} %collective-permute-done.34.refs_6_), channel_id=1, source_target_pairs={{0,1},{1,0},{2,3},{3,2},{4,5},{5,4},{6,7},{7,6},{8,9},{9,8},{10,11... | collective-permute-start | bytes 208904 | tf_op jit(solution)/shard_map/ppermute | solution.py:541
  89.6 1.2 %copy-start.1 = (f32[2,1024,128]{2,1,0:T(8,128)S(1)}, f32[2,1024,128]{2,1,0:T(8,128)}, u32[]{:S(2)}) copy-start(f32[2,1024,128]{2,1,0:T(8,128)} %get-tuple-element.62.fp_ref) | copy-start | bytes 3145732

commit v4 on v3

--- a/solution.py
+++ b/solution.py
@@ -50,11 +50,21 @@
     return halves(jnp.where(column < rank, q, 0.0))
 
 
-def feedback_q_kernel(ranks_ref, fb_ref, q_ref, in_ref, held_ref, out_ref, in_t_ref, q2_ref, sems):
+def feedback_q_kernel(
+    ranks_ref, fb_ref, q_ref, in_ref, held_ref, out_ref, q2_ref, in_t_ref, ranks_own, q_own, in_own, sems, sem_q
+):
     count, rows, _ = held_ref.shape
     width = q_ref.shape[2]
     tile = tile_of(rows)
+    small = [
+        pltpu.make_async_copy(ranks_ref, ranks_own, sem_q.at[0]),
+        pltpu.make_async_copy(q_ref, q_own, sem_q.at[1]),
+        pltpu.make_async_copy(in_ref, in_own, sem_q.at[2]),
+    ]
     copies = []
+    small[2].start()
+    small[0].start()
+    small[1].start()
     for m in range(count):
         for i in range(rows // tile):
             part = pl.ds(i * tile, tile)
@@ -62,9 +72,12 @@
                 pltpu.make_async_copy(fb_ref.at[m, 0, part], held_ref.at[m, part], sems.at[len(copies)])
             )
             copies[-1].start()
-    in_t_ref[...] = in_ref[...].T
-    for m in range(count):
-        q_high, q_low = masked_halves(q_ref[m], ranks_ref[m])
+    small[2].wait()
+    in_t_ref[...] = in_own[...].T
+    small[0].wait()
+    small[1].wait()
+    for m in range(count):
+        q_high, q_low = masked_halves(q_own[m], ranks_own[m])
         q2_ref[m, :, :width] = q_high
         q2_ref[m, :, width:] = q_low
     for m in range(count):
@@ -79,82 +92,67 @@
 def feedback_q(feedback, q_init, inputs, ranks):
     count, _, rows, columns = feedback.shape
     width = q_init.shape[2]
+    far = pl.BlockSpec(memory_space=pltpu.HBM)
     return pl.pallas_call(
         feedback_q_kernel,
-        in_specs=[SMEM, pl.BlockSpec(memory_space=pltpu.HBM), VMEM, VMEM],
-        out_specs=[VMEM, VMEM, VMEM],
+        in_specs=[far] * 4,
+        out_specs=[VMEM] * 4,
         out_shape=[
             in_vmem((count, rows, columns), F32),
-            jax.ShapeDtypeStruct((count, rows, width), F32),
-            jax.ShapeDtypeStruct(inputs.shape[::-1], inputs.dtype),
+            in_vmem((count, rows, width), F32),
+            in_vmem((count, columns, 2 * width), BF16),
+            in_vmem(inputs.shape[::-1], inputs.dtype),
         ],
         scratch_shapes=[
-            pltpu.VMEM((count, columns, 2 * width), BF16),
+            pltpu.SMEM(ranks.shape, ranks.dtype),
+            pltpu.VMEM(q_init.shape, q_init.dtype),
+            pltpu.VMEM(inputs.shape, inputs.dtype),
             pltpu.SemaphoreType.DMA((count * (rows // tile_of(rows)),)),
+            pltpu.SemaphoreType.DMA((3,)),
         ],
         compiler_params=pltpu.CompilerParams(vmem_limit_bytes=16 * MIB),
         name="feedback_q",
-    )(ranks, pltpu.with_memory_space_constraint(feedback, pltpu.HBM), q_init, inputs)
-
-
-def fill_cotangent(blocks, whole_ref):
+    )(*[pltpu.with_memory_space_constraint(x, pltpu.HBM) for x in (ranks, feedback, q_init, inputs)])
+
+
+def fill_cotangent(blocks, at, whole_ref):
     if len(blocks) == 1:
-        whole_ref[...] = blocks[0][0]
+        whole_ref[...] = blocks[0][at]
         return
     me = lax.axis_index("fsdp")
     for r, block in enumerate(blocks):
         width = block.shape[2]
         start = pl.multiple_of((me ^ r) * width, width)
-        whole_ref[:, pl.ds(start, width)] = block[0]
-
-
-def gradient_q(whole, q, rank, inputs_t):
-    width = q.shape[1]
-    q_high, q_low = masked_halves(q, rank)
-    both = mm(whole, jnp.concatenate([q_high, q_low], axis=1))
+        whole_ref[:, pl.ds(start, width)] = block[at]
+
+
+def gradient_q(whole, q2, inputs_t):
+    width = q2.shape[1] // 2
+    both = mm(whole, q2)
     c_high, c_low = halves(both[:, :width] + both[:, width:])
     both = mm(inputs_t, jnp.concatenate([c_high, c_low], axis=1))
     return both[:, :width] + both[:, width:]
 
 
-def at_block(shape, m):
-    return pl.BlockSpec((1, *shape[1:]), lambda *_: (m,) + (0,) * (len(shape) - 1))
-
-
-def block_of(pieces, m):
-    for piece in pieces:
-        if m < piece.shape[0]:
-            return piece, m
-        m -= piece.shape[0]
-    raise ValueError(m)
-
-
-def left_kernel(m, ranks_ref, q_ref, in_ref, fbq_ref, *refs):
+def left_kernel(m, at, q2_ref, in_ref, fbq_ref, *refs):
     *blocks, out_ref, whole_ref = refs
-    fill_cotangent(blocks, whole_ref)
-    out_ref[...] = fbq_ref[0] + gradient_q(whole_ref[...], q_ref[0], ranks_ref[m], in_ref[...])
-
-
-def left(m, blocks, q_init, inputs_t, fbq, ranks):
+    fill_cotangent(blocks, at, whole_ref)
+    out_ref[...] = fbq_ref[m] + gradient_q(whole_ref[...], q2_ref[m], in_ref[...])
+
+
+def left(m, blocks, at, q2, inputs_t, fbq):
     _, rows, width = fbq.shape
-    arrays, indices = zip(*(block_of(pieces, m) for pieces in blocks))
-    shape = (arrays[0].shape[1], q_init.shape[1])
-    return pl.pallas_call(
-        functools.partial(left_kernel, m),
-        grid=(1,),
-        in_specs=[SMEM, at_block(q_init.shape, m), VMEM, at_block(fbq.shape, m)]
-        + [at_block(a.shape, i) for a, i in zip(arrays, indices)],
-        out_specs=[
-            pl.BlockSpec((rows, width), lambda i: (0, 0)),
-            pl.BlockSpec(shape, lambda i: (0, 0)),
-        ],
+    return pl.pallas_call(
+        functools.partial(left_kernel, m, at),
+        in_specs=[VMEM] * (3 + len(blocks)),
+        out_specs=[VMEM, VMEM],
         out_shape=[
             jax.ShapeDtypeStruct((rows, width), F32),
-            jax.ShapeDtypeStruct(shape, BF16),
-        ],
-        compiler_params=params(16),
+            jax.ShapeDtypeStruct((blocks[0].shape[1], q2.shape[1]), BF16),
+        ],
+        compiler_params=pltpu.CompilerParams(vmem_limit_bytes=16 * MIB),
         name=f"left_{m}",
-    )(ranks, q_init, inputs_t, fbq, *arrays)
+    )(q2, inputs_t, fbq, *blocks)
 
 
 GROUPS = 16
@@ -181,40 +179,32 @@
     return (code * down[:, None, :]).reshape(rows, width)
 
 
-def left_code_kernel(m, ranks_ref, q_ref, in_ref, fbq_ref, *refs):
+def left_code_kernel(m, at, q2_ref, in_ref, fbq_ref, *refs):
     *blocks, mine_ref, code_ref, whole_ref, p_ref = refs
-    fill_cotangent(blocks, whole_ref)
-    p = fbq_ref[0] + gradient_q(whole_ref[...], q_ref[0], ranks_ref[m], in_ref[...])
+    fill_cotangent(blocks, at, whole_ref)
+    p = fbq_ref[m] + gradient_q(whole_ref[...], q2_ref[m], in_ref[...])
     p_ref[...] = p.reshape(p_ref.shape)
     low = lax.axis_index("dp") & 1
     mine_ref[...] = p_ref[low]
     encode(p_ref[1 - low], code_ref)
 
 
-def left_code(m, blocks, q_init, inputs_t, fbq, ranks):
+def left_code(m, blocks, at, q2, inputs_t, fbq):
     _, rows, width = fbq.shape
-    arrays, indices = zip(*(block_of(pieces, m) for pieces in blocks))
-    shape = (arrays[0].shape[1], q_init.shape[1])
     half = rows // 2
     return pl.pallas_call(
-        functools.partial(left_code_kernel, m),
-        grid=(1,),
-        in_specs=[SMEM, at_block(q_init.shape, m), VMEM, at_block(fbq.shape, m)]
-        + [at_block(a.shape, i) for a, i in zip(arrays, indices)],
-        out_specs=[
-            pl.BlockSpec((half, width), lambda i: (0, 0)),
-            pl.BlockSpec((half + GROUPS, width), lambda i: (0, 0)),
-            pl.BlockSpec(shape, lambda i: (0, 0)),
-        ],
+        functools.partial(left_code_kernel, m, at),
+        in_specs=[VMEM] * (3 + len(blocks)),
+        out_specs=[VMEM] * 3,
         out_shape=[
             jax.ShapeDtypeStruct((half, width), F32),
             jax.ShapeDtypeStruct((half + GROUPS, width), jnp.int16),
-            jax.ShapeDtypeStruct(shape, BF16),
+            jax.ShapeDtypeStruct((blocks[0].shape[1], q2.shape[1]), BF16),
         ],
         scratch_shapes=[pltpu.VMEM((2, half, width), F32)],
-        compiler_params=params(16),
+        compiler_params=pltpu.CompilerParams(vmem_limit_bytes=16 * MIB),
         name=f"left_code_{m}",
-    )(ranks, q_init, inputs_t, fbq, *arrays)
+    )(q2, inputs_t, fbq, *blocks)
 
 
 def add_kernel(mine_ref, theirs_ref, out_ref):
@@ -428,10 +418,7 @@
                 blocks[c] = y
 
 
-def factor_kernel(terms, ranks_ref, *refs):
-    gram_refs, refs = refs[:terms], refs[terms:]
-    inv_ref, out_ref = refs[-2:]
-    p_refs = refs[:-2]
+def factor_kernel(ranks_ref, gram_ref, inv_ref):
     count, n, _ = inv_ref.shape
     lane = lax.broadcasted_iota(jnp.int32, (8, n), 1)
     sub = lax.broadcasted_iota(jnp.int32, (8, n), 0)
@@ -440,38 +427,64 @@
         free = jnp.where(lane < ranks_ref[m], 0.0, 1.0)
         blocks = []
         for b in range(n // 8):
-            g = tree([ref[m, 8 * b : 8 * b + 8, :] for ref in gram_refs])
+            g = gram_ref[m, 8 * b : 8 * b + 8, :]
             blocks.append(jnp.where(lane == sub + 8 * b, g + free, g))
         work.append(blocks)
     cholesky_inverse(work, n)
     for m in range(count):
         for b in range(n // 8):
             inv_ref[m, 8 * b : 8 * b + 8, :] = jnp.where(lane <= sub + 8 * b, work[m][b], 0.0)
+
+
+def factor(grams, ranks):
+    return pl.pallas_call(
+        factor_kernel,
+        in_specs=[SMEM, VMEM],
+        out_specs=VMEM,
+        out_shape=jax.ShapeDtypeStruct(grams.shape, F32),
+        compiler_params=pltpu.CompilerParams(vmem_limit_bytes=16 * MIB),
+        name="factor",
+    )(ranks, grams)
+
+
+def factor_p_kernel(inv_ref, *refs):
+    *p_refs, out_ref, p3_ref, buf_ref, sems = refs
+    n = inv_ref.shape[1]
+    copies = []
+    for m, p_ref in enumerate(p_refs):
         i_high, i_low = halves(inv_ref[m])
-        p_high, p_low = halves(p_refs[m][...])
+        p_high, p_low = halves(p_ref[...])
         both = mm_nt(p_high, jnp.concatenate([i_high, i_low], axis=0))
-        out_ref[m] = both[:, :n] + both[:, n:] + mm_nt(p_low, i_high)
-
-
-def factor(grams, p, ranks):
-    count = len(p)
-    return pl.pallas_call(
-        functools.partial(factor_kernel, len(grams)),
-        in_specs=[SMEM] + [VMEM] * (len(grams) + count),
-        out_specs=[VMEM, VMEM],
+        result = both[:, :n] + both[:, n:] + mm_nt(p_low, i_high)
+        buf_ref[m] = result
+        copies.append(pltpu.make_async_copy(buf_ref.at[m], out_ref.at[m], sems.at[m]))
+        copies[-1].start()
+        high, low = halves(result)
+        p3_ref[m] = jnp.concatenate([high, low, high], axis=1)
+    for copy in copies:
+        copy.wait()
+
+
+def factor_p_of(inverse, p):
+    count, (rows, width) = len(p), p[0].shape
+    return pl.pallas_call(
+        factor_p_kernel,
+        in_specs=[VMEM] * (1 + count),
+        out_specs=[pl.BlockSpec(memory_space=pltpu.HBM), VMEM],
         out_shape=[
-            jax.ShapeDtypeStruct(grams[0].shape, F32),
-            jax.ShapeDtypeStruct((count, *p[0].shape), F32),
-        ],
-        compiler_params=pltpu.CompilerParams(vmem_limit_bytes=16 * MIB),
-        name="factor",
-    )(ranks, *grams, *p)
-
-
-def error_kernel(count, pieces, groups, fp_ref, inv_ref, *refs):
+            jax.ShapeDtypeStruct((count, rows, width), F32),
+            in_vmem((count, rows, 3 * width), BF16),
+        ],
+        scratch_shapes=[pltpu.VMEM((count, rows, width), F32), pltpu.SemaphoreType.DMA((count,))],
+        compiler_params=pltpu.CompilerParams(vmem_limit_bytes=16 * MIB),
+        name="factor_p",
+    )(inverse, *p)
+
+
+def error_kernel(count, pieces, groups, p3_ref, inv_ref, *refs):
     codes, refs = refs[:pieces], refs[pieces:]
     full_refs, (err_ref, fq_ref, right_ref, q_ref, buf_ref, sems) = refs[:count], refs[count:]
-    rows, width = fp_ref.shape[1:]
+    rows, width = p3_ref.shape[1], inv_ref.shape[1]
     tile = tile_of(rows)
     share = right_ref.shape[1] // pieces
     me = lax.axis_index("fsdp") if pieces > 1 else 0
@@ -494,9 +507,7 @@
         q3 = jnp.concatenate([q_high, q_high, q_low], axis=0)
         for i in range(rows // tile):
             part = pl.ds(i * tile, tile)
-            p_high, p_low = halves(fp_ref[m, part])
-            low_rank = mm(jnp.concatenate([p_high, p_low, p_high], axis=1), q3)
-            buf_ref[m, part] = full_refs[m][part] - low_rank
+            buf_ref[m, part] = full_refs[m][part] - mm(p3_ref[m, part], q3)
             copies.append(
                 pltpu.make_async_copy(buf_ref.at[m, part], err_ref.at[m, 0, part], sems.at[len(copies)])
             )
@@ -508,8 +519,9 @@
         copy.wait()
 
 
-def error(full_grad, factor_p, inverse, codes):
-    count, rows, width = factor_p.shape
+def error(full_grad, p3, inverse, codes):
+    count, rows, _ = p3.shape
+    width = inverse.shape[1]
     columns = full_grad[0].shape[1]
     out = pl.BlockSpec(memory_space=pltpu.HBM)
     groups = groups_of("fsdp") if len(codes) > 1 else []
@@ -529,7 +541,7 @@
         ],
         compiler_params=pltpu.CompilerParams(vmem_limit_bytes=24 * MIB),
         name="error",
-    )(factor_p, inverse, *codes, *[stay(x) for x in full_grad])
+    )(stay(p3), inverse, *codes, *[stay(x) for x in full_grad])
 
 
 def power_of_two(n):
@@ -558,8 +570,7 @@
             for k in range(1, members):
                 held[r ^ (k * bit)] = across(held[r], axis, k * bit)
     order = list(held)
-    values = tie(*[held[r] for r in order], *beside)
-    held, beside = dict(zip(order, values)), values[len(order) :]
+    held[order[-1]], *beside = tie(held[order[-1]], *beside)
     held.update({r ^ 1: across(held[r], axis, 1) for r in order})
     return [held[r] for r in range(len(held))], beside
 
@@ -567,40 +578,34 @@
 def gather_cotangent(cotangent, beside):
     size = lax.axis_size("fsdp")
     count, _, width = cotangent.shape
-    if power_of_two(size) and size > 1 and width % 128 == 0 and count > 1:
-        lists = []
-        for m in range(count):
-            blocks, beside = gather_blocks(cotangent[m : m + 1], "fsdp", beside)
-            lists.append(blocks)
-        blocks = [list(pieces) for pieces in zip(*lists)]
-        return blocks, beside
+    if power_of_two(size) and size > 1 and width % 128 == 0:
+        blocks, beside = gather_blocks(cotangent, "fsdp", beside)
+        return [(blocks, m) for m in range(count)], beside
     whole = lax.all_gather(cotangent, "fsdp", axis=2, tiled=True)
-    return [[whole]], beside
+    return [([whole], m) for m in range(count)], beside
 
 
 def tie(*values):
     return lax.optimization_barrier(values)
 
 
-def sums(gram_part, full_grad, p, ranks):
+def sums(gram_parts, full_grad, p, ranks):
     size = lax.axis_size("fsdp")
     replicas = lax.axis_size("dp")
     count = len(p)
     if not (power_of_two(size) and size > 1):
-        inverse, factor_p = factor([lax.psum(gram_part, "fsdp")], p, ranks)
+        inverse = factor(lax.psum(jnp.stack(gram_parts), "fsdp"), ranks)
         pairs = [right(m, full_grad[m], p[m]) for m in range(count)]
         ordered = [jnp.stack(pair) for pair in pairs]
         odd = (lax.axis_index("fsdp") & 1) == 1
         whole = jnp.stack([jnp.where(odd, x[::-1], x).reshape(-1, x.shape[2]) for x in ordered])
-        return inverse, factor_p, [merge([list(lax.psum(whole, ("fsdp", "dp")))], [], "code")]
+        codes = [merge([list(lax.psum(whole, ("fsdp", "dp")))], [], "code")]
+        return inverse, factor_p_of(inverse, p), codes
     groups = groups_of("fsdp")
 
-    gram_part = gram_part + across(gram_part, "fsdp", 1)
-    for bit, members in groups[:-1]:
-        gram_part = tree([gram_part] + [across(gram_part, "fsdp", k * bit) for k in range(1, members)])
-    grams = [gram_part]
-    for bit, members in groups[-1:]:
-        grams += [across(gram_part, "fsdp", k * bit) for k in range(1, members)]
+    grams = jnp.stack(gram_parts)
+    for bit in bits_of("fsdp"):
+        grams = grams + across(grams, "fsdp", bit)
 
     pairs = [right(m, full_grad[m], p[m]) for m in range(count)]
     terms = [[mine for mine, _ in pairs], [across(other, "fsdp", 1) for _, other in pairs]]
@@ -611,15 +616,16 @@
         terms = [keep]
     code = merge(terms, codes, "code")
     if power_of_two(replicas) and replicas > 1:
-        *grams, code = tie(*grams, code)
         theirs = [across(code, "dp", k) for k in range(1, replicas)]
-        inverse, factor_p = factor(grams, p, ranks)
-        *theirs, inverse, factor_p = tie(*theirs, inverse, factor_p)
+        inverse = factor(grams, ranks)
+        *theirs, inverse = tie(*theirs, inverse)
         code = merge([], [code] + theirs, "code_sum")
     else:
-        inverse, factor_p = factor(grams, p, ranks)
+        inverse = factor(grams, ranks)
         code = merge([[lax.psum(plain(code), "dp")]], [], "code_sum")
-    return inverse, factor_p, gather_blocks(code, "fsdp")[0]
+    code, inverse = tie(code, inverse)
+    codes, made = gather_blocks(code, "fsdp", factor_p_of(inverse, p))
+    return inverse, made, codes
 
 
 def plain_kernel(code_ref, out_ref):
@@ -636,17 +642,18 @@
     )(code)
 
 
-def left_sums(blocks, q_init, inputs_t, held, fbq, ranks):
+def left_sums(blocks, q2, inputs_t, held, fbq):
     replicas = lax.axis_size("dp")
     count = fbq.shape[0]
     if not (power_of_two(replicas) and replicas > 1):
-        parts = [left(m, blocks, q_init, inputs_t, fbq, ranks) for m in range(count)]
+        parts = [left(m, *blocks[m], q2, inputs_t, fbq) for m in range(count)]
         p = lax.psum(jnp.stack([part for part, _ in parts]), "dp")
         full_grad = [full(m, held, inputs_t, parts[m][1]) for m in range(count)]
-        return [p[m] for m in range(count)], full_grad, gram(p)
+        grams = gram(p)
+        return [p[m] for m in range(count)], full_grad, [grams[m] for m in range(count)]
     whole, full_grad = [], []
     for m in range(count):
-        mine, other, cot = left_code(m, blocks, q_init, inputs_t, fbq, ranks)
+        mine, other, cot = left_code(m, *blocks[m], q2, inputs_t, fbq)
         mine = add_code(mine, across(other, "dp", 1))
         for step, bit in enumerate(bits_of("dp")[1:]):
             if step == 0:
@@ -659,15 +666,15 @@
         if len(full_grad) == m:
             full_grad.append(full(m, held, inputs_t, cot))
         whole.append(whole_left(mine, across(mine, "dp", 1)))
-    return [p for p, _ in whole], full_grad, jnp.stack([part for _, part in whole])
+    return [p for p, _ in whole], full_grad, [part for _, part in whole]
 
 
 def local(inputs, cotangent, feedback, q_init, factor_ranks):
     beside = feedback_q(feedback, q_init, inputs, factor_ranks)
-    blocks, (held, fbq, inputs_t) = gather_cotangent(cotangent, beside)
-    p, full_grad, gram_part = left_sums(blocks, q_init, inputs_t, held, fbq, factor_ranks)
-    inverse, factor_p, codes = sums(gram_part, full_grad, p, factor_ranks)
-    new_error, factor_q = error(full_grad, factor_p, inverse, codes)
+    blocks, (held, fbq, q2, inputs_t) = gather_cotangent(cotangent, beside)
+    p, full_grad, gram_parts = left_sums(blocks, q2, inputs_t, held, fbq)
+    inverse, (factor_p, p3), codes = sums(gram_parts, full_grad, p, factor_ranks)
+    new_error, factor_q = error(full_grad, p3, inverse, codes)
     return (factor_p, factor_q, new_error)
 
 

time: 95.8 us -> 86.3 us (0.901)
  starting transfers between devices: 36.9 us -> 31.2 us
  local copies, waits for them, and re-layouts: 5.32 us -> 0.01 us
  waiting for transfers between devices: 22.8 us -> 24 us
    ppermute x39 -> x31, starting transfers between devices: 36.9 us -> 31.2 us  [across(): return lax.ppermute(x, axis, [(i, i ^ bit) for i in range(size)])]
    unnamed x10 -> x4, local copies, waits for them, and re-layouts: 4.33 us -> 0.01 us
    ppermute x39 -> x31, waiting for transfers between devices: 22.8 us -> 24 us  [across(): return lax.ppermute(x, axis, [(i, i ^ bit) for i in range(size)])]
    slice x1 -> x0, local copies, waits for them, and re-layouts: 0.99 us -> none  [gather_cotangent(): blocks, beside = gather_blocks(cotangent[m:m + 1], 'fsdp', beside)]
    pallas_call x4 -> x5, Pallas kernels: 17.7 us -> 18 us  [the longest x1 7.55 us: feedback_q(): pl.pallas_call(feedback_q_kernel, in_specs=[far] * 4, out_specs=[VMEM] *...]
  transfers between devices with their start and end apart: 39 -> 31, of which waited for: 16 -> 19; matrix products, arithmetic and copies ran while one was open for 0% -> 0% of each run, Pallas kernels for 26% -> 27%
where the time goes in v4:
time: 86.3 us; the launch traced here: 86.1 us
  starting transfers between devices  31.2 us (36%)
  Pallas kernels  29.8 us (35%)
  waiting for transfers between devices  24 us (28%)
  between operations  1 us (1%)
    ppermute x31, starting transfers between devices, across(): return lax.ppermute(x, axis, [(i, i ^ bit) for i in range(size)])  31.2 us
    ppermute x31, waiting for transfers between devices, across(): return lax.ppermute(x, axis, [(i, i ^ bit) for i in range(size)])  24 us
    pallas_call x1, Pallas kernels, feedback_q(): pl.pallas_call(feedback_q_kernel, in_specs=[far] * 4, out_specs=[VMEM] *...  7.55 us
    pallas_call x1, Pallas kernels, factor(): pl.pallas_call(factor_kernel, in_specs=[SMEM, VMEM], out_specs=VMEM, out_...  5.61 us
    pallas_call x1, Pallas kernels, error(): pl.pallas_call(functools.partial(error_kernel, count, len(codes), groups)...  4.55 us
    pallas_call x2, Pallas kernels, left_code(): pl.pallas_call(functools.partial(left_code_kernel, m, at), in_specs=[VMEM...  3.44 us
    pallas_call x2, Pallas kernels, full(): pl.pallas_call(functools.partial(full_kernel, m), in_specs=[VMEM, VMEM, V...  2.66 us
    pallas_call x2, Pallas kernels, right(): pl.pallas_call(right_kernel, in_specs=[VMEM, VMEM], out_specs=[VMEM, VMEM...  2.41 us
  transfers between devices with their start and end apart: 31, of which 19 were waited for; matrix products, arithmetic and copies ran while one was open for 0% of the time, Pallas kernels for 27%

profile of v4, /device:TPU:0, one launch (start us, length us, event | category | flops | bytes accessed | tf_op | source)
XLA Modules:
  0.0 86.1 jit_solution(16559494266277727673)
XLA Ops:
  0.6 4.0 %collective-permute-start = (bf16[2,512,128]{2,1,0:T(8,128)(2,1)}, bf16[2,512,128]{2,1,0:T(8,128)(2,1)S(1)}, u32[]{:S(2)}, u32[]{:S(2)}) collective-permute-start(bf16[2,512,128]{2,1,0:T(8,128)(2,1)} %refs_0_.3), channel_id=1, source_target_pairs={{0,6},{1,7},{2,4},{3,5},{4,2},{5,3},{6,0},{7,1},{8,14},{9,15},{10,... | collective-permute-start | bytes 786440 | tf_op jit(solution)/shard_map/ppermute | solution.py:553
  4.6 0.5 collective-permute-start.4
  5.1 0.1 collective-permute-start.2
  5.2 7.6 %feedback_q.1 = (f32[2,1024,1024]{2,1,0:T(8,128)S(1)}, f32[2,1024,128]{2,1,0:T(8,128)S(1)}, bf16[2,1024,256]{2,1,0:T(8,128)(2,1)S(1)}, bf16[1024,512]{1,0:T(8,128)(2,1)S(1)}) custom-call(s32[2]{0:T(128)} %ranks_ref.3, f32[2,1,1024,1024]{3,2,1,0:T(8,128)} %fb_ref.1, f32[2,1024,128]{2,1,0:T(8,128)} %q_ref.1, bf16[512,1024]{1,0:T(8,128)(2,1)} %in_ref.1), custom_call_target="tpu_custom_call" | custom-call | tf_op jit(solution)/shard_map/feedback_q/pallas_call | solution.py:96
  12.8 3.9 %collective-permute-done.4.refs_4_ = bf16[2,512,128]{2,1,0:T(8,128)(2,1)S(1)} collective-permute-done((bf16[2,512,128]{2,1,0:T(8,128)(2,1)}, bf16[2,512,128]{2,1,0:T(8,128)(2,1)S(1)}, u32[]{:S(2)}, u32[]{:S(2)}) %collective-permute-start.4) | collective-permute-done | bytes 262176 | tf_op jit(solution)/shard_map/ppermute | solution.py:553
  16.8 0.3 collective-permute-done.2.refs_2_
  17.0 0.2 collective-permute-start.3
  17.2 0.3 collective-permute-start.6
  17.5 0.7 collective-permute-done.5.refs_5_
  18.3 0.4 collective-permute-done.3.refs_3_
  18.6 0.4 collective-permute-done.6.refs_7_
  19.0 1.7 %left_code_1.1 = (f32[512,128]{1,0:T(8,128)S(1)}, s16[528,128]{1,0:T(8,128)(2,1)S(1)}, bf16[512,1024]{1,0:T(8,128)(2,1)S(1)}) custom-call(bf16[2,1024,256]{2,1,0:T(8,128)(2,1)S(1)} %get-tuple-element.56.q2_ref, bf16[1024,512]{1,0:T(8,128)(2,1)S(1)} %get-tuple-element.57.in_ref, f32[2,1024,128]{2,1,0:T(8,128)S(1)} %get-tuple-element.58.fbq_ref, ...), custom_call_target="tpu_custom_call" | custom-call | tf_op jit(solution)/shard_map/left_code_1/pallas_call | solution.py:195
  20.8 1.8 %collective-permute-start.10 = (s16[528,128]{1,0:T(8,128)(2,1)S(1)}, s16[528,128]{1,0:T(8,128)(2,1)S(1)}, u32[]{:S(2)}, u32[]{:S(2)}) collective-permute-start(s16[528,128]{1,0:T(8,128)(2,1)S(1)} %get-tuple-element.71), channel_id=1, source_target_pairs={{0,8},{8,0},{16,24},{24,16},{1,9},{9,1},{17,25},{25,17},{2,10},{10... | collective-permute-start | bytes 405512 | tf_op jit(solution)/shard_map/ppermute | solution.py:553
  22.6 1.7 %left_code_0.1 = (f32[512,128]{1,0:T(8,128)S(1)}, s16[528,128]{1,0:T(8,128)(2,1)S(1)}, bf16[512,1024]{1,0:T(8,128)(2,1)S(1)}) custom-call(bf16[2,1024,256]{2,1,0:T(8,128)(2,1)S(1)} %get-tuple-element.56.q2_ref, bf16[1024,512]{1,0:T(8,128)(2,1)S(1)} %get-tuple-element.57.in_ref, f32[2,1024,128]{2,1,0:T(8,128)S(1)} %get-tuple-element.58.fbq_ref, ...), custom_call_target="tpu_custom_call" | custom-call | tf_op jit(solution)/shard_map/left_code_0/pallas_call | solution.py:195
  24.3 0.3 collective-permute-start.7
  24.6 1.9 %collective-permute-done.10.theirs_ref = s16[528,128]{1,0:T(8,128)(2,1)S(1)} collective-permute-done((s16[528,128]{1,0:T(8,128)(2,1)S(1)}, s16[528,128]{1,0:T(8,128)(2,1)S(1)}, u32[]{:S(2)}, u32[]{:S(2)}) %collective-permute-start.10) | collective-permute-done | bytes 135200 | tf_op jit(solution)/shard_map/ppermute | solution.py:553
  26.5 0.1 add_code.6.mine_ref
  26.7 2.8 %collective-permute-start.11 = (s16[528,128]{1,0:T(8,128)(2,1)S(1)}, s16[528,128]{1,0:T(8,128)(2,1)S(1)}, u32[]{:S(2)}, u32[]{:S(2)}) collective-permute-start(s16[528,128]{1,0:T(8,128)(2,1)S(1)} %add_code.6.mine_ref), channel_id=1, source_target_pairs={{0,16},{8,24},{16,0},{24,8},{1,17},{9,25},{17,1},{25,9},{2,18},{10... | collective-permute-start | bytes 405512 | tf_op jit(solution)/shard_map/ppermute | solution.py:553
  29.4 1.4 %collective-permute-done.7.theirs_ref = s16[528,128]{1,0:T(8,128)(2,1)S(1)} collective-permute-done((s16[528,128]{1,0:T(8,128)(2,1)S(1)}, s16[528,128]{1,0:T(8,128)(2,1)S(1)}, u32[]{:S(2)}, u32[]{:S(2)}) %collective-permute-start.7) | collective-permute-done | bytes 135200 | tf_op jit(solution)/shard_map/ppermute | solution.py:553
  30.9 0.1 add_code.4.mine_ref
  31.0 2.7 %collective-permute-start.8 = (s16[528,128]{1,0:T(8,128)(2,1)S(1)}, s16[528,128]{1,0:T(8,128)(2,1)S(1)}, u32[]{:S(2)}, u32[]{:S(2)}) collective-permute-start(s16[528,128]{1,0:T(8,128)(2,1)S(1)} %add_code.4.mine_ref), channel_id=1, source_target_pairs={{0,16},{8,24},{16,0},{24,8},{1,17},{9,25},{17,1},{25,9},{2,18},{10... | collective-permute-start | bytes 405512 | tf_op jit(solution)/shard_map/ppermute | solution.py:553
  33.7 1.3 %full_0.1.full_ref.refs_8_ = f32[1024,1024]{1,0:T(8,128)S(1)} custom-call(f32[2,1024,1024]{2,1,0:T(8,128)S(1)} %get-tuple-element.64.held_ref, bf16[1024,512]{1,0:T(8,128)(2,1)S(1)} %get-tuple-element.57.in_ref, bf16[512,1024]{1,0:T(8,128)(2,1)S(1)} %get-tuple-element.65.whole_ref), custom_call_target="tpu_custom_call" | custom-call | tf_op jit(solution)/shard_map/full_0/pallas_call | solution.py:259
  35.0 1.3 %full_1.1.full_ref.refs_9_ = f32[1024,1024]{1,0:T(8,128)S(1)} custom-call(f32[2,1024,1024]{2,1,0:T(8,128)S(1)} %get-tuple-element.64.held_ref, bf16[1024,512]{1,0:T(8,128)(2,1)S(1)} %get-tuple-element.57.in_ref, bf16[512,1024]{1,0:T(8,128)(2,1)S(1)} %get-tuple-element.74.whole_ref), custom_call_target="tpu_custom_call" | custom-call | tf_op jit(solution)/shard_map/full_1/pallas_call | solution.py:259
  36.4 3.0 %collective-permute-done.11.theirs_ref = s16[528,128]{1,0:T(8,128)(2,1)S(1)} collective-permute-done((s16[528,128]{1,0:T(8,128)(2,1)S(1)}, s16[528,128]{1,0:T(8,128)(2,1)S(1)}, u32[]{:S(2)}, u32[]{:S(2)}) %collective-permute-start.11) | collective-permute-done | bytes 135200 | tf_op jit(solution)/shard_map/ppermute | solution.py:553
  39.3 0.2 add_code.7.mine_ref
  39.5 1.7 %collective-permute-done.8.theirs_ref = s16[528,128]{1,0:T(8,128)(2,1)S(1)} collective-permute-done((s16[528,128]{1,0:T(8,128)(2,1)S(1)}, s16[528,128]{1,0:T(8,128)(2,1)S(1)}, u32[]{:S(2)}, u32[]{:S(2)}) %collective-permute-start.8) | collective-permute-done | bytes 135200 | tf_op jit(solution)/shard_map/ppermute | solution.py:553
  41.2 0.7 collective-permute-start.12
  41.9 0.2 add_code.5.mine_ref
  42.1 1.4 %collective-permute-start.9 = (s16[528,128]{1,0:T(8,128)(2,1)S(1)}, s16[528,128]{1,0:T(8,128)(2,1)S(1)}, u32[]{:S(2)}, u32[]{:S(2)}) collective-permute-start(s16[528,128]{1,0:T(8,128)(2,1)S(1)} %add_code.5.mine_ref), channel_id=1, source_target_pairs={{0,8},{8,0},{16,24},{24,16},{1,9},{9,1},{17,25},{25,17},{2,10},{10... | collective-permute-start | bytes 405512 | tf_op jit(solution)/shard_map/ppermute | solution.py:553
  43.5 3.8 %collective-permute-done.12.theirs_ref = s16[528,128]{1,0:T(8,128)(2,1)S(1)} collective-permute-done((s16[528,128]{1,0:T(8,128)(2,1)S(1)}, s16[528,128]{1,0:T(8,128)(2,1)S(1)}, u32[]{:S(2)}, u32[]{:S(2)}) %collective-permute-start.12) | collective-permute-done | bytes 135200 | tf_op jit(solution)/shard_map/ppermute | solution.py:553
  47.3 0.5 whole_left.3
  47.8 1.0 %collective-permute-done.9.theirs_ref = s16[528,128]{1,0:T(8,128)(2,1)S(1)} collective-permute-done((s16[528,128]{1,0:T(8,128)(2,1)S(1)}, s16[528,128]{1,0:T(8,128)(2,1)S(1)}, u32[]{:S(2)}, u32[]{:S(2)}) %collective-permute-start.9) | collective-permute-done | bytes 135200 | tf_op jit(solution)/shard_map/ppermute | solution.py:553
  48.7 0.5 whole_left.2
  49.2 0.1 collective-permute-start.21
  49.3 1.1 %right_0.1 = (f32[512,128]{1,0:T(8,128)S(1)}, f32[512,128]{1,0:T(8,128)S(1)}) custom-call(f32[1024,1024]{1,0:T(8,128)S(1)} %full_0.1.full_ref.refs_8_, f32[1024,128]{1,0:T(8,128)S(1)} %get-tuple-element.68.p_ref.refs_0_), custom_call_target="tpu_custom_call" | custom-call | tf_op jit(solution)/shard_map/right_0/pallas_call | solution.py:292
  50.4 0.6 collective-permute-start.13
  51.0 1.3 %right_1.1 = (f32[512,128]{1,0:T(8,128)S(1)}, f32[512,128]{1,0:T(8,128)S(1)}) custom-call(f32[1024,1024]{1,0:T(8,128)S(1)} %full_1.1.full_ref.refs_9_, f32[1024,128]{1,0:T(8,128)S(1)} %get-tuple-element.77.p_ref.refs_1_), custom_call_target="tpu_custom_call" | custom-call | tf_op jit(solution)/shard_map/right_1/pallas_call | solution.py:292
  52.3 0.1 collective-permute-start.14
  52.4 1.5 %collective-permute-start.22 = (f32[2,128,128]{2,1,0:T(8,128)S(1)}, f32[2,128,128]{2,1,0:T(8,128)S(1)}, u32[]{:S(2)}, u32[]{:S(2)}) collective-permute-start(f32[2,128,128]{2,1,0:T(8,128)S(1)} %fusion), channel_id=1, source_target_pairs={{0,2},{1,3},{2,0},{3,1},{4,6},{5,7},{6,4},{7,5},{8,10},{9,11},{10,... | collective-permute-start | bytes 393224 | tf_op jit(solution)/shard_map/ppermute | solution.py:553
  54.0 0.3 part_2.1
  54.2 1.5 %collective-permute-start.15 = (s16[272,128]{1,0:T(8,128)(2,1)S(1)}, s16[272,128]{1,0:T(8,128)(2,1)S(1)}, u32[]{:S(2)}, u32[]{:S(2)}) collective-permute-start(s16[272,128]{1,0:T(8,128)(2,1)S(1)} %get-tuple-element.83), channel_id=1, source_target_pairs={{0,2},{1,3},{2,0},{3,1},{4,6},{5,7},{6,4},{7,5},{8,10},{9,11},{10,... | collective-permute-start | bytes 208904 | tf_op jit(solution)/shard_map/ppermute | solution.py:553
  55.7 0.8 collective-permute-start.16
  56.5 1.2 %collective-permute-start.17 = (s16[272,128]{1,0:T(8,128)(2,1)S(1)}, s16[272,128]{1,0:T(8,128)(2,1)S(1)}, u32[]{:S(2)}, u32[]{:S(2)}) collective-permute-start(s16[272,128]{1,0:T(8,128)(2,1)S(1)} %get-tuple-element.85), channel_id=1, source_target_pairs={{0,6},{1,7},{2,4},{3,5},{4,2},{5,3},{6,0},{7,1},{8,14},{9,15},{10,... | collective-permute-start | bytes 208904 | tf_op jit(solution)/shard_map/ppermute | solution.py:553
  57.8 1.0 %collective-permute-done.22 = f32[2,128,128]{2,1,0:T(8,128)S(1)} collective-permute-done((f32[2,128,128]{2,1,0:T(8,128)S(1)}, f32[2,128,128]{2,1,0:T(8,128)S(1)}, u32[]{:S(2)}, u32[]{:S(2)}) %collective-permute-start.22) | collective-permute-done | bytes 131104 | tf_op jit(solution)/shard_map/ppermute | solution.py:553
  58.8 1.6 %collective-permute-start.23 = (f32[2,128,128]{2,1,0:T(8,128)S(1)}, f32[2,128,128]{2,1,0:T(8,128)S(1)}, u32[]{:S(2)}, u32[]{:S(2)}) collective-permute-start(f32[2,128,128]{2,1,0:T(8,128)S(1)} %fusion.1), channel_id=1, source_target_pairs={{0,4},{1,5},{2,6},{3,7},{4,0},{5,1},{6,2},{7,3},{8,12},{9,13},{10,... | collective-permute-start | bytes 393224 | tf_op jit(solution)/shard_map/ppermute | solution.py:553
  60.4 2.0 %collective-permute-done.17.refs_4_ = s16[272,128]{1,0:T(8,128)(2,1)S(1)} collective-permute-done((s16[272,128]{1,0:T(8,128)(2,1)S(1)}, s16[272,128]{1,0:T(8,128)(2,1)S(1)}, u32[]{:S(2)}, u32[]{:S(2)}) %collective-permute-start.17) | collective-permute-done | bytes 69664 | tf_op jit(solution)/shard_map/ppermute | solution.py:553
  62.4 0.1 code.1.refs_0_
  62.5 4.4 %collective-permute-start.20 = (s16[272,128]{1,0:T(8,128)(2,1)S(1)}, s16[272,128]{1,0:T(8,128)(2,1)S(1)}, u32[]{:S(2)}, u32[]{:S(2)}) collective-permute-start(s16[272,128]{1,0:T(8,128)(2,1)S(1)} %code.1.refs_0_), channel_id=1, source_target_pairs={{0,24},{8,16},{16,8},{24,0},{1,25},{9,17},{17,9},{25,1},{2,26},{10... | collective-permute-start | bytes 208904 | tf_op jit(solution)/shard_map/ppermute | solution.py:553
  66.9 0.6 collective-permute-start.18
  67.6 5.6 %factor.1.inv_ref = f32[2,128,128]{2,1,0:T(8,128)S(1)} custom-call(s32[2]{0:T(128)S(1)} %copy-done.1, f32[2,128,128]{2,1,0:T(8,128)S(1)} %add.11.gram_ref), custom_call_target="tpu_custom_call" | custom-call | tf_op jit(solution)/shard_map/factor/pallas_call | solution.py:440
  73.2 0.2 code_sum.1.refs_0_
  73.4 1.5 %collective-permute-start.24 = (s16[272,128]{1,0:T(8,128)(2,1)S(1)}, s16[272,128]{1,0:T(8,128)(2,1)S(1)}, u32[]{:S(2)}, u32[]{:S(2)}) collective-permute-start(s16[272,128]{1,0:T(8,128)(2,1)S(1)} %code_sum.1.refs_0_), channel_id=1, source_target_pairs={{0,6},{1,7},{2,4},{3,5},{4,2},{5,3},{6,0},{7,1},{8,14},{9,15},{10,... | collective-permute-start | bytes 208904 | tf_op jit(solution)/shard_map/ppermute | solution.py:553
  74.9 0.8 collective-permute-start.28
  75.7 1.3 %collective-permute-start.26 = (s16[272,128]{1,0:T(8,128)(2,1)S(1)}, s16[272,128]{1,0:T(8,128)(2,1)S(1)}, u32[]{:S(2)}, u32[]{:S(2)}) collective-permute-start(s16[272,128]{1,0:T(8,128)(2,1)S(1)} %code_sum.1.refs_0_), channel_id=1, source_target_pairs={{0,2},{1,3},{2,0},{3,1},{4,6},{5,7},{6,4},{7,5},{8,10},{9,11},{10,... | collective-permute-start | bytes 208904 | tf_op jit(solution)/shard_map/ppermute | solution.py:553
  76.9 1.4 %factor_p.1 = (f32[2,1024,128]{2,1,0:T(8,128)}, bf16[2,1024,384]{2,1,0:T(8,128)(2,1)S(1)}) custom-call(f32[2,128,128]{2,1,0:T(8,128)S(1)} %factor.1.inv_ref, f32[1024,128]{1,0:T(8,128)S(1)} %get-tuple-element.68.p_ref.refs_0_, f32[1024,128]{1,0:T(8,128)S(1)} %get-tuple-element.77.p_ref.refs_1_), custom_call_target="tpu_custom_call" | custom-call | tf_op jit(solution)/shard_map/factor_p/pallas_call | solution.py:470
  78.4 0.6 collective-permute-done.24.refs_6_
  79.0 0.6 collective-permute-done.28.refs_4_
  79.6 0.4 collective-permute-done.26.refs_2_
  80.0 0.2 collective-permute-start.27
  80.1 0.4 collective-permute-start.30
  80.5 0.4 collective-permute-done.29.refs_5_
  80.9 0.4 collective-permute-done.27.refs_3_
  81.2 0.2 collective-permute-done.30.refs_7_
  81.4 4.5 %error.1 = (f32[2,1,1024,1024]{3,2,1,0:T(8,128)}, f32[2,1024,128]{2,1,0:T(8,128)}) custom-call(bf16[2,1024,384]{2,1,0:T(8,128)(2,1)S(1)} %get-tuple-element.97.p3_ref, f32[2,128,128]{2,1,0:T(8,128)S(1)} %factor.1.inv_ref, s16[272,128]{1,0:T(8,128)(2,1)S(1)} %code_sum.1.refs_0_, s16[272,128]{1,0:T(8,128)(2,1)S(1)} %collective-permute-done.25.refs_1_, ...), custom_call_target="tpu_custom_call" | custom-call | tf_op jit(solution)/shard_map/error/pallas_call | solution.py:528
  (25 shorter events, 0.1 us)
Async XLA Ops:
  0.6 18.4 %copy-start = (bf16[2,512,128]{2,1,0:T(8,128)(2,1)S(1)}, bf16[2,512,128]{2,1,0:T(8,128)(2,1)}, u32[]{:S(2)}) copy-start(bf16[2,512,128]{2,1,0:T(8,128)(2,1)} %refs_0_.3) | copy-start | bytes 786436
  0.6 12.2 %collective-permute-start = (bf16[2,512,128]{2,1,0:T(8,128)(2,1)}, bf16[2,512,128]{2,1,0:T(8,128)(2,1)S(1)}, u32[]{:S(2)}, u32[]{:S(2)}) collective-permute-start(bf16[2,512,128]{2,1,0:T(8,128)(2,1)} %refs_0_.3), channel_id=1, source_target_pairs={{0,6},{1,7},{2,4},{3,5},{4,2},{5,3},{6,0},{7,1},{8,14},{9,15},{10,... | collective-permute-start | bytes 786440 | tf_op jit(solution)/shard_map/ppermute | solution.py:553
  4.6 12.1 %collective-permute-start.4 = (bf16[2,512,128]{2,1,0:T(8,128)(2,1)}, bf16[2,512,128]{2,1,0:T(8,128)(2,1)S(1)}, u32[]{:S(2)}, u32[]{:S(2)}) collective-permute-start(bf16[2,512,128]{2,1,0:T(8,128)(2,1)} %refs_0_.3), channel_id=1, source_target_pairs={{0,4},{1,5},{2,6},{3,7},{4,0},{5,1},{6,2},{7,3},{8,12},{9,13},{10,... | collective-permute-start | bytes 786440 | tf_op jit(solution)/shard_map/ppermute | solution.py:553
  5.1 11.9 %collective-permute-start.2 = (bf16[2,512,128]{2,1,0:T(8,128)(2,1)}, bf16[2,512,128]{2,1,0:T(8,128)(2,1)S(1)}, u32[]{:S(2)}, u32[]{:S(2)}) collective-permute-start(bf16[2,512,128]{2,1,0:T(8,128)(2,1)} %refs_0_.3), channel_id=1, source_target_pairs={{0,2},{1,3},{2,0},{3,1},{4,6},{5,7},{6,4},{7,5},{8,10},{9,11},{10,... | collective-permute-start | bytes 786440 | tf_op jit(solution)/shard_map/ppermute | solution.py:553
  5.2 12.3 %collective-permute-start.1 = (bf16[2,512,128]{2,1,0:T(8,128)(2,1)}, bf16[2,512,128]{2,1,0:T(8,128)(2,1)S(1)}, u32[]{:S(2)}, u32[]{:S(2)}) collective-permute-start(bf16[2,512,128]{2,1,0:T(8,128)(2,1)} %refs_0_.3), channel_id=1, source_target_pairs={{0,1},{1,0},{2,3},{3,2},{4,5},{5,4},{6,7},{7,6},{8,9},{9,8},{10,11... | collective-permute-start | bytes 786440 | tf_op jit(solution)/shard_map/ppermute | solution.py:553
  16.7 1.5 %collective-permute-start.5 = (bf16[2,512,128]{2,1,0:T(8,128)(2,1)S(1)}, bf16[2,512,128]{2,1,0:T(8,128)(2,1)S(1)}, u32[]{:S(2)}, u32[]{:S(2)}) collective-permute-start(bf16[2,512,128]{2,1,0:T(8,128)(2,1)S(1)} %collective-permute-done.4.refs_4_), channel_id=1, source_target_pairs={{0,1},{1,0},{2,3},{3,2},{4,5},{5,4},{6,7},{7,6},{8,9},{9,8},{10,11... | collective-permute-start | bytes 786440 | tf_op jit(solution)/shard_map/ppermute | solution.py:553
  17.0 1.6 %collective-permute-start.3 = (bf16[2,512,128]{2,1,0:T(8,128)(2,1)S(1)}, bf16[2,512,128]{2,1,0:T(8,128)(2,1)S(1)}, u32[]{:S(2)}, u32[]{:S(2)}) collective-permute-start(bf16[2,512,128]{2,1,0:T(8,128)(2,1)S(1)} %collective-permute-done.2.refs_2_), channel_id=1, source_target_pairs={{0,1},{1,0},{2,3},{3,2},{4,5},{5,4},{6,7},{7,6},{8,9},{9,8},{10,11... | collective-permute-start | bytes 786440 | tf_op jit(solution)/shard_map/ppermute | solution.py:553
  17.2 1.8 %collective-permute-start.6 = (bf16[2,512,128]{2,1,0:T(8,128)(2,1)S(1)}, bf16[2,512,128]{2,1,0:T(8,128)(2,1)S(1)}, u32[]{:S(2)}, u32[]{:S(2)}) collective-permute-start(bf16[2,512,128]{2,1,0:T(8,128)(2,1)S(1)} %collective-permute-done.refs_6_), channel_id=1, source_target_pairs={{0,1},{1,0},{2,3},{3,2},{4,5},{5,4},{6,7},{7,6},{8,9},{9,8},{10,11... | collective-permute-start | bytes 786440 | tf_op jit(solution)/shard_map/ppermute | solution.py:553
  20.8 5.8 %collective-permute-start.10 = (s16[528,128]{1,0:T(8,128)(2,1)S(1)}, s16[528,128]{1,0:T(8,128)(2,1)S(1)}, u32[]{:S(2)}, u32[]{:S(2)}) collective-permute-start(s16[528,128]{1,0:T(8,128)(2,1)S(1)} %get-tuple-element.71), channel_id=1, source_target_pairs={{0,8},{8,0},{16,24},{24,16},{1,9},{9,1},{17,25},{25,17},{2,10},{10... | collective-permute-start | bytes 405512 | tf_op jit(solution)/shard_map/ppermute | solution.py:553
  24.3 6.5 %collective-permute-start.7 = (s16[528,128]{1,0:T(8,128)(2,1)S(1)}, s16[528,128]{1,0:T(8,128)(2,1)S(1)}, u32[]{:S(2)}, u32[]{:S(2)}) collective-permute-start(s16[528,128]{1,0:T(8,128)(2,1)S(1)} %get-tuple-element.61), channel_id=1, source_target_pairs={{0,8},{8,0},{16,24},{24,16},{1,9},{9,1},{17,25},{25,17},{2,10},{10... | collective-permute-start | bytes 405512 | tf_op jit(solution)/shard_map/ppermute | solution.py:553
  26.7 12.6 %collective-permute-start.11 = (s16[528,128]{1,0:T(8,128)(2,1)S(1)}, s16[528,128]{1,0:T(8,128)(2,1)S(1)}, u32[]{:S(2)}, u32[]{:S(2)}) collective-permute-start(s16[528,128]{1,0:T(8,128)(2,1)S(1)} %add_code.6.mine_ref), channel_id=1, source_target_pairs={{0,16},{8,24},{16,0},{24,8},{1,17},{9,25},{17,1},{25,9},{2,18},{10... | collective-permute-start | bytes 405512 | tf_op jit(solution)/shard_map/ppermute | solution.py:553
  31.0 10.2 %collective-permute-start.8 = (s16[528,128]{1,0:T(8,128)(2,1)S(1)}, s16[528,128]{1,0:T(8,128)(2,1)S(1)}, u32[]{:S(2)}, u32[]{:S(2)}) collective-permute-start(s16[528,128]{1,0:T(8,128)(2,1)S(1)} %add_code.4.mine_ref), channel_id=1, source_target_pairs={{0,16},{8,24},{16,0},{24,8},{1,17},{9,25},{17,1},{25,9},{2,18},{10... | collective-permute-start | bytes 405512 | tf_op jit(solution)/shard_map/ppermute | solution.py:553
  36.3 31.2 %copy-start.1 = (s32[2]{0:T(128)S(1)}, s32[2]{0:T(128)}, u32[]{:S(2)}) copy-start(s32[2]{0:T(128)} %ranks_ref.3) | copy-start | bytes 28
  41.2 6.1 %collective-permute-start.12 = (s16[528,128]{1,0:T(8,128)(2,1)S(1)}, s16[528,128]{1,0:T(8,128)(2,1)S(1)}, u32[]{:S(2)}, u32[]{:S(2)}) collective-permute-start(s16[528,128]{1,0:T(8,128)(2,1)S(1)} %add_code.7.mine_ref), channel_id=1, source_target_pairs={{0,8},{8,0},{16,24},{24,16},{1,9},{9,1},{17,25},{25,17},{2,10},{10... | collective-permute-start | bytes 405512 | tf_op jit(solution)/shard_map/ppermute | solution.py:553
  42.1 6.7 %collective-permute-start.9 = (s16[528,128]{1,0:T(8,128)(2,1)S(1)}, s16[528,128]{1,0:T(8,128)(2,1)S(1)}, u32[]{:S(2)}, u32[]{:S(2)}) collective-permute-start(s16[528,128]{1,0:T(8,128)(2,1)S(1)} %add_code.5.mine_ref), channel_id=1, source_target_pairs={{0,8},{8,0},{16,24},{24,16},{1,9},{9,1},{17,25},{25,17},{2,10},{10... | collective-permute-start | bytes 405512 | tf_op jit(solution)/shard_map/ppermute | solution.py:553
  49.2 3.1 %collective-permute-start.21 = (f32[2,128,128]{2,1,0:T(8,128)S(1)}, f32[2,128,128]{2,1,0:T(8,128)S(1)}, u32[]{:S(2)}, u32[]{:S(2)}) collective-permute-start(f32[2,128,128]{2,1,0:T(8,128)S(1)} %pad_maximum_fusion), channel_id=1, source_target_pairs={{0,1},{1,0},{2,3},{3,2},{4,5},{5,4},{6,7},{7,6},{8,9},{9,8},{10,11... | collective-permute-start | bytes 393224 | tf_op jit(solution)/shard_map/ppermute | solution.py:553
  50.4 3.5 %collective-permute-start.13 = (f32[512,128]{1,0:T(8,128)S(1)}, f32[512,128]{1,0:T(8,128)S(1)}, u32[]{:S(2)}, u32[]{:S(2)}) collective-permute-start(f32[512,128]{1,0:T(8,128)S(1)} %get-tuple-element.79), channel_id=1, source_target_pairs={{0,1},{1,0},{2,3},{3,2},{4,5},{5,4},{6,7},{7,6},{8,9},{9,8},{10,11... | collective-permute-start | bytes 786440 | tf_op jit(solution)/shard_map/ppermute | solution.py:553
  52.3 1.7 %collective-permute-start.14 = (f32[512,128]{1,0:T(8,128)S(1)}, f32[512,128]{1,0:T(8,128)S(1)}, u32[]{:S(2)}, u32[]{:S(2)}) collective-permute-start(f32[512,128]{1,0:T(8,128)S(1)} %get-tuple-element.80), channel_id=1, source_target_pairs={{0,1},{1,0},{2,3},{3,2},{4,5},{5,4},{6,7},{7,6},{8,9},{9,8},{10,11... | collective-permute-start | bytes 786440 | tf_op jit(solution)/shard_map/ppermute | solution.py:553
  52.4 6.4 %collective-permute-start.22 = (f32[2,128,128]{2,1,0:T(8,128)S(1)}, f32[2,128,128]{2,1,0:T(8,128)S(1)}, u32[]{:S(2)}, u32[]{:S(2)}) collective-permute-start(f32[2,128,128]{2,1,0:T(8,128)S(1)} %fusion), channel_id=1, source_target_pairs={{0,2},{1,3},{2,0},{3,1},{4,6},{5,7},{6,4},{7,5},{8,10},{9,11},{10,... | collective-permute-start | bytes 393224 | tf_op jit(solution)/shard_map/ppermute | solution.py:553
  54.2 6.2 %collective-permute-start.15 = (s16[272,128]{1,0:T(8,128)(2,1)S(1)}, s16[272,128]{1,0:T(8,128)(2,1)S(1)}, u32[]{:S(2)}, u32[]{:S(2)}) collective-permute-start(s16[272,128]{1,0:T(8,128)(2,1)S(1)} %get-tuple-element.83), channel_id=1, source_target_pairs={{0,2},{1,3},{2,0},{3,1},{4,6},{5,7},{6,4},{7,5},{8,10},{9,11},{10,... | collective-permute-start | bytes 208904 | tf_op jit(solution)/shard_map/ppermute | solution.py:553
  55.7 4.7 %collective-permute-start.16 = (s16[272,128]{1,0:T(8,128)(2,1)S(1)}, s16[272,128]{1,0:T(8,128)(2,1)S(1)}, u32[]{:S(2)}, u32[]{:S(2)}) collective-permute-start(s16[272,128]{1,0:T(8,128)(2,1)S(1)} %get-tuple-element.84), channel_id=1, source_target_pairs={{0,4},{1,5},{2,6},{3,7},{4,0},{5,1},{6,2},{7,3},{8,12},{9,13},{10,... | collective-permute-start | bytes 208904 | tf_op jit(solution)/shard_map/ppermute | solution.py:553
  56.5 5.9 %collective-permute-start.17 = (s16[272,128]{1,0:T(8,128)(2,1)S(1)}, s16[272,128]{1,0:T(8,128)(2,1)S(1)}, u32[]{:S(2)}, u32[]{:S(2)}) collective-permute-start(s16[272,128]{1,0:T(8,128)(2,1)S(1)} %get-tuple-element.85), channel_id=1, source_target_pairs={{0,6},{1,7},{2,4},{3,5},{4,2},{5,3},{6,0},{7,1},{8,14},{9,15},{10,... | collective-permute-start | bytes 208904 | tf_op jit(solution)/shard_map/ppermute | solution.py:553
  58.8 8.7 %collective-permute-start.23 = (f32[2,128,128]{2,1,0:T(8,128)S(1)}, f32[2,128,128]{2,1,0:T(8,128)S(1)}, u32[]{:S(2)}, u32[]{:S(2)}) collective-permute-start(f32[2,128,128]{2,1,0:T(8,128)S(1)} %fusion.1), channel_id=1, source_target_pairs={{0,4},{1,5},{2,6},{3,7},{4,0},{5,1},{6,2},{7,3},{8,12},{9,13},{10,... | collective-permute-start | bytes 393224 | tf_op jit(solution)/shard_map/ppermute | solution.py:553
  62.5 10.6 %collective-permute-start.20 = (s16[272,128]{1,0:T(8,128)(2,1)S(1)}, s16[272,128]{1,0:T(8,128)(2,1)S(1)}, u32[]{:S(2)}, u32[]{:S(2)}) collective-permute-start(s16[272,128]{1,0:T(8,128)(2,1)S(1)} %code.1.refs_0_), channel_id=1, source_target_pairs={{0,24},{8,16},{16,8},{24,0},{1,25},{9,17},{17,9},{25,1},{2,26},{10... | collective-permute-start | bytes 208904 | tf_op jit(solution)/shard_map/ppermute | solution.py:553
  66.9 6.3 %collective-permute-start.19 = (s16[272,128]{1,0:T(8,128)(2,1)S(1)}, s16[272,128]{1,0:T(8,128)(2,1)S(1)}, u32[]{:S(2)}, u32[]{:S(2)}) collective-permute-start(s16[272,128]{1,0:T(8,128)(2,1)S(1)} %code.1.refs_0_), channel_id=1, source_target_pairs={{0,16},{8,24},{16,0},{24,8},{1,17},{9,25},{17,1},{25,9},{2,18},{10... | collective-permute-start | bytes 208904 | tf_op jit(solution)/shard_map/ppermute | solution.py:553
  66.9 6.3 %collective-permute-start.18 = (s16[272,128]{1,0:T(8,128)(2,1)S(1)}, s16[272,128]{1,0:T(8,128)(2,1)S(1)}, u32[]{:S(2)}, u32[]{:S(2)}) collective-permute-start(s16[272,128]{1,0:T(8,128)(2,1)S(1)} %code.1.refs_0_), channel_id=1, source_target_pairs={{0,8},{8,0},{16,24},{24,16},{1,9},{9,1},{17,25},{25,17},{2,10},{10... | collective-permute-start | bytes 208904 | tf_op jit(solution)/shard_map/ppermute | solution.py:553
  73.4 5.6 %collective-permute-start.24 = (s16[272,128]{1,0:T(8,128)(2,1)S(1)}, s16[272,128]{1,0:T(8,128)(2,1)S(1)}, u32[]{:S(2)}, u32[]{:S(2)}) collective-permute-start(s16[272,128]{1,0:T(8,128)(2,1)S(1)} %code_sum.1.refs_0_), channel_id=1, source_target_pairs={{0,6},{1,7},{2,4},{3,5},{4,2},{5,3},{6,0},{7,1},{8,14},{9,15},{10,... | collective-permute-start | bytes 208904 | tf_op jit(solution)/shard_map/ppermute | solution.py:553
  74.9 4.8 %collective-permute-start.28 = (s16[272,128]{1,0:T(8,128)(2,1)S(1)}, s16[272,128]{1,0:T(8,128)(2,1)S(1)}, u32[]{:S(2)}, u32[]{:S(2)}) collective-permute-start(s16[272,128]{1,0:T(8,128)(2,1)S(1)} %code_sum.1.refs_0_), channel_id=1, source_target_pairs={{0,4},{1,5},{2,6},{3,7},{4,0},{5,1},{6,2},{7,3},{8,12},{9,13},{10,... | collective-permute-start | bytes 208904 | tf_op jit(solution)/shard_map/ppermute | solution.py:553
  75.7 4.3 %collective-permute-start.26 = (s16[272,128]{1,0:T(8,128)(2,1)S(1)}, s16[272,128]{1,0:T(8,128)(2,1)S(1)}, u32[]{:S(2)}, u32[]{:S(2)}) collective-permute-start(s16[272,128]{1,0:T(8,128)(2,1)S(1)} %code_sum.1.refs_0_), channel_id=1, source_target_pairs={{0,2},{1,3},{2,0},{3,1},{4,6},{5,7},{6,4},{7,5},{8,10},{9,11},{10,... | collective-permute-start | bytes 208904 | tf_op jit(solution)/shard_map/ppermute | solution.py:553
  76.9 3.6 %collective-permute-start.25 = (s16[272,128]{1,0:T(8,128)(2,1)S(1)}, s16[272,128]{1,0:T(8,128)(2,1)S(1)}, u32[]{:S(2)}, u32[]{:S(2)}) collective-permute-start(s16[272,128]{1,0:T(8,128)(2,1)S(1)} %code_sum.1.refs_0_), channel_id=1, source_target_pairs={{0,1},{1,0},{2,3},{3,2},{4,5},{5,4},{6,7},{7,6},{8,9},{9,8},{10,11... | collective-permute-start | bytes 208904 | tf_op jit(solution)/shard_map/ppermute | solution.py:553
  79.6 1.3 %collective-permute-start.29 = (s16[272,128]{1,0:T(8,128)(2,1)S(1)}, s16[272,128]{1,0:T(8,128)(2,1)S(1)}, u32[]{:S(2)}, u32[]{:S(2)}) collective-permute-start(s16[272,128]{1,0:T(8,128)(2,1)S(1)} %collective-permute-done.28.refs_4_), channel_id=1, source_target_pairs={{0,1},{1,0},{2,3},{3,2},{4,5},{5,4},{6,7},{7,6},{8,9},{9,8},{10,11... | collective-permute-start | bytes 208904 | tf_op jit(solution)/shard_map/ppermute | solution.py:553
  80.0 1.3 %collective-permute-start.27 = (s16[272,128]{1,0:T(8,128)(2,1)S(1)}, s16[272,128]{1,0:T(8,128)(2,1)S(1)}, u32[]{:S(2)}, u32[]{:S(2)}) collective-permute-start(s16[272,128]{1,0:T(8,128)(2,1)S(1)} %collective-permute-done.26.refs_2_), channel_id=1, source_target_pairs={{0,1},{1,0},{2,3},{3,2},{4,5},{5,4},{6,7},{7,6},{8,9},{9,8},{10,11... | collective-permute-start | bytes 208904 | tf_op jit(solution)/shard_map/ppermute | solution.py:553
  80.1 1.3 %collective-permute-start.30 = (s16[272,128]{1,0:T(8,128)(2,1)S(1)}, s16[272,128]{1,0:T(8,128)(2,1)S(1)}, u32[]{:S(2)}, u32[]{:S(2)}) collective-permute-start(s16[272,128]{1,0:T(8,128)(2,1)S(1)} %collective-permute-done.24.refs_6_), channel_id=1, source_target_pairs={{0,1},{1,0},{2,3},{3,2},{4,5},{5,4},{6,7},{7,6},{8,9},{9,8},{10,11... | collective-permute-start | bytes 208904 | tf_op jit(solution)/shard_map/ppermute | solution.py:553

commit v5 on v4

--- a/solution.py
+++ b/solution.py
@@ -126,30 +126,64 @@
         whole_ref[:, pl.ds(start, width)] = block[at]
 
 
-def gradient_q(whole, q2, inputs_t):
-    width = q2.shape[1] // 2
-    both = mm(whole, q2)
+def cotangent_q(q2_ref, m, pairs, at):
+    terms = []
+    for r, blocks in pairs:
+        if r is None:
+            terms.append(mm(blocks[0][at], q2_ref[m]))
+            continue
+        me = lax.axis_index("fsdp") ^ r
+        width = blocks[0].shape[2]
+        rows = [q2_ref[m, pl.ds(pl.multiple_of((me ^ k) * width, width), width)] for k in range(2)]
+        pair = jnp.concatenate([block[at] for block in blocks], axis=1)
+        terms.append(mm(pair, jnp.concatenate(rows, axis=0)))
+    return sum(terms[1:], terms[0])
+
+
+def paired(keys, refs):
+    if keys == [None]:
+        return [(None, refs)]
+    return [(r, refs[2 * i : 2 * i + 2]) for i, r in enumerate(keys)]
+
+
+def begin_kernel(keys, q2_ref, *refs):
+    *blocks, out_ref = refs
+    for m in range(out_ref.shape[0]):
+        out_ref[m] = cotangent_q(q2_ref, m, paired(keys, blocks), m)
+
+
+def begin(held, keys, q2):
+    blocks = [held[r ^ k] for r in keys for k in range(2)]
+    count, tokens, _ = blocks[0].shape
+    return pl.pallas_call(
+        functools.partial(begin_kernel, keys),
+        in_specs=[VMEM] * (1 + len(blocks)),
+        out_specs=VMEM,
+        out_shape=jax.ShapeDtypeStruct((count, tokens, q2.shape[2]), F32),
+        compiler_params=pltpu.CompilerParams(vmem_limit_bytes=16 * MIB),
+        name="begin",
+    )(q2, *blocks)
+
+
+def gradient_q(both, inputs_t):
+    width = both.shape[1] // 2
     c_high, c_low = halves(both[:, :width] + both[:, width:])
     both = mm(inputs_t, jnp.concatenate([c_high, c_low], axis=1))
     return both[:, :width] + both[:, width:]
 
 
-def left_kernel(m, at, q2_ref, in_ref, fbq_ref, *refs):
-    *blocks, out_ref, whole_ref = refs
-    fill_cotangent(blocks, at, whole_ref)
-    out_ref[...] = fbq_ref[m] + gradient_q(whole_ref[...], q2_ref[m], in_ref[...])
-
-
-def left(m, blocks, at, q2, inputs_t, fbq):
+def left_kernel(m, keys, q2_ref, in_ref, fbq_ref, *refs):
+    *blocks, out_ref = refs
+    out_ref[...] = fbq_ref[m] + gradient_q(cotangent_q(q2_ref, m, paired(keys, blocks), m), in_ref[...])
+
+
+def left(m, keys, blocks, q2, inputs_t, fbq):
     _, rows, width = fbq.shape
     return pl.pallas_call(
-        functools.partial(left_kernel, m, at),
+        functools.partial(left_kernel, m, keys),
         in_specs=[VMEM] * (3 + len(blocks)),
-        out_specs=[VMEM, VMEM],
-        out_shape=[
-            jax.ShapeDtypeStruct((rows, width), F32),
-            jax.ShapeDtypeStruct((blocks[0].shape[1], q2.shape[1]), BF16),
-        ],
+        out_specs=VMEM,
+        out_shape=jax.ShapeDtypeStruct((rows, width), F32),
         compiler_params=pltpu.CompilerParams(vmem_limit_bytes=16 * MIB),
         name=f"left_{m}",
     )(q2, inputs_t, fbq, *blocks)
@@ -179,32 +213,43 @@
     return (code * down[:, None, :]).reshape(rows, width)
 
 
-def left_code_kernel(m, at, q2_ref, in_ref, fbq_ref, *refs):
-    *blocks, mine_ref, code_ref, whole_ref, p_ref = refs
-    fill_cotangent(blocks, at, whole_ref)
-    p = fbq_ref[m] + gradient_q(whole_ref[...], q2_ref[m], in_ref[...])
+def decode_part(ref, part, count):
+    rows, width = ref.shape[0] - GROUPS, ref.shape[1]
+    own, groups = rows // count, GROUPS // count
+    level = ref[rows:].astype(jnp.int32).astype(F32)[part * groups : (part + 1) * groups]
+    down = jnp.exp(level * (1.0 / 32.0)) * (1.0 / 32767.0)
+    code = ref[part * own : (part + 1) * own].astype(jnp.int32).astype(F32)
+    return (code.reshape(groups, own // groups, width) * down[:, None, :]).reshape(own, width)
+
+
+def left_code_kernel(m, keys, q2_ref, in_ref, fbq_ref, *refs):
+    *refs, mine_ref, code_ref, p_ref = refs
+    if keys == [None]:
+        both = cotangent_q(q2_ref, m, paired(keys, refs), m)
+    else:
+        both = refs[0][m] + cotangent_q(q2_ref, m, paired(keys, refs[1:]), m)
+    p = fbq_ref[m] + gradient_q(both, in_ref[...])
     p_ref[...] = p.reshape(p_ref.shape)
     low = lax.axis_index("dp") & 1
     mine_ref[...] = p_ref[low]
     encode(p_ref[1 - low], code_ref)
 
 
-def left_code(m, blocks, at, q2, inputs_t, fbq):
+def left_code(m, keys, begun, blocks, q2, inputs_t, fbq):
     _, rows, width = fbq.shape
     half = rows // 2
     return pl.pallas_call(
-        functools.partial(left_code_kernel, m, at),
-        in_specs=[VMEM] * (3 + len(blocks)),
-        out_specs=[VMEM] * 3,
+        functools.partial(left_code_kernel, m, keys),
+        in_specs=[VMEM] * (3 + len(begun) + len(blocks)),
+        out_specs=[VMEM] * 2,
         out_shape=[
             jax.ShapeDtypeStruct((half, width), F32),
             jax.ShapeDtypeStruct((half + GROUPS, width), jnp.int16),
-            jax.ShapeDtypeStruct((blocks[0].shape[1], q2.shape[1]), BF16),
         ],
         scratch_shapes=[pltpu.VMEM((2, half, width), F32)],
         compiler_params=pltpu.CompilerParams(vmem_limit_bytes=16 * MIB),
         name=f"left_code_{m}",
-    )(q2, inputs_t, fbq, *blocks)
+    )(q2, inputs_t, fbq, *begun, *blocks)
 
 
 def add_kernel(mine_ref, theirs_ref, out_ref):
@@ -223,30 +268,27 @@
     )(mine, theirs)
 
 
-def whole_left_kernel(mine_ref, theirs_ref, p_ref, gram_ref):
-    half, width = mine_ref.shape[0] - GROUPS, mine_ref.shape[1]
-    low = lax.axis_index("dp") & 1
-    p_ref[pl.ds(pl.multiple_of(low * half, half), half)] = decode(mine_ref)
-    p_ref[pl.ds(pl.multiple_of((1 - low) * half, half), half)] = decode(theirs_ref)
-    gram_ref[...] = gram_of(p_ref[...])
-
-
-def whole_left(mine, theirs):
-    half, width = mine.shape[0] - GROUPS, mine.shape[1]
-    return pl.pallas_call(
-        whole_left_kernel,
-        in_specs=[VMEM, VMEM],
+def halves_code_kernel(p_ref, first_ref, second_ref):
+    half = p_ref.shape[0] // 2
+    encode(p_ref[:half], first_ref)
+    encode(p_ref[half:], second_ref)
+
+
+def halves_code(p):
+    code = jax.ShapeDtypeStruct((p.shape[0] // 2 + GROUPS, p.shape[1]), jnp.int16)
+    return pl.pallas_call(
+        halves_code_kernel,
+        in_specs=[VMEM],
         out_specs=[VMEM, VMEM],
-        out_shape=[
-            jax.ShapeDtypeStruct((2 * half, width), F32),
-            jax.ShapeDtypeStruct((width, width), F32),
-        ],
-        compiler_params=pltpu.CompilerParams(vmem_limit_bytes=16 * MIB),
-        name="whole_left",
-    )(mine, theirs)
-
-
-def full_kernel(m, held_ref, in_ref, whole_ref, out_ref):
+        out_shape=[code, code],
+        compiler_params=pltpu.CompilerParams(vmem_limit_bytes=16 * MIB),
+        name="halves_code",
+    )(p)
+
+
+def full_kernel(m, held_ref, in_ref, *refs):
+    *blocks, out_ref, whole_ref = refs
+    fill_cotangent(blocks, m, whole_ref)
     rows = out_ref.shape[0]
     tile = tile_of(rows)
     for i in range(rows // tile):
@@ -254,50 +296,80 @@
         out_ref[part] = held_ref[m, part] + mm(in_ref[part], whole_ref[...])
 
 
-def full(m, held, inputs_t, whole):
+def full(m, held, inputs_t, blocks):
     _, rows, columns = held.shape
     return pl.pallas_call(
         functools.partial(full_kernel, m),
-        in_specs=[VMEM, VMEM, VMEM],
+        in_specs=[VMEM] * (2 + len(blocks)),
         out_specs=VMEM,
         out_shape=in_vmem((rows, columns), F32),
+        scratch_shapes=[pltpu.VMEM((inputs_t.shape[1], columns), BF16)],
         compiler_params=pltpu.CompilerParams(vmem_limit_bytes=16 * MIB),
         name=f"full_{m}",
-    )(stay(held), inputs_t, whole)
-
-
-def right_kernel(full_ref, p_ref, mine_ref, other_ref, both_ref):
-    rows, width = p_ref.shape
-    tile = tile_of(rows)
+    )(stay(held), inputs_t, *blocks)
+
+
+def half_of(halved):
+    return lax.axis_index("dp") & 1 if halved else 0
+
+
+def half_products(full_ref, code_ref, which):
+    half, width = code_ref.shape[0] - GROUPS, code_ref.shape[1]
+    tile = tile_of(half)
+    p = decode(code_ref)
     total = None
-    for i in range(rows // tile):
-        part = pl.ds(i * tile, tile)
-        p_high, p_low = halves(p_ref[part].T)
-        g_high, g_low = halves(full_ref[part])
+    for i in range(half // tile):
+        p_high, p_low = halves(p[i * tile : (i + 1) * tile].T)
+        start = pl.multiple_of(which * half + i * tile, tile)
+        g_high, g_low = halves(full_ref[pl.ds(start, tile)])
         both = mm(jnp.concatenate([p_high, p_low], axis=0), g_high)
         term = both[:width] + both[width:] + mm(p_high, g_low)
         total = term if total is None else total + term
+    return total, gram_of(p)
+
+
+def own_half_kernel(halved, full_ref, code_ref, total_ref, gram_ref):
+    total_ref[...], gram_ref[...] = half_products(full_ref, code_ref, half_of(halved))
+
+
+def own_half(m, halved, full_grad, code):
+    width = code.shape[1]
+    return pl.pallas_call(
+        functools.partial(own_half_kernel, halved),
+        in_specs=[VMEM, VMEM],
+        out_specs=[VMEM, VMEM],
+        out_shape=[
+            jax.ShapeDtypeStruct((width, full_grad.shape[1]), F32),
+            jax.ShapeDtypeStruct((width, width), F32),
+        ],
+        compiler_params=pltpu.CompilerParams(vmem_limit_bytes=16 * MIB),
+        name=f"own_half_{m}",
+    )(stay(full_grad), code)
+
+
+def other_half_kernel(halved, full_ref, code_ref, total_ref, part_ref, mine_ref, other_ref, gram_ref, both_ref):
+    total, gram = half_products(full_ref, code_ref, 1 - half_of(halved))
+    gram_ref[...] = part_ref[...] + gram
+    total = total_ref[...] + total
     lanes = both_ref.shape[2]
-    tiles = total.shape[1] // lanes
-    stacked = [total[:, t * lanes : (t + 1) * lanes] for t in range(tiles)]
+    stacked = [total[:, t : t + lanes] for t in range(0, total.shape[1], lanes)]
     both_ref[...] = jnp.concatenate(stacked, axis=0).reshape(both_ref.shape)
     side = lax.axis_index("fsdp") & 1
     mine_ref[...] = both_ref[side]
     other_ref[...] = both_ref[1 - side]
 
 
-def right(m, full_grad, p):
-    width = p.shape[1]
-    half = full_grad.shape[1] * width // LANES // 2
-    return pl.pallas_call(
-        right_kernel,
-        in_specs=[VMEM, VMEM],
-        out_specs=[VMEM, VMEM],
-        out_shape=[jax.ShapeDtypeStruct((half, LANES), F32)] * 2,
+def other_half(m, halved, full_grad, code, total, part):
+    half = total.size // LANES // 2
+    return pl.pallas_call(
+        functools.partial(other_half_kernel, halved),
+        in_specs=[VMEM] * 4,
+        out_specs=[VMEM] * 3,
+        out_shape=[jax.ShapeDtypeStruct((half, LANES), F32)] * 2 + [jax.ShapeDtypeStruct(part.shape, F32)],
         scratch_shapes=[pltpu.VMEM((2, half, LANES), F32)],
         compiler_params=pltpu.CompilerParams(vmem_limit_bytes=16 * MIB),
-        name=f"right_{m}",
-    )(stay(full_grad), p)
+        name=f"other_half_{m}",
+    )(stay(full_grad), code, total, part)
 
 
 def tree(values):
@@ -359,23 +431,6 @@
     high_t, low_t = halves(p.T)
     both = mm(high_t, jnp.concatenate([high, low], axis=1))
     return both[:, :width] + both[:, width:] + mm(low_t, high)
-
-
-def gram_kernel(p_ref, out_ref):
-    out_ref[0] = gram_of(p_ref[0])
-
-
-def gram(p):
-    count, rows, width = p.shape
-    return pl.pallas_call(
-        gram_kernel,
-        grid=(count,),
-        in_specs=[pl.BlockSpec((1, rows, width), lambda m: (m, 0, 0))],
-        out_specs=pl.BlockSpec((1, width, width), lambda m: (m, 0, 0)),
-        out_shape=jax.ShapeDtypeStruct((count, width, width), F32),
-        compiler_params=params(16),
-        name="gram",
-    )(p)
 
 
 def cholesky_inverse(work, n):
@@ -447,29 +502,34 @@
     )(ranks, grams)
 
 
-def factor_p_kernel(inv_ref, *refs):
-    *p_refs, out_ref, p3_ref, buf_ref, sems = refs
+def factor_p_kernel(halved, inv_ref, *refs):
+    *codes, out_ref, p3_ref, buf_ref, sems = refs
     n = inv_ref.shape[1]
+    which = half_of(halved)
     copies = []
-    for m, p_ref in enumerate(p_refs):
+    for m in range(inv_ref.shape[0]):
         i_high, i_low = halves(inv_ref[m])
-        p_high, p_low = halves(p_ref[...])
-        both = mm_nt(p_high, jnp.concatenate([i_high, i_low], axis=0))
-        result = both[:, :n] + both[:, n:] + mm_nt(p_low, i_high)
-        buf_ref[m] = result
+        i_both = jnp.concatenate([i_high, i_low], axis=0)
+        for code, place in ((codes[2 * m], which), (codes[2 * m + 1], 1 - which)):
+            p_high, p_low = halves(decode(code))
+            rows = p_high.shape[0]
+            part = pl.ds(pl.multiple_of(place * rows, rows), rows)
+            both = mm_nt(p_high, i_both)
+            result = both[:, :n] + both[:, n:] + mm_nt(p_low, i_high)
+            buf_ref[m, part] = result
+            high, low = halves(result)
+            p3_ref[m, part] = jnp.concatenate([high, low, high], axis=1)
         copies.append(pltpu.make_async_copy(buf_ref.at[m], out_ref.at[m], sems.at[m]))
         copies[-1].start()
-        high, low = halves(result)
-        p3_ref[m] = jnp.concatenate([high, low, high], axis=1)
     for copy in copies:
         copy.wait()
 
 
-def factor_p_of(inverse, p):
-    count, (rows, width) = len(p), p[0].shape
-    return pl.pallas_call(
-        factor_p_kernel,
-        in_specs=[VMEM] * (1 + count),
+def factor_p_of(halved, inverse, codes):
+    count, rows, width = len(codes), 2 * (codes[0][0].shape[0] - GROUPS), codes[0][0].shape[1]
+    return pl.pallas_call(
+        functools.partial(factor_p_kernel, halved),
+        in_specs=[VMEM] * (1 + 2 * count),
         out_specs=[pl.BlockSpec(memory_space=pltpu.HBM), VMEM],
         out_shape=[
             jax.ShapeDtypeStruct((count, rows, width), F32),
@@ -478,26 +538,24 @@
         scratch_shapes=[pltpu.VMEM((count, rows, width), F32), pltpu.SemaphoreType.DMA((count,))],
         compiler_params=pltpu.CompilerParams(vmem_limit_bytes=16 * MIB),
         name="factor_p",
-    )(inverse, *p)
+    )(inverse, *[code for pair in codes for code in pair])
 
 
 def error_kernel(count, pieces, groups, p3_ref, inv_ref, *refs):
     codes, refs = refs[:pieces], refs[pieces:]
     full_refs, (err_ref, fq_ref, right_ref, q_ref, buf_ref, sems) = refs[:count], refs[count:]
     rows, width = p3_ref.shape[1], inv_ref.shape[1]
-    tile = tile_of(rows)
+    tile = min(rows, LANES)
     share = right_ref.shape[1] // pieces
     me = lax.axis_index("fsdp") if pieces > 1 else 0
-    for r, code in enumerate(codes):
-        value = decode(code)
-        place = (me ^ r) & 1 if pieces > 1 else 0
-        for bit, members in groups:
-            place = place * members + (((me ^ r) >> (bit.bit_length() - 1)) & (members - 1))
-        at = pl.ds(pl.multiple_of(place * share, share), share)
-        for m in range(count):
-            right_ref[m, at] = value[m * share : (m + 1) * share]
     copies = []
     for m in range(count):
+        for r, code in enumerate(codes):
+            place = (me ^ r) & 1 if pieces > 1 else 0
+            for bit, members in groups:
+                place = place * members + (((me ^ r) >> (bit.bit_length() - 1)) & (members - 1))
+            at = pl.ds(pl.multiple_of(place * share, share), share)
+            right_ref[m, at] = decode_part(code, m, count)
         i_high, i_low = halves(inv_ref[m])
         tiles = [right_ref[m, t : t + width] for t in range(0, right_ref.shape[1], width)]
         r_high, r_low = halves(jnp.concatenate(tiles, axis=1))
@@ -505,8 +563,8 @@
         fq_t = both[:width] + both[width:] + mm(i_high, r_low)
         q_high, q_low = halves(fq_t)
         q3 = jnp.concatenate([q_high, q_high, q_low], axis=0)
-        for i in range(rows // tile):
-            part = pl.ds(i * tile, tile)
+        for start in range(0, rows, tile):
+            part = pl.ds(start, tile)
             buf_ref[m, part] = full_refs[m][part] - mm(p3_ref[m, part], q3)
             copies.append(
                 pltpu.make_async_copy(buf_ref.at[m, part], err_ref.at[m, 0, part], sems.at[len(copies)])
@@ -537,7 +595,7 @@
             pltpu.VMEM((count, columns * width // LANES, LANES), F32),
             pltpu.VMEM((count, columns, width), F32),
             pltpu.VMEM((count, rows, columns), F32),
-            pltpu.SemaphoreType.DMA((count * (rows // tile_of(rows) + 1),)),
+            pltpu.SemaphoreType.DMA((count * (rows // min(rows, LANES) + 1),)),
         ],
         compiler_params=pltpu.CompilerParams(vmem_limit_bytes=24 * MIB),
         name="error",
@@ -563,12 +621,17 @@
     return [(bits[i], 1 << len(bits[i : i + 2])) for i in range(0, len(bits), 2)]
 
 
-def gather_blocks(x, axis, beside=()):
+def gather_slow(x, axis):
     held = {0: x}
     for bit, members in groups_of(axis)[::-1]:
         for r in list(held):
             for k in range(1, members):
                 held[r ^ (k * bit)] = across(held[r], axis, k * bit)
+    return held
+
+
+def gather_blocks(x, axis, beside=()):
+    held = gather_slow(x, axis)
     order = list(held)
     held[order[-1]], *beside = tie(held[order[-1]], *beside)
     held.update({r ^ 1: across(held[r], axis, 1) for r in order})
@@ -577,37 +640,41 @@
 
 def gather_cotangent(cotangent, beside):
     size = lax.axis_size("fsdp")
-    count, _, width = cotangent.shape
-    if power_of_two(size) and size > 1 and width % 128 == 0:
-        blocks, beside = gather_blocks(cotangent, "fsdp", beside)
-        return [(blocks, m) for m in range(count)], beside
-    whole = lax.all_gather(cotangent, "fsdp", axis=2, tiled=True)
-    return [([whole], m) for m in range(count)], beside
+    width = cotangent.shape[2]
+    if not (power_of_two(size) and size > 1 and width % 128 == 0):
+        return [lax.all_gather(cotangent, "fsdp", axis=2, tiled=True)], [None], [], beside
+    held = gather_slow(cotangent, "fsdp")
+    *order, last = list(held)
+    values = tie(*[held[r] for r in order], *beside)
+    held.update(zip(order, values))
+    beside = values[len(order) :]
+    swapped = [across(held[r], "fsdp", 1) for r in order]
+    held[last], *swapped = tie(held[last], *swapped)
+    held.update({r ^ 1: x for r, x in zip(order, swapped)})
+    begun = begin(held, order, beside[2])
+    held[last ^ 1] = across(held[last], "fsdp", 1)
+    return [held[r] for r in range(len(held))], [last], [begun], beside
 
 
 def tie(*values):
     return lax.optimization_barrier(values)
 
 
-def sums(gram_parts, full_grad, p, ranks):
+def sums(halved, grams, pairs, p_codes, ranks):
     size = lax.axis_size("fsdp")
     replicas = lax.axis_size("dp")
-    count = len(p)
     if not (power_of_two(size) and size > 1):
-        inverse = factor(lax.psum(jnp.stack(gram_parts), "fsdp"), ranks)
-        pairs = [right(m, full_grad[m], p[m]) for m in range(count)]
+        inverse = factor(lax.psum(grams, "fsdp"), ranks)
         ordered = [jnp.stack(pair) for pair in pairs]
         odd = (lax.axis_index("fsdp") & 1) == 1
         whole = jnp.stack([jnp.where(odd, x[::-1], x).reshape(-1, x.shape[2]) for x in ordered])
         codes = [merge([list(lax.psum(whole, ("fsdp", "dp")))], [], "code")]
-        return inverse, factor_p_of(inverse, p), codes
+        return inverse, factor_p_of(halved, inverse, p_codes), codes
     groups = groups_of("fsdp")
 
-    grams = jnp.stack(gram_parts)
     for bit in bits_of("fsdp"):
         grams = grams + across(grams, "fsdp", bit)
 
-    pairs = [right(m, full_grad[m], p[m]) for m in range(count)]
     terms = [[mine for mine, _ in pairs], [across(other, "fsdp", 1) for _, other in pairs]]
     codes = []
     for bit, members in groups:
@@ -624,7 +691,7 @@
         inverse = factor(grams, ranks)
         code = merge([[lax.psum(plain(code), "dp")]], [], "code_sum")
     code, inverse = tie(code, inverse)
-    codes, made = gather_blocks(code, "fsdp", factor_p_of(inverse, p))
+    codes, made = gather_blocks(code, "fsdp", factor_p_of(halved, inverse, p_codes))
     return inverse, made, codes
 
 
@@ -642,38 +709,54 @@
     )(code)
 
 
-def left_sums(blocks, q2, inputs_t, held, fbq):
+def left_sums(halved, blocks, keys, begun, q2, inputs_t, held, fbq):
+    count = fbq.shape[0]
+    codes, full_grad, pairs, grams = [], [], [], []
+    if not halved:
+        pairs_of = [None] if keys == [None] else list(range(0, len(blocks), 2))
+        p = lax.psum(jnp.stack([left(m, pairs_of, blocks, q2, inputs_t, fbq) for m in range(count)]), "dp")
+        for m in range(count):
+            full_grad.append(full(m, held, inputs_t, blocks))
+            codes.append(halves_code(p[m]))
+            total, part = own_half(m, halved, full_grad[m], codes[m][0])
+            *pair, part = other_half(m, halved, full_grad[m], codes[m][1], total, part)
+            pairs.append(pair)
+            grams.append(part)
+        return codes, full_grad, pairs, jnp.stack(grams)
+    steps = bits_of("dp")[1:]
+    mines = []
+    late = blocks if keys == [None] else [blocks[r ^ k] for r in keys for k in range(2)]
+    for m in range(count):
+        mine, other = left_code(m, keys, begun, late, q2, inputs_t, fbq)
+        mines.append(add_code(mine, across(other, "dp", 1)))
+    own, late = {}, None
+    for m in range(count)[::-1]:
+        mine, in_t = tie(mines[m], inputs_t)
+        grad = full(m, held, in_t, blocks)
+        for bit in steps:
+            theirs, grad = tie(across(mine, "dp", bit), grad)
+            if late is not None:
+                theirs, *own[late] = tie(theirs, *own[late])
+            mine = add_code(mine, theirs)
+        mines[m] = mine
+        full_grad.insert(0, grad)
+        own[m] = list(own_half(m, halved, grad, mine))
+        late = m
+    for m in range(count):
+        codes.append((mines[m], across(mines[m], "dp", 1)))
+        *pair, part = other_half(m, halved, full_grad[m], codes[m][1], *own[m])
+        pairs.append(pair)
+        grams.append(part)
+    return codes, full_grad, pairs, jnp.stack(grams)
+
+
+def local(inputs, cotangent, feedback, q_init, factor_ranks):
     replicas = lax.axis_size("dp")
-    count = fbq.shape[0]
-    if not (power_of_two(replicas) and replicas > 1):
-        parts = [left(m, *blocks[m], q2, inputs_t, fbq) for m in range(count)]
-        p = lax.psum(jnp.stack([part for part, _ in parts]), "dp")
-        full_grad = [full(m, held, inputs_t, parts[m][1]) for m in range(count)]
-        grams = gram(p)
-        return [p[m] for m in range(count)], full_grad, [grams[m] for m in range(count)]
-    whole, full_grad = [], []
-    for m in range(count):
-        mine, other, cot = left_code(m, *blocks[m], q2, inputs_t, fbq)
-        mine = add_code(mine, across(other, "dp", 1))
-        for step, bit in enumerate(bits_of("dp")[1:]):
-            if step == 0:
-                mine, cot = tie(mine, cot)
-                theirs, grad = tie(across(mine, "dp", bit), full(m, held, inputs_t, cot))
-                full_grad.append(grad)
-            else:
-                theirs = across(mine, "dp", bit)
-            mine = add_code(mine, theirs)
-        if len(full_grad) == m:
-            full_grad.append(full(m, held, inputs_t, cot))
-        whole.append(whole_left(mine, across(mine, "dp", 1)))
-    return [p for p, _ in whole], full_grad, [part for _, part in whole]
-
-
-def local(inputs, cotangent, feedback, q_init, factor_ranks):
+    halved = power_of_two(replicas) and replicas > 1
     beside = feedback_q(feedback, q_init, inputs, factor_ranks)
-    blocks, (held, fbq, q2, inputs_t) = gather_cotangent(cotangent, beside)
-    p, full_grad, gram_parts = left_sums(blocks, q2, inputs_t, held, fbq)
-    inverse, (factor_p, p3), codes = sums(gram_parts, full_grad, p, factor_ranks)
+    blocks, keys, begun, (held, fbq, q2, inputs_t) = gather_cotangent(cotangent, beside)
+    p_codes, full_grad, pairs, grams = left_sums(halved, blocks, keys, begun, q2, inputs_t, held, fbq)
+    inverse, (factor_p, p3), codes = sums(halved, grams, pairs, p_codes, factor_ranks)
     new_error, factor_q = error(full_grad, p3, inverse, codes)
     return (factor_p, factor_q, new_error)
 

time: 86.3 us -> 83.6 us (0.969)
  waiting for transfers between devices: 24 us -> 22.6 us
  Pallas kernels: 29.8 us -> 28.8 us
    ppermute x31, waiting for transfers between devices: 24 us -> 22.6 us  [across(): return lax.ppermute(x, axis, [(i, i ^ bit) for i in range(size)])]
    pallas_call x9 -> x10, Pallas kernels: 10.9 us -> 9.95 us  [the longest x2 3.13 us: full(): pl.pallas_call(functools.partial(full_kernel, m), in_specs=[VMEM] * (2 +...]
  transfers between devices with their start and end apart: 31 -> 31, of which waited for: 19 -> 16; matrix products, arithmetic and copies ran while one was open for 0% -> 0% of each run, Pallas kernels for 27% -> 27%
where the time goes in v5:
time: 83.6 us; the launch traced here: 83.5 us
  starting transfers between devices  31 us (37%)
  Pallas kernels  28.8 us (34%)
  waiting for transfers between devices  22.6 us (27%)
  between operations  1.01 us (1%)
    ppermute x31, starting transfers between devices, across(): return lax.ppermute(x, axis, [(i, i ^ bit) for i in range(size)])  31 us
    ppermute x31, waiting for transfers between devices, across(): return lax.ppermute(x, axis, [(i, i ^ bit) for i in range(size)])  22.6 us
    pallas_call x1, Pallas kernels, feedback_q(): pl.pallas_call(feedback_q_kernel, in_specs=[far] * 4, out_specs=[VMEM] *...  7.55 us
    pallas_call x1, Pallas kernels, factor(): pl.pallas_call(factor_kernel, in_specs=[SMEM, VMEM], out_specs=VMEM, out_...  5.61 us
    pallas_call x1, Pallas kernels, error(): pl.pallas_call(functools.partial(error_kernel, count, len(codes), groups)...  4.47 us
    pallas_call x2, Pallas kernels, full(): pl.pallas_call(functools.partial(full_kernel, m), in_specs=[VMEM] * (2 +...  3.13 us
    pallas_call x2, Pallas kernels, other_half(): pl.pallas_call(functools.partial(other_half_kernel, halved), in_specs=[VM...  1.69 us
    pallas_call x2, Pallas kernels, left_code(): pl.pallas_call(functools.partial(left_code_kernel, m, keys), in_specs=[VM...  1.69 us
  transfers between devices with their start and end apart: 31, of which 16 were waited for; matrix products, arithmetic and copies ran while one was open for 0% of the time, Pallas kernels for 27%

profile of v5, /device:TPU:0, one launch (start us, length us, event | category | flops | bytes accessed | tf_op | source)
XLA Modules:
  0.0 83.5 jit_solution(4959236311074586379)
XLA Ops:
  0.6 3.0 %collective-permute-start.1 = (bf16[2,512,128]{2,1,0:T(8,128)(2,1)}, bf16[2,512,128]{2,1,0:T(8,128)(2,1)S(1)}, u32[]{:S(2)}, u32[]{:S(2)}) collective-permute-start(bf16[2,512,128]{2,1,0:T(8,128)(2,1)} %refs_0_.2), channel_id=1, source_target_pairs={{0,4},{1,5},{2,6},{3,7},{4,0},{5,1},{6,2},{7,3},{8,12},{9,13},{10,... | collective-permute-start | bytes 786440 | tf_op jit(solution)/shard_map/ppermute | solution.py:611
  3.7 1.5 %collective-permute-start = (bf16[2,512,128]{2,1,0:T(8,128)(2,1)}, bf16[2,512,128]{2,1,0:T(8,128)(2,1)S(1)}, u32[]{:S(2)}, u32[]{:S(2)}) collective-permute-start(bf16[2,512,128]{2,1,0:T(8,128)(2,1)} %refs_0_.2), channel_id=1, source_target_pairs={{0,2},{1,3},{2,0},{3,1},{4,6},{5,7},{6,4},{7,5},{8,10},{9,11},{10,... | collective-permute-start | bytes 786440 | tf_op jit(solution)/shard_map/ppermute | solution.py:611
  5.2 0.0 collective-permute-start.2
  5.2 7.6 %feedback_q.1 = (f32[2,1024,1024]{2,1,0:T(8,128)S(1)}, f32[2,1024,128]{2,1,0:T(8,128)S(1)}, bf16[2,1024,256]{2,1,0:T(8,128)(2,1)S(1)}, bf16[1024,512]{1,0:T(8,128)(2,1)S(1)}) custom-call(s32[2]{0:T(128)} %ranks_ref.3, f32[2,1,1024,1024]{3,2,1,0:T(8,128)} %fb_ref.1, f32[2,1024,128]{2,1,0:T(8,128)} %q_ref.1, bf16[512,1024]{1,0:T(8,128)(2,1)} %in_ref.1), custom_call_target="tpu_custom_call" | custom-call | tf_op jit(solution)/shard_map/feedback_q/pallas_call | solution.py:96
  12.8 0.0 collective-permute-done.1.refs_4_
  12.8 0.3 collective-permute-done.refs_2_
  13.1 0.5 collective-permute-start.4
  13.6 0.0 collective-permute-start.5
  13.6 3.4 %collective-permute-done.2.refs_1_.refs_6_ = bf16[2,512,128]{2,1,0:T(8,128)(2,1)S(1)} collective-permute-done((bf16[2,512,128]{2,1,0:T(8,128)(2,1)}, bf16[2,512,128]{2,1,0:T(8,128)(2,1)S(1)}, u32[]{:S(2)}, u32[]{:S(2)}) %collective-permute-start.2) | collective-permute-done | bytes 262176 | tf_op jit(solution)/shard_map/ppermute | solution.py:611
  17.1 0.1 collective-permute-start.6
  17.2 0.6 begin.1.refs_0_
  17.8 0.9 %collective-permute-done.6.refs_2_.refs_7_ = bf16[2,512,128]{2,1,0:T(8,128)(2,1)S(1)} collective-permute-done((bf16[2,512,128]{2,1,0:T(8,128)(2,1)S(1)}, bf16[2,512,128]{2,1,0:T(8,128)(2,1)S(1)}, u32[]{:S(2)}, u32[]{:S(2)}) %collective-permute-start.6) | collective-permute-done | bytes 262176 | tf_op jit(solution)/shard_map/ppermute | solution.py:611
  18.7 0.8 %left_code_1.1 = (f32[512,128]{1,0:T(8,128)S(1)}, s16[528,128]{1,0:T(8,128)(2,1)S(1)}) custom-call(bf16[2,1024,256]{2,1,0:T(8,128)(2,1)S(1)} %get-tuple-element.65.q2_ref, bf16[1024,512]{1,0:T(8,128)(2,1)S(1)} %get-tuple-element.85.in_ref, f32[2,1024,128]{2,1,0:T(8,128)S(1)} %get-tuple-element.67.fbq_ref, f32[2,512,256]{2,1,0:T(8,128)S(1)} %begin.1.refs_0_, ...), custom_call_target="tpu_custom_call" | custom-call | tf_op jit(solution)/shard_map/left_code_1/pallas_call | solution.py:241
  19.5 1.8 %collective-permute-start.9 = (s16[528,128]{1,0:T(8,128)(2,1)S(1)}, s16[528,128]{1,0:T(8,128)(2,1)S(1)}, u32[]{:S(2)}, u32[]{:S(2)}) collective-permute-start(s16[528,128]{1,0:T(8,128)(2,1)S(1)} %get-tuple-element.83), channel_id=1, source_target_pairs={{0,8},{8,0},{16,24},{24,16},{1,9},{9,1},{17,25},{25,17},{2,10},{10... | collective-permute-start | bytes 405512 | tf_op jit(solution)/shard_map/ppermute | solution.py:611
  21.3 0.8 %left_code_0.1 = (f32[512,128]{1,0:T(8,128)S(1)}, s16[528,128]{1,0:T(8,128)(2,1)S(1)}) custom-call(bf16[2,1024,256]{2,1,0:T(8,128)(2,1)S(1)} %get-tuple-element.65.q2_ref, bf16[1024,512]{1,0:T(8,128)(2,1)S(1)} %get-tuple-element.85.in_ref, f32[2,1024,128]{2,1,0:T(8,128)S(1)} %get-tuple-element.67.fbq_ref, f32[2,512,256]{2,1,0:T(8,128)S(1)} %begin.1.refs_0_, ...), custom_call_target="tpu_custom_call" | custom-call | tf_op jit(solution)/shard_map/left_code_0/pallas_call | solution.py:241
  22.2 0.4 collective-permute-start.7
  22.5 3.1 %collective-permute-done.9.theirs_ref = s16[528,128]{1,0:T(8,128)(2,1)S(1)} collective-permute-done((s16[528,128]{1,0:T(8,128)(2,1)S(1)}, s16[528,128]{1,0:T(8,128)(2,1)S(1)}, u32[]{:S(2)}, u32[]{:S(2)}) %collective-permute-start.9) | collective-permute-done | bytes 135200 | tf_op jit(solution)/shard_map/ppermute | solution.py:611
  25.7 0.1 add_code.5.mine_ref
  25.8 3.0 %collective-permute-start.10 = (s16[528,128]{1,0:T(8,128)(2,1)S(1)}, s16[528,128]{1,0:T(8,128)(2,1)S(1)}, u32[]{:S(2)}, u32[]{:S(2)}) collective-permute-start(s16[528,128]{1,0:T(8,128)(2,1)S(1)} %add_code.5.mine_ref), channel_id=1, source_target_pairs={{0,16},{8,24},{16,0},{24,8},{1,17},{9,25},{17,1},{25,9},{2,18},{10... | collective-permute-start | bytes 405512 | tf_op jit(solution)/shard_map/ppermute | solution.py:611
  28.8 0.1 add_code.4.mine_ref
  28.9 2.8 %collective-permute-start.8 = (s16[528,128]{1,0:T(8,128)(2,1)S(1)}, s16[528,128]{1,0:T(8,128)(2,1)S(1)}, u32[]{:S(2)}, u32[]{:S(2)}) collective-permute-start(s16[528,128]{1,0:T(8,128)(2,1)S(1)} %add_code.4.mine_ref), channel_id=1, source_target_pairs={{0,16},{8,24},{16,0},{24,8},{1,17},{9,25},{17,1},{25,9},{2,18},{10... | collective-permute-start | bytes 405512 | tf_op jit(solution)/shard_map/ppermute | solution.py:611
  31.7 1.6 %full_0.1.full_ref.refs_8_ = f32[1024,1024]{1,0:T(8,128)S(1)} custom-call(f32[2,1024,1024]{2,1,0:T(8,128)S(1)} %get-tuple-element.78.held_ref, bf16[1024,512]{1,0:T(8,128)(2,1)S(1)} %get-tuple-element.85.in_ref, bf16[2,512,128]{2,1,0:T(8,128)(2,1)S(1)} %copy-done, bf16[2,512,128]{2,1,0:T(8,128)(2,1)S(1)} %collective-permute-done.3.refs_1_, ...), custom_call_target="tpu_custom_call" | custom-call | tf_op jit(solution)/shard_map/full_0/pallas_call | solution.py:301
  33.2 1.6 %full_1.1.full_ref.refs_9_ = f32[1024,1024]{1,0:T(8,128)S(1)} custom-call(f32[2,1024,1024]{2,1,0:T(8,128)S(1)} %get-tuple-element.78.held_ref, bf16[1024,512]{1,0:T(8,128)(2,1)S(1)} %get-tuple-element.85.in_ref, bf16[2,512,128]{2,1,0:T(8,128)(2,1)S(1)} %copy-done, bf16[2,512,128]{2,1,0:T(8,128)(2,1)S(1)} %collective-permute-done.3.refs_1_, ...), custom_call_target="tpu_custom_call" | custom-call | tf_op jit(solution)/shard_map/full_1/pallas_call | solution.py:301
  34.8 3.5 %collective-permute-done.10.theirs_ref = s16[528,128]{1,0:T(8,128)(2,1)S(1)} collective-permute-done((s16[528,128]{1,0:T(8,128)(2,1)S(1)}, s16[528,128]{1,0:T(8,128)(2,1)S(1)}, u32[]{:S(2)}, u32[]{:S(2)}) %collective-permute-start.10) | collective-permute-done | bytes 135200 | tf_op jit(solution)/shard_map/ppermute | solution.py:611
  38.3 0.2 add_code.6.code_ref.refs_2_
  38.5 1.7 %collective-permute-done.8.theirs_ref = s16[528,128]{1,0:T(8,128)(2,1)S(1)} collective-permute-done((s16[528,128]{1,0:T(8,128)(2,1)S(1)}, s16[528,128]{1,0:T(8,128)(2,1)S(1)}, u32[]{:S(2)}, u32[]{:S(2)}) %collective-permute-start.8) | collective-permute-done | bytes 135200 | tf_op jit(solution)/shard_map/ppermute | solution.py:611
  40.1 0.5 collective-permute-start.12
  40.6 0.7 own_half_1.1
  41.4 0.2 add_code.7.code_ref.refs_0_
  41.5 0.0 copy-start.1
  41.5 1.6 %collective-permute-start.11 = (s16[528,128]{1,0:T(8,128)(2,1)S(1)}, s16[528,128]{1,0:T(8,128)(2,1)S(1)}, u32[]{:S(2)}, u32[]{:S(2)}) collective-permute-start(s16[528,128]{1,0:T(8,128)(2,1)S(1)} %add_code.7.code_ref.refs_0_), channel_id=1, source_target_pairs={{0,8},{8,0},{16,24},{24,16},{1,9},{9,1},{17,25},{25,17},{2,10},{10... | collective-permute-start | bytes 405512 | tf_op jit(solution)/shard_map/ppermute | solution.py:611
  43.1 0.7 own_half_0.1
  43.9 2.3 %collective-permute-done.12.code_ref.refs_3_ = s16[528,128]{1,0:T(8,128)(2,1)S(1)} collective-permute-done((s16[528,128]{1,0:T(8,128)(2,1)S(1)}, s16[528,128]{1,0:T(8,128)(2,1)S(1)}, u32[]{:S(2)}, u32[]{:S(2)}) %collective-permute-start.12) | collective-permute-done | bytes 135200 | tf_op jit(solution)/shard_map/ppermute | solution.py:611
  46.1 0.8 other_half_1.1
  46.9 0.7 collective-permute-done.11.code_ref.refs_1_
  47.6 0.9 %other_half_0.1 = (f32[512,128]{1,0:T(8,128)S(1)}, f32[512,128]{1,0:T(8,128)S(1)}, f32[128,128]{1,0:T(8,128)S(1)}) custom-call(f32[1024,1024]{1,0:T(8,128)S(1)} %full_0.1.full_ref.refs_8_, s16[528,128]{1,0:T(8,128)(2,1)S(1)} %collective-permute-done.11.code_ref.refs_1_, f32[128,1024]{1,0:T(8,128)S(1)} %get-tuple-element.91.total_ref, ...), custom_call_target="tpu_custom_call" | custom-call | tf_op jit(solution)/shard_map/other_half_0/pallas_call | solution.py:364
  48.5 0.1 collective-permute-start.21
  48.6 0.5 collective-permute-start.14
  49.1 0.1 collective-permute-start.13
  49.2 0.8 collective-permute-done.21
  50.0 1.6 %collective-permute-start.22 = (f32[2,128,128]{2,1,0:T(8,128)S(1)}, f32[2,128,128]{2,1,0:T(8,128)S(1)}, u32[]{:S(2)}, u32[]{:S(2)}) collective-permute-start(f32[2,128,128]{2,1,0:T(8,128)S(1)} %fusion), channel_id=1, source_target_pairs={{0,2},{1,3},{2,0},{3,1},{4,6},{5,7},{6,4},{7,5},{8,10},{9,11},{10,... | collective-permute-start | bytes 393224 | tf_op jit(solution)/shard_map/ppermute | solution.py:611
  51.5 0.3 part_2.1
  51.8 0.7 collective-permute-start.15
  52.5 1.5 %collective-permute-start.16 = (s16[272,128]{1,0:T(8,128)(2,1)S(1)}, s16[272,128]{1,0:T(8,128)(2,1)S(1)}, u32[]{:S(2)}, u32[]{:S(2)}) collective-permute-start(s16[272,128]{1,0:T(8,128)(2,1)S(1)} %get-tuple-element.102), channel_id=1, source_target_pairs={{0,4},{1,5},{2,6},{3,7},{4,0},{5,1},{6,2},{7,3},{8,12},{9,13},{10,... | collective-permute-start | bytes 208904 | tf_op jit(solution)/shard_map/ppermute | solution.py:611
  54.0 1.3 %collective-permute-start.17 = (s16[272,128]{1,0:T(8,128)(2,1)S(1)}, s16[272,128]{1,0:T(8,128)(2,1)S(1)}, u32[]{:S(2)}, u32[]{:S(2)}) collective-permute-start(s16[272,128]{1,0:T(8,128)(2,1)S(1)} %get-tuple-element.103), channel_id=1, source_target_pairs={{0,6},{1,7},{2,4},{3,5},{4,2},{5,3},{6,0},{7,1},{8,14},{9,15},{10,... | collective-permute-start | bytes 208904 | tf_op jit(solution)/shard_map/ppermute | solution.py:611
  55.3 1.0 %collective-permute-done.22 = f32[2,128,128]{2,1,0:T(8,128)S(1)} collective-permute-done((f32[2,128,128]{2,1,0:T(8,128)S(1)}, f32[2,128,128]{2,1,0:T(8,128)S(1)}, u32[]{:S(2)}, u32[]{:S(2)}) %collective-permute-start.22) | collective-permute-done | bytes 131104 | tf_op jit(solution)/shard_map/ppermute | solution.py:611
  56.4 1.6 %collective-permute-start.23 = (f32[2,128,128]{2,1,0:T(8,128)S(1)}, f32[2,128,128]{2,1,0:T(8,128)S(1)}, u32[]{:S(2)}, u32[]{:S(2)}) collective-permute-start(f32[2,128,128]{2,1,0:T(8,128)S(1)} %fusion.1), channel_id=1, source_target_pairs={{0,4},{1,5},{2,6},{3,7},{4,0},{5,1},{6,2},{7,3},{8,12},{9,13},{10,... | collective-permute-start | bytes 393224 | tf_op jit(solution)/shard_map/ppermute | solution.py:611
  57.9 1.7 %collective-permute-done.17.refs_4_ = s16[272,128]{1,0:T(8,128)(2,1)S(1)} collective-permute-done((s16[272,128]{1,0:T(8,128)(2,1)S(1)}, s16[272,128]{1,0:T(8,128)(2,1)S(1)}, u32[]{:S(2)}, u32[]{:S(2)}) %collective-permute-start.17) | collective-permute-done | bytes 69664 | tf_op jit(solution)/shard_map/ppermute | solution.py:611
  59.6 0.1 code.1.refs_0_
  59.8 3.4 %collective-permute-start.20 = (s16[272,128]{1,0:T(8,128)(2,1)S(1)}, s16[272,128]{1,0:T(8,128)(2,1)S(1)}, u32[]{:S(2)}, u32[]{:S(2)}) collective-permute-start(s16[272,128]{1,0:T(8,128)(2,1)S(1)} %code.1.refs_0_), channel_id=1, source_target_pairs={{0,24},{8,16},{16,8},{24,0},{1,25},{9,17},{17,9},{25,1},{2,26},{10... | collective-permute-start | bytes 208904 | tf_op jit(solution)/shard_map/ppermute | solution.py:611
  63.2 1.0 %collective-permute-start.18 = (s16[272,128]{1,0:T(8,128)(2,1)S(1)}, s16[272,128]{1,0:T(8,128)(2,1)S(1)}, u32[]{:S(2)}, u32[]{:S(2)}) collective-permute-start(s16[272,128]{1,0:T(8,128)(2,1)S(1)} %code.1.refs_0_), channel_id=1, source_target_pairs={{0,8},{8,0},{16,24},{24,16},{1,9},{9,1},{17,25},{25,17},{2,10},{10... | collective-permute-start | bytes 208904 | tf_op jit(solution)/shard_map/ppermute | solution.py:611
  64.3 5.6 %factor.1.inv_ref = f32[2,128,128]{2,1,0:T(8,128)S(1)} custom-call(s32[2]{0:T(128)S(1)} %copy-done.1, f32[2,128,128]{2,1,0:T(8,128)S(1)} %add.11.gram_ref), custom_call_target="tpu_custom_call" | custom-call | tf_op jit(solution)/shard_map/factor/pallas_call | solution.py:495
  69.9 0.2 code_sum.1.refs_0_
  70.1 1.5 %collective-permute-start.24 = (s16[272,128]{1,0:T(8,128)(2,1)S(1)}, s16[272,128]{1,0:T(8,128)(2,1)S(1)}, u32[]{:S(2)}, u32[]{:S(2)}) collective-permute-start(s16[272,128]{1,0:T(8,128)(2,1)S(1)} %code_sum.1.refs_0_), channel_id=1, source_target_pairs={{0,6},{1,7},{2,4},{3,5},{4,2},{5,3},{6,0},{7,1},{8,14},{9,15},{10,... | collective-permute-start | bytes 208904 | tf_op jit(solution)/shard_map/ppermute | solution.py:611
  71.6 1.5 %collective-permute-start.28 = (s16[272,128]{1,0:T(8,128)(2,1)S(1)}, s16[272,128]{1,0:T(8,128)(2,1)S(1)}, u32[]{:S(2)}, u32[]{:S(2)}) collective-permute-start(s16[272,128]{1,0:T(8,128)(2,1)S(1)} %code_sum.1.refs_0_), channel_id=1, source_target_pairs={{0,4},{1,5},{2,6},{3,7},{4,0},{5,1},{6,2},{7,3},{8,12},{9,13},{10,... | collective-permute-start | bytes 208904 | tf_op jit(solution)/shard_map/ppermute | solution.py:611
  73.1 0.5 collective-permute-start.26
  73.6 1.4 %factor_p.1 = (f32[2,1024,128]{2,1,0:T(8,128)}, bf16[2,1024,384]{2,1,0:T(8,128)(2,1)S(1)}) custom-call(f32[2,128,128]{2,1,0:T(8,128)S(1)} %factor.1.inv_ref, s16[528,128]{1,0:T(8,128)(2,1)S(1)} %add_code.7.code_ref.refs_0_, s16[528,128]{1,0:T(8,128)(2,1)S(1)} %collective-permute-done.11.code_ref.refs_1_, s16[528,128]{1,0:T(8,128)(2,1)S(1)} %add_code.6.code_ref.refs_2_, ...), custom_call_target="tpu_custom_call" | custom-call | tf_op jit(solution)/shard_map/factor_p/pallas_call | solution.py:530
  75.1 0.3 collective-permute-done.24.refs_6_
  75.4 0.7 collective-permute-done.28.refs_4_
  76.1 1.3 %collective-permute-done.26.refs_2_ = s16[272,128]{1,0:T(8,128)(2,1)S(1)} collective-permute-done((s16[272,128]{1,0:T(8,128)(2,1)S(1)}, s16[272,128]{1,0:T(8,128)(2,1)S(1)}, u32[]{:S(2)}, u32[]{:S(2)}) %collective-permute-start.26) | collective-permute-done | bytes 69664 | tf_op jit(solution)/shard_map/ppermute | solution.py:611
  77.4 0.5 collective-permute-start.30
  77.9 0.7 collective-permute-done.27.refs_3_
  78.7 0.2 collective-permute-done.30.refs_7_
  78.8 4.5 %error.1 = (f32[2,1,1024,1024]{3,2,1,0:T(8,128)}, f32[2,1024,128]{2,1,0:T(8,128)}) custom-call(bf16[2,1024,384]{2,1,0:T(8,128)(2,1)S(1)} %get-tuple-element.115.p3_ref, f32[2,128,128]{2,1,0:T(8,128)S(1)} %factor.1.inv_ref, s16[272,128]{1,0:T(8,128)(2,1)S(1)} %code_sum.1.refs_0_, s16[272,128]{1,0:T(8,128)(2,1)S(1)} %collective-permute-done.25.refs_1_, ...), custom_call_target="tpu_custom_call" | custom-call | tf_op jit(solution)/shard_map/error/pallas_call | solution.py:586
  (26 shorter events, 0.1 us)
Async XLA Ops:
  0.6 12.5 %copy-start = (bf16[2,512,128]{2,1,0:T(8,128)(2,1)S(1)}, bf16[2,512,128]{2,1,0:T(8,128)(2,1)}, u32[]{:S(2)}) copy-start(bf16[2,512,128]{2,1,0:T(8,128)(2,1)} %refs_0_.2) | copy-start | bytes 786436
  0.6 12.1 %collective-permute-start.1 = (bf16[2,512,128]{2,1,0:T(8,128)(2,1)}, bf16[2,512,128]{2,1,0:T(8,128)(2,1)S(1)}, u32[]{:S(2)}, u32[]{:S(2)}) collective-permute-start(bf16[2,512,128]{2,1,0:T(8,128)(2,1)} %refs_0_.2), channel_id=1, source_target_pairs={{0,4},{1,5},{2,6},{3,7},{4,0},{5,1},{6,2},{7,3},{8,12},{9,13},{10,... | collective-permute-start | bytes 786440 | tf_op jit(solution)/shard_map/ppermute | solution.py:611
  3.7 9.4 %collective-permute-start = (bf16[2,512,128]{2,1,0:T(8,128)(2,1)}, bf16[2,512,128]{2,1,0:T(8,128)(2,1)S(1)}, u32[]{:S(2)}, u32[]{:S(2)}) collective-permute-start(bf16[2,512,128]{2,1,0:T(8,128)(2,1)} %refs_0_.2), channel_id=1, source_target_pairs={{0,2},{1,3},{2,0},{3,1},{4,6},{5,7},{6,4},{7,5},{8,10},{9,11},{10,... | collective-permute-start | bytes 786440 | tf_op jit(solution)/shard_map/ppermute | solution.py:611
  5.2 11.9 %collective-permute-start.2 = (bf16[2,512,128]{2,1,0:T(8,128)(2,1)}, bf16[2,512,128]{2,1,0:T(8,128)(2,1)S(1)}, u32[]{:S(2)}, u32[]{:S(2)}) collective-permute-start(bf16[2,512,128]{2,1,0:T(8,128)(2,1)} %refs_0_.2), channel_id=1, source_target_pairs={{0,6},{1,7},{2,4},{3,5},{4,2},{5,3},{6,0},{7,1},{8,14},{9,15},{10,... | collective-permute-start | bytes 786440 | tf_op jit(solution)/shard_map/ppermute | solution.py:611
  13.1 3.9 %collective-permute-start.3 = (bf16[2,512,128]{2,1,0:T(8,128)(2,1)S(1)}, bf16[2,512,128]{2,1,0:T(8,128)(2,1)S(1)}, u32[]{:S(2)}, u32[]{:S(2)}) collective-permute-start(bf16[2,512,128]{2,1,0:T(8,128)(2,1)S(1)} %copy-done), channel_id=1, source_target_pairs={{0,1},{1,0},{2,3},{3,2},{4,5},{5,4},{6,7},{7,6},{8,9},{9,8},{10,11... | collective-permute-start | bytes 786440 | tf_op jit(solution)/shard_map/ppermute | solution.py:611
  13.1 3.9 %collective-permute-start.4 = (bf16[2,512,128]{2,1,0:T(8,128)(2,1)S(1)}, bf16[2,512,128]{2,1,0:T(8,128)(2,1)S(1)}, u32[]{:S(2)}, u32[]{:S(2)}) collective-permute-start(bf16[2,512,128]{2,1,0:T(8,128)(2,1)S(1)} %collective-permute-done.refs_2_), channel_id=1, source_target_pairs={{0,1},{1,0},{2,3},{3,2},{4,5},{5,4},{6,7},{7,6},{8,9},{9,8},{10,11... | collective-permute-start | bytes 786440 | tf_op jit(solution)/shard_map/ppermute | solution.py:611
  13.6 3.4 %collective-permute-start.5 = (bf16[2,512,128]{2,1,0:T(8,128)(2,1)S(1)}, bf16[2,512,128]{2,1,0:T(8,128)(2,1)S(1)}, u32[]{:S(2)}, u32[]{:S(2)}) collective-permute-start(bf16[2,512,128]{2,1,0:T(8,128)(2,1)S(1)} %collective-permute-done.1.refs_4_), channel_id=1, source_target_pairs={{0,1},{1,0},{2,3},{3,2},{4,5},{5,4},{6,7},{7,6},{8,9},{9,8},{10,11... | collective-permute-start | bytes 786440 | tf_op jit(solution)/shard_map/ppermute | solution.py:611
  17.1 1.6 %collective-permute-start.6 = (bf16[2,512,128]{2,1,0:T(8,128)(2,1)S(1)}, bf16[2,512,128]{2,1,0:T(8,128)(2,1)S(1)}, u32[]{:S(2)}, u32[]{:S(2)}) collective-permute-start(bf16[2,512,128]{2,1,0:T(8,128)(2,1)S(1)} %collective-permute-done.2.refs_1_.refs_6_), channel_id=1, source_target_pairs={{0,1},{1,0},{2,3},{3,2},{4,5},{5,4},{6,7},{7,6},{8,9},{9,8},{10,11... | collective-permute-start | bytes 786440 | tf_op jit(solution)/shard_map/ppermute | solution.py:611
  19.5 6.1 %collective-permute-start.9 = (s16[528,128]{1,0:T(8,128)(2,1)S(1)}, s16[528,128]{1,0:T(8,128)(2,1)S(1)}, u32[]{:S(2)}, u32[]{:S(2)}) collective-permute-start(s16[528,128]{1,0:T(8,128)(2,1)S(1)} %get-tuple-element.83), channel_id=1, source_target_pairs={{0,8},{8,0},{16,24},{24,16},{1,9},{9,1},{17,25},{25,17},{2,10},{10... | collective-permute-start | bytes 405512 | tf_op jit(solution)/shard_map/ppermute | solution.py:611
  22.2 6.6 %collective-permute-start.7 = (s16[528,128]{1,0:T(8,128)(2,1)S(1)}, s16[528,128]{1,0:T(8,128)(2,1)S(1)}, u32[]{:S(2)}, u32[]{:S(2)}) collective-permute-start(s16[528,128]{1,0:T(8,128)(2,1)S(1)} %get-tuple-element.76), channel_id=1, source_target_pairs={{0,8},{8,0},{16,24},{24,16},{1,9},{9,1},{17,25},{25,17},{2,10},{10... | collective-permute-start | bytes 405512 | tf_op jit(solution)/shard_map/ppermute | solution.py:611
  25.8 12.5 %collective-permute-start.10 = (s16[528,128]{1,0:T(8,128)(2,1)S(1)}, s16[528,128]{1,0:T(8,128)(2,1)S(1)}, u32[]{:S(2)}, u32[]{:S(2)}) collective-permute-start(s16[528,128]{1,0:T(8,128)(2,1)S(1)} %add_code.5.mine_ref), channel_id=1, source_target_pairs={{0,16},{8,24},{16,0},{24,8},{1,17},{9,25},{17,1},{25,9},{2,18},{10... | collective-permute-start | bytes 405512 | tf_op jit(solution)/shard_map/ppermute | solution.py:611
  28.9 11.2 %collective-permute-start.8 = (s16[528,128]{1,0:T(8,128)(2,1)S(1)}, s16[528,128]{1,0:T(8,128)(2,1)S(1)}, u32[]{:S(2)}, u32[]{:S(2)}) collective-permute-start(s16[528,128]{1,0:T(8,128)(2,1)S(1)} %add_code.4.mine_ref), channel_id=1, source_target_pairs={{0,16},{8,24},{16,0},{24,8},{1,17},{9,25},{17,1},{25,9},{2,18},{10... | collective-permute-start | bytes 405512 | tf_op jit(solution)/shard_map/ppermute | solution.py:611
  40.1 6.0 %collective-permute-start.12 = (s16[528,128]{1,0:T(8,128)(2,1)S(1)}, s16[528,128]{1,0:T(8,128)(2,1)S(1)}, u32[]{:S(2)}, u32[]{:S(2)}) collective-permute-start(s16[528,128]{1,0:T(8,128)(2,1)S(1)} %add_code.6.code_ref.refs_2_), channel_id=1, source_target_pairs={{0,8},{8,0},{16,24},{24,16},{1,9},{9,1},{17,25},{25,17},{2,10},{10... | collective-permute-start | bytes 405512 | tf_op jit(solution)/shard_map/ppermute | solution.py:611
  41.5 22.7 %copy-start.1 = (s32[2]{0:T(128)S(1)}, s32[2]{0:T(128)}, u32[]{:S(2)}) copy-start(s32[2]{0:T(128)} %ranks_ref.3) | copy-start | bytes 28
  41.5 6.0 %collective-permute-start.11 = (s16[528,128]{1,0:T(8,128)(2,1)S(1)}, s16[528,128]{1,0:T(8,128)(2,1)S(1)}, u32[]{:S(2)}, u32[]{:S(2)}) collective-permute-start(s16[528,128]{1,0:T(8,128)(2,1)S(1)} %add_code.7.code_ref.refs_0_), channel_id=1, source_target_pairs={{0,8},{8,0},{16,24},{24,16},{1,9},{9,1},{17,25},{25,17},{2,10},{10... | collective-permute-start | bytes 405512 | tf_op jit(solution)/shard_map/ppermute | solution.py:611
  48.5 1.4 %collective-permute-start.21 = (f32[2,128,128]{2,1,0:T(8,128)S(1)}, f32[2,128,128]{2,1,0:T(8,128)S(1)}, u32[]{:S(2)}, u32[]{:S(2)}) collective-permute-start(f32[2,128,128]{2,1,0:T(8,128)S(1)} %pad_maximum_fusion), channel_id=1, source_target_pairs={{0,1},{1,0},{2,3},{3,2},{4,5},{5,4},{6,7},{7,6},{8,9},{9,8},{10,11... | collective-permute-start | bytes 393224 | tf_op jit(solution)/shard_map/ppermute | solution.py:611
  48.6 2.9 %collective-permute-start.14 = (f32[512,128]{1,0:T(8,128)S(1)}, f32[512,128]{1,0:T(8,128)S(1)}, u32[]{:S(2)}, u32[]{:S(2)}) collective-permute-start(f32[512,128]{1,0:T(8,128)S(1)} %get-tuple-element.98), channel_id=1, source_target_pairs={{0,1},{1,0},{2,3},{3,2},{4,5},{5,4},{6,7},{7,6},{8,9},{9,8},{10,11... | collective-permute-start | bytes 786440 | tf_op jit(solution)/shard_map/ppermute | solution.py:611
  49.1 2.4 %collective-permute-start.13 = (f32[512,128]{1,0:T(8,128)S(1)}, f32[512,128]{1,0:T(8,128)S(1)}, u32[]{:S(2)}, u32[]{:S(2)}) collective-permute-start(f32[512,128]{1,0:T(8,128)S(1)} %get-tuple-element.97), channel_id=1, source_target_pairs={{0,1},{1,0},{2,3},{3,2},{4,5},{5,4},{6,7},{7,6},{8,9},{9,8},{10,11... | collective-permute-start | bytes 786440 | tf_op jit(solution)/shard_map/ppermute | solution.py:611
  50.0 6.4 %collective-permute-start.22 = (f32[2,128,128]{2,1,0:T(8,128)S(1)}, f32[2,128,128]{2,1,0:T(8,128)S(1)}, u32[]{:S(2)}, u32[]{:S(2)}) collective-permute-start(f32[2,128,128]{2,1,0:T(8,128)S(1)} %fusion), channel_id=1, source_target_pairs={{0,2},{1,3},{2,0},{3,1},{4,6},{5,7},{6,4},{7,5},{8,10},{9,11},{10,... | collective-permute-start | bytes 393224 | tf_op jit(solution)/shard_map/ppermute | solution.py:611
  51.8 6.2 %collective-permute-start.15 = (s16[272,128]{1,0:T(8,128)(2,1)S(1)}, s16[272,128]{1,0:T(8,128)(2,1)S(1)}, u32[]{:S(2)}, u32[]{:S(2)}) collective-permute-start(s16[272,128]{1,0:T(8,128)(2,1)S(1)} %get-tuple-element.101), channel_id=1, source_target_pairs={{0,2},{1,3},{2,0},{3,1},{4,6},{5,7},{6,4},{7,5},{8,10},{9,11},{10,... | collective-permute-start | bytes 208904 | tf_op jit(solution)/shard_map/ppermute | solution.py:611
  52.5 5.4 %collective-permute-start.16 = (s16[272,128]{1,0:T(8,128)(2,1)S(1)}, s16[272,128]{1,0:T(8,128)(2,1)S(1)}, u32[]{:S(2)}, u32[]{:S(2)}) collective-permute-start(s16[272,128]{1,0:T(8,128)(2,1)S(1)} %get-tuple-element.102), channel_id=1, source_target_pairs={{0,4},{1,5},{2,6},{3,7},{4,0},{5,1},{6,2},{7,3},{8,12},{9,13},{10,... | collective-permute-start | bytes 208904 | tf_op jit(solution)/shard_map/ppermute | solution.py:611
  54.0 5.6 %collective-permute-start.17 = (s16[272,128]{1,0:T(8,128)(2,1)S(1)}, s16[272,128]{1,0:T(8,128)(2,1)S(1)}, u32[]{:S(2)}, u32[]{:S(2)}) collective-permute-start(s16[272,128]{1,0:T(8,128)(2,1)S(1)} %get-tuple-element.103), channel_id=1, source_target_pairs={{0,6},{1,7},{2,4},{3,5},{4,2},{5,3},{6,0},{7,1},{8,14},{9,15},{10,... | collective-permute-start | bytes 208904 | tf_op jit(solution)/shard_map/ppermute | solution.py:611
  56.4 7.9 %collective-permute-start.23 = (f32[2,128,128]{2,1,0:T(8,128)S(1)}, f32[2,128,128]{2,1,0:T(8,128)S(1)}, u32[]{:S(2)}, u32[]{:S(2)}) collective-permute-start(f32[2,128,128]{2,1,0:T(8,128)S(1)} %fusion.1), channel_id=1, source_target_pairs={{0,4},{1,5},{2,6},{3,7},{4,0},{5,1},{6,2},{7,3},{8,12},{9,13},{10,... | collective-permute-start | bytes 393224 | tf_op jit(solution)/shard_map/ppermute | solution.py:611
  59.8 10.1 %collective-permute-start.20 = (s16[272,128]{1,0:T(8,128)(2,1)S(1)}, s16[272,128]{1,0:T(8,128)(2,1)S(1)}, u32[]{:S(2)}, u32[]{:S(2)}) collective-permute-start(s16[272,128]{1,0:T(8,128)(2,1)S(1)} %code.1.refs_0_), channel_id=1, source_target_pairs={{0,24},{8,16},{16,8},{24,0},{1,25},{9,17},{17,9},{25,1},{2,26},{10... | collective-permute-start | bytes 208904 | tf_op jit(solution)/shard_map/ppermute | solution.py:611
  63.2 6.7 %collective-permute-start.19 = (s16[272,128]{1,0:T(8,128)(2,1)S(1)}, s16[272,128]{1,0:T(8,128)(2,1)S(1)}, u32[]{:S(2)}, u32[]{:S(2)}) collective-permute-start(s16[272,128]{1,0:T(8,128)(2,1)S(1)} %code.1.refs_0_), channel_id=1, source_target_pairs={{0,16},{8,24},{16,0},{24,8},{1,17},{9,25},{17,1},{25,9},{2,18},{10... | collective-permute-start | bytes 208904 | tf_op jit(solution)/shard_map/ppermute | solution.py:611
  63.2 6.7 %collective-permute-start.18 = (s16[272,128]{1,0:T(8,128)(2,1)S(1)}, s16[272,128]{1,0:T(8,128)(2,1)S(1)}, u32[]{:S(2)}, u32[]{:S(2)}) collective-permute-start(s16[272,128]{1,0:T(8,128)(2,1)S(1)} %code.1.refs_0_), channel_id=1, source_target_pairs={{0,8},{8,0},{16,24},{24,16},{1,9},{9,1},{17,25},{25,17},{2,10},{10... | collective-permute-start | bytes 208904 | tf_op jit(solution)/shard_map/ppermute | solution.py:611
  70.1 5.3 %collective-permute-start.24 = (s16[272,128]{1,0:T(8,128)(2,1)S(1)}, s16[272,128]{1,0:T(8,128)(2,1)S(1)}, u32[]{:S(2)}, u32[]{:S(2)}) collective-permute-start(s16[272,128]{1,0:T(8,128)(2,1)S(1)} %code_sum.1.refs_0_), channel_id=1, source_target_pairs={{0,6},{1,7},{2,4},{3,5},{4,2},{5,3},{6,0},{7,1},{8,14},{9,15},{10,... | collective-permute-start | bytes 208904 | tf_op jit(solution)/shard_map/ppermute | solution.py:611
  71.6 4.5 %collective-permute-start.28 = (s16[272,128]{1,0:T(8,128)(2,1)S(1)}, s16[272,128]{1,0:T(8,128)(2,1)S(1)}, u32[]{:S(2)}, u32[]{:S(2)}) collective-permute-start(s16[272,128]{1,0:T(8,128)(2,1)S(1)} %code_sum.1.refs_0_), channel_id=1, source_target_pairs={{0,4},{1,5},{2,6},{3,7},{4,0},{5,1},{6,2},{7,3},{8,12},{9,13},{10,... | collective-permute-start | bytes 208904 | tf_op jit(solution)/shard_map/ppermute | solution.py:611
  73.1 4.3 %collective-permute-start.26 = (s16[272,128]{1,0:T(8,128)(2,1)S(1)}, s16[272,128]{1,0:T(8,128)(2,1)S(1)}, u32[]{:S(2)}, u32[]{:S(2)}) collective-permute-start(s16[272,128]{1,0:T(8,128)(2,1)S(1)} %code_sum.1.refs_0_), channel_id=1, source_target_pairs={{0,2},{1,3},{2,0},{3,1},{4,6},{5,7},{6,4},{7,5},{8,10},{9,11},{10,... | collective-permute-start | bytes 208904 | tf_op jit(solution)/shard_map/ppermute | solution.py:611
  73.6 4.3 %collective-permute-start.25 = (s16[272,128]{1,0:T(8,128)(2,1)S(1)}, s16[272,128]{1,0:T(8,128)(2,1)S(1)}, u32[]{:S(2)}, u32[]{:S(2)}) collective-permute-start(s16[272,128]{1,0:T(8,128)(2,1)S(1)} %code_sum.1.refs_0_), channel_id=1, source_target_pairs={{0,1},{1,0},{2,3},{3,2},{4,5},{5,4},{6,7},{7,6},{8,9},{9,8},{10,11... | collective-permute-start | bytes 208904 | tf_op jit(solution)/shard_map/ppermute | solution.py:611
  76.1 1.8 %collective-permute-start.29 = (s16[272,128]{1,0:T(8,128)(2,1)S(1)}, s16[272,128]{1,0:T(8,128)(2,1)S(1)}, u32[]{:S(2)}, u32[]{:S(2)}) collective-permute-start(s16[272,128]{1,0:T(8,128)(2,1)S(1)} %collective-permute-done.28.refs_4_), channel_id=1, source_target_pairs={{0,1},{1,0},{2,3},{3,2},{4,5},{5,4},{6,7},{7,6},{8,9},{9,8},{10,11... | collective-permute-start | bytes 208904 | tf_op jit(solution)/shard_map/ppermute | solution.py:611
  77.4 1.3 %collective-permute-start.27 = (s16[272,128]{1,0:T(8,128)(2,1)S(1)}, s16[272,128]{1,0:T(8,128)(2,1)S(1)}, u32[]{:S(2)}, u32[]{:S(2)}) collective-permute-start(s16[272,128]{1,0:T(8,128)(2,1)S(1)} %collective-permute-done.26.refs_2_), channel_id=1, source_target_pairs={{0,1},{1,0},{2,3},{3,2},{4,5},{5,4},{6,7},{7,6},{8,9},{9,8},{10,11... | collective-permute-start | bytes 208904 | tf_op jit(solution)/shard_map/ppermute | solution.py:611
  77.4 1.4 %collective-permute-start.30 = (s16[272,128]{1,0:T(8,128)(2,1)S(1)}, s16[272,128]{1,0:T(8,128)(2,1)S(1)}, u32[]{:S(2)}, u32[]{:S(2)}) collective-permute-start(s16[272,128]{1,0:T(8,128)(2,1)S(1)} %collective-permute-done.24.refs_6_), channel_id=1, source_target_pairs={{0,1},{1,0},{2,3},{3,2},{4,5},{5,4},{6,7},{7,6},{8,9},{9,8},{10,11... | collective-permute-start | bytes 208904 | tf_op jit(solution)/shard_map/ppermute | solution.py:611

commit v6 on v5

--- a/solution.py
+++ b/solution.py
@@ -734,9 +734,10 @@
         mine, in_t = tie(mines[m], inputs_t)
         grad = full(m, held, in_t, blocks)
         for bit in steps:
-            theirs, grad = tie(across(mine, "dp", bit), grad)
-            if late is not None:
-                theirs, *own[late] = tie(theirs, *own[late])
+            if late is None:
+                theirs, grad = tie(across(mine, "dp", bit), grad)
+            else:
+                theirs, grad, *own[late] = tie(across(mine, "dp", bit), grad, *own[late])
             mine = add_code(mine, theirs)
         mines[m] = mine
         full_grad.insert(0, grad)

time: 83.6 us -> 82.4 us (0.986)
  no operation moved by 1% of the time
where the time goes in v6:
time: 82.4 us; the launch traced here: 82.3 us
  starting transfers between devices  30.5 us (37%)
  Pallas kernels  28.7 us (35%)
  waiting for transfers between devices  21.9 us (27%)
  between operations  1.01 us (1%)
    ppermute x31, starting transfers between devices, across(): return lax.ppermute(x, axis, [(i, i ^ bit) for i in range(size)])  30.5 us
    ppermute x31, waiting for transfers between devices, across(): return lax.ppermute(x, axis, [(i, i ^ bit) for i in range(size)])  21.9 us
    pallas_call x1, Pallas kernels, feedback_q(): pl.pallas_call(feedback_q_kernel, in_specs=[far] * 4, out_specs=[VMEM] *...  7.55 us
    pallas_call x1, Pallas kernels, factor(): pl.pallas_call(factor_kernel, in_specs=[SMEM, VMEM], out_specs=VMEM, out_...  5.61 us
    pallas_call x1, Pallas kernels, error(): pl.pallas_call(functools.partial(error_kernel, count, len(codes), groups)...  4.47 us
    pallas_call x2, Pallas kernels, full(): pl.pallas_call(functools.partial(full_kernel, m), in_specs=[VMEM] * (2 +...  3.13 us
    pallas_call x2, Pallas kernels, other_half(): pl.pallas_call(functools.partial(other_half_kernel, halved), in_specs=[VM...  1.69 us
    pallas_call x2, Pallas kernels, left_code(): pl.pallas_call(functools.partial(left_code_kernel, m, keys), in_specs=[VM...  1.69 us
  transfers between devices with their start and end apart: 31, of which 16 were waited for; matrix products, arithmetic and copies ran while one was open for 0% of the time, Pallas kernels for 27%

profile of v6, /device:TPU:0, one launch (start us, length us, event | category | flops | bytes accessed | tf_op | source)
XLA Modules:
  0.0 82.3 jit_solution(5103776109572283529)
XLA Ops:
  0.6 3.0 %collective-permute-start.1 = (bf16[2,512,128]{2,1,0:T(8,128)(2,1)}, bf16[2,512,128]{2,1,0:T(8,128)(2,1)S(1)}, u32[]{:S(2)}, u32[]{:S(2)}) collective-permute-start(bf16[2,512,128]{2,1,0:T(8,128)(2,1)} %refs_0_.2), channel_id=1, source_target_pairs={{0,4},{1,5},{2,6},{3,7},{4,0},{5,1},{6,2},{7,3},{8,12},{9,13},{10,... | collective-permute-start | bytes 786440 | tf_op jit(solution)/shard_map/ppermute | solution.py:611
  3.7 1.5 %collective-permute-start = (bf16[2,512,128]{2,1,0:T(8,128)(2,1)}, bf16[2,512,128]{2,1,0:T(8,128)(2,1)S(1)}, u32[]{:S(2)}, u32[]{:S(2)}) collective-permute-start(bf16[2,512,128]{2,1,0:T(8,128)(2,1)} %refs_0_.2), channel_id=1, source_target_pairs={{0,2},{1,3},{2,0},{3,1},{4,6},{5,7},{6,4},{7,5},{8,10},{9,11},{10,... | collective-permute-start | bytes 786440 | tf_op jit(solution)/shard_map/ppermute | solution.py:611
  5.2 0.0 collective-permute-start.2
  5.2 7.6 %feedback_q.1 = (f32[2,1024,1024]{2,1,0:T(8,128)S(1)}, f32[2,1024,128]{2,1,0:T(8,128)S(1)}, bf16[2,1024,256]{2,1,0:T(8,128)(2,1)S(1)}, bf16[1024,512]{1,0:T(8,128)(2,1)S(1)}) custom-call(s32[2]{0:T(128)} %ranks_ref.3, f32[2,1,1024,1024]{3,2,1,0:T(8,128)} %fb_ref.1, f32[2,1024,128]{2,1,0:T(8,128)} %q_ref.1, bf16[512,1024]{1,0:T(8,128)(2,1)} %in_ref.1), custom_call_target="tpu_custom_call" | custom-call | tf_op jit(solution)/shard_map/feedback_q/pallas_call | solution.py:96
  12.8 0.3 collective-permute-done.refs_2_
  13.1 0.5 collective-permute-start.4
  13.6 0.0 collective-permute-start.5
  13.6 3.4 %collective-permute-done.2.refs_1_.refs_6_ = bf16[2,512,128]{2,1,0:T(8,128)(2,1)S(1)} collective-permute-done((bf16[2,512,128]{2,1,0:T(8,128)(2,1)}, bf16[2,512,128]{2,1,0:T(8,128)(2,1)S(1)}, u32[]{:S(2)}, u32[]{:S(2)}) %collective-permute-start.2) | collective-permute-done | bytes 262176 | tf_op jit(solution)/shard_map/ppermute | solution.py:611
  17.1 0.0 collective-permute-done.5.refs_5_
  17.1 0.1 collective-permute-start.6
  17.2 0.6 begin.1.refs_0_
  17.8 0.9 %collective-permute-done.6.refs_2_.refs_7_ = bf16[2,512,128]{2,1,0:T(8,128)(2,1)S(1)} collective-permute-done((bf16[2,512,128]{2,1,0:T(8,128)(2,1)S(1)}, bf16[2,512,128]{2,1,0:T(8,128)(2,1)S(1)}, u32[]{:S(2)}, u32[]{:S(2)}) %collective-permute-start.6) | collective-permute-done | bytes 262176 | tf_op jit(solution)/shard_map/ppermute | solution.py:611
  18.7 0.8 %left_code_1.1 = (f32[512,128]{1,0:T(8,128)S(1)}, s16[528,128]{1,0:T(8,128)(2,1)S(1)}) custom-call(bf16[2,1024,256]{2,1,0:T(8,128)(2,1)S(1)} %get-tuple-element.64.q2_ref, bf16[1024,512]{1,0:T(8,128)(2,1)S(1)} %get-tuple-element.82.in_ref, f32[2,1024,128]{2,1,0:T(8,128)S(1)} %get-tuple-element.66.fbq_ref, f32[2,512,256]{2,1,0:T(8,128)S(1)} %begin.1.refs_0_, ...), custom_call_target="tpu_custom_call" | custom-call | tf_op jit(solution)/shard_map/left_code_1/pallas_call | solution.py:241
  19.5 1.8 %collective-permute-start.9 = (s16[528,128]{1,0:T(8,128)(2,1)S(1)}, s16[528,128]{1,0:T(8,128)(2,1)S(1)}, u32[]{:S(2)}, u32[]{:S(2)}) collective-permute-start(s16[528,128]{1,0:T(8,128)(2,1)S(1)} %get-tuple-element.80), channel_id=1, source_target_pairs={{0,8},{8,0},{16,24},{24,16},{1,9},{9,1},{17,25},{25,17},{2,10},{10... | collective-permute-start | bytes 405512 | tf_op jit(solution)/shard_map/ppermute | solution.py:611
  21.3 0.8 %left_code_0.1 = (f32[512,128]{1,0:T(8,128)S(1)}, s16[528,128]{1,0:T(8,128)(2,1)S(1)}) custom-call(bf16[2,1024,256]{2,1,0:T(8,128)(2,1)S(1)} %get-tuple-element.64.q2_ref, bf16[1024,512]{1,0:T(8,128)(2,1)S(1)} %get-tuple-element.82.in_ref, f32[2,1024,128]{2,1,0:T(8,128)S(1)} %get-tuple-element.66.fbq_ref, f32[2,512,256]{2,1,0:T(8,128)S(1)} %begin.1.refs_0_, ...), custom_call_target="tpu_custom_call" | custom-call | tf_op jit(solution)/shard_map/left_code_0/pallas_call | solution.py:241
  22.2 0.4 collective-permute-start.7
  22.5 3.1 %collective-permute-done.9.theirs_ref = s16[528,128]{1,0:T(8,128)(2,1)S(1)} collective-permute-done((s16[528,128]{1,0:T(8,128)(2,1)S(1)}, s16[528,128]{1,0:T(8,128)(2,1)S(1)}, u32[]{:S(2)}, u32[]{:S(2)}) %collective-permute-start.9) | collective-permute-done | bytes 135200 | tf_op jit(solution)/shard_map/ppermute | solution.py:611
  25.7 0.1 add_code.5.mine_ref
  25.8 3.0 %collective-permute-start.10 = (s16[528,128]{1,0:T(8,128)(2,1)S(1)}, s16[528,128]{1,0:T(8,128)(2,1)S(1)}, u32[]{:S(2)}, u32[]{:S(2)}) collective-permute-start(s16[528,128]{1,0:T(8,128)(2,1)S(1)} %add_code.5.mine_ref), channel_id=1, source_target_pairs={{0,16},{8,24},{16,0},{24,8},{1,17},{9,25},{17,1},{25,9},{2,18},{10... | collective-permute-start | bytes 405512 | tf_op jit(solution)/shard_map/ppermute | solution.py:611
  28.8 0.1 add_code.4.mine_ref
  28.9 2.8 %collective-permute-start.8 = (s16[528,128]{1,0:T(8,128)(2,1)S(1)}, s16[528,128]{1,0:T(8,128)(2,1)S(1)}, u32[]{:S(2)}, u32[]{:S(2)}) collective-permute-start(s16[528,128]{1,0:T(8,128)(2,1)S(1)} %add_code.4.mine_ref), channel_id=1, source_target_pairs={{0,16},{8,24},{16,0},{24,8},{1,17},{9,25},{17,1},{25,9},{2,18},{10... | collective-permute-start | bytes 405512 | tf_op jit(solution)/shard_map/ppermute | solution.py:611
  31.7 1.6 %full_0.1.full_ref.refs_8_ = f32[1024,1024]{1,0:T(8,128)S(1)} custom-call(f32[2,1024,1024]{2,1,0:T(8,128)S(1)} %get-tuple-element.77.held_ref, bf16[1024,512]{1,0:T(8,128)(2,1)S(1)} %get-tuple-element.82.in_ref, bf16[2,512,128]{2,1,0:T(8,128)(2,1)S(1)} %copy-done, bf16[2,512,128]{2,1,0:T(8,128)(2,1)S(1)} %collective-permute-done.3.refs_1_, ...), custom_call_target="tpu_custom_call" | custom-call | tf_op jit(solution)/shard_map/full_0/pallas_call | solution.py:301
  33.2 1.6 %full_1.1.full_ref.refs_9_ = f32[1024,1024]{1,0:T(8,128)S(1)} custom-call(f32[2,1024,1024]{2,1,0:T(8,128)S(1)} %get-tuple-element.77.held_ref, bf16[1024,512]{1,0:T(8,128)(2,1)S(1)} %get-tuple-element.82.in_ref, bf16[2,512,128]{2,1,0:T(8,128)(2,1)S(1)} %copy-done, bf16[2,512,128]{2,1,0:T(8,128)(2,1)S(1)} %collective-permute-done.3.refs_1_, ...), custom_call_target="tpu_custom_call" | custom-call | tf_op jit(solution)/shard_map/full_1/pallas_call | solution.py:301
  34.8 3.5 %collective-permute-done.10.theirs_ref = s16[528,128]{1,0:T(8,128)(2,1)S(1)} collective-permute-done((s16[528,128]{1,0:T(8,128)(2,1)S(1)}, s16[528,128]{1,0:T(8,128)(2,1)S(1)}, u32[]{:S(2)}, u32[]{:S(2)}) %collective-permute-start.10) | collective-permute-done | bytes 135200 | tf_op jit(solution)/shard_map/ppermute | solution.py:611
  38.3 0.2 add_code.6.code_ref.refs_2_
  38.5 0.4 collective-permute-start.12
  39.0 0.7 own_half_1.1
  39.7 0.6 collective-permute-done.8.theirs_ref
  40.2 0.2 add_code.7.code_ref.refs_0_
  40.4 0.0 copy-start.1
  40.4 1.2 %collective-permute-start.11 = (s16[528,128]{1,0:T(8,128)(2,1)S(1)}, s16[528,128]{1,0:T(8,128)(2,1)S(1)}, u32[]{:S(2)}, u32[]{:S(2)}) collective-permute-start(s16[528,128]{1,0:T(8,128)(2,1)S(1)} %add_code.7.code_ref.refs_0_), channel_id=1, source_target_pairs={{0,8},{8,0},{16,24},{24,16},{1,9},{9,1},{17,25},{25,17},{2,10},{10... | collective-permute-start | bytes 405512 | tf_op jit(solution)/shard_map/ppermute | solution.py:611
  41.6 0.7 own_half_0.1
  42.3 2.6 %collective-permute-done.12.code_ref.refs_3_ = s16[528,128]{1,0:T(8,128)(2,1)S(1)} collective-permute-done((s16[528,128]{1,0:T(8,128)(2,1)S(1)}, s16[528,128]{1,0:T(8,128)(2,1)S(1)}, u32[]{:S(2)}, u32[]{:S(2)}) %collective-permute-start.12) | collective-permute-done | bytes 135200 | tf_op jit(solution)/shard_map/ppermute | solution.py:611
  44.9 0.8 other_half_1.1
  45.7 0.7 collective-permute-done.11.code_ref.refs_1_
  46.4 0.9 %other_half_0.1 = (f32[512,128]{1,0:T(8,128)S(1)}, f32[512,128]{1,0:T(8,128)S(1)}, f32[128,128]{1,0:T(8,128)S(1)}) custom-call(f32[1024,1024]{1,0:T(8,128)S(1)} %full_0.1.full_ref.refs_8_, s16[528,128]{1,0:T(8,128)(2,1)S(1)} %collective-permute-done.11.code_ref.refs_1_, f32[128,1024]{1,0:T(8,128)S(1)} %get-tuple-element.89.total_ref, ...), custom_call_target="tpu_custom_call" | custom-call | tf_op jit(solution)/shard_map/other_half_0/pallas_call | solution.py:364
  47.3 0.1 collective-permute-start.21
  47.4 0.5 collective-permute-start.14
  47.9 0.1 collective-permute-start.13
  48.0 0.8 collective-permute-done.21
  48.8 1.5 %collective-permute-start.22 = (f32[2,128,128]{2,1,0:T(8,128)S(1)}, f32[2,128,128]{2,1,0:T(8,128)S(1)}, u32[]{:S(2)}, u32[]{:S(2)}) collective-permute-start(f32[2,128,128]{2,1,0:T(8,128)S(1)} %fusion), channel_id=1, source_target_pairs={{0,2},{1,3},{2,0},{3,1},{4,6},{5,7},{6,4},{7,5},{8,10},{9,11},{10,... | collective-permute-start | bytes 393224 | tf_op jit(solution)/shard_map/ppermute | solution.py:611
  50.3 0.3 part_2.1
  50.6 0.7 collective-permute-start.15
  51.3 1.5 %collective-permute-start.16 = (s16[272,128]{1,0:T(8,128)(2,1)S(1)}, s16[272,128]{1,0:T(8,128)(2,1)S(1)}, u32[]{:S(2)}, u32[]{:S(2)}) collective-permute-start(s16[272,128]{1,0:T(8,128)(2,1)S(1)} %get-tuple-element.100), channel_id=1, source_target_pairs={{0,4},{1,5},{2,6},{3,7},{4,0},{5,1},{6,2},{7,3},{8,12},{9,13},{10,... | collective-permute-start | bytes 208904 | tf_op jit(solution)/shard_map/ppermute | solution.py:611
  52.8 1.3 %collective-permute-start.17 = (s16[272,128]{1,0:T(8,128)(2,1)S(1)}, s16[272,128]{1,0:T(8,128)(2,1)S(1)}, u32[]{:S(2)}, u32[]{:S(2)}) collective-permute-start(s16[272,128]{1,0:T(8,128)(2,1)S(1)} %get-tuple-element.101), channel_id=1, source_target_pairs={{0,6},{1,7},{2,4},{3,5},{4,2},{5,3},{6,0},{7,1},{8,14},{9,15},{10,... | collective-permute-start | bytes 208904 | tf_op jit(solution)/shard_map/ppermute | solution.py:611
  54.1 1.0 %collective-permute-done.22 = f32[2,128,128]{2,1,0:T(8,128)S(1)} collective-permute-done((f32[2,128,128]{2,1,0:T(8,128)S(1)}, f32[2,128,128]{2,1,0:T(8,128)S(1)}, u32[]{:S(2)}, u32[]{:S(2)}) %collective-permute-start.22) | collective-permute-done | bytes 131104 | tf_op jit(solution)/shard_map/ppermute | solution.py:611
  55.2 1.6 %collective-permute-start.23 = (f32[2,128,128]{2,1,0:T(8,128)S(1)}, f32[2,128,128]{2,1,0:T(8,128)S(1)}, u32[]{:S(2)}, u32[]{:S(2)}) collective-permute-start(f32[2,128,128]{2,1,0:T(8,128)S(1)} %fusion.1), channel_id=1, source_target_pairs={{0,4},{1,5},{2,6},{3,7},{4,0},{5,1},{6,2},{7,3},{8,12},{9,13},{10,... | collective-permute-start | bytes 393224 | tf_op jit(solution)/shard_map/ppermute | solution.py:611
  56.8 1.7 %collective-permute-done.17.refs_4_ = s16[272,128]{1,0:T(8,128)(2,1)S(1)} collective-permute-done((s16[272,128]{1,0:T(8,128)(2,1)S(1)}, s16[272,128]{1,0:T(8,128)(2,1)S(1)}, u32[]{:S(2)}, u32[]{:S(2)}) %collective-permute-start.17) | collective-permute-done | bytes 69664 | tf_op jit(solution)/shard_map/ppermute | solution.py:611
  58.4 0.1 code.1.refs_0_
  58.6 3.4 %collective-permute-start.20 = (s16[272,128]{1,0:T(8,128)(2,1)S(1)}, s16[272,128]{1,0:T(8,128)(2,1)S(1)}, u32[]{:S(2)}, u32[]{:S(2)}) collective-permute-start(s16[272,128]{1,0:T(8,128)(2,1)S(1)} %code.1.refs_0_), channel_id=1, source_target_pairs={{0,24},{8,16},{16,8},{24,0},{1,25},{9,17},{17,9},{25,1},{2,26},{10... | collective-permute-start | bytes 208904 | tf_op jit(solution)/shard_map/ppermute | solution.py:611
  62.0 1.1 %collective-permute-start.18 = (s16[272,128]{1,0:T(8,128)(2,1)S(1)}, s16[272,128]{1,0:T(8,128)(2,1)S(1)}, u32[]{:S(2)}, u32[]{:S(2)}) collective-permute-start(s16[272,128]{1,0:T(8,128)(2,1)S(1)} %code.1.refs_0_), channel_id=1, source_target_pairs={{0,8},{8,0},{16,24},{24,16},{1,9},{9,1},{17,25},{25,17},{2,10},{10... | collective-permute-start | bytes 208904 | tf_op jit(solution)/shard_map/ppermute | solution.py:611
  63.1 5.6 %factor.1.inv_ref = f32[2,128,128]{2,1,0:T(8,128)S(1)} custom-call(s32[2]{0:T(128)S(1)} %copy-done.1, f32[2,128,128]{2,1,0:T(8,128)S(1)} %add.11.gram_ref), custom_call_target="tpu_custom_call" | custom-call | tf_op jit(solution)/shard_map/factor/pallas_call | solution.py:495
  68.7 0.2 code_sum.1.refs_0_
  68.9 1.5 %collective-permute-start.24 = (s16[272,128]{1,0:T(8,128)(2,1)S(1)}, s16[272,128]{1,0:T(8,128)(2,1)S(1)}, u32[]{:S(2)}, u32[]{:S(2)}) collective-permute-start(s16[272,128]{1,0:T(8,128)(2,1)S(1)} %code_sum.1.refs_0_), channel_id=1, source_target_pairs={{0,6},{1,7},{2,4},{3,5},{4,2},{5,3},{6,0},{7,1},{8,14},{9,15},{10,... | collective-permute-start | bytes 208904 | tf_op jit(solution)/shard_map/ppermute | solution.py:611
  70.4 1.5 %collective-permute-start.28 = (s16[272,128]{1,0:T(8,128)(2,1)S(1)}, s16[272,128]{1,0:T(8,128)(2,1)S(1)}, u32[]{:S(2)}, u32[]{:S(2)}) collective-permute-start(s16[272,128]{1,0:T(8,128)(2,1)S(1)} %code_sum.1.refs_0_), channel_id=1, source_target_pairs={{0,4},{1,5},{2,6},{3,7},{4,0},{5,1},{6,2},{7,3},{8,12},{9,13},{10,... | collective-permute-start | bytes 208904 | tf_op jit(solution)/shard_map/ppermute | solution.py:611
  71.9 0.5 collective-permute-start.26
  72.4 1.4 %factor_p.1 = (f32[2,1024,128]{2,1,0:T(8,128)}, bf16[2,1024,384]{2,1,0:T(8,128)(2,1)S(1)}) custom-call(f32[2,128,128]{2,1,0:T(8,128)S(1)} %factor.1.inv_ref, s16[528,128]{1,0:T(8,128)(2,1)S(1)} %add_code.7.code_ref.refs_0_, s16[528,128]{1,0:T(8,128)(2,1)S(1)} %collective-permute-done.11.code_ref.refs_1_, s16[528,128]{1,0:T(8,128)(2,1)S(1)} %add_code.6.code_ref.refs_2_, ...), custom_call_target="tpu_custom_call" | custom-call | tf_op jit(solution)/shard_map/factor_p/pallas_call | solution.py:530
  73.9 0.3 collective-permute-done.24.refs_6_
  74.2 0.7 collective-permute-done.28.refs_4_
  74.9 1.3 %collective-permute-done.26.refs_2_ = s16[272,128]{1,0:T(8,128)(2,1)S(1)} collective-permute-done((s16[272,128]{1,0:T(8,128)(2,1)S(1)}, s16[272,128]{1,0:T(8,128)(2,1)S(1)}, u32[]{:S(2)}, u32[]{:S(2)}) %collective-permute-start.26) | collective-permute-done | bytes 69664 | tf_op jit(solution)/shard_map/ppermute | solution.py:611
  76.2 0.5 collective-permute-start.30
  76.7 0.7 collective-permute-done.27.refs_3_
  77.5 0.2 collective-permute-done.30.refs_7_
  77.6 4.5 %error.1 = (f32[2,1,1024,1024]{3,2,1,0:T(8,128)}, f32[2,1024,128]{2,1,0:T(8,128)}) custom-call(bf16[2,1024,384]{2,1,0:T(8,128)(2,1)S(1)} %get-tuple-element.113.p3_ref, f32[2,128,128]{2,1,0:T(8,128)S(1)} %factor.1.inv_ref, s16[272,128]{1,0:T(8,128)(2,1)S(1)} %code_sum.1.refs_0_, s16[272,128]{1,0:T(8,128)(2,1)S(1)} %collective-permute-done.25.refs_1_, ...), custom_call_target="tpu_custom_call" | custom-call | tf_op jit(solution)/shard_map/error/pallas_call | solution.py:586
  (26 shorter events, 0.1 us)
Async XLA Ops:
  0.6 12.5 %copy-start = (bf16[2,512,128]{2,1,0:T(8,128)(2,1)S(1)}, bf16[2,512,128]{2,1,0:T(8,128)(2,1)}, u32[]{:S(2)}) copy-start(bf16[2,512,128]{2,1,0:T(8,128)(2,1)} %refs_0_.2) | copy-start | bytes 786436
  0.6 12.1 %collective-permute-start.1 = (bf16[2,512,128]{2,1,0:T(8,128)(2,1)}, bf16[2,512,128]{2,1,0:T(8,128)(2,1)S(1)}, u32[]{:S(2)}, u32[]{:S(2)}) collective-permute-start(bf16[2,512,128]{2,1,0:T(8,128)(2,1)} %refs_0_.2), channel_id=1, source_target_pairs={{0,4},{1,5},{2,6},{3,7},{4,0},{5,1},{6,2},{7,3},{8,12},{9,13},{10,... | collective-permute-start | bytes 786440 | tf_op jit(solution)/shard_map/ppermute | solution.py:611
  3.7 9.4 %collective-permute-start = (bf16[2,512,128]{2,1,0:T(8,128)(2,1)}, bf16[2,512,128]{2,1,0:T(8,128)(2,1)S(1)}, u32[]{:S(2)}, u32[]{:S(2)}) collective-permute-start(bf16[2,512,128]{2,1,0:T(8,128)(2,1)} %refs_0_.2), channel_id=1, source_target_pairs={{0,2},{1,3},{2,0},{3,1},{4,6},{5,7},{6,4},{7,5},{8,10},{9,11},{10,... | collective-permute-start | bytes 786440 | tf_op jit(solution)/shard_map/ppermute | solution.py:611
  5.2 11.9 %collective-permute-start.2 = (bf16[2,512,128]{2,1,0:T(8,128)(2,1)}, bf16[2,512,128]{2,1,0:T(8,128)(2,1)S(1)}, u32[]{:S(2)}, u32[]{:S(2)}) collective-permute-start(bf16[2,512,128]{2,1,0:T(8,128)(2,1)} %refs_0_.2), channel_id=1, source_target_pairs={{0,6},{1,7},{2,4},{3,5},{4,2},{5,3},{6,0},{7,1},{8,14},{9,15},{10,... | collective-permute-start | bytes 786440 | tf_op jit(solution)/shard_map/ppermute | solution.py:611
  13.1 3.9 %collective-permute-start.3 = (bf16[2,512,128]{2,1,0:T(8,128)(2,1)S(1)}, bf16[2,512,128]{2,1,0:T(8,128)(2,1)S(1)}, u32[]{:S(2)}, u32[]{:S(2)}) collective-permute-start(bf16[2,512,128]{2,1,0:T(8,128)(2,1)S(1)} %copy-done), channel_id=1, source_target_pairs={{0,1},{1,0},{2,3},{3,2},{4,5},{5,4},{6,7},{7,6},{8,9},{9,8},{10,11... | collective-permute-start | bytes 786440 | tf_op jit(solution)/shard_map/ppermute | solution.py:611
  13.1 3.9 %collective-permute-start.4 = (bf16[2,512,128]{2,1,0:T(8,128)(2,1)S(1)}, bf16[2,512,128]{2,1,0:T(8,128)(2,1)S(1)}, u32[]{:S(2)}, u32[]{:S(2)}) collective-permute-start(bf16[2,512,128]{2,1,0:T(8,128)(2,1)S(1)} %collective-permute-done.refs_2_), channel_id=1, source_target_pairs={{0,1},{1,0},{2,3},{3,2},{4,5},{5,4},{6,7},{7,6},{8,9},{9,8},{10,11... | collective-permute-start | bytes 786440 | tf_op jit(solution)/shard_map/ppermute | solution.py:611
  13.6 3.4 %collective-permute-start.5 = (bf16[2,512,128]{2,1,0:T(8,128)(2,1)S(1)}, bf16[2,512,128]{2,1,0:T(8,128)(2,1)S(1)}, u32[]{:S(2)}, u32[]{:S(2)}) collective-permute-start(bf16[2,512,128]{2,1,0:T(8,128)(2,1)S(1)} %collective-permute-done.1.refs_4_), channel_id=1, source_target_pairs={{0,1},{1,0},{2,3},{3,2},{4,5},{5,4},{6,7},{7,6},{8,9},{9,8},{10,11... | collective-permute-start | bytes 786440 | tf_op jit(solution)/shard_map/ppermute | solution.py:611
  17.1 1.6 %collective-permute-start.6 = (bf16[2,512,128]{2,1,0:T(8,128)(2,1)S(1)}, bf16[2,512,128]{2,1,0:T(8,128)(2,1)S(1)}, u32[]{:S(2)}, u32[]{:S(2)}) collective-permute-start(bf16[2,512,128]{2,1,0:T(8,128)(2,1)S(1)} %collective-permute-done.2.refs_1_.refs_6_), channel_id=1, source_target_pairs={{0,1},{1,0},{2,3},{3,2},{4,5},{5,4},{6,7},{7,6},{8,9},{9,8},{10,11... | collective-permute-start | bytes 786440 | tf_op jit(solution)/shard_map/ppermute | solution.py:611
  19.5 6.1 %collective-permute-start.9 = (s16[528,128]{1,0:T(8,128)(2,1)S(1)}, s16[528,128]{1,0:T(8,128)(2,1)S(1)}, u32[]{:S(2)}, u32[]{:S(2)}) collective-permute-start(s16[528,128]{1,0:T(8,128)(2,1)S(1)} %get-tuple-element.80), channel_id=1, source_target_pairs={{0,8},{8,0},{16,24},{24,16},{1,9},{9,1},{17,25},{25,17},{2,10},{10... | collective-permute-start | bytes 405512 | tf_op jit(solution)/shard_map/ppermute | solution.py:611
  22.2 6.6 %collective-permute-start.7 = (s16[528,128]{1,0:T(8,128)(2,1)S(1)}, s16[528,128]{1,0:T(8,128)(2,1)S(1)}, u32[]{:S(2)}, u32[]{:S(2)}) collective-permute-start(s16[528,128]{1,0:T(8,128)(2,1)S(1)} %get-tuple-element.75), channel_id=1, source_target_pairs={{0,8},{8,0},{16,24},{24,16},{1,9},{9,1},{17,25},{25,17},{2,10},{10... | collective-permute-start | bytes 405512 | tf_op jit(solution)/shard_map/ppermute | solution.py:611
  25.8 12.5 %collective-permute-start.10 = (s16[528,128]{1,0:T(8,128)(2,1)S(1)}, s16[528,128]{1,0:T(8,128)(2,1)S(1)}, u32[]{:S(2)}, u32[]{:S(2)}) collective-permute-start(s16[528,128]{1,0:T(8,128)(2,1)S(1)} %add_code.5.mine_ref), channel_id=1, source_target_pairs={{0,16},{8,24},{16,0},{24,8},{1,17},{9,25},{17,1},{25,9},{2,18},{10... | collective-permute-start | bytes 405512 | tf_op jit(solution)/shard_map/ppermute | solution.py:611
  28.9 11.3 %collective-permute-start.8 = (s16[528,128]{1,0:T(8,128)(2,1)S(1)}, s16[528,128]{1,0:T(8,128)(2,1)S(1)}, u32[]{:S(2)}, u32[]{:S(2)}) collective-permute-start(s16[528,128]{1,0:T(8,128)(2,1)S(1)} %add_code.4.mine_ref), channel_id=1, source_target_pairs={{0,16},{8,24},{16,0},{24,8},{1,17},{9,25},{17,1},{25,9},{2,18},{10... | collective-permute-start | bytes 405512 | tf_op jit(solution)/shard_map/ppermute | solution.py:611
  38.5 6.4 %collective-permute-start.12 = (s16[528,128]{1,0:T(8,128)(2,1)S(1)}, s16[528,128]{1,0:T(8,128)(2,1)S(1)}, u32[]{:S(2)}, u32[]{:S(2)}) collective-permute-start(s16[528,128]{1,0:T(8,128)(2,1)S(1)} %add_code.6.code_ref.refs_2_), channel_id=1, source_target_pairs={{0,8},{8,0},{16,24},{24,16},{1,9},{9,1},{17,25},{25,17},{2,10},{10... | collective-permute-start | bytes 405512 | tf_op jit(solution)/shard_map/ppermute | solution.py:611
  40.4 22.6 %copy-start.1 = (s32[2]{0:T(128)S(1)}, s32[2]{0:T(128)}, u32[]{:S(2)}) copy-start(s32[2]{0:T(128)} %ranks_ref.3) | copy-start | bytes 28
  40.4 6.0 %collective-permute-start.11 = (s16[528,128]{1,0:T(8,128)(2,1)S(1)}, s16[528,128]{1,0:T(8,128)(2,1)S(1)}, u32[]{:S(2)}, u32[]{:S(2)}) collective-permute-start(s16[528,128]{1,0:T(8,128)(2,1)S(1)} %add_code.7.code_ref.refs_0_), channel_id=1, source_target_pairs={{0,8},{8,0},{16,24},{24,16},{1,9},{9,1},{17,25},{25,17},{2,10},{10... | collective-permute-start | bytes 405512 | tf_op jit(solution)/shard_map/ppermute | solution.py:611
  47.3 1.4 %collective-permute-start.21 = (f32[2,128,128]{2,1,0:T(8,128)S(1)}, f32[2,128,128]{2,1,0:T(8,128)S(1)}, u32[]{:S(2)}, u32[]{:S(2)}) collective-permute-start(f32[2,128,128]{2,1,0:T(8,128)S(1)} %pad_maximum_fusion), channel_id=1, source_target_pairs={{0,1},{1,0},{2,3},{3,2},{4,5},{5,4},{6,7},{7,6},{8,9},{9,8},{10,11... | collective-permute-start | bytes 393224 | tf_op jit(solution)/shard_map/ppermute | solution.py:611
  47.4 2.9 %collective-permute-start.14 = (f32[512,128]{1,0:T(8,128)S(1)}, f32[512,128]{1,0:T(8,128)S(1)}, u32[]{:S(2)}, u32[]{:S(2)}) collective-permute-start(f32[512,128]{1,0:T(8,128)S(1)} %get-tuple-element.96), channel_id=1, source_target_pairs={{0,1},{1,0},{2,3},{3,2},{4,5},{5,4},{6,7},{7,6},{8,9},{9,8},{10,11... | collective-permute-start | bytes 786440 | tf_op jit(solution)/shard_map/ppermute | solution.py:611
  47.9 2.4 %collective-permute-start.13 = (f32[512,128]{1,0:T(8,128)S(1)}, f32[512,128]{1,0:T(8,128)S(1)}, u32[]{:S(2)}, u32[]{:S(2)}) collective-permute-start(f32[512,128]{1,0:T(8,128)S(1)} %get-tuple-element.95), channel_id=1, source_target_pairs={{0,1},{1,0},{2,3},{3,2},{4,5},{5,4},{6,7},{7,6},{8,9},{9,8},{10,11... | collective-permute-start | bytes 786440 | tf_op jit(solution)/shard_map/ppermute | solution.py:611
  48.8 6.4 %collective-permute-start.22 = (f32[2,128,128]{2,1,0:T(8,128)S(1)}, f32[2,128,128]{2,1,0:T(8,128)S(1)}, u32[]{:S(2)}, u32[]{:S(2)}) collective-permute-start(f32[2,128,128]{2,1,0:T(8,128)S(1)} %fusion), channel_id=1, source_target_pairs={{0,2},{1,3},{2,0},{3,1},{4,6},{5,7},{6,4},{7,5},{8,10},{9,11},{10,... | collective-permute-start | bytes 393224 | tf_op jit(solution)/shard_map/ppermute | solution.py:611
  50.6 6.2 %collective-permute-start.15 = (s16[272,128]{1,0:T(8,128)(2,1)S(1)}, s16[272,128]{1,0:T(8,128)(2,1)S(1)}, u32[]{:S(2)}, u32[]{:S(2)}) collective-permute-start(s16[272,128]{1,0:T(8,128)(2,1)S(1)} %get-tuple-element.99), channel_id=1, source_target_pairs={{0,2},{1,3},{2,0},{3,1},{4,6},{5,7},{6,4},{7,5},{8,10},{9,11},{10,... | collective-permute-start | bytes 208904 | tf_op jit(solution)/shard_map/ppermute | solution.py:611
  51.3 5.4 %collective-permute-start.16 = (s16[272,128]{1,0:T(8,128)(2,1)S(1)}, s16[272,128]{1,0:T(8,128)(2,1)S(1)}, u32[]{:S(2)}, u32[]{:S(2)}) collective-permute-start(s16[272,128]{1,0:T(8,128)(2,1)S(1)} %get-tuple-element.100), channel_id=1, source_target_pairs={{0,4},{1,5},{2,6},{3,7},{4,0},{5,1},{6,2},{7,3},{8,12},{9,13},{10,... | collective-permute-start | bytes 208904 | tf_op jit(solution)/shard_map/ppermute | solution.py:611
  52.8 5.6 %collective-permute-start.17 = (s16[272,128]{1,0:T(8,128)(2,1)S(1)}, s16[272,128]{1,0:T(8,128)(2,1)S(1)}, u32[]{:S(2)}, u32[]{:S(2)}) collective-permute-start(s16[272,128]{1,0:T(8,128)(2,1)S(1)} %get-tuple-element.101), channel_id=1, source_target_pairs={{0,6},{1,7},{2,4},{3,5},{4,2},{5,3},{6,0},{7,1},{8,14},{9,15},{10,... | collective-permute-start | bytes 208904 | tf_op jit(solution)/shard_map/ppermute | solution.py:611
  55.2 7.9 %collective-permute-start.23 = (f32[2,128,128]{2,1,0:T(8,128)S(1)}, f32[2,128,128]{2,1,0:T(8,128)S(1)}, u32[]{:S(2)}, u32[]{:S(2)}) collective-permute-start(f32[2,128,128]{2,1,0:T(8,128)S(1)} %fusion.1), channel_id=1, source_target_pairs={{0,4},{1,5},{2,6},{3,7},{4,0},{5,1},{6,2},{7,3},{8,12},{9,13},{10,... | collective-permute-start | bytes 393224 | tf_op jit(solution)/shard_map/ppermute | solution.py:611
  58.6 10.1 %collective-permute-start.20 = (s16[272,128]{1,0:T(8,128)(2,1)S(1)}, s16[272,128]{1,0:T(8,128)(2,1)S(1)}, u32[]{:S(2)}, u32[]{:S(2)}) collective-permute-start(s16[272,128]{1,0:T(8,128)(2,1)S(1)} %code.1.refs_0_), channel_id=1, source_target_pairs={{0,24},{8,16},{16,8},{24,0},{1,25},{9,17},{17,9},{25,1},{2,26},{10... | collective-permute-start | bytes 208904 | tf_op jit(solution)/shard_map/ppermute | solution.py:611
  61.9 6.7 %collective-permute-start.19 = (s16[272,128]{1,0:T(8,128)(2,1)S(1)}, s16[272,128]{1,0:T(8,128)(2,1)S(1)}, u32[]{:S(2)}, u32[]{:S(2)}) collective-permute-start(s16[272,128]{1,0:T(8,128)(2,1)S(1)} %code.1.refs_0_), channel_id=1, source_target_pairs={{0,16},{8,24},{16,0},{24,8},{1,17},{9,25},{17,1},{25,9},{2,18},{10... | collective-permute-start | bytes 208904 | tf_op jit(solution)/shard_map/ppermute | solution.py:611
  62.0 6.8 %collective-permute-start.18 = (s16[272,128]{1,0:T(8,128)(2,1)S(1)}, s16[272,128]{1,0:T(8,128)(2,1)S(1)}, u32[]{:S(2)}, u32[]{:S(2)}) collective-permute-start(s16[272,128]{1,0:T(8,128)(2,1)S(1)} %code.1.refs_0_), channel_id=1, source_target_pairs={{0,8},{8,0},{16,24},{24,16},{1,9},{9,1},{17,25},{25,17},{2,10},{10... | collective-permute-start | bytes 208904 | tf_op jit(solution)/shard_map/ppermute | solution.py:611
  68.9 5.3 %collective-permute-start.24 = (s16[272,128]{1,0:T(8,128)(2,1)S(1)}, s16[272,128]{1,0:T(8,128)(2,1)S(1)}, u32[]{:S(2)}, u32[]{:S(2)}) collective-permute-start(s16[272,128]{1,0:T(8,128)(2,1)S(1)} %code_sum.1.refs_0_), channel_id=1, source_target_pairs={{0,6},{1,7},{2,4},{3,5},{4,2},{5,3},{6,0},{7,1},{8,14},{9,15},{10,... | collective-permute-start | bytes 208904 | tf_op jit(solution)/shard_map/ppermute | solution.py:611
  70.4 4.5 %collective-permute-start.28 = (s16[272,128]{1,0:T(8,128)(2,1)S(1)}, s16[272,128]{1,0:T(8,128)(2,1)S(1)}, u32[]{:S(2)}, u32[]{:S(2)}) collective-permute-start(s16[272,128]{1,0:T(8,128)(2,1)S(1)} %code_sum.1.refs_0_), channel_id=1, source_target_pairs={{0,4},{1,5},{2,6},{3,7},{4,0},{5,1},{6,2},{7,3},{8,12},{9,13},{10,... | collective-permute-start | bytes 208904 | tf_op jit(solution)/shard_map/ppermute | solution.py:611
  71.9 4.3 %collective-permute-start.26 = (s16[272,128]{1,0:T(8,128)(2,1)S(1)}, s16[272,128]{1,0:T(8,128)(2,1)S(1)}, u32[]{:S(2)}, u32[]{:S(2)}) collective-permute-start(s16[272,128]{1,0:T(8,128)(2,1)S(1)} %code_sum.1.refs_0_), channel_id=1, source_target_pairs={{0,2},{1,3},{2,0},{3,1},{4,6},{5,7},{6,4},{7,5},{8,10},{9,11},{10,... | collective-permute-start | bytes 208904 | tf_op jit(solution)/shard_map/ppermute | solution.py:611
  72.4 4.3 %collective-permute-start.25 = (s16[272,128]{1,0:T(8,128)(2,1)S(1)}, s16[272,128]{1,0:T(8,128)(2,1)S(1)}, u32[]{:S(2)}, u32[]{:S(2)}) collective-permute-start(s16[272,128]{1,0:T(8,128)(2,1)S(1)} %code_sum.1.refs_0_), channel_id=1, source_target_pairs={{0,1},{1,0},{2,3},{3,2},{4,5},{5,4},{6,7},{7,6},{8,9},{9,8},{10,11... | collective-permute-start | bytes 208904 | tf_op jit(solution)/shard_map/ppermute | solution.py:611
  74.9 1.8 %collective-permute-start.29 = (s16[272,128]{1,0:T(8,128)(2,1)S(1)}, s16[272,128]{1,0:T(8,128)(2,1)S(1)}, u32[]{:S(2)}, u32[]{:S(2)}) collective-permute-start(s16[272,128]{1,0:T(8,128)(2,1)S(1)} %collective-permute-done.28.refs_4_), channel_id=1, source_target_pairs={{0,1},{1,0},{2,3},{3,2},{4,5},{5,4},{6,7},{7,6},{8,9},{9,8},{10,11... | collective-permute-start | bytes 208904 | tf_op jit(solution)/shard_map/ppermute | solution.py:611
  76.2 1.3 %collective-permute-start.27 = (s16[272,128]{1,0:T(8,128)(2,1)S(1)}, s16[272,128]{1,0:T(8,128)(2,1)S(1)}, u32[]{:S(2)}, u32[]{:S(2)}) collective-permute-start(s16[272,128]{1,0:T(8,128)(2,1)S(1)} %collective-permute-done.26.refs_2_), channel_id=1, source_target_pairs={{0,1},{1,0},{2,3},{3,2},{4,5},{5,4},{6,7},{7,6},{8,9},{9,8},{10,11... | collective-permute-start | bytes 208904 | tf_op jit(solution)/shard_map/ppermute | solution.py:611
  76.2 1.4 %collective-permute-start.30 = (s16[272,128]{1,0:T(8,128)(2,1)S(1)}, s16[272,128]{1,0:T(8,128)(2,1)S(1)}, u32[]{:S(2)}, u32[]{:S(2)}) collective-permute-start(s16[272,128]{1,0:T(8,128)(2,1)S(1)} %collective-permute-done.24.refs_6_), channel_id=1, source_target_pairs={{0,1},{1,0},{2,3},{3,2},{4,5},{5,4},{6,7},{7,6},{8,9},{9,8},{10,11... | collective-permute-start | bytes 208904 | tf_op jit(solution)/shard_map/ppermute | solution.py:611

commit v7 on v6

--- a/solution.py
+++ b/solution.py
@@ -191,6 +191,7 @@
 
 GROUPS = 16
 LANES = 128
+NEAR = 3
 
 
 def encode(x, out_ref):
@@ -436,16 +437,21 @@
 def cholesky_inverse(work, n):
     lane = lax.broadcasted_iota(jnp.int32, (8, n), 1)
     sub = lax.broadcasted_iota(jnp.int32, (8, n), 0)
+    last = n // 8
 
     def wide(x):
         return jnp.broadcast_to(x, (8, n))
 
-    for b in range(n // 8):
+    def columns_of(x, at):
+        return [wide(x[:, at + j : at + j + 1]) for j in range(8)]
+
+    carried = [columns_of(blocks[0], 0) for blocks in work]
+    for b in range(last):
         at = 8 * b
+        inside = (lane >= at) & (lane < at + 8)
         panels = []
-        for blocks in work:
+        for columns, blocks in zip(carried, work):
             head = blocks[b]
-            columns = [wide(head[:, at + j : at + j + 1]) for j in range(8)]
             scales, lows, tops = [], [], []
             for s in range(8):
                 scale = lax.rsqrt(wide(columns[s][s : s + 1, :]))
@@ -460,17 +466,36 @@
                 tops.append(jnp.where((lane > at + s) & (lane < at + 8), 0.0, row))
             blocks[b] = head
             panels.append((scales, lows, tops))
-        for c in range(b + 1, n // 8):
-            for blocks, (scales, lows, tops) in zip(work, panels):
+        near = min(b + 1 + NEAR, last)
+        for c in range(b + 1, near):
+            for i, (blocks, (scales, lows, tops)) in enumerate(zip(work, panels)):
                 x = blocks[c]
-                columns = [wide(x[:, at + j : at + j + 1]) for j in range(8)]
-                y = jnp.where((lane >= at) & (lane < at + 8), 0.0, x)
+                columns = columns_of(x, at)
+                following = columns_of(x, at + 8) if c == b + 1 else []
+                y = jnp.where(inside, 0.0, x)
                 for s in range(8):
                     low = columns[s] * scales[s]
                     for j in range(s + 1, 8):
                         columns[j] = columns[j] - low * wide(lows[s][j : j + 1, :])
                     y = y - low * tops[s]
+                    following = [f - low * wide(low[j : j + 1, :]) for j, f in enumerate(following)]
                 blocks[c] = y
+                if following:
+                    carried[i] = following
+        if near < last:
+            for blocks, (scales, lows, tops) in zip(work, panels):
+                top = tops[0]
+                for s in range(1, 8):
+                    top = jnp.where(sub == s, tops[s], top)
+                update = lax.dot_general(
+                    blocks[b],
+                    top,
+                    (((0,), (0,)), ((), ())),
+                    precision=lax.Precision.HIGHEST,
+                    preferred_element_type=F32,
+                )
+                for c in range(near, last):
+                    blocks[c] = jnp.where(inside, 0.0, blocks[c]) - update[8 * c : 8 * c + 8]
 
 
 def factor_kernel(ranks_ref, gram_ref, inv_ref):

time: 82.4 us -> 81.7 us (level)
  transfers between devices with their start and end apart: 31 -> 31, of which waited for: 16 -> 16; matrix products, arithmetic and copies ran while one was open for 0% -> 0% of each run, Pallas kernels for 27% -> 26%
where the time goes in v7:
time: 81.7 us; the launch traced here: 81.5 us
  starting transfers between devices  30.5 us (37%)
  Pallas kernels  28 us (34%)
  waiting for transfers between devices  21.9 us (27%)
  between operations  1.01 us (1%)
    ppermute x31, starting transfers between devices, across(): return lax.ppermute(x, axis, [(i, i ^ bit) for i in range(size)])  30.5 us
    ppermute x31, waiting for transfers between devices, across(): return lax.ppermute(x, axis, [(i, i ^ bit) for i in range(size)])  21.9 us
    pallas_call x1, Pallas kernels, feedback_q(): pl.pallas_call(feedback_q_kernel, in_specs=[far] * 4, out_specs=[VMEM] *...  7.55 us
    pallas_call x1, Pallas kernels, factor(): pl.pallas_call(factor_kernel, in_specs=[SMEM, VMEM], out_specs=VMEM, out_...  4.86 us
    pallas_call x1, Pallas kernels, error(): pl.pallas_call(functools.partial(error_kernel, count, len(codes), groups)...  4.48 us
    pallas_call x2, Pallas kernels, full(): pl.pallas_call(functools.partial(full_kernel, m), in_specs=[VMEM] * (2 +...  3.13 us
    pallas_call x2, Pallas kernels, other_half(): pl.pallas_call(functools.partial(other_half_kernel, halved), in_specs=[VM...  1.69 us
    pallas_call x2, Pallas kernels, left_code(): pl.pallas_call(functools.partial(left_code_kernel, m, keys), in_specs=[VM...  1.69 us
  transfers between devices with their start and end apart: 31, of which 16 were waited for; matrix products, arithmetic and copies ran while one was open for 0% of the time, Pallas kernels for 26%

profile of v7, /device:TPU:0, one launch (start us, length us, event | category | flops | bytes accessed | tf_op | source)
XLA Modules:
  0.0 81.5 jit_solution(12722417018790864948)
XLA Ops:
  0.6 3.0 %collective-permute-start.1 = (bf16[2,512,128]{2,1,0:T(8,128)(2,1)}, bf16[2,512,128]{2,1,0:T(8,128)(2,1)S(1)}, u32[]{:S(2)}, u32[]{:S(2)}) collective-permute-start(bf16[2,512,128]{2,1,0:T(8,128)(2,1)} %refs_0_.2), channel_id=1, source_target_pairs={{0,4},{1,5},{2,6},{3,7},{4,0},{5,1},{6,2},{7,3},{8,12},{9,13},{10,... | collective-permute-start | bytes 786440 | tf_op jit(solution)/shard_map/ppermute | solution.py:636
  3.7 1.5 %collective-permute-start = (bf16[2,512,128]{2,1,0:T(8,128)(2,1)}, bf16[2,512,128]{2,1,0:T(8,128)(2,1)S(1)}, u32[]{:S(2)}, u32[]{:S(2)}) collective-permute-start(bf16[2,512,128]{2,1,0:T(8,128)(2,1)} %refs_0_.2), channel_id=1, source_target_pairs={{0,2},{1,3},{2,0},{3,1},{4,6},{5,7},{6,4},{7,5},{8,10},{9,11},{10,... | collective-permute-start | bytes 786440 | tf_op jit(solution)/shard_map/ppermute | solution.py:636
  5.2 0.0 collective-permute-start.2
  5.2 7.6 %feedback_q.1 = (f32[2,1024,1024]{2,1,0:T(8,128)S(1)}, f32[2,1024,128]{2,1,0:T(8,128)S(1)}, bf16[2,1024,256]{2,1,0:T(8,128)(2,1)S(1)}, bf16[1024,512]{1,0:T(8,128)(2,1)S(1)}) custom-call(s32[2]{0:T(128)} %ranks_ref.3, f32[2,1,1024,1024]{3,2,1,0:T(8,128)} %fb_ref.1, f32[2,1024,128]{2,1,0:T(8,128)} %q_ref.1, bf16[512,1024]{1,0:T(8,128)(2,1)} %in_ref.1), custom_call_target="tpu_custom_call" | custom-call | tf_op jit(solution)/shard_map/feedback_q/pallas_call | solution.py:96
  12.8 0.3 collective-permute-done.refs_2_
  13.1 0.0 collective-permute-start.3
  13.1 0.5 collective-permute-start.4
  13.6 0.0 collective-permute-start.5
  13.6 3.4 %collective-permute-done.2.refs_1_.refs_6_ = bf16[2,512,128]{2,1,0:T(8,128)(2,1)S(1)} collective-permute-done((bf16[2,512,128]{2,1,0:T(8,128)(2,1)}, bf16[2,512,128]{2,1,0:T(8,128)(2,1)S(1)}, u32[]{:S(2)}, u32[]{:S(2)}) %collective-permute-start.2) | collective-permute-done | bytes 262176 | tf_op jit(solution)/shard_map/ppermute | solution.py:636
  17.1 0.1 collective-permute-start.6
  17.2 0.6 begin.1.refs_0_
  17.8 0.9 %collective-permute-done.6.refs_2_.refs_7_ = bf16[2,512,128]{2,1,0:T(8,128)(2,1)S(1)} collective-permute-done((bf16[2,512,128]{2,1,0:T(8,128)(2,1)S(1)}, bf16[2,512,128]{2,1,0:T(8,128)(2,1)S(1)}, u32[]{:S(2)}, u32[]{:S(2)}) %collective-permute-start.6) | collective-permute-done | bytes 262176 | tf_op jit(solution)/shard_map/ppermute | solution.py:636
  18.7 0.8 %left_code_1.1 = (f32[512,128]{1,0:T(8,128)S(1)}, s16[528,128]{1,0:T(8,128)(2,1)S(1)}) custom-call(bf16[2,1024,256]{2,1,0:T(8,128)(2,1)S(1)} %get-tuple-element.64.q2_ref, bf16[1024,512]{1,0:T(8,128)(2,1)S(1)} %get-tuple-element.82.in_ref, f32[2,1024,128]{2,1,0:T(8,128)S(1)} %get-tuple-element.66.fbq_ref, f32[2,512,256]{2,1,0:T(8,128)S(1)} %begin.1.refs_0_, ...), custom_call_target="tpu_custom_call" | custom-call | tf_op jit(solution)/shard_map/left_code_1/pallas_call | solution.py:242
  19.5 1.8 %collective-permute-start.9 = (s16[528,128]{1,0:T(8,128)(2,1)S(1)}, s16[528,128]{1,0:T(8,128)(2,1)S(1)}, u32[]{:S(2)}, u32[]{:S(2)}) collective-permute-start(s16[528,128]{1,0:T(8,128)(2,1)S(1)} %get-tuple-element.80), channel_id=1, source_target_pairs={{0,8},{8,0},{16,24},{24,16},{1,9},{9,1},{17,25},{25,17},{2,10},{10... | collective-permute-start | bytes 405512 | tf_op jit(solution)/shard_map/ppermute | solution.py:636
  21.3 0.8 %left_code_0.1 = (f32[512,128]{1,0:T(8,128)S(1)}, s16[528,128]{1,0:T(8,128)(2,1)S(1)}) custom-call(bf16[2,1024,256]{2,1,0:T(8,128)(2,1)S(1)} %get-tuple-element.64.q2_ref, bf16[1024,512]{1,0:T(8,128)(2,1)S(1)} %get-tuple-element.82.in_ref, f32[2,1024,128]{2,1,0:T(8,128)S(1)} %get-tuple-element.66.fbq_ref, f32[2,512,256]{2,1,0:T(8,128)S(1)} %begin.1.refs_0_, ...), custom_call_target="tpu_custom_call" | custom-call | tf_op jit(solution)/shard_map/left_code_0/pallas_call | solution.py:242
  22.2 0.4 collective-permute-start.7
  22.5 3.1 %collective-permute-done.9.theirs_ref = s16[528,128]{1,0:T(8,128)(2,1)S(1)} collective-permute-done((s16[528,128]{1,0:T(8,128)(2,1)S(1)}, s16[528,128]{1,0:T(8,128)(2,1)S(1)}, u32[]{:S(2)}, u32[]{:S(2)}) %collective-permute-start.9) | collective-permute-done | bytes 135200 | tf_op jit(solution)/shard_map/ppermute | solution.py:636
  25.7 0.1 add_code.5.mine_ref
  25.8 3.0 %collective-permute-start.10 = (s16[528,128]{1,0:T(8,128)(2,1)S(1)}, s16[528,128]{1,0:T(8,128)(2,1)S(1)}, u32[]{:S(2)}, u32[]{:S(2)}) collective-permute-start(s16[528,128]{1,0:T(8,128)(2,1)S(1)} %add_code.5.mine_ref), channel_id=1, source_target_pairs={{0,16},{8,24},{16,0},{24,8},{1,17},{9,25},{17,1},{25,9},{2,18},{10... | collective-permute-start | bytes 405512 | tf_op jit(solution)/shard_map/ppermute | solution.py:636
  28.8 0.1 add_code.4.mine_ref
  28.9 2.8 %collective-permute-start.8 = (s16[528,128]{1,0:T(8,128)(2,1)S(1)}, s16[528,128]{1,0:T(8,128)(2,1)S(1)}, u32[]{:S(2)}, u32[]{:S(2)}) collective-permute-start(s16[528,128]{1,0:T(8,128)(2,1)S(1)} %add_code.4.mine_ref), channel_id=1, source_target_pairs={{0,16},{8,24},{16,0},{24,8},{1,17},{9,25},{17,1},{25,9},{2,18},{10... | collective-permute-start | bytes 405512 | tf_op jit(solution)/shard_map/ppermute | solution.py:636
  31.7 1.6 %full_0.1.full_ref.refs_8_ = f32[1024,1024]{1,0:T(8,128)S(1)} custom-call(f32[2,1024,1024]{2,1,0:T(8,128)S(1)} %get-tuple-element.77.held_ref, bf16[1024,512]{1,0:T(8,128)(2,1)S(1)} %get-tuple-element.82.in_ref, bf16[2,512,128]{2,1,0:T(8,128)(2,1)S(1)} %copy-done, bf16[2,512,128]{2,1,0:T(8,128)(2,1)S(1)} %collective-permute-done.3.refs_1_, ...), custom_call_target="tpu_custom_call" | custom-call | tf_op jit(solution)/shard_map/full_0/pallas_call | solution.py:302
  33.2 1.6 %full_1.1.full_ref.refs_9_ = f32[1024,1024]{1,0:T(8,128)S(1)} custom-call(f32[2,1024,1024]{2,1,0:T(8,128)S(1)} %get-tuple-element.77.held_ref, bf16[1024,512]{1,0:T(8,128)(2,1)S(1)} %get-tuple-element.82.in_ref, bf16[2,512,128]{2,1,0:T(8,128)(2,1)S(1)} %copy-done, bf16[2,512,128]{2,1,0:T(8,128)(2,1)S(1)} %collective-permute-done.3.refs_1_, ...), custom_call_target="tpu_custom_call" | custom-call | tf_op jit(solution)/shard_map/full_1/pallas_call | solution.py:302
  34.8 3.5 %collective-permute-done.10.theirs_ref = s16[528,128]{1,0:T(8,128)(2,1)S(1)} collective-permute-done((s16[528,128]{1,0:T(8,128)(2,1)S(1)}, s16[528,128]{1,0:T(8,128)(2,1)S(1)}, u32[]{:S(2)}, u32[]{:S(2)}) %collective-permute-start.10) | collective-permute-done | bytes 135200 | tf_op jit(solution)/shard_map/ppermute | solution.py:636
  38.3 0.2 add_code.6.code_ref.refs_2_
  38.5 0.4 collective-permute-start.12
  39.0 0.7 own_half_1.1
  39.7 0.6 collective-permute-done.8.theirs_ref
  40.2 0.2 add_code.7.code_ref.refs_0_
  40.4 0.0 copy-start.1
  40.4 1.2 %collective-permute-start.11 = (s16[528,128]{1,0:T(8,128)(2,1)S(1)}, s16[528,128]{1,0:T(8,128)(2,1)S(1)}, u32[]{:S(2)}, u32[]{:S(2)}) collective-permute-start(s16[528,128]{1,0:T(8,128)(2,1)S(1)} %add_code.7.code_ref.refs_0_), channel_id=1, source_target_pairs={{0,8},{8,0},{16,24},{24,16},{1,9},{9,1},{17,25},{25,17},{2,10},{10... | collective-permute-start | bytes 405512 | tf_op jit(solution)/shard_map/ppermute | solution.py:636
  41.6 0.7 own_half_0.1
  42.3 2.6 %collective-permute-done.12.code_ref.refs_3_ = s16[528,128]{1,0:T(8,128)(2,1)S(1)} collective-permute-done((s16[528,128]{1,0:T(8,128)(2,1)S(1)}, s16[528,128]{1,0:T(8,128)(2,1)S(1)}, u32[]{:S(2)}, u32[]{:S(2)}) %collective-permute-start.12) | collective-permute-done | bytes 135200 | tf_op jit(solution)/shard_map/ppermute | solution.py:636
  44.9 0.8 other_half_1.1
  45.7 0.7 collective-permute-done.11.code_ref.refs_1_
  46.4 0.9 %other_half_0.1 = (f32[512,128]{1,0:T(8,128)S(1)}, f32[512,128]{1,0:T(8,128)S(1)}, f32[128,128]{1,0:T(8,128)S(1)}) custom-call(f32[1024,1024]{1,0:T(8,128)S(1)} %full_0.1.full_ref.refs_8_, s16[528,128]{1,0:T(8,128)(2,1)S(1)} %collective-permute-done.11.code_ref.refs_1_, f32[128,1024]{1,0:T(8,128)S(1)} %get-tuple-element.89.total_ref, ...), custom_call_target="tpu_custom_call" | custom-call | tf_op jit(solution)/shard_map/other_half_0/pallas_call | solution.py:365
  47.3 0.1 collective-permute-start.21
  47.4 0.5 collective-permute-start.14
  47.9 0.1 collective-permute-start.13
  48.0 0.8 collective-permute-done.21
  48.8 1.5 %collective-permute-start.22 = (f32[2,128,128]{2,1,0:T(8,128)S(1)}, f32[2,128,128]{2,1,0:T(8,128)S(1)}, u32[]{:S(2)}, u32[]{:S(2)}) collective-permute-start(f32[2,128,128]{2,1,0:T(8,128)S(1)} %fusion), channel_id=1, source_target_pairs={{0,2},{1,3},{2,0},{3,1},{4,6},{5,7},{6,4},{7,5},{8,10},{9,11},{10,... | collective-permute-start | bytes 393224 | tf_op jit(solution)/shard_map/ppermute | solution.py:636
  50.3 0.3 part_2.1
  50.6 0.7 collective-permute-start.15
  51.3 1.5 %collective-permute-start.16 = (s16[272,128]{1,0:T(8,128)(2,1)S(1)}, s16[272,128]{1,0:T(8,128)(2,1)S(1)}, u32[]{:S(2)}, u32[]{:S(2)}) collective-permute-start(s16[272,128]{1,0:T(8,128)(2,1)S(1)} %get-tuple-element.100), channel_id=1, source_target_pairs={{0,4},{1,5},{2,6},{3,7},{4,0},{5,1},{6,2},{7,3},{8,12},{9,13},{10,... | collective-permute-start | bytes 208904 | tf_op jit(solution)/shard_map/ppermute | solution.py:636
  52.8 1.3 %collective-permute-start.17 = (s16[272,128]{1,0:T(8,128)(2,1)S(1)}, s16[272,128]{1,0:T(8,128)(2,1)S(1)}, u32[]{:S(2)}, u32[]{:S(2)}) collective-permute-start(s16[272,128]{1,0:T(8,128)(2,1)S(1)} %get-tuple-element.101), channel_id=1, source_target_pairs={{0,6},{1,7},{2,4},{3,5},{4,2},{5,3},{6,0},{7,1},{8,14},{9,15},{10,... | collective-permute-start | bytes 208904 | tf_op jit(solution)/shard_map/ppermute | solution.py:636
  54.1 1.0 %collective-permute-done.22 = f32[2,128,128]{2,1,0:T(8,128)S(1)} collective-permute-done((f32[2,128,128]{2,1,0:T(8,128)S(1)}, f32[2,128,128]{2,1,0:T(8,128)S(1)}, u32[]{:S(2)}, u32[]{:S(2)}) %collective-permute-start.22) | collective-permute-done | bytes 131104 | tf_op jit(solution)/shard_map/ppermute | solution.py:636
  55.2 1.6 %collective-permute-start.23 = (f32[2,128,128]{2,1,0:T(8,128)S(1)}, f32[2,128,128]{2,1,0:T(8,128)S(1)}, u32[]{:S(2)}, u32[]{:S(2)}) collective-permute-start(f32[2,128,128]{2,1,0:T(8,128)S(1)} %fusion.1), channel_id=1, source_target_pairs={{0,4},{1,5},{2,6},{3,7},{4,0},{5,1},{6,2},{7,3},{8,12},{9,13},{10,... | collective-permute-start | bytes 393224 | tf_op jit(solution)/shard_map/ppermute | solution.py:636
  56.8 1.7 %collective-permute-done.17.refs_4_ = s16[272,128]{1,0:T(8,128)(2,1)S(1)} collective-permute-done((s16[272,128]{1,0:T(8,128)(2,1)S(1)}, s16[272,128]{1,0:T(8,128)(2,1)S(1)}, u32[]{:S(2)}, u32[]{:S(2)}) %collective-permute-start.17) | collective-permute-done | bytes 69664 | tf_op jit(solution)/shard_map/ppermute | solution.py:636
  58.4 0.1 code.1.refs_0_
  58.6 3.4 %collective-permute-start.20 = (s16[272,128]{1,0:T(8,128)(2,1)S(1)}, s16[272,128]{1,0:T(8,128)(2,1)S(1)}, u32[]{:S(2)}, u32[]{:S(2)}) collective-permute-start(s16[272,128]{1,0:T(8,128)(2,1)S(1)} %code.1.refs_0_), channel_id=1, source_target_pairs={{0,24},{8,16},{16,8},{24,0},{1,25},{9,17},{17,9},{25,1},{2,26},{10... | collective-permute-start | bytes 208904 | tf_op jit(solution)/shard_map/ppermute | solution.py:636
  62.0 1.1 %collective-permute-start.18 = (s16[272,128]{1,0:T(8,128)(2,1)S(1)}, s16[272,128]{1,0:T(8,128)(2,1)S(1)}, u32[]{:S(2)}, u32[]{:S(2)}) collective-permute-start(s16[272,128]{1,0:T(8,128)(2,1)S(1)} %code.1.refs_0_), channel_id=1, source_target_pairs={{0,8},{8,0},{16,24},{24,16},{1,9},{9,1},{17,25},{25,17},{2,10},{10... | collective-permute-start | bytes 208904 | tf_op jit(solution)/shard_map/ppermute | solution.py:636
  63.1 4.9 %factor.1.inv_ref = f32[2,128,128]{2,1,0:T(8,128)S(1)} custom-call(s32[2]{0:T(128)S(1)} %copy-done.1, f32[2,128,128]{2,1,0:T(8,128)S(1)} %add.11.gram_ref), custom_call_target="tpu_custom_call" | custom-call | tf_op jit(solution)/shard_map/factor/pallas_call | solution.py:520
  68.0 0.2 code_sum.1.refs_0_
  68.1 1.5 %collective-permute-start.24 = (s16[272,128]{1,0:T(8,128)(2,1)S(1)}, s16[272,128]{1,0:T(8,128)(2,1)S(1)}, u32[]{:S(2)}, u32[]{:S(2)}) collective-permute-start(s16[272,128]{1,0:T(8,128)(2,1)S(1)} %code_sum.1.refs_0_), channel_id=1, source_target_pairs={{0,6},{1,7},{2,4},{3,5},{4,2},{5,3},{6,0},{7,1},{8,14},{9,15},{10,... | collective-permute-start | bytes 208904 | tf_op jit(solution)/shard_map/ppermute | solution.py:636
  69.7 1.5 %collective-permute-start.28 = (s16[272,128]{1,0:T(8,128)(2,1)S(1)}, s16[272,128]{1,0:T(8,128)(2,1)S(1)}, u32[]{:S(2)}, u32[]{:S(2)}) collective-permute-start(s16[272,128]{1,0:T(8,128)(2,1)S(1)} %code_sum.1.refs_0_), channel_id=1, source_target_pairs={{0,4},{1,5},{2,6},{3,7},{4,0},{5,1},{6,2},{7,3},{8,12},{9,13},{10,... | collective-permute-start | bytes 208904 | tf_op jit(solution)/shard_map/ppermute | solution.py:636
  71.2 0.5 collective-permute-start.26
  71.7 1.4 %factor_p.1 = (f32[2,1024,128]{2,1,0:T(8,128)}, bf16[2,1024,384]{2,1,0:T(8,128)(2,1)S(1)}) custom-call(f32[2,128,128]{2,1,0:T(8,128)S(1)} %factor.1.inv_ref, s16[528,128]{1,0:T(8,128)(2,1)S(1)} %add_code.7.code_ref.refs_0_, s16[528,128]{1,0:T(8,128)(2,1)S(1)} %collective-permute-done.11.code_ref.refs_1_, s16[528,128]{1,0:T(8,128)(2,1)S(1)} %add_code.6.code_ref.refs_2_, ...), custom_call_target="tpu_custom_call" | custom-call | tf_op jit(solution)/shard_map/factor_p/pallas_call | solution.py:555
  73.1 0.3 collective-permute-done.24.refs_6_
  73.4 0.7 collective-permute-done.28.refs_4_
  74.2 1.3 %collective-permute-done.26.refs_2_ = s16[272,128]{1,0:T(8,128)(2,1)S(1)} collective-permute-done((s16[272,128]{1,0:T(8,128)(2,1)S(1)}, s16[272,128]{1,0:T(8,128)(2,1)S(1)}, u32[]{:S(2)}, u32[]{:S(2)}) %collective-permute-start.26) | collective-permute-done | bytes 69664 | tf_op jit(solution)/shard_map/ppermute | solution.py:636
  75.5 0.5 collective-permute-start.30
  76.0 0.7 collective-permute-done.27.refs_3_
  76.7 0.2 collective-permute-done.30.refs_7_
  76.9 4.5 %error.1 = (f32[2,1,1024,1024]{3,2,1,0:T(8,128)}, f32[2,1024,128]{2,1,0:T(8,128)}) custom-call(bf16[2,1024,384]{2,1,0:T(8,128)(2,1)S(1)} %get-tuple-element.113.p3_ref, f32[2,128,128]{2,1,0:T(8,128)S(1)} %factor.1.inv_ref, s16[272,128]{1,0:T(8,128)(2,1)S(1)} %code_sum.1.refs_0_, s16[272,128]{1,0:T(8,128)(2,1)S(1)} %collective-permute-done.25.refs_1_, ...), custom_call_target="tpu_custom_call" | custom-call | tf_op jit(solution)/shard_map/error/pallas_call | solution.py:611
  (26 shorter events, 0.1 us)
Async XLA Ops:
  0.6 12.5 %copy-start = (bf16[2,512,128]{2,1,0:T(8,128)(2,1)S(1)}, bf16[2,512,128]{2,1,0:T(8,128)(2,1)}, u32[]{:S(2)}) copy-start(bf16[2,512,128]{2,1,0:T(8,128)(2,1)} %refs_0_.2) | copy-start | bytes 786436
  0.6 12.1 %collective-permute-start.1 = (bf16[2,512,128]{2,1,0:T(8,128)(2,1)}, bf16[2,512,128]{2,1,0:T(8,128)(2,1)S(1)}, u32[]{:S(2)}, u32[]{:S(2)}) collective-permute-start(bf16[2,512,128]{2,1,0:T(8,128)(2,1)} %refs_0_.2), channel_id=1, source_target_pairs={{0,4},{1,5},{2,6},{3,7},{4,0},{5,1},{6,2},{7,3},{8,12},{9,13},{10,... | collective-permute-start | bytes 786440 | tf_op jit(solution)/shard_map/ppermute | solution.py:636
  3.7 9.4 %collective-permute-start = (bf16[2,512,128]{2,1,0:T(8,128)(2,1)}, bf16[2,512,128]{2,1,0:T(8,128)(2,1)S(1)}, u32[]{:S(2)}, u32[]{:S(2)}) collective-permute-start(bf16[2,512,128]{2,1,0:T(8,128)(2,1)} %refs_0_.2), channel_id=1, source_target_pairs={{0,2},{1,3},{2,0},{3,1},{4,6},{5,7},{6,4},{7,5},{8,10},{9,11},{10,... | collective-permute-start | bytes 786440 | tf_op jit(solution)/shard_map/ppermute | solution.py:636
  5.2 11.9 %collective-permute-start.2 = (bf16[2,512,128]{2,1,0:T(8,128)(2,1)}, bf16[2,512,128]{2,1,0:T(8,128)(2,1)S(1)}, u32[]{:S(2)}, u32[]{:S(2)}) collective-permute-start(bf16[2,512,128]{2,1,0:T(8,128)(2,1)} %refs_0_.2), channel_id=1, source_target_pairs={{0,6},{1,7},{2,4},{3,5},{4,2},{5,3},{6,0},{7,1},{8,14},{9,15},{10,... | collective-permute-start | bytes 786440 | tf_op jit(solution)/shard_map/ppermute | solution.py:636
  13.1 3.9 %collective-permute-start.3 = (bf16[2,512,128]{2,1,0:T(8,128)(2,1)S(1)}, bf16[2,512,128]{2,1,0:T(8,128)(2,1)S(1)}, u32[]{:S(2)}, u32[]{:S(2)}) collective-permute-start(bf16[2,512,128]{2,1,0:T(8,128)(2,1)S(1)} %copy-done), channel_id=1, source_target_pairs={{0,1},{1,0},{2,3},{3,2},{4,5},{5,4},{6,7},{7,6},{8,9},{9,8},{10,11... | collective-permute-start | bytes 786440 | tf_op jit(solution)/shard_map/ppermute | solution.py:636
  13.1 3.9 %collective-permute-start.4 = (bf16[2,512,128]{2,1,0:T(8,128)(2,1)S(1)}, bf16[2,512,128]{2,1,0:T(8,128)(2,1)S(1)}, u32[]{:S(2)}, u32[]{:S(2)}) collective-permute-start(bf16[2,512,128]{2,1,0:T(8,128)(2,1)S(1)} %collective-permute-done.refs_2_), channel_id=1, source_target_pairs={{0,1},{1,0},{2,3},{3,2},{4,5},{5,4},{6,7},{7,6},{8,9},{9,8},{10,11... | collective-permute-start | bytes 786440 | tf_op jit(solution)/shard_map/ppermute | solution.py:636
  13.6 3.4 %collective-permute-start.5 = (bf16[2,512,128]{2,1,0:T(8,128)(2,1)S(1)}, bf16[2,512,128]{2,1,0:T(8,128)(2,1)S(1)}, u32[]{:S(2)}, u32[]{:S(2)}) collective-permute-start(bf16[2,512,128]{2,1,0:T(8,128)(2,1)S(1)} %collective-permute-done.1.refs_4_), channel_id=1, source_target_pairs={{0,1},{1,0},{2,3},{3,2},{4,5},{5,4},{6,7},{7,6},{8,9},{9,8},{10,11... | collective-permute-start | bytes 786440 | tf_op jit(solution)/shard_map/ppermute | solution.py:636
  17.1 1.6 %collective-permute-start.6 = (bf16[2,512,128]{2,1,0:T(8,128)(2,1)S(1)}, bf16[2,512,128]{2,1,0:T(8,128)(2,1)S(1)}, u32[]{:S(2)}, u32[]{:S(2)}) collective-permute-start(bf16[2,512,128]{2,1,0:T(8,128)(2,1)S(1)} %collective-permute-done.2.refs_1_.refs_6_), channel_id=1, source_target_pairs={{0,1},{1,0},{2,3},{3,2},{4,5},{5,4},{6,7},{7,6},{8,9},{9,8},{10,11... | collective-permute-start | bytes 786440 | tf_op jit(solution)/shard_map/ppermute | solution.py:636
  19.5 6.1 %collective-permute-start.9 = (s16[528,128]{1,0:T(8,128)(2,1)S(1)}, s16[528,128]{1,0:T(8,128)(2,1)S(1)}, u32[]{:S(2)}, u32[]{:S(2)}) collective-permute-start(s16[528,128]{1,0:T(8,128)(2,1)S(1)} %get-tuple-element.80), channel_id=1, source_target_pairs={{0,8},{8,0},{16,24},{24,16},{1,9},{9,1},{17,25},{25,17},{2,10},{10... | collective-permute-start | bytes 405512 | tf_op jit(solution)/shard_map/ppermute | solution.py:636
  22.2 6.6 %collective-permute-start.7 = (s16[528,128]{1,0:T(8,128)(2,1)S(1)}, s16[528,128]{1,0:T(8,128)(2,1)S(1)}, u32[]{:S(2)}, u32[]{:S(2)}) collective-permute-start(s16[528,128]{1,0:T(8,128)(2,1)S(1)} %get-tuple-element.75), channel_id=1, source_target_pairs={{0,8},{8,0},{16,24},{24,16},{1,9},{9,1},{17,25},{25,17},{2,10},{10... | collective-permute-start | bytes 405512 | tf_op jit(solution)/shard_map/ppermute | solution.py:636
  25.8 12.5 %collective-permute-start.10 = (s16[528,128]{1,0:T(8,128)(2,1)S(1)}, s16[528,128]{1,0:T(8,128)(2,1)S(1)}, u32[]{:S(2)}, u32[]{:S(2)}) collective-permute-start(s16[528,128]{1,0:T(8,128)(2,1)S(1)} %add_code.5.mine_ref), channel_id=1, source_target_pairs={{0,16},{8,24},{16,0},{24,8},{1,17},{9,25},{17,1},{25,9},{2,18},{10... | collective-permute-start | bytes 405512 | tf_op jit(solution)/shard_map/ppermute | solution.py:636
  28.9 11.3 %collective-permute-start.8 = (s16[528,128]{1,0:T(8,128)(2,1)S(1)}, s16[528,128]{1,0:T(8,128)(2,1)S(1)}, u32[]{:S(2)}, u32[]{:S(2)}) collective-permute-start(s16[528,128]{1,0:T(8,128)(2,1)S(1)} %add_code.4.mine_ref), channel_id=1, source_target_pairs={{0,16},{8,24},{16,0},{24,8},{1,17},{9,25},{17,1},{25,9},{2,18},{10... | collective-permute-start | bytes 405512 | tf_op jit(solution)/shard_map/ppermute | solution.py:636
  38.5 6.4 %collective-permute-start.12 = (s16[528,128]{1,0:T(8,128)(2,1)S(1)}, s16[528,128]{1,0:T(8,128)(2,1)S(1)}, u32[]{:S(2)}, u32[]{:S(2)}) collective-permute-start(s16[528,128]{1,0:T(8,128)(2,1)S(1)} %add_code.6.code_ref.refs_2_), channel_id=1, source_target_pairs={{0,8},{8,0},{16,24},{24,16},{1,9},{9,1},{17,25},{25,17},{2,10},{10... | collective-permute-start | bytes 405512 | tf_op jit(solution)/shard_map/ppermute | solution.py:636
  40.4 22.6 %copy-start.1 = (s32[2]{0:T(128)S(1)}, s32[2]{0:T(128)}, u32[]{:S(2)}) copy-start(s32[2]{0:T(128)} %ranks_ref.3) | copy-start | bytes 28
  40.4 6.0 %collective-permute-start.11 = (s16[528,128]{1,0:T(8,128)(2,1)S(1)}, s16[528,128]{1,0:T(8,128)(2,1)S(1)}, u32[]{:S(2)}, u32[]{:S(2)}) collective-permute-start(s16[528,128]{1,0:T(8,128)(2,1)S(1)} %add_code.7.code_ref.refs_0_), channel_id=1, source_target_pairs={{0,8},{8,0},{16,24},{24,16},{1,9},{9,1},{17,25},{25,17},{2,10},{10... | collective-permute-start | bytes 405512 | tf_op jit(solution)/shard_map/ppermute | solution.py:636
  47.3 1.4 %collective-permute-start.21 = (f32[2,128,128]{2,1,0:T(8,128)S(1)}, f32[2,128,128]{2,1,0:T(8,128)S(1)}, u32[]{:S(2)}, u32[]{:S(2)}) collective-permute-start(f32[2,128,128]{2,1,0:T(8,128)S(1)} %pad_maximum_fusion), channel_id=1, source_target_pairs={{0,1},{1,0},{2,3},{3,2},{4,5},{5,4},{6,7},{7,6},{8,9},{9,8},{10,11... | collective-permute-start | bytes 393224 | tf_op jit(solution)/shard_map/ppermute | solution.py:636
  47.4 2.9 %collective-permute-start.14 = (f32[512,128]{1,0:T(8,128)S(1)}, f32[512,128]{1,0:T(8,128)S(1)}, u32[]{:S(2)}, u32[]{:S(2)}) collective-permute-start(f32[512,128]{1,0:T(8,128)S(1)} %get-tuple-element.96), channel_id=1, source_target_pairs={{0,1},{1,0},{2,3},{3,2},{4,5},{5,4},{6,7},{7,6},{8,9},{9,8},{10,11... | collective-permute-start | bytes 786440 | tf_op jit(solution)/shard_map/ppermute | solution.py:636
  47.9 2.4 %collective-permute-start.13 = (f32[512,128]{1,0:T(8,128)S(1)}, f32[512,128]{1,0:T(8,128)S(1)}, u32[]{:S(2)}, u32[]{:S(2)}) collective-permute-start(f32[512,128]{1,0:T(8,128)S(1)} %get-tuple-element.95), channel_id=1, source_target_pairs={{0,1},{1,0},{2,3},{3,2},{4,5},{5,4},{6,7},{7,6},{8,9},{9,8},{10,11... | collective-permute-start | bytes 786440 | tf_op jit(solution)/shard_map/ppermute | solution.py:636
  48.8 6.4 %collective-permute-start.22 = (f32[2,128,128]{2,1,0:T(8,128)S(1)}, f32[2,128,128]{2,1,0:T(8,128)S(1)}, u32[]{:S(2)}, u32[]{:S(2)}) collective-permute-start(f32[2,128,128]{2,1,0:T(8,128)S(1)} %fusion), channel_id=1, source_target_pairs={{0,2},{1,3},{2,0},{3,1},{4,6},{5,7},{6,4},{7,5},{8,10},{9,11},{10,... | collective-permute-start | bytes 393224 | tf_op jit(solution)/shard_map/ppermute | solution.py:636
  50.6 6.2 %collective-permute-start.15 = (s16[272,128]{1,0:T(8,128)(2,1)S(1)}, s16[272,128]{1,0:T(8,128)(2,1)S(1)}, u32[]{:S(2)}, u32[]{:S(2)}) collective-permute-start(s16[272,128]{1,0:T(8,128)(2,1)S(1)} %get-tuple-element.99), channel_id=1, source_target_pairs={{0,2},{1,3},{2,0},{3,1},{4,6},{5,7},{6,4},{7,5},{8,10},{9,11},{10,... | collective-permute-start | bytes 208904 | tf_op jit(solution)/shard_map/ppermute | solution.py:636
  51.3 5.4 %collective-permute-start.16 = (s16[272,128]{1,0:T(8,128)(2,1)S(1)}, s16[272,128]{1,0:T(8,128)(2,1)S(1)}, u32[]{:S(2)}, u32[]{:S(2)}) collective-permute-start(s16[272,128]{1,0:T(8,128)(2,1)S(1)} %get-tuple-element.100), channel_id=1, source_target_pairs={{0,4},{1,5},{2,6},{3,7},{4,0},{5,1},{6,2},{7,3},{8,12},{9,13},{10,... | collective-permute-start | bytes 208904 | tf_op jit(solution)/shard_map/ppermute | solution.py:636
  52.8 5.6 %collective-permute-start.17 = (s16[272,128]{1,0:T(8,128)(2,1)S(1)}, s16[272,128]{1,0:T(8,128)(2,1)S(1)}, u32[]{:S(2)}, u32[]{:S(2)}) collective-permute-start(s16[272,128]{1,0:T(8,128)(2,1)S(1)} %get-tuple-element.101), channel_id=1, source_target_pairs={{0,6},{1,7},{2,4},{3,5},{4,2},{5,3},{6,0},{7,1},{8,14},{9,15},{10,... | collective-permute-start | bytes 208904 | tf_op jit(solution)/shard_map/ppermute | solution.py:636
  55.2 7.9 %collective-permute-start.23 = (f32[2,128,128]{2,1,0:T(8,128)S(1)}, f32[2,128,128]{2,1,0:T(8,128)S(1)}, u32[]{:S(2)}, u32[]{:S(2)}) collective-permute-start(f32[2,128,128]{2,1,0:T(8,128)S(1)} %fusion.1), channel_id=1, source_target_pairs={{0,4},{1,5},{2,6},{3,7},{4,0},{5,1},{6,2},{7,3},{8,12},{9,13},{10,... | collective-permute-start | bytes 393224 | tf_op jit(solution)/shard_map/ppermute | solution.py:636
  58.6 9.4 %collective-permute-start.20 = (s16[272,128]{1,0:T(8,128)(2,1)S(1)}, s16[272,128]{1,0:T(8,128)(2,1)S(1)}, u32[]{:S(2)}, u32[]{:S(2)}) collective-permute-start(s16[272,128]{1,0:T(8,128)(2,1)S(1)} %code.1.refs_0_), channel_id=1, source_target_pairs={{0,24},{8,16},{16,8},{24,0},{1,25},{9,17},{17,9},{25,1},{2,26},{10... | collective-permute-start | bytes 208904 | tf_op jit(solution)/shard_map/ppermute | solution.py:636
  61.9 6.0 %collective-permute-start.19 = (s16[272,128]{1,0:T(8,128)(2,1)S(1)}, s16[272,128]{1,0:T(8,128)(2,1)S(1)}, u32[]{:S(2)}, u32[]{:S(2)}) collective-permute-start(s16[272,128]{1,0:T(8,128)(2,1)S(1)} %code.1.refs_0_), channel_id=1, source_target_pairs={{0,16},{8,24},{16,0},{24,8},{1,17},{9,25},{17,1},{25,9},{2,18},{10... | collective-permute-start | bytes 208904 | tf_op jit(solution)/shard_map/ppermute | solution.py:636
  62.0 6.0 %collective-permute-start.18 = (s16[272,128]{1,0:T(8,128)(2,1)S(1)}, s16[272,128]{1,0:T(8,128)(2,1)S(1)}, u32[]{:S(2)}, u32[]{:S(2)}) collective-permute-start(s16[272,128]{1,0:T(8,128)(2,1)S(1)} %code.1.refs_0_), channel_id=1, source_target_pairs={{0,8},{8,0},{16,24},{24,16},{1,9},{9,1},{17,25},{25,17},{2,10},{10... | collective-permute-start | bytes 208904 | tf_op jit(solution)/shard_map/ppermute | solution.py:636
  68.1 5.3 %collective-permute-start.24 = (s16[272,128]{1,0:T(8,128)(2,1)S(1)}, s16[272,128]{1,0:T(8,128)(2,1)S(1)}, u32[]{:S(2)}, u32[]{:S(2)}) collective-permute-start(s16[272,128]{1,0:T(8,128)(2,1)S(1)} %code_sum.1.refs_0_), channel_id=1, source_target_pairs={{0,6},{1,7},{2,4},{3,5},{4,2},{5,3},{6,0},{7,1},{8,14},{9,15},{10,... | collective-permute-start | bytes 208904 | tf_op jit(solution)/shard_map/ppermute | solution.py:636
  69.7 4.5 %collective-permute-start.28 = (s16[272,128]{1,0:T(8,128)(2,1)S(1)}, s16[272,128]{1,0:T(8,128)(2,1)S(1)}, u32[]{:S(2)}, u32[]{:S(2)}) collective-permute-start(s16[272,128]{1,0:T(8,128)(2,1)S(1)} %code_sum.1.refs_0_), channel_id=1, source_target_pairs={{0,4},{1,5},{2,6},{3,7},{4,0},{5,1},{6,2},{7,3},{8,12},{9,13},{10,... | collective-permute-start | bytes 208904 | tf_op jit(solution)/shard_map/ppermute | solution.py:636
  71.2 4.3 %collective-permute-start.26 = (s16[272,128]{1,0:T(8,128)(2,1)S(1)}, s16[272,128]{1,0:T(8,128)(2,1)S(1)}, u32[]{:S(2)}, u32[]{:S(2)}) collective-permute-start(s16[272,128]{1,0:T(8,128)(2,1)S(1)} %code_sum.1.refs_0_), channel_id=1, source_target_pairs={{0,2},{1,3},{2,0},{3,1},{4,6},{5,7},{6,4},{7,5},{8,10},{9,11},{10,... | collective-permute-start | bytes 208904 | tf_op jit(solution)/shard_map/ppermute | solution.py:636
  71.7 4.3 %collective-permute-start.25 = (s16[272,128]{1,0:T(8,128)(2,1)S(1)}, s16[272,128]{1,0:T(8,128)(2,1)S(1)}, u32[]{:S(2)}, u32[]{:S(2)}) collective-permute-start(s16[272,128]{1,0:T(8,128)(2,1)S(1)} %code_sum.1.refs_0_), channel_id=1, source_target_pairs={{0,1},{1,0},{2,3},{3,2},{4,5},{5,4},{6,7},{7,6},{8,9},{9,8},{10,11... | collective-permute-start | bytes 208904 | tf_op jit(solution)/shard_map/ppermute | solution.py:636
  74.2 1.8 %collective-permute-start.29 = (s16[272,128]{1,0:T(8,128)(2,1)S(1)}, s16[272,128]{1,0:T(8,128)(2,1)S(1)}, u32[]{:S(2)}, u32[]{:S(2)}) collective-permute-start(s16[272,128]{1,0:T(8,128)(2,1)S(1)} %collective-permute-done.28.refs_4_), channel_id=1, source_target_pairs={{0,1},{1,0},{2,3},{3,2},{4,5},{5,4},{6,7},{7,6},{8,9},{9,8},{10,11... | collective-permute-start | bytes 208904 | tf_op jit(solution)/shard_map/ppermute | solution.py:636
  75.5 1.3 %collective-permute-start.27 = (s16[272,128]{1,0:T(8,128)(2,1)S(1)}, s16[272,128]{1,0:T(8,128)(2,1)S(1)}, u32[]{:S(2)}, u32[]{:S(2)}) collective-permute-start(s16[272,128]{1,0:T(8,128)(2,1)S(1)} %collective-permute-done.26.refs_2_), channel_id=1, source_target_pairs={{0,1},{1,0},{2,3},{3,2},{4,5},{5,4},{6,7},{7,6},{8,9},{9,8},{10,11... | collective-permute-start | bytes 208904 | tf_op jit(solution)/shard_map/ppermute | solution.py:636
  75.5 1.4 %collective-permute-start.30 = (s16[272,128]{1,0:T(8,128)(2,1)S(1)}, s16[272,128]{1,0:T(8,128)(2,1)S(1)}, u32[]{:S(2)}, u32[]{:S(2)}) collective-permute-start(s16[272,128]{1,0:T(8,128)(2,1)S(1)} %collective-permute-done.24.refs_6_), channel_id=1, source_target_pairs={{0,1},{1,0},{2,3},{3,2},{4,5},{5,4},{6,7},{7,6},{8,9},{9,8},{10,11... | collective-permute-start | bytes 208904 | tf_op jit(solution)/shard_map/ppermute | solution.py:636

commit v8 on v7

--- a/solution.py
+++ b/solution.py
@@ -574,6 +574,12 @@
     share = right_ref.shape[1] // pieces
     me = lax.axis_index("fsdp") if pieces > 1 else 0
     copies = []
+
+    def send_right(m, fq_t):
+        q_ref[m] = fq_t.T
+        copies.append(pltpu.make_async_copy(q_ref.at[m], fq_ref.at[m], sems.at[len(copies)]))
+        copies[-1].start()
+
     for m in range(count):
         for r, code in enumerate(codes):
             place = (me ^ r) & 1 if pieces > 1 else 0
@@ -588,6 +594,8 @@
         fq_t = both[:width] + both[width:] + mm(i_high, r_low)
         q_high, q_low = halves(fq_t)
         q3 = jnp.concatenate([q_high, q_high, q_low], axis=0)
+        if m > 0:
+            send_right(m, fq_t)
         for start in range(0, rows, tile):
             part = pl.ds(start, tile)
             buf_ref[m, part] = full_refs[m][part] - mm(p3_ref[m, part], q3)
@@ -595,9 +603,8 @@
                 pltpu.make_async_copy(buf_ref.at[m, part], err_ref.at[m, 0, part], sems.at[len(copies)])
             )
             copies[-1].start()
-        q_ref[m] = fq_t.T
-        copies.append(pltpu.make_async_copy(q_ref.at[m], fq_ref.at[m], sems.at[len(copies)]))
-        copies[-1].start()
+        if m == 0:
+            send_right(m, fq_t)
     for copy in copies:
         copy.wait()
 

time: 81.7 us -> 81.7 us (level)
  no operation moved by 1% of the time
where the time goes in v8:
time: 81.7 us; the launch traced here: 81.5 us
  starting transfers between devices  30.5 us (37%)
  Pallas kernels  28 us (34%)
  waiting for transfers between devices  21.9 us (27%)
  between operations  1.01 us (1%)
    ppermute x31, starting transfers between devices, across(): return lax.ppermute(x, axis, [(i, i ^ bit) for i in range(size)])  30.5 us
    ppermute x31, waiting for transfers between devices, across(): return lax.ppermute(x, axis, [(i, i ^ bit) for i in range(size)])  21.9 us
    pallas_call x1, Pallas kernels, feedback_q(): pl.pallas_call(feedback_q_kernel, in_specs=[far] * 4, out_specs=[VMEM] *...  7.55 us
    pallas_call x1, Pallas kernels, factor(): pl.pallas_call(factor_kernel, in_specs=[SMEM, VMEM], out_specs=VMEM, out_...  4.86 us
    pallas_call x1, Pallas kernels, error(): pl.pallas_call(functools.partial(error_kernel, count, len(codes), groups)...  4.48 us
    pallas_call x2, Pallas kernels, full(): pl.pallas_call(functools.partial(full_kernel, m), in_specs=[VMEM] * (2 +...  3.13 us
    pallas_call x2, Pallas kernels, other_half(): pl.pallas_call(functools.partial(other_half_kernel, halved), in_specs=[VM...  1.69 us
    pallas_call x2, Pallas kernels, left_code(): pl.pallas_call(functools.partial(left_code_kernel, m, keys), in_specs=[VM...  1.69 us
  transfers between devices with their start and end apart: 31, of which 16 were waited for; matrix products, arithmetic and copies ran while one was open for 0% of the time, Pallas kernels for 26%

profile of v8, /device:TPU:0, one launch (start us, length us, event | category | flops | bytes accessed | tf_op | source)
XLA Modules:
  0.0 81.5 jit_solution(1490738055737578563)
XLA Ops:
  0.6 3.0 %collective-permute-start.1 = (bf16[2,512,128]{2,1,0:T(8,128)(2,1)}, bf16[2,512,128]{2,1,0:T(8,128)(2,1)S(1)}, u32[]{:S(2)}, u32[]{:S(2)}) collective-permute-start(bf16[2,512,128]{2,1,0:T(8,128)(2,1)} %refs_0_.2), channel_id=1, source_target_pairs={{0,4},{1,5},{2,6},{3,7},{4,0},{5,1},{6,2},{7,3},{8,12},{9,13},{10,... | collective-permute-start | bytes 786440 | tf_op jit(solution)/shard_map/ppermute | solution.py:643
  3.7 1.5 %collective-permute-start = (bf16[2,512,128]{2,1,0:T(8,128)(2,1)}, bf16[2,512,128]{2,1,0:T(8,128)(2,1)S(1)}, u32[]{:S(2)}, u32[]{:S(2)}) collective-permute-start(bf16[2,512,128]{2,1,0:T(8,128)(2,1)} %refs_0_.2), channel_id=1, source_target_pairs={{0,2},{1,3},{2,0},{3,1},{4,6},{5,7},{6,4},{7,5},{8,10},{9,11},{10,... | collective-permute-start | bytes 786440 | tf_op jit(solution)/shard_map/ppermute | solution.py:643
  5.2 0.0 collective-permute-start.2
  5.2 7.6 %feedback_q.1 = (f32[2,1024,1024]{2,1,0:T(8,128)S(1)}, f32[2,1024,128]{2,1,0:T(8,128)S(1)}, bf16[2,1024,256]{2,1,0:T(8,128)(2,1)S(1)}, bf16[1024,512]{1,0:T(8,128)(2,1)S(1)}) custom-call(s32[2]{0:T(128)} %ranks_ref.3, f32[2,1,1024,1024]{3,2,1,0:T(8,128)} %fb_ref.1, f32[2,1024,128]{2,1,0:T(8,128)} %q_ref.1, bf16[512,1024]{1,0:T(8,128)(2,1)} %in_ref.1), custom_call_target="tpu_custom_call" | custom-call | tf_op jit(solution)/shard_map/feedback_q/pallas_call | solution.py:96
  12.8 0.3 collective-permute-done.refs_2_
  13.1 0.0 collective-permute-start.3
  13.1 0.5 collective-permute-start.4
  13.6 0.0 collective-permute-start.5
  13.6 3.4 %collective-permute-done.2.refs_1_.refs_6_ = bf16[2,512,128]{2,1,0:T(8,128)(2,1)S(1)} collective-permute-done((bf16[2,512,128]{2,1,0:T(8,128)(2,1)}, bf16[2,512,128]{2,1,0:T(8,128)(2,1)S(1)}, u32[]{:S(2)}, u32[]{:S(2)}) %collective-permute-start.2) | collective-permute-done | bytes 262176 | tf_op jit(solution)/shard_map/ppermute | solution.py:643
  17.1 0.1 collective-permute-start.6
  17.2 0.6 begin.1.refs_0_
  17.8 0.9 %collective-permute-done.6.refs_2_.refs_7_ = bf16[2,512,128]{2,1,0:T(8,128)(2,1)S(1)} collective-permute-done((bf16[2,512,128]{2,1,0:T(8,128)(2,1)S(1)}, bf16[2,512,128]{2,1,0:T(8,128)(2,1)S(1)}, u32[]{:S(2)}, u32[]{:S(2)}) %collective-permute-start.6) | collective-permute-done | bytes 262176 | tf_op jit(solution)/shard_map/ppermute | solution.py:643
  18.7 0.8 %left_code_1.1 = (f32[512,128]{1,0:T(8,128)S(1)}, s16[528,128]{1,0:T(8,128)(2,1)S(1)}) custom-call(bf16[2,1024,256]{2,1,0:T(8,128)(2,1)S(1)} %get-tuple-element.64.q2_ref, bf16[1024,512]{1,0:T(8,128)(2,1)S(1)} %get-tuple-element.82.in_ref, f32[2,1024,128]{2,1,0:T(8,128)S(1)} %get-tuple-element.66.fbq_ref, f32[2,512,256]{2,1,0:T(8,128)S(1)} %begin.1.refs_0_, ...), custom_call_target="tpu_custom_call" | custom-call | tf_op jit(solution)/shard_map/left_code_1/pallas_call | solution.py:242
  19.5 1.8 %collective-permute-start.9 = (s16[528,128]{1,0:T(8,128)(2,1)S(1)}, s16[528,128]{1,0:T(8,128)(2,1)S(1)}, u32[]{:S(2)}, u32[]{:S(2)}) collective-permute-start(s16[528,128]{1,0:T(8,128)(2,1)S(1)} %get-tuple-element.80), channel_id=1, source_target_pairs={{0,8},{8,0},{16,24},{24,16},{1,9},{9,1},{17,25},{25,17},{2,10},{10... | collective-permute-start | bytes 405512 | tf_op jit(solution)/shard_map/ppermute | solution.py:643
  21.3 0.8 %left_code_0.1 = (f32[512,128]{1,0:T(8,128)S(1)}, s16[528,128]{1,0:T(8,128)(2,1)S(1)}) custom-call(bf16[2,1024,256]{2,1,0:T(8,128)(2,1)S(1)} %get-tuple-element.64.q2_ref, bf16[1024,512]{1,0:T(8,128)(2,1)S(1)} %get-tuple-element.82.in_ref, f32[2,1024,128]{2,1,0:T(8,128)S(1)} %get-tuple-element.66.fbq_ref, f32[2,512,256]{2,1,0:T(8,128)S(1)} %begin.1.refs_0_, ...), custom_call_target="tpu_custom_call" | custom-call | tf_op jit(solution)/shard_map/left_code_0/pallas_call | solution.py:242
  22.2 0.4 collective-permute-start.7
  22.5 3.1 %collective-permute-done.9.theirs_ref = s16[528,128]{1,0:T(8,128)(2,1)S(1)} collective-permute-done((s16[528,128]{1,0:T(8,128)(2,1)S(1)}, s16[528,128]{1,0:T(8,128)(2,1)S(1)}, u32[]{:S(2)}, u32[]{:S(2)}) %collective-permute-start.9) | collective-permute-done | bytes 135200 | tf_op jit(solution)/shard_map/ppermute | solution.py:643
  25.7 0.1 add_code.5.mine_ref
  25.8 3.0 %collective-permute-start.10 = (s16[528,128]{1,0:T(8,128)(2,1)S(1)}, s16[528,128]{1,0:T(8,128)(2,1)S(1)}, u32[]{:S(2)}, u32[]{:S(2)}) collective-permute-start(s16[528,128]{1,0:T(8,128)(2,1)S(1)} %add_code.5.mine_ref), channel_id=1, source_target_pairs={{0,16},{8,24},{16,0},{24,8},{1,17},{9,25},{17,1},{25,9},{2,18},{10... | collective-permute-start | bytes 405512 | tf_op jit(solution)/shard_map/ppermute | solution.py:643
  28.8 0.1 add_code.4.mine_ref
  28.9 2.8 %collective-permute-start.8 = (s16[528,128]{1,0:T(8,128)(2,1)S(1)}, s16[528,128]{1,0:T(8,128)(2,1)S(1)}, u32[]{:S(2)}, u32[]{:S(2)}) collective-permute-start(s16[528,128]{1,0:T(8,128)(2,1)S(1)} %add_code.4.mine_ref), channel_id=1, source_target_pairs={{0,16},{8,24},{16,0},{24,8},{1,17},{9,25},{17,1},{25,9},{2,18},{10... | collective-permute-start | bytes 405512 | tf_op jit(solution)/shard_map/ppermute | solution.py:643
  31.7 1.6 %full_0.1.full_ref.refs_8_ = f32[1024,1024]{1,0:T(8,128)S(1)} custom-call(f32[2,1024,1024]{2,1,0:T(8,128)S(1)} %get-tuple-element.77.held_ref, bf16[1024,512]{1,0:T(8,128)(2,1)S(1)} %get-tuple-element.82.in_ref, bf16[2,512,128]{2,1,0:T(8,128)(2,1)S(1)} %copy-done, bf16[2,512,128]{2,1,0:T(8,128)(2,1)S(1)} %collective-permute-done.3.refs_1_, ...), custom_call_target="tpu_custom_call" | custom-call | tf_op jit(solution)/shard_map/full_0/pallas_call | solution.py:302
  33.2 1.6 %full_1.1.full_ref.refs_9_ = f32[1024,1024]{1,0:T(8,128)S(1)} custom-call(f32[2,1024,1024]{2,1,0:T(8,128)S(1)} %get-tuple-element.77.held_ref, bf16[1024,512]{1,0:T(8,128)(2,1)S(1)} %get-tuple-element.82.in_ref, bf16[2,512,128]{2,1,0:T(8,128)(2,1)S(1)} %copy-done, bf16[2,512,128]{2,1,0:T(8,128)(2,1)S(1)} %collective-permute-done.3.refs_1_, ...), custom_call_target="tpu_custom_call" | custom-call | tf_op jit(solution)/shard_map/full_1/pallas_call | solution.py:302
  34.8 3.5 %collective-permute-done.10.theirs_ref = s16[528,128]{1,0:T(8,128)(2,1)S(1)} collective-permute-done((s16[528,128]{1,0:T(8,128)(2,1)S(1)}, s16[528,128]{1,0:T(8,128)(2,1)S(1)}, u32[]{:S(2)}, u32[]{:S(2)}) %collective-permute-start.10) | collective-permute-done | bytes 135200 | tf_op jit(solution)/shard_map/ppermute | solution.py:643
  38.3 0.2 add_code.6.code_ref.refs_2_
  38.5 0.4 collective-permute-start.12
  39.0 0.7 own_half_1.1
  39.7 0.6 collective-permute-done.8.theirs_ref
  40.2 0.2 add_code.7.code_ref.refs_0_
  40.4 0.0 copy-start.1
  40.4 1.2 %collective-permute-start.11 = (s16[528,128]{1,0:T(8,128)(2,1)S(1)}, s16[528,128]{1,0:T(8,128)(2,1)S(1)}, u32[]{:S(2)}, u32[]{:S(2)}) collective-permute-start(s16[528,128]{1,0:T(8,128)(2,1)S(1)} %add_code.7.code_ref.refs_0_), channel_id=1, source_target_pairs={{0,8},{8,0},{16,24},{24,16},{1,9},{9,1},{17,25},{25,17},{2,10},{10... | collective-permute-start | bytes 405512 | tf_op jit(solution)/shard_map/ppermute | solution.py:643
  41.6 0.7 own_half_0.1
  42.3 2.6 %collective-permute-done.12.code_ref.refs_3_ = s16[528,128]{1,0:T(8,128)(2,1)S(1)} collective-permute-done((s16[528,128]{1,0:T(8,128)(2,1)S(1)}, s16[528,128]{1,0:T(8,128)(2,1)S(1)}, u32[]{:S(2)}, u32[]{:S(2)}) %collective-permute-start.12) | collective-permute-done | bytes 135200 | tf_op jit(solution)/shard_map/ppermute | solution.py:643
  44.9 0.8 other_half_1.1
  45.7 0.7 collective-permute-done.11.code_ref.refs_1_
  46.4 0.9 %other_half_0.1 = (f32[512,128]{1,0:T(8,128)S(1)}, f32[512,128]{1,0:T(8,128)S(1)}, f32[128,128]{1,0:T(8,128)S(1)}) custom-call(f32[1024,1024]{1,0:T(8,128)S(1)} %full_0.1.full_ref.refs_8_, s16[528,128]{1,0:T(8,128)(2,1)S(1)} %collective-permute-done.11.code_ref.refs_1_, f32[128,1024]{1,0:T(8,128)S(1)} %get-tuple-element.89.total_ref, ...), custom_call_target="tpu_custom_call" | custom-call | tf_op jit(solution)/shard_map/other_half_0/pallas_call | solution.py:365
  47.3 0.1 collective-permute-start.21
  47.4 0.5 collective-permute-start.14
  47.9 0.1 collective-permute-start.13
  48.0 0.8 collective-permute-done.21
  48.8 1.5 %collective-permute-start.22 = (f32[2,128,128]{2,1,0:T(8,128)S(1)}, f32[2,128,128]{2,1,0:T(8,128)S(1)}, u32[]{:S(2)}, u32[]{:S(2)}) collective-permute-start(f32[2,128,128]{2,1,0:T(8,128)S(1)} %fusion), channel_id=1, source_target_pairs={{0,2},{1,3},{2,0},{3,1},{4,6},{5,7},{6,4},{7,5},{8,10},{9,11},{10,... | collective-permute-start | bytes 393224 | tf_op jit(solution)/shard_map/ppermute | solution.py:643
  50.3 0.3 part_2.1
  50.6 0.7 collective-permute-start.15
  51.3 1.5 %collective-permute-start.16 = (s16[272,128]{1,0:T(8,128)(2,1)S(1)}, s16[272,128]{1,0:T(8,128)(2,1)S(1)}, u32[]{:S(2)}, u32[]{:S(2)}) collective-permute-start(s16[272,128]{1,0:T(8,128)(2,1)S(1)} %get-tuple-element.100), channel_id=1, source_target_pairs={{0,4},{1,5},{2,6},{3,7},{4,0},{5,1},{6,2},{7,3},{8,12},{9,13},{10,... | collective-permute-start | bytes 208904 | tf_op jit(solution)/shard_map/ppermute | solution.py:643
  52.8 1.3 %collective-permute-start.17 = (s16[272,128]{1,0:T(8,128)(2,1)S(1)}, s16[272,128]{1,0:T(8,128)(2,1)S(1)}, u32[]{:S(2)}, u32[]{:S(2)}) collective-permute-start(s16[272,128]{1,0:T(8,128)(2,1)S(1)} %get-tuple-element.101), channel_id=1, source_target_pairs={{0,6},{1,7},{2,4},{3,5},{4,2},{5,3},{6,0},{7,1},{8,14},{9,15},{10,... | collective-permute-start | bytes 208904 | tf_op jit(solution)/shard_map/ppermute | solution.py:643
  54.1 1.0 %collective-permute-done.22 = f32[2,128,128]{2,1,0:T(8,128)S(1)} collective-permute-done((f32[2,128,128]{2,1,0:T(8,128)S(1)}, f32[2,128,128]{2,1,0:T(8,128)S(1)}, u32[]{:S(2)}, u32[]{:S(2)}) %collective-permute-start.22) | collective-permute-done | bytes 131104 | tf_op jit(solution)/shard_map/ppermute | solution.py:643
  55.2 1.6 %collective-permute-start.23 = (f32[2,128,128]{2,1,0:T(8,128)S(1)}, f32[2,128,128]{2,1,0:T(8,128)S(1)}, u32[]{:S(2)}, u32[]{:S(2)}) collective-permute-start(f32[2,128,128]{2,1,0:T(8,128)S(1)} %fusion.1), channel_id=1, source_target_pairs={{0,4},{1,5},{2,6},{3,7},{4,0},{5,1},{6,2},{7,3},{8,12},{9,13},{10,... | collective-permute-start | bytes 393224 | tf_op jit(solution)/shard_map/ppermute | solution.py:643
  56.8 1.7 %collective-permute-done.17.refs_4_ = s16[272,128]{1,0:T(8,128)(2,1)S(1)} collective-permute-done((s16[272,128]{1,0:T(8,128)(2,1)S(1)}, s16[272,128]{1,0:T(8,128)(2,1)S(1)}, u32[]{:S(2)}, u32[]{:S(2)}) %collective-permute-start.17) | collective-permute-done | bytes 69664 | tf_op jit(solution)/shard_map/ppermute | solution.py:643
  58.4 0.1 code.1.refs_0_
  58.6 3.4 %collective-permute-start.20 = (s16[272,128]{1,0:T(8,128)(2,1)S(1)}, s16[272,128]{1,0:T(8,128)(2,1)S(1)}, u32[]{:S(2)}, u32[]{:S(2)}) collective-permute-start(s16[272,128]{1,0:T(8,128)(2,1)S(1)} %code.1.refs_0_), channel_id=1, source_target_pairs={{0,24},{8,16},{16,8},{24,0},{1,25},{9,17},{17,9},{25,1},{2,26},{10... | collective-permute-start | bytes 208904 | tf_op jit(solution)/shard_map/ppermute | solution.py:643
  62.0 1.1 %collective-permute-start.18 = (s16[272,128]{1,0:T(8,128)(2,1)S(1)}, s16[272,128]{1,0:T(8,128)(2,1)S(1)}, u32[]{:S(2)}, u32[]{:S(2)}) collective-permute-start(s16[272,128]{1,0:T(8,128)(2,1)S(1)} %code.1.refs_0_), channel_id=1, source_target_pairs={{0,8},{8,0},{16,24},{24,16},{1,9},{9,1},{17,25},{25,17},{2,10},{10... | collective-permute-start | bytes 208904 | tf_op jit(solution)/shard_map/ppermute | solution.py:643
  63.1 4.9 %factor.1.inv_ref = f32[2,128,128]{2,1,0:T(8,128)S(1)} custom-call(s32[2]{0:T(128)S(1)} %copy-done.1, f32[2,128,128]{2,1,0:T(8,128)S(1)} %add.11.gram_ref), custom_call_target="tpu_custom_call" | custom-call | tf_op jit(solution)/shard_map/factor/pallas_call | solution.py:520
  68.0 0.2 code_sum.1.refs_0_
  68.1 1.5 %collective-permute-start.24 = (s16[272,128]{1,0:T(8,128)(2,1)S(1)}, s16[272,128]{1,0:T(8,128)(2,1)S(1)}, u32[]{:S(2)}, u32[]{:S(2)}) collective-permute-start(s16[272,128]{1,0:T(8,128)(2,1)S(1)} %code_sum.1.refs_0_), channel_id=1, source_target_pairs={{0,6},{1,7},{2,4},{3,5},{4,2},{5,3},{6,0},{7,1},{8,14},{9,15},{10,... | collective-permute-start | bytes 208904 | tf_op jit(solution)/shard_map/ppermute | solution.py:643
  69.7 1.5 %collective-permute-start.28 = (s16[272,128]{1,0:T(8,128)(2,1)S(1)}, s16[272,128]{1,0:T(8,128)(2,1)S(1)}, u32[]{:S(2)}, u32[]{:S(2)}) collective-permute-start(s16[272,128]{1,0:T(8,128)(2,1)S(1)} %code_sum.1.refs_0_), channel_id=1, source_target_pairs={{0,4},{1,5},{2,6},{3,7},{4,0},{5,1},{6,2},{7,3},{8,12},{9,13},{10,... | collective-permute-start | bytes 208904 | tf_op jit(solution)/shard_map/ppermute | solution.py:643
  71.2 0.5 collective-permute-start.26
  71.7 1.4 %factor_p.1 = (f32[2,1024,128]{2,1,0:T(8,128)}, bf16[2,1024,384]{2,1,0:T(8,128)(2,1)S(1)}) custom-call(f32[2,128,128]{2,1,0:T(8,128)S(1)} %factor.1.inv_ref, s16[528,128]{1,0:T(8,128)(2,1)S(1)} %add_code.7.code_ref.refs_0_, s16[528,128]{1,0:T(8,128)(2,1)S(1)} %collective-permute-done.11.code_ref.refs_1_, s16[528,128]{1,0:T(8,128)(2,1)S(1)} %add_code.6.code_ref.refs_2_, ...), custom_call_target="tpu_custom_call" | custom-call | tf_op jit(solution)/shard_map/factor_p/pallas_call | solution.py:555
  73.1 0.3 collective-permute-done.24.refs_6_
  73.4 0.7 collective-permute-done.28.refs_4_
  74.2 1.3 %collective-permute-done.26.refs_2_ = s16[272,128]{1,0:T(8,128)(2,1)S(1)} collective-permute-done((s16[272,128]{1,0:T(8,128)(2,1)S(1)}, s16[272,128]{1,0:T(8,128)(2,1)S(1)}, u32[]{:S(2)}, u32[]{:S(2)}) %collective-permute-start.26) | collective-permute-done | bytes 69664 | tf_op jit(solution)/shard_map/ppermute | solution.py:643
  75.5 0.5 collective-permute-start.30
  76.0 0.7 collective-permute-done.27.refs_3_
  76.7 0.2 collective-permute-done.30.refs_7_
  76.9 4.5 %error.1 = (f32[2,1,1024,1024]{3,2,1,0:T(8,128)}, f32[2,1024,128]{2,1,0:T(8,128)}) custom-call(bf16[2,1024,384]{2,1,0:T(8,128)(2,1)S(1)} %get-tuple-element.113.p3_ref, f32[2,128,128]{2,1,0:T(8,128)S(1)} %factor.1.inv_ref, s16[272,128]{1,0:T(8,128)(2,1)S(1)} %code_sum.1.refs_0_, s16[272,128]{1,0:T(8,128)(2,1)S(1)} %collective-permute-done.25.refs_1_, ...), custom_call_target="tpu_custom_call" | custom-call | tf_op jit(solution)/shard_map/error/pallas_call | solution.py:618
  (26 shorter events, 0.1 us)
Async XLA Ops:
  0.6 12.5 %copy-start = (bf16[2,512,128]{2,1,0:T(8,128)(2,1)S(1)}, bf16[2,512,128]{2,1,0:T(8,128)(2,1)}, u32[]{:S(2)}) copy-start(bf16[2,512,128]{2,1,0:T(8,128)(2,1)} %refs_0_.2) | copy-start | bytes 786436
  0.6 12.1 %collective-permute-start.1 = (bf16[2,512,128]{2,1,0:T(8,128)(2,1)}, bf16[2,512,128]{2,1,0:T(8,128)(2,1)S(1)}, u32[]{:S(2)}, u32[]{:S(2)}) collective-permute-start(bf16[2,512,128]{2,1,0:T(8,128)(2,1)} %refs_0_.2), channel_id=1, source_target_pairs={{0,4},{1,5},{2,6},{3,7},{4,0},{5,1},{6,2},{7,3},{8,12},{9,13},{10,... | collective-permute-start | bytes 786440 | tf_op jit(solution)/shard_map/ppermute | solution.py:643
  3.7 9.4 %collective-permute-start = (bf16[2,512,128]{2,1,0:T(8,128)(2,1)}, bf16[2,512,128]{2,1,0:T(8,128)(2,1)S(1)}, u32[]{:S(2)}, u32[]{:S(2)}) collective-permute-start(bf16[2,512,128]{2,1,0:T(8,128)(2,1)} %refs_0_.2), channel_id=1, source_target_pairs={{0,2},{1,3},{2,0},{3,1},{4,6},{5,7},{6,4},{7,5},{8,10},{9,11},{10,... | collective-permute-start | bytes 786440 | tf_op jit(solution)/shard_map/ppermute | solution.py:643
  5.2 11.9 %collective-permute-start.2 = (bf16[2,512,128]{2,1,0:T(8,128)(2,1)}, bf16[2,512,128]{2,1,0:T(8,128)(2,1)S(1)}, u32[]{:S(2)}, u32[]{:S(2)}) collective-permute-start(bf16[2,512,128]{2,1,0:T(8,128)(2,1)} %refs_0_.2), channel_id=1, source_target_pairs={{0,6},{1,7},{2,4},{3,5},{4,2},{5,3},{6,0},{7,1},{8,14},{9,15},{10,... | collective-permute-start | bytes 786440 | tf_op jit(solution)/shard_map/ppermute | solution.py:643
  13.1 3.9 %collective-permute-start.3 = (bf16[2,512,128]{2,1,0:T(8,128)(2,1)S(1)}, bf16[2,512,128]{2,1,0:T(8,128)(2,1)S(1)}, u32[]{:S(2)}, u32[]{:S(2)}) collective-permute-start(bf16[2,512,128]{2,1,0:T(8,128)(2,1)S(1)} %copy-done), channel_id=1, source_target_pairs={{0,1},{1,0},{2,3},{3,2},{4,5},{5,4},{6,7},{7,6},{8,9},{9,8},{10,11... | collective-permute-start | bytes 786440 | tf_op jit(solution)/shard_map/ppermute | solution.py:643
  13.1 3.9 %collective-permute-start.4 = (bf16[2,512,128]{2,1,0:T(8,128)(2,1)S(1)}, bf16[2,512,128]{2,1,0:T(8,128)(2,1)S(1)}, u32[]{:S(2)}, u32[]{:S(2)}) collective-permute-start(bf16[2,512,128]{2,1,0:T(8,128)(2,1)S(1)} %collective-permute-done.refs_2_), channel_id=1, source_target_pairs={{0,1},{1,0},{2,3},{3,2},{4,5},{5,4},{6,7},{7,6},{8,9},{9,8},{10,11... | collective-permute-start | bytes 786440 | tf_op jit(solution)/shard_map/ppermute | solution.py:643
  13.6 3.4 %collective-permute-start.5 = (bf16[2,512,128]{2,1,0:T(8,128)(2,1)S(1)}, bf16[2,512,128]{2,1,0:T(8,128)(2,1)S(1)}, u32[]{:S(2)}, u32[]{:S(2)}) collective-permute-start(bf16[2,512,128]{2,1,0:T(8,128)(2,1)S(1)} %collective-permute-done.1.refs_4_), channel_id=1, source_target_pairs={{0,1},{1,0},{2,3},{3,2},{4,5},{5,4},{6,7},{7,6},{8,9},{9,8},{10,11... | collective-permute-start | bytes 786440 | tf_op jit(solution)/shard_map/ppermute | solution.py:643
  17.1 1.6 %collective-permute-start.6 = (bf16[2,512,128]{2,1,0:T(8,128)(2,1)S(1)}, bf16[2,512,128]{2,1,0:T(8,128)(2,1)S(1)}, u32[]{:S(2)}, u32[]{:S(2)}) collective-permute-start(bf16[2,512,128]{2,1,0:T(8,128)(2,1)S(1)} %collective-permute-done.2.refs_1_.refs_6_), channel_id=1, source_target_pairs={{0,1},{1,0},{2,3},{3,2},{4,5},{5,4},{6,7},{7,6},{8,9},{9,8},{10,11... | collective-permute-start | bytes 786440 | tf_op jit(solution)/shard_map/ppermute | solution.py:643
  19.5 6.1 %collective-permute-start.9 = (s16[528,128]{1,0:T(8,128)(2,1)S(1)}, s16[528,128]{1,0:T(8,128)(2,1)S(1)}, u32[]{:S(2)}, u32[]{:S(2)}) collective-permute-start(s16[528,128]{1,0:T(8,128)(2,1)S(1)} %get-tuple-element.80), channel_id=1, source_target_pairs={{0,8},{8,0},{16,24},{24,16},{1,9},{9,1},{17,25},{25,17},{2,10},{10... | collective-permute-start | bytes 405512 | tf_op jit(solution)/shard_map/ppermute | solution.py:643
  22.2 6.6 %collective-permute-start.7 = (s16[528,128]{1,0:T(8,128)(2,1)S(1)}, s16[528,128]{1,0:T(8,128)(2,1)S(1)}, u32[]{:S(2)}, u32[]{:S(2)}) collective-permute-start(s16[528,128]{1,0:T(8,128)(2,1)S(1)} %get-tuple-element.75), channel_id=1, source_target_pairs={{0,8},{8,0},{16,24},{24,16},{1,9},{9,1},{17,25},{25,17},{2,10},{10... | collective-permute-start | bytes 405512 | tf_op jit(solution)/shard_map/ppermute | solution.py:643
  25.8 12.5 %collective-permute-start.10 = (s16[528,128]{1,0:T(8,128)(2,1)S(1)}, s16[528,128]{1,0:T(8,128)(2,1)S(1)}, u32[]{:S(2)}, u32[]{:S(2)}) collective-permute-start(s16[528,128]{1,0:T(8,128)(2,1)S(1)} %add_code.5.mine_ref), channel_id=1, source_target_pairs={{0,16},{8,24},{16,0},{24,8},{1,17},{9,25},{17,1},{25,9},{2,18},{10... | collective-permute-start | bytes 405512 | tf_op jit(solution)/shard_map/ppermute | solution.py:643
  28.9 11.3 %collective-permute-start.8 = (s16[528,128]{1,0:T(8,128)(2,1)S(1)}, s16[528,128]{1,0:T(8,128)(2,1)S(1)}, u32[]{:S(2)}, u32[]{:S(2)}) collective-permute-start(s16[528,128]{1,0:T(8,128)(2,1)S(1)} %add_code.4.mine_ref), channel_id=1, source_target_pairs={{0,16},{8,24},{16,0},{24,8},{1,17},{9,25},{17,1},{25,9},{2,18},{10... | collective-permute-start | bytes 405512 | tf_op jit(solution)/shard_map/ppermute | solution.py:643
  38.5 6.4 %collective-permute-start.12 = (s16[528,128]{1,0:T(8,128)(2,1)S(1)}, s16[528,128]{1,0:T(8,128)(2,1)S(1)}, u32[]{:S(2)}, u32[]{:S(2)}) collective-permute-start(s16[528,128]{1,0:T(8,128)(2,1)S(1)} %add_code.6.code_ref.refs_2_), channel_id=1, source_target_pairs={{0,8},{8,0},{16,24},{24,16},{1,9},{9,1},{17,25},{25,17},{2,10},{10... | collective-permute-start | bytes 405512 | tf_op jit(solution)/shard_map/ppermute | solution.py:643
  40.4 22.6 %copy-start.1 = (s32[2]{0:T(128)S(1)}, s32[2]{0:T(128)}, u32[]{:S(2)}) copy-start(s32[2]{0:T(128)} %ranks_ref.3) | copy-start | bytes 28
  40.4 6.0 %collective-permute-start.11 = (s16[528,128]{1,0:T(8,128)(2,1)S(1)}, s16[528,128]{1,0:T(8,128)(2,1)S(1)}, u32[]{:S(2)}, u32[]{:S(2)}) collective-permute-start(s16[528,128]{1,0:T(8,128)(2,1)S(1)} %add_code.7.code_ref.refs_0_), channel_id=1, source_target_pairs={{0,8},{8,0},{16,24},{24,16},{1,9},{9,1},{17,25},{25,17},{2,10},{10... | collective-permute-start | bytes 405512 | tf_op jit(solution)/shard_map/ppermute | solution.py:643
  47.3 1.4 %collective-permute-start.21 = (f32[2,128,128]{2,1,0:T(8,128)S(1)}, f32[2,128,128]{2,1,0:T(8,128)S(1)}, u32[]{:S(2)}, u32[]{:S(2)}) collective-permute-start(f32[2,128,128]{2,1,0:T(8,128)S(1)} %pad_maximum_fusion), channel_id=1, source_target_pairs={{0,1},{1,0},{2,3},{3,2},{4,5},{5,4},{6,7},{7,6},{8,9},{9,8},{10,11... | collective-permute-start | bytes 393224 | tf_op jit(solution)/shard_map/ppermute | solution.py:643
  47.4 2.9 %collective-permute-start.14 = (f32[512,128]{1,0:T(8,128)S(1)}, f32[512,128]{1,0:T(8,128)S(1)}, u32[]{:S(2)}, u32[]{:S(2)}) collective-permute-start(f32[512,128]{1,0:T(8,128)S(1)} %get-tuple-element.96), channel_id=1, source_target_pairs={{0,1},{1,0},{2,3},{3,2},{4,5},{5,4},{6,7},{7,6},{8,9},{9,8},{10,11... | collective-permute-start | bytes 786440 | tf_op jit(solution)/shard_map/ppermute | solution.py:643
  47.9 2.4 %collective-permute-start.13 = (f32[512,128]{1,0:T(8,128)S(1)}, f32[512,128]{1,0:T(8,128)S(1)}, u32[]{:S(2)}, u32[]{:S(2)}) collective-permute-start(f32[512,128]{1,0:T(8,128)S(1)} %get-tuple-element.95), channel_id=1, source_target_pairs={{0,1},{1,0},{2,3},{3,2},{4,5},{5,4},{6,7},{7,6},{8,9},{9,8},{10,11... | collective-permute-start | bytes 786440 | tf_op jit(solution)/shard_map/ppermute | solution.py:643
  48.8 6.4 %collective-permute-start.22 = (f32[2,128,128]{2,1,0:T(8,128)S(1)}, f32[2,128,128]{2,1,0:T(8,128)S(1)}, u32[]{:S(2)}, u32[]{:S(2)}) collective-permute-start(f32[2,128,128]{2,1,0:T(8,128)S(1)} %fusion), channel_id=1, source_target_pairs={{0,2},{1,3},{2,0},{3,1},{4,6},{5,7},{6,4},{7,5},{8,10},{9,11},{10,... | collective-permute-start | bytes 393224 | tf_op jit(solution)/shard_map/ppermute | solution.py:643
  50.6 6.2 %collective-permute-start.15 = (s16[272,128]{1,0:T(8,128)(2,1)S(1)}, s16[272,128]{1,0:T(8,128)(2,1)S(1)}, u32[]{:S(2)}, u32[]{:S(2)}) collective-permute-start(s16[272,128]{1,0:T(8,128)(2,1)S(1)} %get-tuple-element.99), channel_id=1, source_target_pairs={{0,2},{1,3},{2,0},{3,1},{4,6},{5,7},{6,4},{7,5},{8,10},{9,11},{10,... | collective-permute-start | bytes 208904 | tf_op jit(solution)/shard_map/ppermute | solution.py:643
  51.3 5.4 %collective-permute-start.16 = (s16[272,128]{1,0:T(8,128)(2,1)S(1)}, s16[272,128]{1,0:T(8,128)(2,1)S(1)}, u32[]{:S(2)}, u32[]{:S(2)}) collective-permute-start(s16[272,128]{1,0:T(8,128)(2,1)S(1)} %get-tuple-element.100), channel_id=1, source_target_pairs={{0,4},{1,5},{2,6},{3,7},{4,0},{5,1},{6,2},{7,3},{8,12},{9,13},{10,... | collective-permute-start | bytes 208904 | tf_op jit(solution)/shard_map/ppermute | solution.py:643
  52.8 5.6 %collective-permute-start.17 = (s16[272,128]{1,0:T(8,128)(2,1)S(1)}, s16[272,128]{1,0:T(8,128)(2,1)S(1)}, u32[]{:S(2)}, u32[]{:S(2)}) collective-permute-start(s16[272,128]{1,0:T(8,128)(2,1)S(1)} %get-tuple-element.101), channel_id=1, source_target_pairs={{0,6},{1,7},{2,4},{3,5},{4,2},{5,3},{6,0},{7,1},{8,14},{9,15},{10,... | collective-permute-start | bytes 208904 | tf_op jit(solution)/shard_map/ppermute | solution.py:643
  55.2 7.9 %collective-permute-start.23 = (f32[2,128,128]{2,1,0:T(8,128)S(1)}, f32[2,128,128]{2,1,0:T(8,128)S(1)}, u32[]{:S(2)}, u32[]{:S(2)}) collective-permute-start(f32[2,128,128]{2,1,0:T(8,128)S(1)} %fusion.1), channel_id=1, source_target_pairs={{0,4},{1,5},{2,6},{3,7},{4,0},{5,1},{6,2},{7,3},{8,12},{9,13},{10,... | collective-permute-start | bytes 393224 | tf_op jit(solution)/shard_map/ppermute | solution.py:643
  58.6 9.4 %collective-permute-start.20 = (s16[272,128]{1,0:T(8,128)(2,1)S(1)}, s16[272,128]{1,0:T(8,128)(2,1)S(1)}, u32[]{:S(2)}, u32[]{:S(2)}) collective-permute-start(s16[272,128]{1,0:T(8,128)(2,1)S(1)} %code.1.refs_0_), channel_id=1, source_target_pairs={{0,24},{8,16},{16,8},{24,0},{1,25},{9,17},{17,9},{25,1},{2,26},{10... | collective-permute-start | bytes 208904 | tf_op jit(solution)/shard_map/ppermute | solution.py:643
  61.9 6.0 %collective-permute-start.19 = (s16[272,128]{1,0:T(8,128)(2,1)S(1)}, s16[272,128]{1,0:T(8,128)(2,1)S(1)}, u32[]{:S(2)}, u32[]{:S(2)}) collective-permute-start(s16[272,128]{1,0:T(8,128)(2,1)S(1)} %code.1.refs_0_), channel_id=1, source_target_pairs={{0,16},{8,24},{16,0},{24,8},{1,17},{9,25},{17,1},{25,9},{2,18},{10... | collective-permute-start | bytes 208904 | tf_op jit(solution)/shard_map/ppermute | solution.py:643
  62.0 6.0 %collective-permute-start.18 = (s16[272,128]{1,0:T(8,128)(2,1)S(1)}, s16[272,128]{1,0:T(8,128)(2,1)S(1)}, u32[]{:S(2)}, u32[]{:S(2)}) collective-permute-start(s16[272,128]{1,0:T(8,128)(2,1)S(1)} %code.1.refs_0_), channel_id=1, source_target_pairs={{0,8},{8,0},{16,24},{24,16},{1,9},{9,1},{17,25},{25,17},{2,10},{10... | collective-permute-start | bytes 208904 | tf_op jit(solution)/shard_map/ppermute | solution.py:643
  68.1 5.3 %collective-permute-start.24 = (s16[272,128]{1,0:T(8,128)(2,1)S(1)}, s16[272,128]{1,0:T(8,128)(2,1)S(1)}, u32[]{:S(2)}, u32[]{:S(2)}) collective-permute-start(s16[272,128]{1,0:T(8,128)(2,1)S(1)} %code_sum.1.refs_0_), channel_id=1, source_target_pairs={{0,6},{1,7},{2,4},{3,5},{4,2},{5,3},{6,0},{7,1},{8,14},{9,15},{10,... | collective-permute-start | bytes 208904 | tf_op jit(solution)/shard_map/ppermute | solution.py:643
  69.7 4.5 %collective-permute-start.28 = (s16[272,128]{1,0:T(8,128)(2,1)S(1)}, s16[272,128]{1,0:T(8,128)(2,1)S(1)}, u32[]{:S(2)}, u32[]{:S(2)}) collective-permute-start(s16[272,128]{1,0:T(8,128)(2,1)S(1)} %code_sum.1.refs_0_), channel_id=1, source_target_pairs={{0,4},{1,5},{2,6},{3,7},{4,0},{5,1},{6,2},{7,3},{8,12},{9,13},{10,... | collective-permute-start | bytes 208904 | tf_op jit(solution)/shard_map/ppermute | solution.py:643
  71.2 4.3 %collective-permute-start.26 = (s16[272,128]{1,0:T(8,128)(2,1)S(1)}, s16[272,128]{1,0:T(8,128)(2,1)S(1)}, u32[]{:S(2)}, u32[]{:S(2)}) collective-permute-start(s16[272,128]{1,0:T(8,128)(2,1)S(1)} %code_sum.1.refs_0_), channel_id=1, source_target_pairs={{0,2},{1,3},{2,0},{3,1},{4,6},{5,7},{6,4},{7,5},{8,10},{9,11},{10,... | collective-permute-start | bytes 208904 | tf_op jit(solution)/shard_map/ppermute | solution.py:643
  71.7 4.3 %collective-permute-start.25 = (s16[272,128]{1,0:T(8,128)(2,1)S(1)}, s16[272,128]{1,0:T(8,128)(2,1)S(1)}, u32[]{:S(2)}, u32[]{:S(2)}) collective-permute-start(s16[272,128]{1,0:T(8,128)(2,1)S(1)} %code_sum.1.refs_0_), channel_id=1, source_target_pairs={{0,1},{1,0},{2,3},{3,2},{4,5},{5,4},{6,7},{7,6},{8,9},{9,8},{10,11... | collective-permute-start | bytes 208904 | tf_op jit(solution)/shard_map/ppermute | solution.py:643
  74.2 1.8 %collective-permute-start.29 = (s16[272,128]{1,0:T(8,128)(2,1)S(1)}, s16[272,128]{1,0:T(8,128)(2,1)S(1)}, u32[]{:S(2)}, u32[]{:S(2)}) collective-permute-start(s16[272,128]{1,0:T(8,128)(2,1)S(1)} %collective-permute-done.28.refs_4_), channel_id=1, source_target_pairs={{0,1},{1,0},{2,3},{3,2},{4,5},{5,4},{6,7},{7,6},{8,9},{9,8},{10,11... | collective-permute-start | bytes 208904 | tf_op jit(solution)/shard_map/ppermute | solution.py:643
  75.5 1.3 %collective-permute-start.27 = (s16[272,128]{1,0:T(8,128)(2,1)S(1)}, s16[272,128]{1,0:T(8,128)(2,1)S(1)}, u32[]{:S(2)}, u32[]{:S(2)}) collective-permute-start(s16[272,128]{1,0:T(8,128)(2,1)S(1)} %collective-permute-done.26.refs_2_), channel_id=1, source_target_pairs={{0,1},{1,0},{2,3},{3,2},{4,5},{5,4},{6,7},{7,6},{8,9},{9,8},{10,11... | collective-permute-start | bytes 208904 | tf_op jit(solution)/shard_map/ppermute | solution.py:643
  75.5 1.4 %collective-permute-start.30 = (s16[272,128]{1,0:T(8,128)(2,1)S(1)}, s16[272,128]{1,0:T(8,128)(2,1)S(1)}, u32[]{:S(2)}, u32[]{:S(2)}) collective-permute-start(s16[272,128]{1,0:T(8,128)(2,1)S(1)} %collective-permute-done.24.refs_6_), channel_id=1, source_target_pairs={{0,1},{1,0},{2,3},{3,2},{4,5},{5,4},{6,7},{7,6},{8,9},{9,8},{10,11... | collective-permute-start | bytes 208904 | tf_op jit(solution)/shard_map/ppermute | solution.py:643
